TPU v7x, 32 devices: a whole 2x2x4 slice. The times are simulated.
32 devices in a mesh: wide: 8 (over z, y), narrow: 4 (over x, core).
Axes of the slice: x: 2, y: 2, z: 4, core: 2. Of those that a mesh axis runs over, the one named last changes fastest.
Arguments:
- images: float32 [3, 64, 1024], P(None, ('wide', 'narrow')), may hold values from -0.5 to 0.49
- noise_seeds: int32 [64], P(('wide', 'narrow')), may hold values from 0 to 1073741823
- valid_shape: int32 [64, 2], P(('wide', 'narrow')), may hold values from 11 to 32, as said below
- conv_in: float32 [378, 512], P(None, 'narrow')
- mixer: float32 [3, 512, 512], P(None, None, 'narrow')
- conv_out: float32 [512, 756], P('narrow')
- hidden_bias: float32 [3, 2, 512], P(None, None, 'narrow')
- flow_params: float32 [3852], replicated
- conv_in_first: float32 [378, 512], P(None, 'narrow')
- mixer_first: float32 [3, 512, 512], P(None, None, 'narrow')
- conv_out_first: float32 [512, 756], P('narrow')
- bias_first: float32 [3, 2, 512], P(None, None, 'narrow')
- flow_first: float32 [3852], replicated, may hold values from -0.1 to 0.1
- conv_in_second: float32 [378, 512], P(None, 'narrow'), may hold values from 3.8146972e-08 to 1.5258789e-07
- mixer_second: float32 [3, 512, 512], P(None, None, 'narrow'), may hold values from 3.8146972e-08 to 1.5258789e-07
- conv_out_second: float32 [512, 756], P('narrow'), may hold values from 3.8146972e-08 to 1.5258789e-07
- bias_second: float32 [3, 2, 512], P(None, None, 'narrow'), may hold values from 1.5258789e-07 to 6.1035155e-07
- flow_second: float32 [3852], replicated, may hold values from 0.0004 to 0.0016
Outputs:
- conv_in_new: float32 [378, 512], P(None, 'narrow')
- mixer_new: float32 [3, 512, 512], P(None, None, 'narrow')
- conv_out_new: float32 [512, 756], P('narrow')
- bias_new: float32 [3, 2, 512], P(None, None, 'narrow')
- flow_new: float32 [3852], replicated
- conv_in_moment: float32 [378, 512], P(None, 'narrow')
- mixer_moment: float32 [3, 512, 512], P(None, None, 'narrow')
- conv_out_moment: float32 [512, 756], P('narrow')
- bias_moment: float32 [3, 2, 512], P(None, None, 'narrow')
- flow_moment: float32 [3852], replicated
- conv_in_square: float32 [378, 512], P(None, 'narrow')
- mixer_square: float32 [3, 512, 512], P(None, None, 'narrow')
- conv_out_square: float32 [512, 756], P('narrow')
- bias_square: float32 [3, 2, 512], P(None, None, 'narrow')
- flow_square: float32 [3852], replicated
- conv_in_half: bfloat16 [378, 512], P(None, 'narrow')
- mixer_half: bfloat16 [3, 512, 512], P(None, None, 'narrow')
- conv_out_half: bfloat16 [512, 756], P('narrow')
- weight_norms: float32 [15], replicated
- update_norms: float32 [15], replicated
- loss_sum: float32 [], replicated
- valid_dims: float32 [], replicated
Inputs may be any that keep to these rules, and one draw needn't show every extreme that they name: A pixel of image b is valid where its row is under valid_shape[b,0] and its column under valid_shape[b,1].
All inputs are finite; a program needn't handle non-finite values.
Results may differ from a plain program's by a relative error of at most 0.0013.
The roundings to bfloat16 on the way count: a program that leaves them out, or rounds other values in their place, can miss the bound.
Values may be sent and summed in bfloat16 or wider, within the bound.
No kernel may reach another device: no remote copies, remote signals or barrier semaphores. Data moves between devices by JAX's collectives and lax.ppermute only.
A program may use at most 128 MiB of HBM per device.

v0:
```python
import jax
import jax.numpy as jnp
from jax import lax
from jax.sharding import PartitionSpec as P

C1 = 12
IMG_SIDE = 32
STEP = 5


HIGHEST_PRECISION = lax.Precision.HIGHEST
LOG_TWO_PI = 1.8378770664093453
LOG_TWO = 0.6931471805599453
FIRST_BETA = 0.5
SECOND_BETA = 0.5
EPSILON = 1e-06
WEIGHT_DECAY = 0.01
LEARN_RATE = 0.25
TAP_OFFSETS = [(-1, -1), (-1, 0), (-1, 1), (0, -1), (0, 0), (0, 1), (1, -1), (1, 0), (1, 1)]


def noise_field(seed_values, grid_side):
    pixel_count = grid_side * grid_side
    position = jnp.arange(3 * pixel_count, dtype=jnp.int32).reshape(3, 1, pixel_count)
    hashed = seed_values.astype(jnp.int32).reshape(1, -1, 1) + position * jnp.int32(-1640531527)
    hashed = hashed ^ lax.shift_right_logical(hashed, jnp.full_like(hashed, 15))
    hashed = hashed * jnp.int32(739267321)
    hashed = hashed ^ lax.shift_right_logical(hashed, jnp.full_like(hashed, 13))
    return ((hashed & jnp.int32(16777215)).astype(jnp.float32) + 0.5) * 2.0 ** (-24)


def pixel_weights(valid_shape, image_side, level_index):
    block_side = 2**level_index
    grid_side = image_side // block_side
    starts = jnp.arange(grid_side, dtype=jnp.int32) * block_side
    row_share = (
        jnp.clip(valid_shape[:, 0:1] - starts[None, :], 0, block_side).astype(jnp.float32)
        / block_side
    )
    col_share = (
        jnp.clip(valid_shape[:, 1:2] - starts[None, :], 0, block_side).astype(jnp.float32)
        / block_side
    )
    return (row_share[:, :, None] * col_share[:, None, :]).reshape(1, -1)


def squeeze_grid(values, image_count, grid_side):
    channels = values.shape[0]
    half_side = grid_side // 2
    values = values.reshape(channels, image_count, half_side, 2, half_side, 2).transpose(
        0, 3, 5, 1, 2, 4
    )
    return values.reshape(channels * 4, image_count * half_side * half_side)


def unsqueeze_grid(values, image_count, grid_side):
    channels = values.shape[0] // 4
    half_side = grid_side // 2
    values = values.reshape(channels, 2, 2, image_count, half_side, half_side).transpose(
        0, 3, 4, 1, 5, 2
    )
    return values.reshape(channels, image_count * grid_side * grid_side)


def tap_sum(values, image_count, grid_side, direction):
    channels = values.shape[0] // 9
    padded = jnp.pad(
        values.reshape(9, channels, image_count, grid_side, grid_side),
        ((0, 0), (0, 0), (0, 0), (1, 1), (1, 1)),
    )
    result = jnp.zeros((channels, image_count, grid_side, grid_side), values.dtype)
    for tap_index, (row_step, col_step) in enumerate(TAP_OFFSETS):
        row_start = 1 + direction * row_step
        col_start = 1 + direction * col_step
        result = (
            result
            + padded[
                tap_index,
                :,
                :,
                row_start : row_start + grid_side,
                col_start : col_start + grid_side,
            ]
        )
    return result.reshape(channels, -1)


def tap_stack(values, image_count, grid_side, direction):
    channels = values.shape[0]
    padded = jnp.pad(
        values.reshape(channels, image_count, grid_side, grid_side),
        ((0, 0), (0, 0), (1, 1), (1, 1)),
    )
    shifted = []
    for row_step, col_step in TAP_OFFSETS:
        row_start = 1 + direction * row_step
        col_start = 1 + direction * col_step
        shifted.append(
            padded[:, :, row_start : row_start + grid_side, col_start : col_start + grid_side]
        )
    return jnp.stack(shifted, 0).reshape(9 * channels, image_count * grid_side * grid_side)


def row_bounds(base):
    return [0, 9 * base // 2, 27 * base // 2, 63 * base // 2]


def col_bounds(base):
    return [0, 9 * base, 27 * base, 63 * base]


def flow_bounds(base):
    lengths = [
        5 * base + 3 * base * base // 2,
        10 * base + 6 * base * base,
        24 * base + 16 * base * base,
    ]
    return [0, lengths[0], lengths[0] + lengths[1], lengths[0] + lengths[1] + lengths[2]]


def unpack_level(segment, channels, is_last):
    half = channels // 2
    names = ["bias", "logs", "block", "outbias", "outscale"]
    lengths = [channels, channels, channels * channels, channels, channels]
    if is_last:
        names = names + ["priorbias"]
        lengths = lengths + [2 * channels]
    else:
        names = names + ["priormatrix", "priorbias"]
        lengths = lengths + [half * channels, channels]
    pieces = {}
    offset = 0
    for name, length in zip(names, lengths):
        pieces[name] = segment[offset : offset + length]
        offset = offset + length
    pieces["block"] = pieces["block"].reshape(channels, channels)
    if not is_last:
        pieces["priormatrix"] = pieces["priormatrix"].reshape(half, channels)
    return pieces


def triangle_factors(block):
    channels = block.shape[0]
    lower = jnp.tril(block, -1) + jnp.eye(channels, dtype=block.dtype)
    signs = (1 - 2 * (jnp.arange(channels) % 2)).astype(block.dtype)
    upper = jnp.triu(block, 1) + jnp.diag(signs * jnp.exp(jnp.diagonal(block)))
    return (lower, upper)


def mixing_matrix(block):
    lower, upper = triangle_factors(block)
    return jnp.dot(lower, upper, precision=HIGHEST_PRECISION)[::-1]


def lower_solve(lower, values):
    channels = lower.shape[0]
    strict = jnp.tril(lower, -1)
    solved = jnp.zeros_like(values)
    for index in range(channels):
        carried = jnp.dot(strict[index], solved, precision=HIGHEST_PRECISION)
        solved = solved.at[index].set(values[index] - carried)
    return solved


def upper_solve(upper, values):
    channels = upper.shape[0]
    strict = jnp.triu(upper, 1)
    diagonal = jnp.diagonal(upper)
    solved = jnp.zeros_like(values)
    for index in range(channels - 1, -1, -1):
        carried = jnp.dot(strict[index], solved, precision=HIGHEST_PRECISION)
        solved = solved.at[index].set((values[index] - carried) / diagonal[index])
    return solved


def gaussian_log(latent, mean, log_scale):
    return -0.5 * (LOG_TWO_PI + 2.0 * log_scale + (latent - mean) ** 2 * jnp.exp(-2.0 * log_scale))


def level_pre(flow_state, segment, share_total, channels, is_last):
    pieces = unpack_level(segment, channels, is_last)
    normed = (flow_state + pieces["bias"][:, None]) * jnp.exp(pieces["logs"])[:, None]
    mixed = jnp.dot(mixing_matrix(pieces["block"]), normed, precision=HIGHEST_PRECISION)
    pre_term = -share_total * (jnp.sum(pieces["logs"]) + jnp.sum(jnp.diagonal(pieces["block"])))
    return (mixed[: channels // 2], mixed[channels // 2 :], pre_term)


def level_post(
    first_half, second_half, net_raw, segment, shares, channels, is_last, image_count, grid_side
):
    pieces = unpack_level(segment, channels, is_last)
    half = channels // 2
    output = (net_raw + pieces["outbias"][:, None]) * jnp.exp(3.0 * pieces["outscale"])[:, None]
    logit = output[half:] + 2.0
    latent = (second_half + output[:half]) * jax.nn.sigmoid(logit)
    log_det = jnp.sum(shares * jax.nn.log_sigmoid(logit))
    if is_last:
        joined = jnp.concatenate([first_half, latent], 0)
        prior_bias = pieces["priorbias"]
        log_prior = jnp.sum(
            shares * gaussian_log(joined, prior_bias[:channels, None], prior_bias[channels:, None])
        )
        after = first_half
    else:
        stats = (
            jnp.dot(pieces["priormatrix"].T, first_half, precision=HIGHEST_PRECISION)
            + pieces["priorbias"][:, None]
        )
        log_prior = jnp.sum(shares * gaussian_log(latent, stats[:half], stats[half:]))
        after = squeeze_grid(first_half, image_count, grid_side)
    return (after, latent, -(log_det + log_prior))


def level_invert(first_half, latent, net_raw, segment, channels, is_last):
    pieces = unpack_level(segment, channels, is_last)
    half = channels // 2
    output = (net_raw + pieces["outbias"][:, None]) * jnp.exp(3.0 * pieces["outscale"])[:, None]
    second_half = latent / jax.nn.sigmoid(output[half:] + 2.0) - output[:half]
    mixed = jnp.concatenate([first_half, second_half], 0)
    lower, upper = triangle_factors(pieces["block"])
    solved = lower_solve(lower, mixed[::-1])
    normed = upper_solve(upper, solved)
    level_input = normed * jnp.exp(-pieces["logs"])[:, None] - pieces["bias"][:, None]
    return (level_input, second_half)


def silu_slope(values):
    sigmoid_values = jax.nn.sigmoid(values)
    return sigmoid_values * (1.0 + values * (1.0 - sigmoid_values))


def contract_rows(first_matrix, second_matrix):
    return lax.dot_general(
        first_matrix, second_matrix, (((0,), (0,)), ((), ())), preferred_element_type=jnp.float32
    )


def contract_columns(first_matrix, second_matrix):
    return lax.dot_general(
        first_matrix, second_matrix, (((1,), (1,)), ((), ())), preferred_element_type=jnp.float32
    )


def coupling_forward(first_half, rows_in, mix_cols, rows_out, biases, group_count, grid_side):
    sent = first_half.astype(jnp.bfloat16)
    sent = lax.all_gather(sent, "narrow", axis=1, tiled=True)
    stacked = tap_stack(sent, group_count, grid_side, 1)
    hidden_one = contract_rows(rows_in, stacked) + biases[0][:, None]
    gathered = jax.nn.silu(hidden_one).astype(jnp.bfloat16)
    gathered = lax.all_gather(gathered, "narrow", axis=0, tiled=True)
    hidden_two = contract_rows(mix_cols, gathered) + biases[1][:, None]
    active_two = jax.nn.silu(hidden_two).astype(jnp.bfloat16)
    partial_out = tap_sum(contract_rows(rows_out, active_two), group_count, grid_side, 1)
    net_raw = lax.psum_scatter(
        partial_out.astype(jnp.bfloat16), "narrow", scatter_dimension=1, tiled=True
    ).astype(jnp.float32)
    return (net_raw, (stacked, hidden_one, gathered, hidden_two, active_two))


def coupling_backward(grad_raw, saved, rows_in, mix_cols, rows_out, group_count, grid_side):
    stacked, hidden_one, gathered, hidden_two, active_two = saved
    grad_all = grad_raw.astype(jnp.bfloat16)
    grad_all = lax.all_gather(grad_all, "narrow", axis=1, tiled=True)
    grad_spread = tap_stack(grad_all, group_count, grid_side, -1)
    grad_rows_out = contract_columns(active_two, grad_spread)
    grad_act_two = jnp.dot(rows_out, grad_spread, preferred_element_type=jnp.float32)
    grad_two = (grad_act_two * silu_slope(hidden_two)).astype(jnp.bfloat16)
    grad_mix = contract_columns(gathered, grad_two)
    grad_act_one = jnp.dot(mix_cols, grad_two, preferred_element_type=jnp.float32)
    grad_act_one = lax.psum_scatter(
        grad_act_one.astype(jnp.bfloat16), "narrow", scatter_dimension=0, tiled=True
    ).astype(jnp.float32)
    grad_one = (grad_act_one * silu_slope(hidden_one)).astype(jnp.bfloat16)
    grad_rows_in = contract_columns(stacked, grad_one)
    grad_stacked = jnp.dot(rows_in, grad_one, preferred_element_type=jnp.float32)
    grad_input = tap_sum(grad_stacked, group_count, grid_side, -1)
    grad_input = lax.psum_scatter(grad_input, "narrow", scatter_dimension=1, tiled=True)
    grad_bias = jnp.stack(
        [jnp.sum(grad_one.astype(jnp.float32), 1), jnp.sum(grad_two.astype(jnp.float32), 1)]
    )
    return (grad_input, grad_rows_in, grad_mix, grad_rows_out, grad_bias)


def lamb_moments(weight, gradient, first_old, second_old):
    first_new = FIRST_BETA * first_old + (1.0 - FIRST_BETA) * gradient
    second_new = SECOND_BETA * second_old + (1.0 - SECOND_BETA) * gradient * gradient
    update = (
        first_new
        / (1.0 - FIRST_BETA**STEP)
        / (jnp.sqrt(second_new / (1.0 - SECOND_BETA**STEP)) + EPSILON)
        + WEIGHT_DECAY * weight
    )
    return (first_new, second_new, update)


def group_squares(arrays, base):
    row_edges, col_edges, seg_edges = (row_bounds(base), col_bounds(base), flow_bounds(base))
    sums = [jnp.sum(arrays[0][row_edges[index] : row_edges[index + 1]] ** 2) for index in range(3)]
    sums = sums + [jnp.sum(arrays[1][index] ** 2) for index in range(3)]
    sums = sums + [
        jnp.sum(arrays[2][:, col_edges[index] : col_edges[index + 1]] ** 2) for index in range(3)
    ]
    sums = sums + [jnp.sum(arrays[3][index] ** 2) for index in range(3)]
    sums = sums + [
        jnp.sum(arrays[4][seg_edges[index] : seg_edges[index + 1]] ** 2) for index in range(3)
    ]
    return jnp.stack(sums)


def apply_ratio(weights, updates, ratio, base):
    row_edges, col_edges, seg_edges = (row_bounds(base), col_bounds(base), flow_bounds(base))
    new_in = jnp.concatenate(
        [
            weights[0][row_edges[index] : row_edges[index + 1]]
            - LEARN_RATE * ratio[index] * updates[0][row_edges[index] : row_edges[index + 1]]
            for index in range(3)
        ],
        0,
    )
    new_mix = weights[1] - LEARN_RATE * ratio[3:6][:, None, None] * updates[1]
    new_out = jnp.concatenate(
        [
            weights[2][:, col_edges[index] : col_edges[index + 1]]
            - LEARN_RATE * ratio[6 + index] * updates[2][:, col_edges[index] : col_edges[index + 1]]
            for index in range(3)
        ],
        1,
    )
    new_bias = weights[3] - LEARN_RATE * ratio[9:12][:, None, None] * updates[3]
    new_flow = jnp.concatenate(
        [
            weights[4][seg_edges[index] : seg_edges[index + 1]]
            - LEARN_RATE * ratio[12 + index] * updates[4][seg_edges[index] : seg_edges[index + 1]]
            for index in range(3)
        ]
    )
    return (new_in, new_mix, new_out, new_bias, new_flow)


def body(
    images,
    noise_seeds,
    valid_shape,
    conv_in,
    mixer,
    conv_out,
    hidden_bias,
    flow_params,
    conv_in_first,
    mixer_first,
    conv_out_first,
    bias_first,
    flow_first,
    conv_in_second,
    mixer_second,
    conv_out_second,
    bias_second,
    flow_second,
):
    local_count = images.shape[1]
    own_count = jnp.sum((valid_shape[:, 0] * valid_shape[:, 1]).astype(jnp.float32))
    valid_dims = 3.0 * lax.psum(own_count, ("wide", "narrow"))
    pixels = images + noise_field(noise_seeds, IMG_SIDE) / 256.0
    flow_state = squeeze_grid(pixels.reshape(3, -1), local_count, IMG_SIDE)
    row_edges, col_edges, seg_edges = (row_bounds(C1), col_bounds(C1), flow_bounds(C1))
    half_in = conv_in.astype(jnp.bfloat16)
    half_mix = mixer.astype(jnp.bfloat16)
    half_out = conv_out.astype(jnp.bfloat16)
    group_count = local_count * lax.axis_size("narrow")
    records = []
    loss_local = jnp.zeros((), jnp.float32)
    for level_index in range(3):
        channels = C1 * 2**level_index
        grid_side = IMG_SIDE // 2 ** (level_index + 1)
        is_last = level_index == 2
        shares = pixel_weights(valid_shape, IMG_SIDE, level_index + 1)
        segment = flow_params[seg_edges[level_index] : seg_edges[level_index + 1]]
        first_half, second_half, pre_term = level_pre(
            flow_state, segment, jnp.sum(shares), channels, is_last
        )
        net_raw, saved = coupling_forward(
            first_half,
            half_in[row_edges[level_index] : row_edges[level_index + 1]],
            half_mix[level_index],
            half_out[:, col_edges[level_index] : col_edges[level_index + 1]],
            hidden_bias[level_index],
            group_count,
            grid_side,
        )
        after, latent, post_term = level_post(
            first_half,
            second_half,
            net_raw,
            segment,
            shares,
            channels,
            is_last,
            local_count,
            grid_side,
        )
        loss_local = loss_local + pre_term + post_term
        records.append(latent)
        flow_state = after
    scale_seed = 1.0 / (valid_dims * LOG_TWO)
    rebuilt = flow_state
    grad_after = jnp.zeros_like(flow_state)
    grads_in = [None, None, None]
    grads_mix = [None, None, None]
    grads_out = [None, None, None]
    grads_bias = [None, None, None]
    grads_flow = [None, None, None]
    for level_index in (2, 1, 0):
        channels = C1 * 2**level_index
        grid_side = IMG_SIDE // 2 ** (level_index + 1)
        is_last = level_index == 2
        shares = pixel_weights(valid_shape, IMG_SIDE, level_index + 1)
        share_total = jnp.sum(shares)
        segment = flow_params[seg_edges[level_index] : seg_edges[level_index + 1]]
        in_rows = half_in[row_edges[level_index] : row_edges[level_index + 1]]
        mix_cols = half_mix[level_index]
        out_rows = half_out[:, col_edges[level_index] : col_edges[level_index + 1]]
        first_half = rebuilt if is_last else unsqueeze_grid(rebuilt, local_count, grid_side)
        net_raw, saved = coupling_forward(
            first_half,
            in_rows,
            mix_cols,
            out_rows,
            hidden_bias[level_index],
            group_count,
            grid_side,
        )
        level_input, second_half = level_invert(
            first_half, records[level_index], net_raw, segment, channels, is_last
        )
        rebuilt = level_input

        def post_piece(half_one, half_two, raw_values, segment_values):
            return level_post(
                half_one,
                half_two,
                raw_values,
                segment_values,
                shares,
                channels,
                is_last,
                local_count,
                grid_side,
            )

        post_values, pull_post = jax.vjp(post_piece, first_half, second_half, net_raw, segment)
        after_cotangent = jnp.zeros_like(post_values[0]) if is_last else grad_after
        grad_first, grad_second, grad_raw, grad_segment = pull_post(
            (after_cotangent, jnp.zeros_like(post_values[1]), scale_seed)
        )
        grad_net, grad_rows_in, grad_mix, grad_rows_out, grad_bias = coupling_backward(
            grad_raw, saved, in_rows, mix_cols, out_rows, group_count, grid_side
        )

        def pre_piece(state_values, segment_values):
            return level_pre(state_values, segment_values, share_total, channels, is_last)

        unused, pull_pre = jax.vjp(pre_piece, level_input, segment)
        grad_after, grad_pre_segment = pull_pre((grad_first + grad_net, grad_second, scale_seed))
        grads_in[level_index] = grad_rows_in
        grads_mix[level_index] = grad_mix
        grads_out[level_index] = grad_rows_out
        grads_bias[level_index] = grad_bias
        grads_flow[level_index] = grad_segment + grad_pre_segment
    net_grads = (
        jnp.concatenate(grads_in, 0),
        jnp.stack(grads_mix),
        jnp.concatenate(grads_out, 1),
        jnp.stack(grads_bias),
    )
    grad_in, grad_mixer, grad_out, grad_hidden = lax.psum(
        (net_grads[0], net_grads[1], net_grads[2], net_grads[3]), "wide"
    )
    grad_flow, loss_total = lax.psum((jnp.concatenate(grads_flow), loss_local), ("wide", "narrow"))
    weights = (conv_in, mixer, conv_out, hidden_bias, flow_params)
    gradients = (grad_in, grad_mixer, grad_out, grad_hidden, grad_flow)
    firsts_old = (conv_in_first, mixer_first, conv_out_first, bias_first, flow_first)
    seconds_old = (conv_in_second, mixer_second, conv_out_second, bias_second, flow_second)
    moved = [
        lamb_moments(weight, gradient, first_old, second_old)
        for weight, gradient, first_old, second_old in zip(
            weights, gradients, firsts_old, seconds_old
        )
    ]
    updates = tuple((entry[2] for entry in moved))
    weight_squares = group_squares(weights, C1)
    update_squares = group_squares(updates, C1)
    shard_weight, shard_update = lax.psum((weight_squares[:12], update_squares[:12]), "narrow")
    weight_norms = jnp.sqrt(jnp.concatenate([shard_weight, weight_squares[12:]]))
    update_norms = jnp.sqrt(jnp.concatenate([shard_update, update_squares[12:]]))
    fresh = apply_ratio(weights, updates, weight_norms / update_norms, C1)
    loss_sum = loss_total / LOG_TWO + 8.0 * valid_dims
    return (
        fresh[0],
        fresh[1],
        fresh[2],
        fresh[3],
        fresh[4],
        moved[0][0],
        moved[1][0],
        moved[2][0],
        moved[3][0],
        moved[4][0],
        moved[0][1],
        moved[1][1],
        moved[2][1],
        moved[3][1],
        moved[4][1],
        fresh[0].astype(jnp.bfloat16),
        fresh[1].astype(jnp.bfloat16),
        fresh[2].astype(jnp.bfloat16),
        weight_norms,
        update_norms,
        loss_sum,
        valid_dims,
    )


def solution(mesh):
    placed = (
        P(None, ("wide", "narrow"), None),
        P(("wide", "narrow")),
        P(("wide", "narrow"), None),
        P(None, "narrow"),
        P(None, None, "narrow"),
        P("narrow", None),
        P(None, None, "narrow"),
        P(),
        P(None, "narrow"),
        P(None, None, "narrow"),
        P("narrow", None),
        P(None, None, "narrow"),
        P(),
        P(None, "narrow"),
        P(None, None, "narrow"),
        P("narrow", None),
        P(None, None, "narrow"),
        P(),
    )
    return jax.shard_map(
        body,
        mesh=mesh,
        in_specs=placed,
        out_specs=(
            P(None, "narrow"),
            P(None, None, "narrow"),
            P("narrow", None),
            P(None, None, "narrow"),
            P(),
            P(None, "narrow"),
            P(None, None, "narrow"),
            P("narrow", None),
            P(None, None, "narrow"),
            P(),
            P(None, "narrow"),
            P(None, None, "narrow"),
            P("narrow", None),
            P(None, None, "narrow"),
            P(),
            P(None, "narrow"),
            P(None, None, "narrow"),
            P("narrow", None),
            P(),
            P(),
            P(),
            P(),
        ),
        check_vma=False,
    )
```

profile of v0, /device:TPU:0, one launch (start us, length us, event | category | flops | bytes accessed | tf_op | source)
XLA Modules:
  0.0 822.9 jit_solution(5937055878132801354)
XLA Ops:
  28.8 6.2 all-gather
  37.0 5.6 all_gather.42
  44.7 5.2 all_gather.43
  51.1 41.2 %psum.64 = f32[]{:T(128)} all-reduce(f32[]{:T(128)} %convert_reduce_fusion.6), channel_id=1, replica_groups=mesh['wide'=8,'narrow'=4] {'wide','narrow'}, use_global_device_ids=true, to_apply=%region_20.21 | all-reduce | flops 1 | bytes 8 | tf_op jit(solution)/shard_map/psum | solution.py:362
  100.8 3.5 reshape.5104
  104.6 8.0 all_gather.44
  113.3 2.8 reshape.5105
  119.8 5.2 all_gather.53
  127.5 6.8 fusion.420
  142.8 5.4 all_gather.48
  245.1 16.4 %reduce-scatter.28.cloned.1.call-done = f32[24,32]{0,1:T(8,128)} async-done(((f32[24,128]{0,1:T(8,128)}), f32[24,32]{0,1:T(8,128)}) %reduce-scatter.28.cloned.1.call-update) | async-done | bytes 3088 | tf_op jit(solution)/shard_map/reduce_scatter | solution.py:277
  264.2 5.4 all_gather.45
  272.2 3.0 reshape.5108
  276.9 7.3 all_gather.46
  287.3 2.8 reshape.5109
  290.1 6.9 fusion.423
  298.8 19.4 %reduce-scatter.36.cloned.1.call-done = bf16[128,24]{1,0:T(8,128)(2,1)} async-done(((bf16[512,24]{1,0:T(8,128)(2,1)}), bf16[128,24]{1,0:T(8,128)(2,1)}) %reduce-scatter.36.cloned.1.call-update) | async-done | bytes 6160
  321.7 5.3 all_gather.52
  335.1 3.9 reshape.5162
  339.0 16.6 %reduce-scatter.40.cloned.1.call-done = bf16[128,512]{1,0:T(8,128)(2,1)} async-done(((bf16[512,512]{1,0:T(8,128)(2,1)}), bf16[128,512]{1,0:T(8,128)(2,1)}) %reduce-scatter.40.cloned.1.call-update) | async-done | bytes 131088
  359.7 2.9 reshape.5176
  395.8 8.1 stack.409
  410.9 5.5 scatter_fusion.2
  461.4 7.2 all_gather.47
  472.1 3.2 reshape.5159
  475.4 2.4 multiply_convert_fusion.2
  485.9 3.0 scatter_fusion.1
  498.7 2.5 convolution_bitcast_fusion.2
  502.1 5.3 reshape.5163
  507.4 5.2 fusion.389
  518.9 3.3 multiply_convert_fusion.1
  523.2 5.3 reshape.5164
  528.5 5.5 fusion.392
  543.4 18.6 %reduce-scatter.26.cloned.1.call-done = bf16[12,512]{1,0:T(8,128)(2,1)} async-done(((bf16[12,2048]{1,0:T(8,128)(2,1)}), bf16[12,512]{1,0:T(8,128)(2,1)}) %reduce-scatter.26.cloned.1.call-update) | async-done | bytes 12304 | tf_op jit(solution)/shard_map/reduce_scatter | solution.py:254
  566.4 5.2 all_gather.51
  587.2 7.2 reshape.5166
  596.6 2.5 copy.619
  610.4 2.3 convolution_bitcast_fusion.7
  613.7 17.0 %reduce-scatter.38.cloned.1.call-done = bf16[128,2048]{1,0:T(8,128)(2,1)} async-done(((bf16[512,2048]{1,0:T(8,128)(2,1)}), bf16[128,2048]{1,0:T(8,128)(2,1)}) %reduce-scatter.38.cloned.1.call-update) | async-done | bytes 524304
  635.3 21.7 %psum.68 = f32[3,2,128]{2,1,0:T(2,128)S(1)} all-reduce(f32[3,2,128]{2,1,0:T(2,128)S(1)} %pad_maximum_fusion.5), channel_id=1, replica_groups=mesh['wide'=8,'narrow'=4] {'wide'}, use_global_device_ids=true, to_apply=%region_44.45 | all-reduce | flops 768 | bytes 6144 | tf_op jit(solution)/shard_map/psum | solution.py:475
  657.0 2.2 reshape.5179
  670.2 13.8 %reduce-scatter.32.cloned.1.call-done = f32[6,512]{1,0:T(8,128)} async-done(((f32[6,2048]{1,0:T(8,128)}), f32[6,512]{1,0:T(8,128)}) %reduce-scatter.32.cloned.1.call-update) | async-done | bytes 12304 | tf_op jit(solution)/shard_map/reduce_scatter | solution.py:277
  688.7 2.2 scatter_fusion
  691.2 40.8 %all-reduce.63 = (f32[3852]{0:T(1024)S(1)}, f32[]{:T(128)}) all-reduce(f32[3852]{0:T(1024)S(1)} %concatenate.430, f32[]{:T(128)S(6)} %add.1925), channel_id=1, replica_groups=mesh['wide'=8,'narrow'=4] {'wide','narrow'}, use_global_device_ids=true, to_apply=%region_78.79 | all-reduce | flops 3853 | bytes 30824 | tf_op jit(solution)/shard_map/psum | solution.py:478
  735.2 39.1 %all-reduce.68.cloned.1.call-done = (f32[378,128]{1,0:T(8,128)}, f32[3,512,128]{2,1,0:T(8,128)}, f32[128,756]{0,1:T(8,128)}) async-done(((f32[378,128]{1,0:T(8,128)}, f32[3,512,128]{2,1,0:T(8,128)}, f32[128,756]{0,1:T(8,128)}), (f32[378,128]{1,0:T(8,128)}, f32[3,512,128]{2,1,0:T(8,128)}, f32[128,756]{0,1:T(8,128)})) %all-reduce.68.cloned.1.call-update) | async-done | bytes 1367056 | tf_op jit(solution)/shard_map/psum | solution.py:475
  783.4 7.8 stack.522
  791.2 6.8 all-reduce.65
  798.1 4.5 fusion.959
  (1412 shorter events, 354.5 us)
Async XLA Ops:
  7.2 108.9 %reduce-scatter.22.cloned.1.call-start = ((), (), s32[]{:S(2)}) async-start(), calls=%async_computation.11 | async-start | bytes 40960 | tf_op jit(solution)/shard_map/reduce_scatter | solution.py:254
  16.5 87.8 %copy-start.232 = (f32[128]{0:T(128)}, f32[128]{0:T(128)S(1)}, u32[]{:S(2)}) copy-start(f32[128]{0:T(128)S(1)} %get-tuple-element.2517) | copy-start | bytes 1540
  16.5 96.1 %copy-start.198 = (f32[128]{0:T(128)}, f32[128]{0:T(128)S(1)}, u32[]{:S(2)}) copy-start(f32[128]{0:T(128)S(1)} %get-tuple-element.2516) | copy-start | bytes 1540
  22.5 113.4 %copy-start.1 = (f32[48,48]{0,1:T(8,128)}, f32[48,48]{0,1:T(8,128)S(1)}, u32[]{:S(2)}) copy-start(f32[48,48]{0,1:T(8,128)S(1)} %get-tuple-element.2372) | copy-start | bytes 27652
  23.1 217.8 %copy-start.60 = (bf16[378,128]{1,0:T(8,128)(2,1)}, bf16[378,128]{1,0:T(8,128)(2,1)S(1)}, u32[]{:S(2)}) copy-start(bf16[378,128]{1,0:T(8,128)(2,1)S(1)} %convert_element_type.341) | copy-start | bytes 290308
  23.2 102.6 %copy-start.85 = (bf16[128,756]{0,1:T(8,128)(2,1)}, bf16[128,756]{0,1:T(8,128)(2,1)S(1)}, u32[]{:S(2)}) copy-start(bf16[128,756]{0,1:T(8,128)(2,1)S(1)} %convert_element_type.345) | copy-start | bytes 580612
  23.3 309.1 %copy-start.19 = (bf16[3,512,128]{2,1,0:T(8,128)(2,1)}, bf16[3,512,128]{2,1,0:T(8,128)(2,1)S(1)}, u32[]{:S(2)}) copy-start(bf16[3,512,128]{2,1,0:T(8,128)(2,1)S(1)} %convert_element_type.343) | copy-start | bytes 1179652
  27.8 123.8 %copy-start.123 = (f32[24,128]{1,0:T(8,128)}, f32[24,128]{1,0:T(8,128)S(1)}, u32[]{:S(2)}) copy-start(f32[24,128]{1,0:T(8,128)S(1)} %fusion.650) | copy-start | bytes 36868
  42.8 83.0 %copy-start.76 = (f32[128,128]{0,1:T(8,128)}, f32[128,128]{0,1:T(8,128)S(1)}, u32[]{:S(2)}) copy-start(f32[128,128]{0,1:T(8,128)S(1)} %fusion.16) | copy-start | bytes 196612
  44.5 195.0 %reduce-scatter.42.cloned.1.call-start = ((), (), s32[]{:S(2)}) async-start(), calls=%async_computation.23 | async-start | bytes 163840
  44.7 105.3 %copy-start.158 = (s32[2]{0:T(128)}, s32[2]{0:T(128)S(1)}, u32[]{:S(2)}) copy-start(s32[2]{0:T(128)S(1)} %get-tuple-element.2312) | copy-start | bytes 28
  44.7 105.3 %copy-start.160 = (s32[2]{0:T(128)}, s32[2]{0:T(128)S(1)}, u32[]{:S(2)}) copy-start(s32[2]{0:T(128)S(1)} %get-tuple-element.2313) | copy-start | bytes 28
  118.4 143.8 %copy-start.83 = (f32[24,32]{0,1:T(8,128)}, f32[24,32]{0,1:T(8,128)S(1)}, u32[]{:S(2)}) copy-start(f32[24,32]{0,1:T(8,128)S(1)} %get-tuple-element.2456) | copy-start | bytes 9220
  127.5 116.8 %reduce-scatter.34.cloned.1.call-start = ((), (), s32[]{:S(2)}) async-start(), calls=%async_computation.19 | async-start | bytes 163840
  135.8 125.7 %reduce-scatter.28.cloned.1.call-start = ((), (), s32[]{:S(2)}) async-start(), calls=%async_computation.16 | async-start | bytes 81920 | tf_op jit(solution)/shard_map/reduce_scatter | solution.py:277
  150.2 148.3 %copy-start.107 = (f32[12,24]{1,0:T(8,128)}, f32[12,24]{1,0:T(8,128)S(1)}, u32[]{:S(2)}) copy-start(f32[12,24]{1,0:T(8,128)S(1)} %reshape.5167) | copy-start | bytes 3460
  151.0 41.1 %copy-start.170 = (f32[128]{0:T(128)}, f32[128]{0:T(128)S(1)}, u32[]{:S(2)}) copy-start(f32[128]{0:T(128)S(1)} %mul.1171) | copy-start | bytes 1540
  165.0 75.3 %copy-start.109 = (f32[128,128]{0,1:T(8,128)S(1)}, f32[128,128]{0,1:T(8,128)}, u32[]{:S(2)}) copy-start(f32[128,128]{0,1:T(8,128)} %get-tuple-element.2649) | copy-start | bytes 196612
  242.6 75.6 %reduce-scatter.36.cloned.1.call-start = ((), (), s32[]{:S(2)}) async-start(), calls=%async_computation.20 | async-start | bytes 163840
  298.4 57.2 %reduce-scatter.40.cloned.1.call-start = ((), (), s32[]{:S(2)}) async-start(), calls=%async_computation.22 | async-start | bytes 655360
  333.8 125.2 %reduce-scatter.30.cloned.1.call-start = ((), (), s32[]{:S(2)}) async-start(), calls=%async_computation.17 | async-start | bytes 40960 | tf_op jit(solution)/shard_map/reduce_scatter | solution.py:277
  371.0 127.7 %all-gather.4.cloned.1.call-start = ((), (), s32[]{:S(2)}) async-start(), calls=%async_computation.12 | async-start | bytes 2621440 | tf_op jit(solution)/shard_map/all_gather | solution.py:250
  373.4 145.5 %all-gather.6.cloned.1.call-start = ((), (), s32[]{:S(2)}) async-start(), calls=%async_computation.14 | async-start | bytes 2621440 | tf_op jit(solution)/shard_map/all_gather | solution.py:250
  410.9 47.2 %copy-start.71 = (f32[128,512]{0,1:T(8,128)S(1)}, f32[128,512]{0,1:T(8,128)}, u32[]{:S(2)}) copy-start(f32[128,512]{0,1:T(8,128)} %copy-done.69) | copy-start | bytes 786436
  410.9 47.2 %copy-start.73 = (bf16[216,512]{0,1:T(8,128)(2,1)S(1)}, bf16[216,512]{0,1:T(8,128)(2,1)}, u32[]{:S(2)}) copy-start(bf16[216,512]{0,1:T(8,128)(2,1)} %copy-done.72) | copy-start | bytes 663556
  419.0 40.0 %copy-start.101 = (f32[12,128]{1,0:T(8,128)S(1)}, f32[12,128]{1,0:T(8,128)}, u32[]{:S(2)}) copy-start(f32[12,128]{1,0:T(8,128)} %get-tuple-element.2458) | copy-start | bytes 18436
  419.0 40.0 %copy-start.102 = (f32[12,128]{1,0:T(8,128)S(1)}, f32[12,128]{1,0:T(8,128)}, u32[]{:S(2)}) copy-start(f32[12,128]{1,0:T(8,128)} %get-tuple-element.2462) | copy-start | bytes 18436
  419.0 40.0 %copy-start.108 = (f32[12,24]{1,0:T(8,128)S(1)}, f32[12,24]{1,0:T(8,128)}, u32[]{:S(2)}) copy-start(f32[12,24]{1,0:T(8,128)} %copy-done.107) | copy-start | bytes 3460
  419.2 40.6 %copy-start.127 = (f32[12,128]{1,0:T(8,128)S(1)}, f32[12,128]{1,0:T(8,128)}, u32[]{:S(2)}) copy-start(f32[12,128]{1,0:T(8,128)} %copy-done.126) | copy-start | bytes 18436
  419.2 40.6 %copy-start.138 = (f32[24,24]{1,0:T(8,128)S(1)}, f32[24,24]{1,0:T(8,128)}, u32[]{:S(2)}) copy-start(f32[24,24]{1,0:T(8,128)} %copy-done.137) | copy-start | bytes 6916
  419.2 40.6 %copy-start.240 = (f32[24]{0:T(128)S(1)}, f32[24]{0:T(128)}, u32[]{:S(2)}) copy-start(f32[24]{0:T(128)} %copy-done.239) | copy-start | bytes 292
  419.3 40.6 %copy-start.242 = (f32[24]{0:T(128)S(1)}, f32[24]{0:T(128)}, u32[]{:S(2)}) copy-start(f32[24]{0:T(128)} %copy-done.241) | copy-start | bytes 292
  419.3 40.6 %copy-start.243 = (f32[24]{0:T(128)S(1)}, f32[24]{0:T(128)}, u32[]{:S(2)}) copy-start(f32[24]{0:T(128)} %get-tuple-element.2497) | copy-start | bytes 292
  477.9 65.5 %reduce-scatter.24.cloned.1.call-start = ((), (), s32[]{:S(2)}) async-start(), calls=%async_computation.13 | async-start | bytes 81920 | tf_op jit(solution)/shard_map/reduce_scatter | solution.py:254
  518.6 43.4 %reduce-scatter.26.cloned.1.call-start = ((), (), s32[]{:S(2)}) async-start(), calls=%async_computation.15 | async-start | bytes 81920 | tf_op jit(solution)/shard_map/reduce_scatter | solution.py:254
  542.0 88.8 %reduce-scatter.38.cloned.1.call-start = ((), (), s32[]{:S(2)}) async-start(), calls=%async_computation.21 | async-start | bytes 2621440
  564.2 44.4 %copy-start.79 = (f32[6,512]{1,0:T(8,128)}, f32[6,512]{1,0:T(8,128)S(1)}, u32[]{:S(2)}) copy-start(f32[6,512]{1,0:T(8,128)S(1)} %get-tuple-element.2436) | copy-start | bytes 36868
  565.0 43.6 %copy-start.81 = (f32[6,512]{1,0:T(8,128)}, f32[6,512]{1,0:T(8,128)S(1)}, u32[]{:S(2)}) copy-start(f32[6,512]{1,0:T(8,128)S(1)} %get-tuple-element.2439) | copy-start | bytes 36868
  599.2 84.8 %reduce-scatter.32.cloned.1.call-start = ((), (), s32[]{:S(2)}) async-start(), calls=%async_computation.18 | async-start | bytes 81920 | tf_op jit(solution)/shard_map/reduce_scatter | solution.py:277
  668.0 64.6 %copy-start.133 = (f32[3852]{0:T(1024)S(1)}, f32[3852]{0:T(1024)}, u32[]{:S(2)}) copy-start(f32[3852]{0:T(1024)} %param.366) | copy-start | bytes 46228
  668.0 64.6 %copy-start.134 = (f32[3852]{0:T(1024)S(1)}, f32[3852]{0:T(1024)}, u32[]{:S(2)}) copy-start(f32[3852]{0:T(1024)} %param.371) | copy-start | bytes 46228
  668.0 106.2 %copy-start.18 = (f32[378,128]{1,0:T(8,128)S(1)}, f32[378,128]{1,0:T(8,128)}, u32[]{:S(2)}) copy-start(f32[378,128]{1,0:T(8,128)} %param.357) | copy-start | bytes 580612
  668.0 106.2 %copy-start.93 = (f32[378,128]{1,0:T(8,128)S(1)}, f32[378,128]{1,0:T(8,128)}, u32[]{:S(2)}) copy-start(f32[378,128]{1,0:T(8,128)} %param.362) | copy-start | bytes 580612
  668.0 106.2 %copy-start.94 = (f32[378,128]{1,0:T(8,128)S(1)}, f32[378,128]{1,0:T(8,128)}, u32[]{:S(2)}) copy-start(f32[378,128]{1,0:T(8,128)} %param.367) | copy-start | bytes 580612
  668.1 106.2 %all-reduce.68.cloned.1.call-start = ((), (), s32[]{:S(2)}) async-start(), calls=%async_computation.24 | async-start | bytes 2744320 | tf_op jit(solution)/shard_map/psum | solution.py:475
  670.1 107.8 %copy-start.11 = (f32[128,756]{0,1:T(8,128)S(1)}, f32[128,756]{0,1:T(8,128)}, u32[]{:S(2)}) copy-start(f32[128,756]{0,1:T(8,128)} %param.359) | copy-start | bytes 1161220
  670.1 107.8 %copy-start.61 = (f32[128,756]{0,1:T(8,128)S(1)}, f32[128,756]{0,1:T(8,128)}, u32[]{:S(2)}) copy-start(f32[128,756]{0,1:T(8,128)} %param.364) | copy-start | bytes 1161220
  670.2 107.8 %copy-start.62 = (f32[128,756]{0,1:T(8,128)S(1)}, f32[128,756]{0,1:T(8,128)}, u32[]{:S(2)}) copy-start(f32[128,756]{0,1:T(8,128)} %param.369) | copy-start | bytes 1161220
  (214 other events, 3166.9 us)
Sparse Core Ops, SparseCore 0:
  44.6 20.8 reduce-scatter.21
  127.6 18.8 reduce-scatter.41
  149.5 19.6 reduce-scatter.33
  242.7 18.6 reduce-scatter.27
  298.6 19.5 reduce-scatter.35
  333.9 21.6 reduce-scatter.39
  371.1 19.3 reduce-scatter.29
  392.8 22.8 all-gather.3
  478.0 23.2 all-gather.5
  518.7 19.8 reduce-scatter.23
  542.1 19.8 reduce-scatter.25
  599.3 31.3 reduce-scatter.37
  668.1 15.7 reduce-scatter.31
  688.7 85.4 all-reduce.67
where the time goes:
time: 835 us; the launch traced here: 823 us
  local copies, waits for them, and re-layouts  188 us (23%)
  blocking collectives  176 us (21%)
  matrix products  158 us (19%)
  waiting for transfers between devices  141 us (17%)
  other arithmetic  117 us (14%)
  between operations  40.6 us (5%)
    dot_general x84, matrix products, upper_solve(): carried = jnp.dot(strict[index], solved, precision=HIGHEST_PRECISION)  101 us
    unnamed x19, waiting for transfers between devices  53.3 us
    psum x1, blocking collectives, body(): valid_dims = 3.0 * lax.psum(own_count, ('wide', 'narrow'))  41.2 us
    psum x1, blocking collectives, body(): lax.psum((jnp.concatenate(grads_flow), loss_local), ('wide', 'narrow'))  40.8 us
    psum x1, waiting for transfers between devices, body(): lax.psum((net_grads[0], net_grads[1], net_grads[2], net_grads[3]), 'wide')  39.1 us
    unnamed x572, local copies, waits for them, and re-layouts  33.1 us
    add x11, other arithmetic, tap_sum(): result + padded[tap_index, :, :, row_start:row_start + grid_side, col_sta...  32.5 us
    reduce_scatter x3, waiting for transfers between devices, coupling_backward(): lax.psum_scatter(grad_input, 'narrow', scatter_dimension=1, tiled=True)  30.2 us
  transfers between devices with their start and end apart: 14, of which 7 were waited for; matrix products, arithmetic and copies ran while one was open for 37% of the time, Pallas kernels for 0%

commit v1 on v0

v1 whole, which is shorter than its diff:
```python
import functools
import jax
import jax.numpy as jnp
from jax import lax
from jax.experimental import pallas as pl
from jax.experimental.pallas import tpu as pltpu
from jax.sharding import PartitionSpec as P

C1 = 12
IMG_SIDE = 32
STEP = 5
HIGHEST_PRECISION = lax.Precision.HIGHEST
LOG_TWO_PI = 1.8378770664093453
LOG_TWO = 0.6931471805599453
FIRST_BETA = 0.5
SECOND_BETA = 0.5
EPSILON = 1e-06
WEIGHT_DECAY = 0.01
LEARN_RATE = 0.25
TAPS = [(-1, -1), (-1, 0), (-1, 1), (0, -1), (0, 0), (0, 1), (1, -1), (1, 0), (1, 1)]
F32 = jnp.float32
BF16 = jnp.bfloat16
HID = 512
LANE = 128
LEVELS = 3
FLOW_ROWS = 32
LOSS_ROW = 31
VMEM_BYTES = 50 * 1024 * 1024


def round_up(value, unit):
    return (value + unit - 1) // unit * unit


def chan(level):
    return C1 * 2**level


def side(level):
    return IMG_SIDE // 2 ** (level + 1)


def real_positions(level, images):
    return images * side(level) ** 2


def positions(level, images):
    return round_up(real_positions(level, images), LANE)


def in_rows(level):
    return 9 * chan(level) // 2


def first_rows(level):
    return round_up(in_rows(level) + 6, 16)


def second_bias_row(level):
    return first_rows(level) - 4


def last_rows(level):
    return round_up(9 * chan(level), 16)


def pack_rows(level):
    return first_rows(level) + HID + last_rows(level)


def flow_lengths():
    return [5 * C1 + 3 * C1 * C1 // 2, 10 * C1 + 6 * C1 * C1, 24 * C1 + 16 * C1 * C1]


def flow_size():
    return sum(flow_lengths())


def flow_offsets(level):
    start = sum(flow_lengths()[:level])
    channels = chan(level)
    offsets = {"bias": start, "logs": start + channels, "block": start + 2 * channels}
    start = start + 2 * channels + channels * channels
    offsets["outbias"] = start
    offsets["outscale"] = start + channels
    start = start + 2 * channels
    if level < LEVELS - 1:
        offsets["priormatrix"] = start
        start = start + channels // 2 * channels
    offsets["priorbias"] = start
    return offsets


def column_names(level):
    channels = chan(level)
    offsets = flow_offsets(level)
    names = [
        ("bias", offsets["bias"]),
        ("logs", offsets["logs"]),
        ("outbias", offsets["outbias"]),
        ("outscale", offsets["outscale"]),
        ("priorbias", offsets["priorbias"]),
    ]
    if level == LEVELS - 1:
        names = names + [("priorscale", offsets["priorbias"] + channels)]
    return names


def exact_dot(first, second):
    return jnp.dot(first, second, precision=HIGHEST_PRECISION, preferred_element_type=F32)


def exact_rows(first, second):
    return lax.dot_general(
        first,
        second,
        (((0,), (0,)), ((), ())),
        precision=HIGHEST_PRECISION,
        preferred_element_type=F32,
    )


def exact_columns(first, second):
    return lax.dot_general(
        first,
        second,
        (((1,), (1,)), ((), ())),
        precision=HIGHEST_PRECISION,
        preferred_element_type=F32,
    )


def plain_dot(first, second):
    return jnp.dot(first, second, preferred_element_type=F32)


def contract_rows(first, second):
    return lax.dot_general(first, second, (((0,), (0,)), ((), ())), preferred_element_type=F32)


def contract_columns(first, second):
    return lax.dot_general(first, second, (((1,), (1,)), ((), ())), preferred_element_type=F32)


def iota(shape, axis):
    return lax.broadcasted_iota(jnp.int32, shape, axis)


def rounded(values):
    return values.astype(BF16).astype(F32)


def split_three(values):
    high = rounded(values)
    rest = values - high
    middle = rounded(rest)
    return [high, middle, rest - middle]


def move_lanes(values, chooser, transposed=False):
    rows = values.shape[0]
    padded = round_up(rows, 8)
    if padded > rows:
        values = jnp.concatenate([values, jnp.zeros((padded - rows, values.shape[1]), F32)], 0)
    pieces = jnp.concatenate(split_three(values), 0).astype(BF16)
    moved = contract_columns(pieces, chooser) if transposed else plain_dot(pieces, chooser)
    moved = moved[:padded] + moved[padded : 2 * padded] + moved[2 * padded :]
    return moved[:rows]


def squeeze_chooser(grid, images):
    count = images * grid * grid
    source = iota((count, count), 0)
    target = iota((count, count), 1)
    shift = grid.bit_length() - 1
    image = lax.shift_right_logical(source, 2 * shift)
    row = lax.shift_right_logical(source, shift) & (grid - 1)
    column = source & (grid - 1)
    half = grid // 2
    place = (
        ((row & 1) * 2 + (column & 1)) * (images * half * half)
        + image * (half * half)
        + lax.shift_right_logical(row, 1) * half
        + lax.shift_right_logical(column, 1)
    )
    return (place == target).astype(F32).astype(BF16)


def order_chooser(channels, stride):
    row = iota((4 * channels, 4 * stride), 0)
    column = iota((4 * channels, 4 * stride), 1)
    return ((row & 3) * stride + lax.shift_right_logical(row, 2) == column).astype(F32)


def squeeze(values, chooser, lanes_out):
    channels, count = values.shape
    moved = move_lanes(values, chooser)
    quarter = count // 4
    stacked = jnp.concatenate([moved[:, k * quarter : (k + 1) * quarter] for k in range(4)], 0)
    ordered = exact_dot(order_chooser(channels, channels), stacked)
    if lanes_out > quarter:
        ordered = jnp.concatenate([ordered, jnp.zeros((4 * channels, lanes_out - quarter), F32)], 1)
    return ordered


def unsqueeze(values, chooser, count):
    channels = values.shape[0] // 4
    quarter = count // 4
    stacked = exact_rows(order_chooser(channels, channels), values)
    laid = jnp.concatenate(
        [stacked[k * channels : (k + 1) * channels, :quarter] for k in range(4)], 1
    )
    return move_lanes(laid, chooser, transposed=True)


def slope_roll(values, step):
    step = step % LANE
    while step:
        part = 16 if step >= 16 else 1 << (step.bit_length() - 1)
        values = pltpu.roll(values, 0, 1, stride=part, stride_axis=0)
        step = step - part
    return values


def flow_block(flat, offset, rows, width):
    padded = round_up(rows, 8)
    start = offset + width * iota((padded, FLOW_ROWS), 0)
    line = lax.shift_right_logical(start, 7)
    column = iota((padded, FLOW_ROWS), 1)
    base = -offset % LANE
    if base:
        flat = pltpu.roll(flat, base, 1)
    here = exact_dot((line == column).astype(F32), flat)
    after = exact_dot((line + 1 == column).astype(F32), flat)
    here = slope_roll(here, -width)
    after = slope_roll(after, -width)
    lane = iota((padded, LANE), 1)
    begin = (offset + width * iota((padded, LANE), 0)) & (LANE - 1)
    chosen = jnp.where(lane + begin < LANE, here, after)
    return chosen[:rows, :width]


def flow_block_back(values, offset, rows, width):
    padded = round_up(rows, 8)
    base = offset % LANE
    over = max(base + width - LANE, 0)
    parts = [values[:, width - over :]] if over else []
    if base > over:
        parts.append(jnp.zeros((rows, base - over), F32))
    parts.append(values[:, : width - over])
    if base + width < LANE:
        parts.append(jnp.zeros((rows, LANE - base - width), F32))
    block = jnp.concatenate(parts, 1)
    if padded > rows:
        block = jnp.concatenate([block, jnp.zeros((padded - rows, LANE), F32)], 0)
    block = slope_roll(block, width)
    lane = iota((padded, LANE), 1)
    begin = (offset + width * iota((padded, LANE), 0)) & (LANE - 1)
    here = jnp.where(lane >= begin, block, 0.0)
    after = jnp.where(lane >= begin, 0.0, block)
    line = lax.shift_right_logical(offset + width * iota((FLOW_ROWS, padded), 1), 7)
    row = iota((FLOW_ROWS, padded), 0)
    return exact_dot((line == row).astype(F32), here) + exact_dot(
        (line + 1 == row).astype(F32), after
    )


def flow_column(turned, offset, length):
    line, begin = offset // LANE, offset % LANE
    if begin + length <= LANE:
        return turned[begin : begin + length, line : line + 1]
    return jnp.concatenate(
        [turned[begin:, line : line + 1], turned[: begin + length - LANE, line + 1 : line + 2]], 0
    )


def flow_column_back(values, offset):
    length = values.shape[0]
    line, begin = offset // LANE, offset % LANE
    lane = iota((LANE, LANE), 1)
    head = min(length, LANE - begin)
    parts = []
    if begin:
        parts.append(jnp.zeros((begin, 1), F32))
    parts.append(values[:head])
    if begin + head < LANE:
        parts.append(jnp.zeros((LANE - begin - head, 1), F32))
    column = jnp.concatenate(parts, 0) if len(parts) > 1 else parts[0]
    term = jnp.where(lane == line, column, 0.0)
    if head < length:
        column = jnp.concatenate([values[head:], jnp.zeros((LANE - length + head, 1), F32)], 0)
        term = term + jnp.where(lane == line + 1, column, 0.0)
    return term


def to_flat_rows(values):
    size = values.shape[0]
    row = values.reshape(1, size)
    row = jnp.concatenate([row, jnp.zeros((1, FLOW_ROWS * LANE - size), F32)], 1)
    return row.reshape(FLOW_ROWS, LANE)


def from_flat_rows(values, size):
    return values.reshape(1, FLOW_ROWS * LANE)[:, :size].reshape(size)


def triangles(block):
    channels = block.shape[0]
    row = iota((channels, channels), 0)
    column = iota((channels, channels), 1)
    signs = (1 - 2 * (row & 1)).astype(F32)
    diagonal = signs * jnp.exp(jnp.where(row == column, block, 0.0))
    lower = jnp.where(row > column, block, jnp.where(row == column, 1.0, 0.0))
    upper = jnp.where(row < column, block, jnp.where(row == column, diagonal, 0.0))
    reverse = (row + column == channels - 1).astype(F32)
    return lower, upper, reverse, diagonal


def tap_masks(level, images):
    grid = side(level)
    count = positions(level, images)
    lane = iota((8, count), 1)
    shift = grid.bit_length() - 1
    row = lax.shift_right_logical(lane, shift) & (grid - 1)
    column = lane & (grid - 1)
    inside = lane < real_positions(level, images)
    masks = {}
    for row_step in (-1, 0, 1):
        for column_step in (-1, 0, 1):
            good = (
                (row + row_step >= 0)
                & (row + row_step < grid)
                & (column + column_step >= 0)
                & (column + column_step < grid)
                & inside
            )
            masks[(row_step, column_step)] = jnp.where(good, 1.0, 0.0)[0:1]
    return masks


def tap_read(values, masks, level, row_step, column_step):
    count = values.shape[1]
    offset = (row_step * side(level) + column_step) % count
    if offset:
        values = pltpu.roll(values, count - offset, 1)
    if (row_step, column_step) != (0, 0):
        values = values * masks[(row_step, column_step)]
    return values


def tap_stack(values, masks, level, direction):
    return [
        tap_read(values, masks, level, direction * row_step, direction * column_step)
        for row_step, column_step in TAPS
    ]


def tap_sum(values, masks, level, direction, channels):
    total = None
    for tap, (row_step, column_step) in enumerate(TAPS):
        term = tap_read(
            values[tap * channels : (tap + 1) * channels],
            masks,
            level,
            direction * row_step,
            direction * column_step,
        )
        total = term if total is None else total + term
    return total


def pack_kernel(conv_in_ref, mixer_ref, conv_out_ref, bias_ref, *out_refs):
    in_start = 0
    out_start = 0
    turned = jnp.concatenate(
        [
            conv_out_ref[...],
            jnp.zeros((LANE, round_up(conv_out_ref.shape[1], LANE) - conv_out_ref.shape[1]), F32),
        ],
        1,
    ).T
    for level in range(LEVELS):
        out_ref = out_refs[level]
        rows, columns = in_rows(level), 9 * chan(level)
        top = first_rows(level)
        ones = split_three(bias_ref[level, 0:1, :])
        twos = split_three(bias_ref[level, 1:2, :])
        gap = second_bias_row(level) - rows - 3
        pieces = [conv_in_ref[in_start : in_start + rows, :]] + ones
        if gap:
            pieces.append(jnp.zeros((gap, LANE), F32))
        pieces = pieces + twos + [jnp.zeros((1, LANE), F32)]
        out_ref[0:top, :] = jnp.concatenate(pieces, 0).astype(BF16)
        out_ref[top : top + HID, :] = mixer_ref[level].astype(BF16)
        tail = turned[out_start : out_start + columns]
        if last_rows(level) > columns:
            tail = jnp.concatenate([tail, jnp.zeros((last_rows(level) - columns, LANE), F32)], 0)
        out_ref[top + HID :, :] = tail.astype(BF16)
        in_start = in_start + rows
        out_start = out_start + columns


def flow_pre_kernel(seed_ref, valid_ref, image_ref, flow_ref, *out_refs):
    images = image_ref.shape[1]
    flat = to_flat_rows(flow_ref[...])
    turned = jnp.concatenate([flat, jnp.zeros((LANE - FLOW_ROWS, LANE), F32)], 0).T
    blocks = IMG_SIDE * IMG_SIDE // 256
    pieces = []
    for image in range(images):
        position = iota((8, IMG_SIDE * IMG_SIDE), 0) * (IMG_SIDE * IMG_SIDE) + iota(
            (8, IMG_SIDE * IMG_SIDE), 1
        )
        hashed = seed_ref[image] + position * jnp.int32(-1640531527)
        hashed = hashed ^ lax.shift_right_logical(hashed, jnp.full_like(hashed, 15))
        hashed = hashed * jnp.int32(739267321)
        hashed = hashed ^ lax.shift_right_logical(hashed, jnp.full_like(hashed, 13))
        field = ((hashed & jnp.int32(16777215)).astype(F32) + 0.5) * 2.0 ** (-24)
        pixel = jnp.concatenate(
            [image_ref[:, image, :], jnp.zeros((5, IMG_SIDE * IMG_SIDE), F32)], 0
        )
        pixel = pixel + field / 256.0
        for block in range(blocks):
            pieces.append(pixel[:, block * 256 : (block + 1) * 256])
    stacked = jnp.concatenate(pieces, 0)
    source = iota((256, 256), 0)
    target = iota((256, 256), 1)
    row = lax.shift_right_logical(source, 5)
    column = source & 31
    place = (
        ((row & 1) * 2 + (column & 1)) * 64
        + lax.shift_right_logical(row, 1) * 16
        + lax.shift_right_logical(column, 1)
    )
    moved = move_lanes(stacked, (place == target).astype(F32).astype(BF16))
    quarters = []
    for k in range(4):
        quarters.append(
            jnp.concatenate(
                [
                    moved[piece * 8 : (piece + 1) * 8, k * 64 : (k + 1) * 64]
                    for piece in range(images * blocks)
                ],
                1,
            )
        )
    state = exact_dot(order_chooser(3, 8), jnp.concatenate(quarters, 0))
    at = 0
    for level in range(LEVELS):
        channels = chan(level)
        grid = side(level)
        count = positions(level, images)
        offsets = flow_offsets(level)
        block = flow_block(flat, offsets["block"], channels, channels)
        names = column_names(level)
        columns = [flow_column(turned, offset, channels) for _, offset in names]
        lane = iota((channels, LANE), 1)
        held = jnp.zeros((channels, LANE), F32)
        for index, column in enumerate(columns):
            held = jnp.where(lane == index, column, held)
        normed = (state + columns[0]) * jnp.exp(columns[1])
        lower, upper, reverse, _ = triangles(block)
        mixing = exact_dot(exact_dot(reverse, lower), upper)
        mixed = exact_dot(mixing, normed)
        lane = iota((8, count), 1)
        shift = grid.bit_length() - 1
        image = lax.shift_right_logical(lane, 2 * shift)
        row = lax.shift_right_logical(lane, shift) & (grid - 1)
        column = lane & (grid - 1)
        high = jnp.zeros((8, count), jnp.int32)
        wide = jnp.zeros((8, count), jnp.int32)
        for index in range(images):
            high = jnp.where(image == index, valid_ref[index, 0], high)
            wide = jnp.where(image == index, valid_ref[index, 1], wide)
        unit = 2 ** (level + 1)
        row_share = jnp.clip(high - row * unit, 0, unit).astype(F32) / unit
        column_share = jnp.clip(wide - column * unit, 0, unit).astype(F32) / unit
        share = jnp.where(image < images, row_share * column_share, 0.0)
        normed_ref, mixed_ref, share_ref, held_ref, block_ref = out_refs[at : at + 5]
        at = at + 5
        normed_ref[...] = normed
        mixed_ref[...] = mixed
        share_ref[...] = share
        held_ref[...] = held
        block_ref[...] = jnp.concatenate(
            [block, jnp.zeros((channels, LANE - channels), F32)], 1
        )
        if level < LEVELS - 1:
            prior = flow_block(flat, offsets["priormatrix"], channels // 2, channels)
            out_refs[at][...] = jnp.concatenate(
                [prior, jnp.zeros((channels // 2, LANE - channels), F32)], 1
            )
            at = at + 1
            state = squeeze(
                mixed[: channels // 2], squeeze_chooser(grid, images), positions(level + 1, images)
            )


def silu_parts(values):
    sigmoid = 1.0 / (1.0 + jnp.exp(-values))
    active = values * sigmoid
    slope = sigmoid + active * (1.0 - sigmoid)
    return active, slope


def net_kernel(level, images, narrow, *refs):
    is_last = level == LEVELS - 1
    index_ref = refs[0]
    weight_refs = refs[1 : 1 + narrow]
    mixed_ref, share_ref, held_ref = refs[1 + narrow : 4 + narrow]
    at = 4 + narrow
    prior_ref = None
    if not is_last:
        prior_ref = refs[at]
        at = at + 1
    keep_ref, send_ref, grad_ref, small_ref = refs[at : at + 4]
    at = at + 4
    prior_grad_ref = None
    if not is_last:
        prior_grad_ref = refs[at]
        at = at + 1
    order_ref, slope_one_ref, slope_two_ref, one_ref, two_ref = refs[at:]
    me = index_ref[0]
    channels = chan(level)
    half = channels // 2
    count = positions(level, images)
    top, rows = first_rows(level), in_rows(level)
    tail, used = last_rows(level), 9 * channels
    masks = tap_masks(level, images)
    width = HID // narrow

    def weights(start, length):
        return jnp.concatenate([ref[start : start + length, :] for ref in weight_refs], 1)

    for r_in in range(narrow):
        start = pl.multiple_of(top + (me ^ r_in) * width, 16)
        for r_out in range(narrow):
            order_ref[r_in * width : (r_in + 1) * width, r_out * LANE : (r_out + 1) * LANE] = (
                weight_refs[r_out][pl.ds(start, width), :]
            )
    weight_in = weights(0, top)
    weight_mix = order_ref[...]
    weight_out = weights(top + HID, tail)
    first = mixed_ref[0:half, :]
    second = mixed_ref[half:channels, :]
    share = share_ref[0:1, :]
    pieces = tap_stack(rounded(first), masks, level, 1)
    pieces.append(jnp.ones((3, count), F32))
    pieces.append(jnp.zeros((top - rows - 3, count), F32))
    stacked = jnp.concatenate(pieces, 0).astype(BF16)
    pick = jnp.where(
        (iota((16, count), 0) >= 12) & (iota((16, count), 0) < 15), 1.0, 0.0
    ).astype(BF16)
    hidden_one = contract_rows(weight_in, stacked)
    active, slope = silu_parts(hidden_one)
    slope_one_ref[...] = slope
    one_ref[...] = active.astype(BF16)
    hidden_two = contract_rows(weight_mix, one_ref[...]) + contract_rows(weights(top - 16, 16), pick)
    active, slope = silu_parts(hidden_two)
    slope_two_ref[...] = slope
    two_ref[...] = active.astype(BF16)
    spread = plain_dot(weight_out, two_ref[...])
    net_raw = tap_sum(spread, masks, level, 1, channels)
    held = held_ref[...]
    out_bias, out_scale = held[:, 2:3], held[:, 3:4]
    growth = jnp.exp(3.0 * out_scale)
    output = (net_raw + out_bias) * growth
    logit = output[half:] + 2.0
    sigmoid = 1.0 / (1.0 + jnp.exp(-logit))
    latent = (second + output[:half]) * sigmoid
    log_sigmoid = jnp.minimum(logit, 0.0) - jnp.log1p(jnp.exp(-jnp.abs(logit)))
    if is_last:
        joined = jnp.concatenate([first, latent], 0)
        mean, scale = held[:, 4:5], held[:, 5:6]
        mean = jnp.broadcast_to(mean, joined.shape)
        scale = jnp.broadcast_to(scale, joined.shape)
    else:
        joined = latent
        prior = prior_ref[...][:, :channels]
        stats = exact_rows(prior, first) + held[:, 4:5]
        mean, scale = stats[:half], stats[half:]
    gap = joined - mean
    shrink = jnp.exp(-2.0 * scale)
    square = gap * gap * shrink
    log_prior = -0.5 * (LOG_TWO_PI + 2.0 * scale + square)
    total = jnp.sum(jnp.sum(share * log_sigmoid, 0, keepdims=True), 1, keepdims=True) + jnp.sum(
        jnp.sum(share * log_prior, 0, keepdims=True), 1, keepdims=True
    )
    logs_total = jnp.sum(held[:, 1:2], 0, keepdims=True)
    share_total = jnp.sum(share, 1, keepdims=True)
    grad_joined = share * (gap * shrink)
    grad_scale = share * (1.0 - square)
    grad_latent = grad_joined[half:] if is_last else grad_joined
    grad_logit = (grad_latent * latent - share) * (1.0 - sigmoid)
    grad_second = grad_latent * sigmoid
    grad_output = jnp.concatenate([grad_second, grad_logit], 0)
    grad_net = grad_output * growth
    lane = iota((channels, LANE), 1)
    small = jnp.zeros((channels, LANE), F32)

    def put(small, index, values):
        return jnp.where(lane == index, jnp.sum(values, 1, keepdims=True), small)

    small = put(small, 2, grad_net)
    small = put(small, 3, 3.0 * grad_output * output)
    if is_last:
        small = put(small, 4, -grad_joined)
        small = put(small, 5, grad_scale)
        grad_first = grad_joined[:half]
    else:
        grad_stats = jnp.concatenate([-grad_joined, grad_scale], 0)
        small = put(small, 4, grad_stats)
        grad_first = exact_dot(prior, grad_stats)
        prior_grad = exact_columns(first, grad_stats)
        prior_grad_ref[...] = jnp.concatenate(
            [prior_grad, jnp.zeros((half, LANE - channels), F32)], 1
        )
    small = jnp.where(lane == 6, -total, small)
    small = jnp.where(lane == 7, share_total, small)
    small_ref[...] = small
    pieces = tap_stack(rounded(grad_net), masks, level, -1)
    if tail > used:
        pieces.append(jnp.zeros((tail - used, count), F32))
    grad_spread = jnp.concatenate(pieces, 0).astype(BF16)

    def store(start, values):
        for r in range(narrow):
            ref = send_ref if r & 1 else keep_ref
            ref[r // 2, start : start + values.shape[0], :] = values[:, r * LANE : (r + 1) * LANE]

    store(top + HID, contract_columns(grad_spread, two_ref[...]))
    grad_two = (contract_rows(weight_out, grad_spread) * slope_two_ref[...]).astype(BF16)
    grad_mix = contract_columns(one_ref[...], grad_two)
    for r_in in range(narrow):
        start = pl.multiple_of(top + (me ^ r_in) * width, 16)
        for r_out in range(narrow):
            ref = send_ref if r_out & 1 else keep_ref
            ref[r_out // 2, pl.ds(start, width), :] = grad_mix[
                r_in * width : (r_in + 1) * width, r_out * LANE : (r_out + 1) * LANE
            ]
    grad_one = (plain_dot(weight_mix, grad_two) * slope_one_ref[...]).astype(BF16)
    grad_in = contract_columns(stacked, grad_one)
    store(0, grad_in[: top - 16])
    store(top - 16, grad_in[top - 16 :] + contract_columns(pick, grad_two))
    grad_stack = plain_dot(weight_in, grad_one)
    grad_first = grad_first + tap_sum(grad_stack, masks, level, -1, half)
    grad_ref[...] = jnp.concatenate([grad_first, grad_second], 0)


def flow_post_kernel(images, *refs):
    count_ref = refs[0]
    out_ref = refs[-1]
    at = 1
    per_level = []
    for level in range(LEVELS):
        number = 5 if level == LEVELS - 1 else 6
        per_level.append(refs[at : at + number])
        at = at + number
    turned = jnp.zeros((LANE, LANE), F32)
    flat = jnp.zeros((FLOW_ROWS, LANE), F32)
    loss = jnp.zeros((1, 1), F32)
    carried = None
    for level in (2, 1, 0):
        channels = chan(level)
        half = channels // 2
        grad_ref, normed_ref, held_ref, block_ref, small_ref = per_level[level][:5]
        offsets = flow_offsets(level)
        grad = grad_ref[...]
        if carried is not None:
            grad = grad + jnp.concatenate([carried, jnp.zeros_like(carried)], 0)
        normed = normed_ref[...]
        held = held_ref[...]
        small = small_ref[...]
        block = block_ref[...][:, :channels]
        lower, upper, reverse, diagonal = triangles(block)
        mixing_left = exact_dot(reverse, lower)
        grad_normed = exact_rows(exact_dot(mixing_left, upper), grad)
        grad_mixing = exact_dot(reverse, exact_columns(grad, normed))
        grad_lower = exact_columns(grad_mixing, upper)
        grad_upper = exact_rows(lower, grad_mixing)
        share_total = small[0:1, 7:8]
        row = iota((channels, channels), 0)
        column = iota((channels, channels), 1)
        grad_block = jnp.where(
            row > column,
            grad_lower,
            jnp.where(row < column, grad_upper, grad_upper * diagonal - share_total),
        )
        growth = jnp.exp(held[:, 1:2])
        grad_state = grad_normed * growth
        grad_bias = jnp.sum(grad_state, 1, keepdims=True)
        grad_logs = jnp.sum(grad_normed * normed, 1, keepdims=True) - share_total
        flat = flat + flow_block_back(grad_block, offsets["block"], channels, channels)
        for index, (name, offset) in enumerate(column_names(level)):
            if name == "bias":
                values = grad_bias
            elif name == "logs":
                values = grad_logs
            else:
                values = small[:, index : index + 1]
            turned = turned + flow_column_back(values, offset)
        if level < LEVELS - 1:
            flat = flat + flow_block_back(
                per_level[level][5][...][:, :channels], offsets["priormatrix"], half, channels
            )
        logs_total = jnp.sum(held[:, 1:2], 0, keepdims=True)
        trace = jnp.sum(
            jnp.sum(jnp.where(row == column, block, 0.0), 0, keepdims=True), 1, keepdims=True
        )
        loss = loss + small[0:1, 6:7] - share_total * (logs_total + trace)
        if level > 0:
            grid = side(level - 1)
            carried = unsqueeze(
                grad_state, squeeze_chooser(grid, images), images * grid * grid
            )
    flat = flat + turned.T[:FLOW_ROWS]
    pixels = jnp.zeros((), F32)
    for index in range(images):
        pixels = pixels + (count_ref[index, 0] * count_ref[index, 1]).astype(F32)
    row = iota((FLOW_ROWS, LANE), 0)
    lane = iota((FLOW_ROWS, LANE), 1)
    flat = jnp.where((row == LOSS_ROW) & (lane == 0), loss, flat)
    flat = jnp.where((row == LOSS_ROW) & (lane == 1), pixels, flat)
    out_ref[...] = flat


def moments(weight, gradient, first_old, second_old):
    first_new = FIRST_BETA * first_old + (1.0 - FIRST_BETA) * gradient
    second_new = SECOND_BETA * second_old + (1.0 - SECOND_BETA) * gradient * gradient
    update = (
        first_new
        / (1.0 - FIRST_BETA**STEP)
        / (jnp.sqrt(second_new / (1.0 - SECOND_BETA**STEP)) + EPSILON)
        + WEIGHT_DECAY * weight
    )
    return first_new, second_new, update


def total_of(values):
    return jnp.sum(jnp.sum(values, 0, keepdims=True), 1, keepdims=True)


def squares_rows(sums):
    row = iota((16, LANE), 0)
    held = jnp.zeros((16, LANE), F32)
    for index, value in enumerate(sums):
        held = jnp.where(row == index, value, held)
    return held


def group_totals(values_in, values_mix, values_out, values_bias):
    row = iota(values_in.shape, 0)
    lane = iota(values_out.shape, 1)
    sums = []
    start = 0
    for level in range(LEVELS):
        inside = (row >= start) & (row < start + in_rows(level))
        sums.append(total_of(jnp.where(inside, values_in, 0.0)))
        start = start + in_rows(level)
    for level in range(LEVELS):
        sums.append(total_of(values_mix[level]))
    start = 0
    for level in range(LEVELS):
        inside = (lane >= start) & (lane < start + 9 * chan(level))
        sums.append(total_of(jnp.where(inside, values_out, 0.0)))
        start = start + 9 * chan(level)
    for level in range(LEVELS):
        sums.append(total_of(values_bias[2 * level : 2 * level + 2]))
    return sums


def flow_masks():
    place = iota((FLOW_ROWS, LANE), 0) * LANE + iota((FLOW_ROWS, LANE), 1)
    masks = []
    start = 0
    for length in flow_lengths():
        masks.append((place >= start) & (place < start + length))
        start = start + length
    return masks


def moment_kernel(
    grad_refs_and_rest_count,
    *refs,
):
    grads = refs[:3]
    flow_grad_ref = refs[3]
    weight_in, weight_mix, weight_out, weight_bias = refs[4:8]
    first_in, first_mix, first_out, first_bias = refs[8:12]
    second_in, second_mix, second_out, second_bias = refs[12:16]
    outs = refs[16:]
    total = flow_grad_ref[LOSS_ROW : LOSS_ROW + 1, :]
    valid_dims = 3.0 * total[:, 1:2]
    scale = 1.0 / (valid_dims * LOG_TWO)
    grad_in = jnp.concatenate([grads[level][0 : in_rows(level), :] for level in range(LEVELS)], 0)
    columns = weight_out.shape[1]
    tails = [
        grads[level][first_rows(level) + HID : first_rows(level) + HID + 9 * chan(level), :]
        for level in range(LEVELS)
    ]
    tails.append(jnp.zeros((round_up(columns, LANE) - columns, LANE), F32))
    grad_out = jnp.concatenate(tails, 0).T[:, :columns]
    bias_rows = []
    for level in range(LEVELS):
        bias_rows.append(grads[level][in_rows(level) : in_rows(level) + 1, :])
        bias_rows.append(grads[level][second_bias_row(level) : second_bias_row(level) + 1, :])
    grad_bias = jnp.concatenate(bias_rows, 0)
    bias = weight_bias[...].reshape(2 * LEVELS, LANE)
    new_in = moments(weight_in[...], grad_in * scale, first_in[...], second_in[...])
    new_out = moments(weight_out[...], grad_out * scale, first_out[...], second_out[...])
    new_bias = moments(
        bias,
        grad_bias * scale,
        first_bias[...].reshape(2 * LEVELS, LANE),
        second_bias[...].reshape(2 * LEVELS, LANE),
    )
    mix_squares = []
    mix_updates = []
    for level in range(LEVELS):
        top = first_rows(level)
        new_mix = moments(
            weight_mix[level],
            grads[level][top : top + HID, :] * scale,
            first_mix[level],
            second_mix[level],
        )
        outs[1][level] = new_mix[0]
        outs[5][level] = new_mix[1]
        outs[9][level] = new_mix[2]
        mix_squares.append(weight_mix[level] * weight_mix[level])
        mix_updates.append(new_mix[2] * new_mix[2])
    for index, values in ((0, new_in), (2, new_out), (3, new_bias)):
        for kind in range(3):
            value = values[kind]
            if index == 3:
                value = value.reshape(LEVELS, 2, LANE)
            outs[4 * kind + index][...] = value
    weight_sums = group_totals(
        weight_in[...] * weight_in[...], mix_squares, weight_out[...] * weight_out[...], bias * bias
    )
    update_sums = group_totals(
        new_in[2] * new_in[2], mix_updates, new_out[2] * new_out[2], new_bias[2] * new_bias[2]
    )
    lane = iota((16, LANE), 1)
    outs[12][...] = jnp.where(lane == 0, squares_rows(weight_sums), squares_rows(update_sums))


def apply_kernel(*refs):
    sums_ref, flow_grad_ref = refs[0:2]
    weight_in, weight_mix, weight_out, weight_bias = refs[2:6]
    update_in, update_mix, update_out, update_bias = refs[6:10]
    flow_ref, flow_first_ref, flow_second_ref = refs[10:13]
    (
        new_in,
        new_mix,
        new_out,
        new_bias,
        new_flow,
        half_in,
        half_mix,
        half_out,
        flow_moment,
        flow_square,
        norm_ref,
    ) = refs[13:]
    total = flow_grad_ref[LOSS_ROW : LOSS_ROW + 1, :]
    valid_dims = 3.0 * total[:, 1:2]
    scale = 1.0 / (valid_dims * LOG_TWO)
    flow = to_flat_rows(flow_ref[...])
    size = flow_ref.shape[0]
    place = iota((FLOW_ROWS, LANE), 0) * LANE + iota((FLOW_ROWS, LANE), 1)
    flow_grad = jnp.where(place < size, flow_grad_ref[...] * scale, 0.0)
    first_new, second_new, update = moments(
        flow, flow_grad, to_flat_rows(flow_first_ref[...]), to_flat_rows(flow_second_ref[...])
    )
    sums = sums_ref[...]
    weight_norms = [jnp.sqrt(sums[index : index + 1, 0:1]) for index in range(12)]
    update_norms = [jnp.sqrt(sums[index : index + 1, 1:2]) for index in range(12)]
    masks = flow_masks()
    for mask in masks:
        weight_norms.append(jnp.sqrt(total_of(jnp.where(mask, flow * flow, 0.0))))
        update_norms.append(jnp.sqrt(total_of(jnp.where(mask, update * update, 0.0))))
    rates = [
        LEARN_RATE * (weight_norm / update_norm)
        for weight_norm, update_norm in zip(weight_norms, update_norms)
    ]
    rate = jnp.zeros((FLOW_ROWS, LANE), F32)
    for mask, value in zip(masks, rates[12:]):
        rate = jnp.where(mask, value, rate)
    new_flow[...] = from_flat_rows(flow - rate * update, size)
    flow_moment[...] = from_flat_rows(first_new, size)
    flow_square[...] = from_flat_rows(second_new, size)
    row = iota(weight_in.shape, 0)
    edge_one, edge_two = in_rows(0), in_rows(0) + in_rows(1)
    rate = jnp.where(row < edge_one, rates[0], jnp.where(row < edge_two, rates[1], rates[2]))
    fresh = weight_in[...] - rate * update_in[...]
    new_in[...] = fresh
    half_in[...] = fresh.astype(BF16)
    for level in range(LEVELS):
        fresh = weight_mix[level] - rates[3 + level] * update_mix[level]
        new_mix[level] = fresh
        half_mix[level] = fresh.astype(BF16)
    lane = iota(weight_out.shape, 1)
    edge_one, edge_two = 9 * chan(0), 9 * chan(0) + 9 * chan(1)
    rate = jnp.where(lane < edge_one, rates[6], jnp.where(lane < edge_two, rates[7], rates[8]))
    fresh = weight_out[...] - rate * update_out[...]
    new_out[...] = fresh
    half_out[...] = fresh.astype(BF16)
    for level in range(LEVELS):
        new_bias[level] = weight_bias[level] - rates[9 + level] * update_bias[level]
    lane = iota((8, LANE), 1)
    row = iota((8, LANE), 0)
    held = jnp.zeros((8, LANE), F32)
    for index in range(15):
        held = jnp.where((row == 0) & (lane == index), weight_norms[index], held)
        held = jnp.where((row == 1) & (lane == index), update_norms[index], held)
    loss_sum = total[:, 0:1] / LOG_TWO + 8.0 * valid_dims
    held = jnp.where((row == 2) & (lane == 0), loss_sum, held)
    held = jnp.where((row == 2) & (lane == 1), valid_dims, held)
    norm_ref[...] = held


def spec_vmem():
    return pl.BlockSpec(memory_space=pltpu.VMEM)


def spec_smem():
    return pl.BlockSpec(memory_space=pltpu.SMEM)


def call(kernel, outs, scalars, arrays, scratch=(), name=None):
    return pl.pallas_call(
        kernel,
        out_shape=tuple(jax.ShapeDtypeStruct(shape, dtype) for shape, dtype in outs),
        in_specs=[spec_smem()] * len(scalars) + [spec_vmem()] * len(arrays),
        out_specs=tuple(spec_vmem() for _ in outs),
        scratch_shapes=list(scratch),
        compiler_params=pltpu.CompilerParams(vmem_limit_bytes=VMEM_BYTES),
        name=name,
    )(*scalars, *arrays)


def run_pack(conv_in, mixer, conv_out, hidden_bias):
    outs = [((pack_rows(level), LANE), BF16) for level in range(LEVELS)]
    return call(pack_kernel, outs, (), (conv_in, mixer, conv_out, hidden_bias), name="pack")


def run_flow_pre(noise_seeds, valid_shape, images, flow_params):
    count = images.shape[1]
    outs = []
    for level in range(LEVELS):
        channels = chan(level)
        places = positions(level, count)
        outs = outs + [
            ((channels, places), F32),
            ((channels, places), F32),
            ((8, places), F32),
            ((channels, LANE), F32),
            ((channels, LANE), F32),
        ]
        if level < LEVELS - 1:
            outs.append(((channels // 2, LANE), F32))
    flat = call(
        flow_pre_kernel, outs, (noise_seeds, valid_shape), (images, flow_params), name="flow_pre"
    )
    grouped = []
    at = 0
    for level in range(LEVELS):
        number = 6 if level < LEVELS - 1 else 5
        grouped.append(flat[at : at + number])
        at = at + number
    return grouped


def run_net(level, images, index, weights, pre):
    narrow = len(weights)
    channels = chan(level)
    count = positions(level, images)
    outs = [
        ((narrow // 2, pack_rows(level), LANE), F32),
        ((narrow // 2, pack_rows(level), LANE), F32),
        ((channels, count), F32),
        ((channels, LANE), F32),
    ]
    arrays = list(weights) + [pre[1], pre[2], pre[3]]
    if level < LEVELS - 1:
        arrays.append(pre[5])
        outs.append(((channels // 2, LANE), F32))
    scratch = [
        pltpu.VMEM((HID, HID), BF16),
        pltpu.VMEM((HID, count), F32),
        pltpu.VMEM((HID, count), F32),
        pltpu.VMEM((HID, count), BF16),
        pltpu.VMEM((HID, count), BF16),
    ]
    return call(
        functools.partial(net_kernel, level, images, narrow),
        outs,
        (index,),
        arrays,
        scratch,
        name="net_%d" % (level + 1),
    )


def run_flow_post(images, valid_shape, pre, results):
    arrays = []
    for level in range(LEVELS):
        arrays = arrays + [
            results[level][2],
            pre[level][0],
            pre[level][3],
            pre[level][4],
            results[level][3],
        ]
        if level < LEVELS - 1:
            arrays.append(results[level][4])
    return call(
        functools.partial(flow_post_kernel, images),
        [((FLOW_ROWS, LANE), F32)],
        (valid_shape,),
        arrays,
        name="flow_post",
    )[0]


def swap(values, axis, step):
    size = lax.axis_size(axis)
    return lax.ppermute(values, axis, [(index, index ^ step) for index in range(size)])


def gather_narrow(shard):
    held = [shard]
    step = 1
    while step < lax.axis_size("narrow"):
        held = held + [swap(value, "narrow", step) for value in held]
        step = 2 * step
    return held


def sum_everywhere(values):
    for axis in ("narrow", "wide"):
        step = 1
        while step < lax.axis_size(axis):
            values = values + swap(values, axis, step)
            step = 2 * step
    return values


def halve(values, axis, step):
    index = lax.axis_index(axis)
    rows = values.shape[0] // 2
    upper = (index & step) != 0
    low, high = values[:rows], values[rows:]
    sent = jnp.where(upper, low, high)
    kept = jnp.where(upper, high, low)
    return kept + swap(sent, axis, step)


def unhalve(values, axis, step):
    upper = (lax.axis_index(axis) & step) != 0
    other = swap(values, axis, step)
    return jnp.concatenate([jnp.where(upper, other, values), jnp.where(upper, values, other)], 0)


def sum_wide(values):
    rows = values.shape[0]
    size = lax.axis_size("wide")
    steps = []
    step = 1
    while step < size:
        steps.append(step)
        step = 2 * step
    split = [step for step in steps if step < 8]
    unit = 8 * 2 ** len(split)
    padded = round_up(rows, unit)
    if padded > rows:
        values = jnp.pad(values, ((0, padded - rows), (0, 0)))
    for step in split:
        values = halve(values, "wide", step)
    for step in steps[len(split) :]:
        values = values + swap(values, "wide", step)
    for step in split[::-1]:
        values = unhalve(values, "wide", step)
    return values


def reduce_level(keep, send):
    paired = keep + swap(send, "narrow", 1)
    shard = paired[0] + swap(paired[1], "narrow", 2)
    return sum_wide(shard)


def body(
    images,
    noise_seeds,
    valid_shape,
    conv_in,
    mixer,
    conv_out,
    hidden_bias,
    flow_params,
    conv_in_first,
    mixer_first,
    conv_out_first,
    bias_first,
    flow_first,
    conv_in_second,
    mixer_second,
    conv_out_second,
    bias_second,
    flow_second,
):
    count = images.shape[1]
    index = lax.axis_index("narrow").astype(jnp.int32).reshape(1)
    packed = run_pack(conv_in, mixer, conv_out, hidden_bias)
    gathered = [None] * LEVELS
    for level in (2, 1, 0):
        gathered[level] = gather_narrow(packed[level])
    pre = run_flow_pre(noise_seeds, valid_shape, images, flow_params)
    results = [None] * LEVELS
    grads = [None] * LEVELS
    for level in (2, 1, 0):
        results[level] = run_net(level, count, index, gathered[level], pre[level])
        grads[level] = reduce_level(results[level][0], results[level][1])
    flow_grad = sum_everywhere(run_flow_post(count, valid_shape, pre, results))
    weights = (conv_in, mixer, conv_out, hidden_bias)
    shapes = [(weight.shape, F32) for weight in weights]
    moved = call(
        functools.partial(moment_kernel, 0),
        shapes * 3 + [((16, LANE), F32)],
        (),
        tuple(grads)
        + (flow_grad,)
        + weights
        + (conv_in_first, mixer_first, conv_out_first, bias_first)
        + (conv_in_second, mixer_second, conv_out_second, bias_second),
        name="moments",
    )
    sums = moved[12]
    step = 1
    while step < lax.axis_size("narrow"):
        sums = sums + swap(sums, "narrow", step)
        step = 2 * step
    flow_shape = (flow_params.shape, F32)
    fresh = call(
        apply_kernel,
        shapes
        + [flow_shape]
        + [(weight.shape, BF16) for weight in weights[:3]]
        + [flow_shape, flow_shape, ((8, LANE), F32)],
        (),
        (sums, flow_grad)
        + weights
        + tuple(moved[8:12])
        + (flow_params, flow_first, flow_second),
        name="apply",
    )
    norms = fresh[10]
    return (
        fresh[0],
        fresh[1],
        fresh[2],
        fresh[3],
        fresh[4],
        moved[0],
        moved[1],
        moved[2],
        moved[3],
        fresh[8],
        moved[4],
        moved[5],
        moved[6],
        moved[7],
        fresh[9],
        fresh[5],
        fresh[6],
        fresh[7],
        norms[0, :15],
        norms[1, :15],
        norms[2, 0],
        norms[2, 1],
    )


def solution(mesh):
    placed = (
        P(None, ("wide", "narrow"), None),
        P(("wide", "narrow")),
        P(("wide", "narrow"), None),
        P(None, "narrow"),
        P(None, None, "narrow"),
        P("narrow", None),
        P(None, None, "narrow"),
        P(),
    )
    state = (P(None, "narrow"), P(None, None, "narrow"), P("narrow", None), P(None, None, "narrow"), P())
    return jax.shard_map(
        body,
        mesh=mesh,
        in_specs=placed + state + state,
        out_specs=state * 3 + state[:3] + (P(),) * 4,
        check_vma=False,
    )
```

time: 835 us -> 162 us (0.19); the launches traced: 823 us -> 161 us
  blocking collectives: 176 us -> 0 us
  local copies, waits for them, and re-layouts: 188 us -> 16.1 us
  matrix products: 158 us -> 0 us
  other arithmetic: 117 us -> 9.98 us
  waiting for transfers between devices: 141 us -> 73 us
  between operations: 40.6 us -> 1.21 us
  starting transfers between devices: 1.18 us -> 37.4 us
  Pallas kernels: 0 us -> 23.6 us
    dot_general x225 -> x0, matrix products: 158 us -> none  [the longest x84 101 us: upper_solve(): carried = jnp.dot(strict[index], solved, precision=HIGHEST_PRECISION)]
    psum x4 -> x0, blocking collectives: 110 us -> none  [the longest x1 41.2 us: body(): valid_dims = 3.0 * lax.psum(own_count, ('wide', 'narrow'))]
    ppermute x0 -> x40, waiting for transfers between devices: none -> 73 us  [swap(): lax.ppermute(values, axis, [(index, index ^ step) for index in range(size)])]
    all_gather x11 -> x0, blocking collectives: 66 us -> none  [the longest x5 29.4 us: coupling_forward(): sent = lax.all_gather(sent, 'narrow', axis=1, tiled=True)]
    reshape x45 -> x0, local copies, waits for them, and re-layouts: 53.6 us -> none  [the longest x8 23.1 us: tap_stack(): jnp.stack(shifted, 0)]
    unnamed x19 -> x0, waiting for transfers between devices: 53.3 us -> none
    reduce_scatter x6 -> x0, waiting for transfers between devices: 48.8 us -> none  [the longest x3 30.2 us: coupling_backward(): lax.psum_scatter(grad_input, 'narrow', scatter_dimension=1, tiled=True)]
    psum x1 -> x0, waiting for transfers between devices: 39.1 us -> none  [body(): lax.psum((net_grads[0], net_grads[1], net_grads[2], net_grads[3]), 'wide')]
  transfers between devices with their start and end apart: 14 -> 40, of which waited for: 7 -> 26; matrix products, arithmetic and copies ran while one was open for 37% -> 7% of each run, Pallas kernels for 0% -> 9%
where the time goes in v1:
time: 162 us; the launch traced here: 161 us
  waiting for transfers between devices  73 us (45%)
  starting transfers between devices  37.4 us (23%)
  Pallas kernels  23.6 us (15%)
  local copies, waits for them, and re-layouts  16.1 us (10%)
  other arithmetic  9.98 us (6%)
    ppermute x40, waiting for transfers between devices, swap(): lax.ppermute(values, axis, [(index, index ^ step) for index in range(size)])  73 us
    ppermute x40, starting transfers between devices, swap(): lax.ppermute(values, axis, [(index, index ^ step) for index in range(size)])  37.4 us
    pallas_call x8, Pallas kernels, call(): pl.pallas_call(kernel, out_shape=tuple((jax.ShapeDtypeStruct(shape, dtype...  23.6 us
    unnamed x65, local copies, waits for them, and re-layouts  14.1 us
  transfers between devices with their start and end apart: 40, of which 26 were waited for; matrix products, arithmetic and copies ran while one was open for 7% of the time, Pallas kernels for 9%

profile of v1, /device:TPU:0, one launch (start us, length us, event | category | flops | bytes accessed | tf_op | source)
XLA Modules:
  0.0 161.2 jit_solution(1825122765097273891)
XLA Ops:
  0.7 1.2 copy.40.conv_out_ref.refs_6_.refs_4_
  5.3 2.6 %collective-permute-start.1 = (bf16[688,128]{1,0:T(8,128)(2,1)S(1)}, bf16[688,128]{1,0:T(8,128)(2,1)S(1)}, u32[]{:S(2)}, u32[]{:S(2)}) collective-permute-start(bf16[688,128]{1,0:T(8,128)(2,1)S(1)} %get-tuple-element.80.refs_1_), channel_id=1, source_target_pairs={{0,2},{1,3},{2,0},{3,1},{4,6},{5,7},{6,4},{7,5},{8,10},{9,11},{10,... | collective-permute-start | bytes 528392 | tf_op jit(solution)/shard_map/ppermute | solution.py:1028
  7.9 1.3 collective-permute-start.2
  9.2 4.7 %flow_pre.1 = (f32[12,512]{1,0:T(8,128)S(1)}, f32[12,512]{1,0:T(8,128)S(1)}, f32[8,512]{1,0:T(8,128)S(1)}, f32[12,128]{1,0:T(8,128)S(1)}, f32[12,128]{1,0:T(8,12...) custom-call(s32[2]{0:T(128)S(1)} %copy-done.22, ...), custom_call_target="tpu_custom_call" | custom-call | tf_op jit(solution)/shard_map/flow_pre/pallas_call | solution.py:931
  13.9 2.8 %collective-permute-done.2.refs_4_ = bf16[688,128]{1,0:T(8,128)(2,1)S(1)} collective-permute-done((bf16[688,128]{1,0:T(8,128)(2,1)S(1)}, bf16[688,128]{1,0:T(8,128)(2,1)S(1)}, u32[]{:S(2)}, u32[]{:S(2)}) %collective-permute-start.2) | collective-permute-done | bytes 176160 | tf_op jit(solution)/shard_map/ppermute | solution.py:1028
  16.7 2.9 %net_1.1 = (f32[2,688,128]{2,1,0:T(8,128)S(1)}, f32[2,688,128]{2,1,0:T(8,128)S(1)}, f32[12,512]{1,0:T(8,128)S(1)}, f32[12,128]{1,0:T(8,128)S(1)}, f32[6,128]{1,0:T(8,128)S(1)}) custom-call(s32[1]{0:T(128)} %bitcast.refs_0_, bf16[688,128]{1,0:T(8,128)(2,1)S(1)} %get-tuple-element.80.refs_1_, bf16[688,128]{1,0:T(8,128)(2,1)S(1)} %collective-permute-done.refs_2_, ...), custom_call_target="tpu_custom_call" | custom-call | tf_op jit(solution)/shard_map/net_1/pallas_call | solution.py:931
  20.1 1.8 %collective-permute-start.12 = (bf16[864,128]{1,0:T(8,128)(2,1)S(1)}, bf16[864,128]{1,0:T(8,128)(2,1)S(1)}, u32[]{:S(2)}, u32[]{:S(2)}) collective-permute-start(bf16[864,128]{1,0:T(8,128)(2,1)S(1)} %get-tuple-element.87.refs_1_), channel_id=1, source_target_pairs={{0,2},{1,3},{2,0},{3,1},{4,6},{5,7},{6,4},{7,5},{8,10},{9,11},{10,... | collective-permute-start | bytes 663560 | tf_op jit(solution)/shard_map/ppermute | solution.py:1028
  22.1 1.8 %collective-permute-start.13 = (bf16[864,128]{1,0:T(8,128)(2,1)S(1)}, bf16[864,128]{1,0:T(8,128)(2,1)S(1)}, u32[]{:S(2)}, u32[]{:S(2)}) collective-permute-start(bf16[864,128]{1,0:T(8,128)(2,1)S(1)} %collective-permute-done.11.refs_2_), channel_id=1, source_target_pairs={{0,2},{1,3},{2,0},{3,1},{4,6},{5,7},{6,4},{7,5},{8,10},{9,11},{10,... | collective-permute-start | bytes 663560 | tf_op jit(solution)/shard_map/ppermute | solution.py:1028
  25.1 3.3 %collective-permute-done.12.refs_3_ = bf16[864,128]{1,0:T(8,128)(2,1)S(1)} collective-permute-done((bf16[864,128]{1,0:T(8,128)(2,1)S(1)}, bf16[864,128]{1,0:T(8,128)(2,1)S(1)}, u32[]{:S(2)}, u32[]{:S(2)}) %collective-permute-start.12) | collective-permute-done | bytes 221216 | tf_op jit(solution)/shard_map/ppermute | solution.py:1028
  28.4 4.7 %collective-permute-done.13.refs_4_ = bf16[864,128]{1,0:T(8,128)(2,1)S(1)} collective-permute-done((bf16[864,128]{1,0:T(8,128)(2,1)S(1)}, bf16[864,128]{1,0:T(8,128)(2,1)S(1)}, u32[]{:S(2)}, u32[]{:S(2)}) %collective-permute-start.13) | collective-permute-done | bytes 221216 | tf_op jit(solution)/shard_map/ppermute | solution.py:1028
  33.2 3.0 %net_2.1 = (f32[2,864,128]{2,1,0:T(8,128)S(1)}, f32[2,864,128]{2,1,0:T(8,128)}, f32[24,128]{1,0:T(8,128)S(1)}, f32[24,128]{1,0:T(8,128)S(1)}, f32[12,128]{1,0:T(8,128)S(1)}) custom-call(s32[1]{0:T(128)} %bitcast.refs_0_, bf16[864,128]{1,0:T(8,128)(2,1)S(1)} %get-tuple-element.87.refs_1_, bf16[864,128]{1,0:T(8,128)(2,1)S(1)} %collective-permute-done.11.refs_2_, ...), custom_call_target="tpu_custom_call" | custom-call | tf_op jit(solution)/shard_map/net_2/pallas_call | solution.py:931
  36.2 1.8 %collective-permute-start.23 = (bf16[1168,128]{1,0:T(8,128)(2,1)S(1)}, bf16[1168,128]{1,0:T(8,128)(2,1)S(1)}, u32[]{:S(2)}, u32[]{:S(2)}) collective-permute-start(bf16[1168,128]{1,0:T(8,128)(2,1)S(1)} %get-tuple-element.94.refs_1_), channel_id=1, source_target_pairs={{0,2},{1,3},{2,0},{3,1},{4,6},{5,7},{6,4},{7,5},{8,10},{9,11},{10,... | collective-permute-start | bytes 897032 | tf_op jit(solution)/shard_map/ppermute | solution.py:1028
  38.2 2.3 %collective-permute-done.4 = f32[688,128]{1,0:T(8,128)} collective-permute-done((f32[688,128]{1,0:T(8,128)}, f32[688,128]{1,0:T(8,128)}, u32[]{:S(2)}, u32[]{:S(2)}) %collective-permute-start.4) | collective-permute-done | bytes 352288 | tf_op jit(solution)/shard_map/ppermute | solution.py:1028
  42.3 1.8 %collective-permute-start.5 = (f32[352,128]{1,0:T(8,128)}, f32[352,128]{1,0:T(8,128)}, u32[]{:S(2)}, u32[]{:S(2)}) collective-permute-start(f32[352,128]{1,0:T(8,128)} %slice_select_fusion.2), channel_id=1, source_target_pairs={{0,4},{4,0},{8,12},{12,8},{16,20},{20,16},{24,28},{28,24},{1,5},{5... | collective-permute-start | bytes 540680 | tf_op jit(solution)/shard_map/ppermute | solution.py:1028
  44.1 2.6 %collective-permute-done.23.refs_3_ = bf16[1168,128]{1,0:T(8,128)(2,1)S(1)} collective-permute-done((bf16[1168,128]{1,0:T(8,128)(2,1)S(1)}, bf16[1168,128]{1,0:T(8,128)(2,1)S(1)}, u32[]{:S(2)}, u32[]{:S(2)}) %collective-permute-start.23) | collective-permute-done | bytes 299040 | tf_op jit(solution)/shard_map/ppermute | solution.py:1028
  47.5 5.2 %collective-permute-done.24.refs_4_ = bf16[1168,128]{1,0:T(8,128)(2,1)S(1)} collective-permute-done((bf16[1168,128]{1,0:T(8,128)(2,1)S(1)}, bf16[1168,128]{1,0:T(8,128)(2,1)S(1)}, u32[]{:S(2)}, u32[]{:S(2)}) %collective-permute-start.24) | collective-permute-done | bytes 299040 | tf_op jit(solution)/shard_map/ppermute | solution.py:1028
  53.6 2.4 %net_3.1 = (f32[2,1168,128]{2,1,0:T(8,128)S(1)}, f32[2,1168,128]{2,1,0:T(8,128)S(1)}, f32[48,128]{1,0:T(8,128)S(1)}, f32[48,128]{1,0:T(8,128)S(1)}) custom-call(s32[1]{0:T(128)} %bitcast.refs_0_, bf16[1168,128]{1,0:T(8,128)(2,1)S(1)} %get-tuple-element.94.refs_1_, bf16[1168,128]{1,0:T(8,128)(2,1)S(1)} %collective-permute-done.22.refs_2_, ...), custom_call_target="tpu_custom_call" | custom-call | tf_op jit(solution)/shard_map/net_3/pallas_call | solution.py:931
  56.0 4.3 %flow_post.1 = f32[32,128]{1,0:T(8,128)S(1)} custom-call(s32[2,2]{1,0:T(2,128)S(1)} %copy-done.17, f32[12,512]{1,0:T(8,128)S(1)} %get-tuple-element.100.refs_1_, f32[12,512]{1,0:T(8,128)S(1)} %get-tuple-element.101.refs_2_, f32[12,128]{1,0:T(8,128)S(1)} %get-tuple-element.83.refs_7_.refs_3_, f32[12,128]{1,0:T(8,128)S(1)} %get-tuple-element.102.refs_4_, ...), custom_call_target="tpu_custom_call" | custom-call | tf_op jit(solution)/shard_map/flow_post/pallas_call | solution.py:931
  60.4 1.2 collective-permute-done.33
  61.6 1.8 %collective-permute-start.34 = (f32[32,128]{1,0:T(8,128)S(1)}, f32[32,128]{1,0:T(8,128)S(1)}, u32[]{:S(2)}, u32[]{:S(2)}) collective-permute-start(f32[32,128]{1,0:T(8,128)S(1)} %add.87), channel_id=1, source_target_pairs={{0,2},{1,3},{2,0},{3,1},{4,6},{5,7},{6,4},{7,5},{8,10},{9,11},{10,... | collective-permute-start | bytes 49160 | tf_op jit(solution)/shard_map/ppermute | solution.py:1028
  63.4 2.0 %collective-permute-done.34 = f32[32,128]{1,0:T(8,128)S(1)} collective-permute-done((f32[32,128]{1,0:T(8,128)S(1)}, f32[32,128]{1,0:T(8,128)S(1)}, u32[]{:S(2)}, u32[]{:S(2)}) %collective-permute-start.34) | collective-permute-done | bytes 16416 | tf_op jit(solution)/shard_map/ppermute | solution.py:1028
  65.4 1.8 %collective-permute-start.35 = (f32[32,128]{1,0:T(8,128)S(1)}, f32[32,128]{1,0:T(8,128)S(1)}, u32[]{:S(2)}, u32[]{:S(2)}) collective-permute-start(f32[32,128]{1,0:T(8,128)S(1)} %add.88), channel_id=1, source_target_pairs={{0,4},{4,0},{8,12},{12,8},{16,20},{20,16},{24,28},{28,24},{1,5},{5... | collective-permute-start | bytes 49160 | tf_op jit(solution)/shard_map/ppermute | solution.py:1028
  67.2 1.3 add.77
  68.5 1.3 select_add_fusion.2
  69.8 1.6 %collective-permute-start.6 = (f32[176,128]{1,0:T(8,128)S(1)}, f32[176,128]{1,0:T(8,128)S(1)}, u32[]{:S(2)}, u32[]{:S(2)}) collective-permute-start(f32[176,128]{1,0:T(8,128)S(1)} %slice_select_fusion.5), channel_id=1, source_target_pairs={{0,8},{4,12},{8,0},{12,4},{16,24},{20,28},{24,16},{28,20},{1,9},{5... | collective-permute-start | bytes 270344 | tf_op jit(solution)/shard_map/ppermute | solution.py:1028
  71.5 1.6 collective-permute-start.15
  73.1 1.4 collective-permute-done.6
  74.4 2.7 %collective-permute-start.7 = (f32[88,128]{1,0:T(8,128)S(1)}, f32[88,128]{1,0:T(8,128)S(1)}, u32[]{:S(2)}, u32[]{:S(2)}) collective-permute-start(f32[88,128]{1,0:T(8,128)S(1)} %slice_select_fusion.8), channel_id=1, source_target_pairs={{0,16},{4,20},{8,24},{12,28},{16,0},{20,4},{24,8},{28,12},{1,17},{... | collective-permute-start | bytes 135176 | tf_op jit(solution)/shard_map/ppermute | solution.py:1028
  77.1 1.6 %collective-permute-start.36 = (f32[32,128]{1,0:T(8,128)S(1)}, f32[32,128]{1,0:T(8,128)S(1)}, u32[]{:S(2)}, u32[]{:S(2)}) collective-permute-start(f32[32,128]{1,0:T(8,128)S(1)} %add.89), channel_id=1, source_target_pairs={{0,8},{4,12},{8,0},{12,4},{16,24},{20,28},{24,16},{28,20},{1,9},{5... | collective-permute-start | bytes 49160 | tf_op jit(solution)/shard_map/ppermute | solution.py:1028
  78.8 2.2 %collective-permute-done.36 = f32[32,128]{1,0:T(8,128)S(1)} collective-permute-done((f32[32,128]{1,0:T(8,128)S(1)}, f32[32,128]{1,0:T(8,128)S(1)}, u32[]{:S(2)}, u32[]{:S(2)}) %collective-permute-start.36) | collective-permute-done | bytes 16416 | tf_op jit(solution)/shard_map/ppermute | solution.py:1028
  81.5 1.2 copy.43.refs_14_
  82.7 3.5 %collective-permute-done.37 = f32[32,128]{1,0:T(8,128)S(1)} collective-permute-done((f32[32,128]{1,0:T(8,128)S(1)}, f32[32,128]{1,0:T(8,128)S(1)}, u32[]{:S(2)}, u32[]{:S(2)}) %collective-permute-start.37) | collective-permute-done | bytes 16416 | tf_op jit(solution)/shard_map/ppermute | solution.py:1028
  87.9 3.2 %collective-permute-done.8 = f32[88,128]{1,0:T(8,128)S(1)} collective-permute-done((f32[88,128]{1,0:T(8,128)S(1)}, f32[88,128]{1,0:T(8,128)S(1)}, u32[]{:S(2)}, u32[]{:S(2)}) %collective-permute-start.8) | collective-permute-done | bytes 45088 | tf_op jit(solution)/shard_map/ppermute | solution.py:1028
  92.3 1.4 add.82
  93.8 1.7 %collective-permute-start.26 = (f32[1168,128]{1,0:T(8,128)S(1)}, f32[1168,128]{1,0:T(8,128)S(1)}, u32[]{:S(2)}, u32[]{:S(2)}) collective-permute-start(f32[1168,128]{1,0:T(8,128)S(1)} %slice_bitcast_fusion), channel_id=1, source_target_pairs={{0,2},{1,3},{2,0},{3,1},{4,6},{5,7},{6,4},{7,5},{8,10},{9,11},{10,... | collective-permute-start | bytes 1794056 | tf_op jit(solution)/shard_map/ppermute | solution.py:1028
  96.5 1.2 collective-permute-start.17
  97.6 5.6 %collective-permute-done.10 = f32[352,128]{1,0:T(8,128)S(1)} collective-permute-done((f32[352,128]{1,0:T(8,128)S(1)}, f32[352,128]{1,0:T(8,128)S(1)}, u32[]{:S(2)}, u32[]{:S(2)}) %collective-permute-start.10) | collective-permute-done | bytes 180256 | tf_op jit(solution)/shard_map/ppermute | solution.py:1028
  105.7 5.4 %collective-permute-done.27 = f32[608,128]{1,0:T(8,128)S(1)} collective-permute-done((f32[608,128]{1,0:T(8,128)S(1)}, f32[608,128]{1,0:T(8,128)S(1)}, u32[]{:S(2)}, u32[]{:S(2)}) %collective-permute-start.27) | collective-permute-done | bytes 311328 | tf_op jit(solution)/shard_map/ppermute | solution.py:1028
  112.7 3.8 %collective-permute-done.28 = f32[304,128]{1,0:T(8,128)S(1)} collective-permute-done((f32[304,128]{1,0:T(8,128)S(1)}, f32[304,128]{1,0:T(8,128)S(1)}, u32[]{:S(2)}, u32[]{:S(2)}) %collective-permute-start.28) | collective-permute-done | bytes 155680 | tf_op jit(solution)/shard_map/ppermute | solution.py:1028
  117.5 1.5 collective-permute-done.19
  119.0 3.5 %collective-permute-done.29 = f32[152,128]{1,0:T(8,128)S(1)} collective-permute-done((f32[152,128]{1,0:T(8,128)S(1)}, f32[152,128]{1,0:T(8,128)S(1)}, u32[]{:S(2)}, u32[]{:S(2)}) %collective-permute-start.29) | collective-permute-done | bytes 77856 | tf_op jit(solution)/shard_map/ppermute | solution.py:1028
  123.6 5.1 %collective-permute-done.30 = f32[152,128]{1,0:T(8,128)S(1)} collective-permute-done((f32[152,128]{1,0:T(8,128)S(1)}, f32[152,128]{1,0:T(8,128)S(1)}, u32[]{:S(2)}, u32[]{:S(2)}) %collective-permute-start.30) | collective-permute-done | bytes 77856 | tf_op jit(solution)/shard_map/ppermute | solution.py:1028
  129.6 4.4 %collective-permute-done.31 = f32[304,128]{1,0:T(8,128)S(1)} collective-permute-done((f32[304,128]{1,0:T(8,128)S(1)}, f32[304,128]{1,0:T(8,128)S(1)}, u32[]{:S(2)}, u32[]{:S(2)}) %collective-permute-start.31) | collective-permute-done | bytes 155680 | tf_op jit(solution)/shard_map/ppermute | solution.py:1028
  135.3 5.8 %collective-permute-done.32 = f32[608,128]{1,0:T(8,128)S(1)} collective-permute-done((f32[608,128]{1,0:T(8,128)S(1)}, f32[608,128]{1,0:T(8,128)S(1)}, u32[]{:S(2)}, u32[]{:S(2)}) %collective-permute-start.32) | collective-permute-done | bytes 311328 | tf_op jit(solution)/shard_map/ppermute | solution.py:1028
  142.1 4.9 %moments.1 = (f32[378,128]{1,0:T(8,128)}, f32[3,512,128]{2,1,0:T(8,128)}, f32[128,756]{1,0:T(8,128)S(1)}, f32[3,2,128]{2,1,0:T(2,128)}, f32[378,128]{1,0:T(8,128...) custom-call(f32[704,128]{1,0:T(8,128)S(1)} %pad_maximum_fusion.2.ref, ...), custom_call_target="tpu_custom_call" | custom-call | tf_op jit(solution)/shard_map/moments/pallas_call | solution.py:931
  147.0 1.2 collective-permute-done.38
  148.8 1.4 collective-permute-start.39
  157.0 1.4 apply.1
  (159 shorter events, 33.2 us)
Async XLA Ops:
  0.7 8.5 %copy-start.9 = (f32[3852]{0:T(1024)S(1)}, f32[3852]{0:T(1024)}, u32[]{:S(2)}) copy-start(f32[3852]{0:T(1024)} %refs_10_.2) | copy-start | bytes 46228
  0.7 8.5 %copy-start.17 = (s32[2,2]{1,0:T(2,128)S(1)}, s32[2,2]{1,0:T(2,128)}, u32[]{:S(2)}) copy-start(s32[2,2]{1,0:T(2,128)} %refs_0_.1) | copy-start | bytes 52
  0.7 8.5 %copy-start.22 = (s32[2]{0:T(128)S(1)}, s32[2]{0:T(128)}, u32[]{:S(2)}) copy-start(s32[2]{0:T(128)} %seed_ref.1) | copy-start | bytes 28
  0.7 8.5 %copy-start.14 = (f32[3,2,1024]{2,1,0:T(2,128)S(1)}, f32[3,2,1024]{2,1,0:T(2,128)}, u32[]{:S(2)}) copy-start(f32[3,2,1024]{2,1,0:T(2,128)} %image_ref.1) | copy-start | bytes 73732
  4.8 3.1 %collective-permute-start = (bf16[688,128]{1,0:T(8,128)(2,1)S(1)}, bf16[688,128]{1,0:T(8,128)(2,1)S(1)}, u32[]{:S(2)}, u32[]{:S(2)}) collective-permute-start(bf16[688,128]{1,0:T(8,128)(2,1)S(1)} %get-tuple-element.80.refs_1_), channel_id=1, source_target_pairs={{0,1},{1,0},{2,3},{3,2},{4,5},{5,4},{6,7},{7,6},{8,9},{9,8},{10,11... | collective-permute-start | bytes 528392 | tf_op jit(solution)/shard_map/ppermute | solution.py:1028
  5.3 8.6 %collective-permute-start.1 = (bf16[688,128]{1,0:T(8,128)(2,1)S(1)}, bf16[688,128]{1,0:T(8,128)(2,1)S(1)}, u32[]{:S(2)}, u32[]{:S(2)}) collective-permute-start(bf16[688,128]{1,0:T(8,128)(2,1)S(1)} %get-tuple-element.80.refs_1_), channel_id=1, source_target_pairs={{0,2},{1,3},{2,0},{3,1},{4,6},{5,7},{6,4},{7,5},{8,10},{9,11},{10,... | collective-permute-start | bytes 528392 | tf_op jit(solution)/shard_map/ppermute | solution.py:1028
  7.9 8.8 %collective-permute-start.2 = (bf16[688,128]{1,0:T(8,128)(2,1)S(1)}, bf16[688,128]{1,0:T(8,128)(2,1)S(1)}, u32[]{:S(2)}, u32[]{:S(2)}) collective-permute-start(bf16[688,128]{1,0:T(8,128)(2,1)S(1)} %collective-permute-done.refs_2_), channel_id=1, source_target_pairs={{0,2},{1,3},{2,0},{3,1},{4,6},{5,7},{6,4},{7,5},{8,10},{9,11},{10,... | collective-permute-start | bytes 528392 | tf_op jit(solution)/shard_map/ppermute | solution.py:1028
  19.6 4.3 %collective-permute-start.3 = (f32[2,688,128]{2,1,0:T(8,128)S(1)}, f32[2,688,128]{2,1,0:T(8,128)S(1)}, u32[]{:S(2)}, u32[]{:S(2)}) collective-permute-start(f32[2,688,128]{2,1,0:T(8,128)S(1)} %get-tuple-element.86), channel_id=1, source_target_pairs={{0,1},{1,0},{2,3},{3,2},{4,5},{5,4},{6,7},{7,6},{8,9},{9,8},{10,11... | collective-permute-start | bytes 2113544 | tf_op jit(solution)/shard_map/ppermute | solution.py:1028
  19.6 2.5 %collective-permute-start.11 = (bf16[864,128]{1,0:T(8,128)(2,1)S(1)}, bf16[864,128]{1,0:T(8,128)(2,1)S(1)}, u32[]{:S(2)}, u32[]{:S(2)}) collective-permute-start(bf16[864,128]{1,0:T(8,128)(2,1)S(1)} %get-tuple-element.87.refs_1_), channel_id=1, source_target_pairs={{0,1},{1,0},{2,3},{3,2},{4,5},{5,4},{6,7},{7,6},{8,9},{9,8},{10,11... | collective-permute-start | bytes 663560 | tf_op jit(solution)/shard_map/ppermute | solution.py:1028
  20.1 8.3 %collective-permute-start.12 = (bf16[864,128]{1,0:T(8,128)(2,1)S(1)}, bf16[864,128]{1,0:T(8,128)(2,1)S(1)}, u32[]{:S(2)}, u32[]{:S(2)}) collective-permute-start(bf16[864,128]{1,0:T(8,128)(2,1)S(1)} %get-tuple-element.87.refs_1_), channel_id=1, source_target_pairs={{0,2},{1,3},{2,0},{3,1},{4,6},{5,7},{6,4},{7,5},{8,10},{9,11},{10,... | collective-permute-start | bytes 663560 | tf_op jit(solution)/shard_map/ppermute | solution.py:1028
  22.1 11.0 %collective-permute-start.13 = (bf16[864,128]{1,0:T(8,128)(2,1)S(1)}, bf16[864,128]{1,0:T(8,128)(2,1)S(1)}, u32[]{:S(2)}, u32[]{:S(2)}) collective-permute-start(bf16[864,128]{1,0:T(8,128)(2,1)S(1)} %collective-permute-done.11.refs_2_), channel_id=1, source_target_pairs={{0,2},{1,3},{2,0},{3,1},{4,6},{5,7},{6,4},{7,5},{8,10},{9,11},{10,... | collective-permute-start | bytes 663560 | tf_op jit(solution)/shard_map/ppermute | solution.py:1028
  24.0 12.2 %copy-start.27 = (f32[2,688,128]{2,1,0:T(8,128)}, f32[2,688,128]{2,1,0:T(8,128)S(1)}, u32[]{:S(2)}) copy-start(f32[2,688,128]{2,1,0:T(8,128)S(1)} %add.72) | copy-start | bytes 2113540
  24.8 15.7 %collective-permute-start.4 = (f32[688,128]{1,0:T(8,128)}, f32[688,128]{1,0:T(8,128)}, u32[]{:S(2)}, u32[]{:S(2)}) collective-permute-start(f32[688,128]{1,0:T(8,128)} %slice_bitcast_fusion.4), channel_id=1, source_target_pairs={{0,2},{1,3},{2,0},{3,1},{4,6},{5,7},{6,4},{7,5},{8,10},{9,11},{10,... | collective-permute-start | bytes 1056776 | tf_op jit(solution)/shard_map/ppermute | solution.py:1028
  25.1 12.9 %collective-permute-start.22 = (bf16[1168,128]{1,0:T(8,128)(2,1)S(1)}, bf16[1168,128]{1,0:T(8,128)(2,1)S(1)}, u32[]{:S(2)}, u32[]{:S(2)}) collective-permute-start(bf16[1168,128]{1,0:T(8,128)(2,1)S(1)} %get-tuple-element.94.refs_1_), channel_id=1, source_target_pairs={{0,1},{1,0},{2,3},{3,2},{4,5},{5,4},{6,7},{7,6},{8,9},{9,8},{10,11... | collective-permute-start | bytes 897032 | tf_op jit(solution)/shard_map/ppermute | solution.py:1028
  36.2 31.0 %collective-permute-start.14 = (f32[2,864,128]{2,1,0:T(8,128)}, f32[2,864,128]{2,1,0:T(8,128)}, u32[]{:S(2)}, u32[]{:S(2)}) collective-permute-start(f32[2,864,128]{2,1,0:T(8,128)} %get-tuple-element.93), channel_id=1, source_target_pairs={{0,1},{1,0},{2,3},{3,2},{4,5},{5,4},{6,7},{7,6},{8,9},{9,8},{10,11... | collective-permute-start | bytes 2654216 | tf_op jit(solution)/shard_map/ppermute | solution.py:1028
  36.2 10.6 %collective-permute-start.23 = (bf16[1168,128]{1,0:T(8,128)(2,1)S(1)}, bf16[1168,128]{1,0:T(8,128)(2,1)S(1)}, u32[]{:S(2)}, u32[]{:S(2)}) collective-permute-start(bf16[1168,128]{1,0:T(8,128)(2,1)S(1)} %get-tuple-element.94.refs_1_), channel_id=1, source_target_pairs={{0,2},{1,3},{2,0},{3,1},{4,6},{5,7},{6,4},{7,5},{8,10},{9,11},{10,... | collective-permute-start | bytes 897032 | tf_op jit(solution)/shard_map/ppermute | solution.py:1028
  37.9 14.7 %collective-permute-start.24 = (bf16[1168,128]{1,0:T(8,128)(2,1)S(1)}, bf16[1168,128]{1,0:T(8,128)(2,1)S(1)}, u32[]{:S(2)}, u32[]{:S(2)}) collective-permute-start(bf16[1168,128]{1,0:T(8,128)(2,1)S(1)} %collective-permute-done.22.refs_2_), channel_id=1, source_target_pairs={{0,2},{1,3},{2,0},{3,1},{4,6},{5,7},{6,4},{7,5},{8,10},{9,11},{10,... | collective-permute-start | bytes 897032 | tf_op jit(solution)/shard_map/ppermute | solution.py:1028
  41.6 11.1 %copy-start.24 = (f32[688,128]{1,0:T(8,128)}, f32[688,128]{1,0:T(8,128)S(1)}, u32[]{:S(2)}) copy-start(f32[688,128]{1,0:T(8,128)S(1)} %fusion.2) | copy-start | bytes 1056772
  42.3 26.1 %collective-permute-start.5 = (f32[352,128]{1,0:T(8,128)}, f32[352,128]{1,0:T(8,128)}, u32[]{:S(2)}, u32[]{:S(2)}) collective-permute-start(f32[352,128]{1,0:T(8,128)} %slice_select_fusion.2), channel_id=1, source_target_pairs={{0,4},{4,0},{8,12},{12,8},{16,20},{20,16},{24,28},{28,24},{1,5},{5... | collective-permute-start | bytes 540680 | tf_op jit(solution)/shard_map/ppermute | solution.py:1028
  60.3 1.2 collective-permute-start.33
  61.6 3.8 %collective-permute-start.34 = (f32[32,128]{1,0:T(8,128)S(1)}, f32[32,128]{1,0:T(8,128)S(1)}, u32[]{:S(2)}, u32[]{:S(2)}) collective-permute-start(f32[32,128]{1,0:T(8,128)S(1)} %add.87), channel_id=1, source_target_pairs={{0,2},{1,3},{2,0},{3,1},{4,6},{5,7},{6,4},{7,5},{8,10},{9,11},{10,... | collective-permute-start | bytes 49160 | tf_op jit(solution)/shard_map/ppermute | solution.py:1028
  63.4 29.0 %collective-permute-start.25 = (f32[2,1168,128]{2,1,0:T(8,128)}, f32[2,1168,128]{2,1,0:T(8,128)}, u32[]{:S(2)}, u32[]{:S(2)}) collective-permute-start(f32[2,1168,128]{2,1,0:T(8,128)} %copy-done.23), channel_id=1, source_target_pairs={{0,1},{1,0},{2,3},{3,2},{4,5},{5,4},{6,7},{7,6},{8,9},{9,8},{10,11... | collective-permute-start | bytes 3588104 | tf_op jit(solution)/shard_map/ppermute | solution.py:1028
  65.4 11.7 %collective-permute-start.35 = (f32[32,128]{1,0:T(8,128)S(1)}, f32[32,128]{1,0:T(8,128)S(1)}, u32[]{:S(2)}, u32[]{:S(2)}) collective-permute-start(f32[32,128]{1,0:T(8,128)S(1)} %add.88), channel_id=1, source_target_pairs={{0,4},{4,0},{8,12},{12,8},{16,20},{20,16},{24,28},{28,24},{1,5},{5... | collective-permute-start | bytes 49160 | tf_op jit(solution)/shard_map/ppermute | solution.py:1028
  68.5 12.5 %copy-start.26 = (f32[2,864,128]{2,1,0:T(8,128)}, f32[2,864,128]{2,1,0:T(8,128)S(1)}, u32[]{:S(2)}) copy-start(f32[2,864,128]{2,1,0:T(8,128)S(1)} %add.77) | copy-start | bytes 2654212
  68.5 12.8 %copy-start.28 = (f32[128,756]{0,1:T(8,128)S(1)}, f32[128,756]{0,1:T(8,128)}, u32[]{:S(2)}) copy-start(f32[128,756]{0,1:T(8,128)} %param.28) | copy-start | bytes 1161220
  69.8 4.6 %collective-permute-start.6 = (f32[176,128]{1,0:T(8,128)S(1)}, f32[176,128]{1,0:T(8,128)S(1)}, u32[]{:S(2)}, u32[]{:S(2)}) collective-permute-start(f32[176,128]{1,0:T(8,128)S(1)} %slice_select_fusion.5), channel_id=1, source_target_pairs={{0,8},{4,12},{8,0},{12,4},{16,24},{20,28},{24,16},{28,20},{1,9},{5... | collective-permute-start | bytes 270344 | tf_op jit(solution)/shard_map/ppermute | solution.py:1028
  71.5 14.7 %collective-permute-start.15 = (f32[864,128]{1,0:T(8,128)S(1)}, f32[864,128]{1,0:T(8,128)S(1)}, u32[]{:S(2)}, u32[]{:S(2)}) collective-permute-start(f32[864,128]{1,0:T(8,128)S(1)} %slice_bitcast_fusion.2), channel_id=1, source_target_pairs={{0,2},{1,3},{2,0},{3,1},{4,6},{5,7},{6,4},{7,5},{8,10},{9,11},{10,... | collective-permute-start | bytes 1327112 | tf_op jit(solution)/shard_map/ppermute | solution.py:1028
  74.4 11.7 %collective-permute-start.7 = (f32[88,128]{1,0:T(8,128)S(1)}, f32[88,128]{1,0:T(8,128)S(1)}, u32[]{:S(2)}, u32[]{:S(2)}) collective-permute-start(f32[88,128]{1,0:T(8,128)S(1)} %slice_select_fusion.8), channel_id=1, source_target_pairs={{0,16},{4,20},{8,24},{12,28},{16,0},{20,4},{24,8},{28,12},{1,17},{... | collective-permute-start | bytes 135176 | tf_op jit(solution)/shard_map/ppermute | solution.py:1028
  77.1 3.8 %collective-permute-start.36 = (f32[32,128]{1,0:T(8,128)S(1)}, f32[32,128]{1,0:T(8,128)S(1)}, u32[]{:S(2)}, u32[]{:S(2)}) collective-permute-start(f32[32,128]{1,0:T(8,128)S(1)} %add.89), channel_id=1, source_target_pairs={{0,8},{4,12},{8,0},{12,4},{16,24},{20,28},{24,16},{28,20},{1,9},{5... | collective-permute-start | bytes 49160 | tf_op jit(solution)/shard_map/ppermute | solution.py:1028
  80.9 5.2 %collective-permute-start.37 = (f32[32,128]{1,0:T(8,128)S(1)}, f32[32,128]{1,0:T(8,128)S(1)}, u32[]{:S(2)}, u32[]{:S(2)}) collective-permute-start(f32[32,128]{1,0:T(8,128)S(1)} %add.90), channel_id=1, source_target_pairs={{0,16},{4,20},{8,24},{12,28},{16,0},{20,4},{24,8},{28,12},{1,17},{... | collective-permute-start | bytes 49160 | tf_op jit(solution)/shard_map/ppermute | solution.py:1028
  86.1 5.0 %collective-permute-start.8 = (f32[88,128]{1,0:T(8,128)S(1)}, f32[88,128]{1,0:T(8,128)S(1)}, u32[]{:S(2)}, u32[]{:S(2)}) collective-permute-start(f32[88,128]{1,0:T(8,128)S(1)} %select_add_fusion.8), channel_id=1, source_target_pairs={{0,16},{4,20},{8,24},{12,28},{16,0},{20,4},{24,8},{28,12},{1,17},{... | collective-permute-start | bytes 135176 | tf_op jit(solution)/shard_map/ppermute | solution.py:1028
  87.3 9.1 %collective-permute-start.16 = (f32[448,128]{1,0:T(8,128)S(1)}, f32[448,128]{1,0:T(8,128)S(1)}, u32[]{:S(2)}, u32[]{:S(2)}) collective-permute-start(f32[448,128]{1,0:T(8,128)S(1)} %slice_select_fusion.1), channel_id=1, source_target_pairs={{0,4},{4,0},{8,12},{12,8},{16,20},{20,16},{24,28},{28,24},{1,5},{5... | collective-permute-start | bytes 688136 | tf_op jit(solution)/shard_map/ppermute | solution.py:1028
  91.2 4.6 %collective-permute-start.9 = (f32[176,128]{1,0:T(8,128)S(1)}, f32[176,128]{1,0:T(8,128)S(1)}, u32[]{:S(2)}, u32[]{:S(2)}) collective-permute-start(f32[176,128]{1,0:T(8,128)S(1)} %pad_maximum_fusion.8), channel_id=1, source_target_pairs={{0,8},{4,12},{8,0},{12,4},{16,24},{20,28},{24,16},{28,20},{1,9},{5... | collective-permute-start | bytes 270344 | tf_op jit(solution)/shard_map/ppermute | solution.py:1028
  93.8 10.2 %collective-permute-start.26 = (f32[1168,128]{1,0:T(8,128)S(1)}, f32[1168,128]{1,0:T(8,128)S(1)}, u32[]{:S(2)}, u32[]{:S(2)}) collective-permute-start(f32[1168,128]{1,0:T(8,128)S(1)} %slice_bitcast_fusion), channel_id=1, source_target_pairs={{0,2},{1,3},{2,0},{3,1},{4,6},{5,7},{6,4},{7,5},{8,10},{9,11},{10,... | collective-permute-start | bytes 1794056 | tf_op jit(solution)/shard_map/ppermute | solution.py:1028
  95.8 7.4 %collective-permute-start.10 = (f32[352,128]{1,0:T(8,128)S(1)}, f32[352,128]{1,0:T(8,128)S(1)}, u32[]{:S(2)}, u32[]{:S(2)}) collective-permute-start(f32[352,128]{1,0:T(8,128)S(1)} %pad_maximum_fusion.5), channel_id=1, source_target_pairs={{0,4},{4,0},{8,12},{12,8},{16,20},{20,16},{24,28},{28,24},{1,5},{5... | collective-permute-start | bytes 540680 | tf_op jit(solution)/shard_map/ppermute | solution.py:1028
  96.5 8.2 %collective-permute-start.17 = (f32[224,128]{1,0:T(8,128)S(1)}, f32[224,128]{1,0:T(8,128)S(1)}, u32[]{:S(2)}, u32[]{:S(2)}) collective-permute-start(f32[224,128]{1,0:T(8,128)S(1)} %slice_select_fusion.4), channel_id=1, source_target_pairs={{0,8},{4,12},{8,0},{12,4},{16,24},{20,28},{24,16},{28,20},{1,9},{5... | collective-permute-start | bytes 344072 | tf_op jit(solution)/shard_map/ppermute | solution.py:1028
  104.1 7.0 %collective-permute-start.27 = (f32[608,128]{1,0:T(8,128)S(1)}, f32[608,128]{1,0:T(8,128)S(1)}, u32[]{:S(2)}, u32[]{:S(2)}) collective-permute-start(f32[608,128]{1,0:T(8,128)S(1)} %slice_select_fusion), channel_id=1, source_target_pairs={{0,4},{4,0},{8,12},{12,8},{16,20},{20,16},{24,28},{28,24},{1,5},{5... | collective-permute-start | bytes 933896 | tf_op jit(solution)/shard_map/ppermute | solution.py:1028
  104.7 7.4 %collective-permute-start.18 = (f32[112,128]{1,0:T(8,128)S(1)}, f32[112,128]{1,0:T(8,128)S(1)}, u32[]{:S(2)}, u32[]{:S(2)}) collective-permute-start(f32[112,128]{1,0:T(8,128)S(1)} %slice_select_fusion.7), channel_id=1, source_target_pairs={{0,16},{4,20},{8,24},{12,28},{16,0},{20,4},{24,8},{28,12},{1,17},{... | collective-permute-start | bytes 172040 | tf_op jit(solution)/shard_map/ppermute | solution.py:1028
  111.2 5.3 %collective-permute-start.28 = (f32[304,128]{1,0:T(8,128)S(1)}, f32[304,128]{1,0:T(8,128)S(1)}, u32[]{:S(2)}, u32[]{:S(2)}) collective-permute-start(f32[304,128]{1,0:T(8,128)S(1)} %slice_select_fusion.3), channel_id=1, source_target_pairs={{0,8},{4,12},{8,0},{12,4},{16,24},{20,28},{24,16},{28,20},{1,9},{5... | collective-permute-start | bytes 466952 | tf_op jit(solution)/shard_map/ppermute | solution.py:1028
  112.2 6.8 %collective-permute-start.19 = (f32[112,128]{1,0:T(8,128)S(1)}, f32[112,128]{1,0:T(8,128)S(1)}, u32[]{:S(2)}, u32[]{:S(2)}) collective-permute-start(f32[112,128]{1,0:T(8,128)S(1)} %select_add_fusion.7), channel_id=1, source_target_pairs={{0,16},{4,20},{8,24},{12,28},{16,0},{20,4},{24,8},{28,12},{1,17},{... | collective-permute-start | bytes 172040 | tf_op jit(solution)/shard_map/ppermute | solution.py:1028
  116.5 6.0 %collective-permute-start.29 = (f32[152,128]{1,0:T(8,128)S(1)}, f32[152,128]{1,0:T(8,128)S(1)}, u32[]{:S(2)}, u32[]{:S(2)}) collective-permute-start(f32[152,128]{1,0:T(8,128)S(1)} %slice_select_fusion.6), channel_id=1, source_target_pairs={{0,16},{4,20},{8,24},{12,28},{16,0},{20,4},{24,8},{28,12},{1,17},{... | collective-permute-start | bytes 233480 | tf_op jit(solution)/shard_map/ppermute | solution.py:1028
  122.5 6.2 %collective-permute-start.30 = (f32[152,128]{1,0:T(8,128)S(1)}, f32[152,128]{1,0:T(8,128)S(1)}, u32[]{:S(2)}, u32[]{:S(2)}) collective-permute-start(f32[152,128]{1,0:T(8,128)S(1)} %select_add_fusion.6), channel_id=1, source_target_pairs={{0,16},{4,20},{8,24},{12,28},{16,0},{20,4},{24,8},{28,12},{1,17},{... | collective-permute-start | bytes 233480 | tf_op jit(solution)/shard_map/ppermute | solution.py:1028
  122.9 6.1 %collective-permute-start.20 = (f32[224,128]{1,0:T(8,128)S(1)}, f32[224,128]{1,0:T(8,128)S(1)}, u32[]{:S(2)}, u32[]{:S(2)}) collective-permute-start(f32[224,128]{1,0:T(8,128)S(1)} %pad_maximum_fusion.7), channel_id=1, source_target_pairs={{0,8},{4,12},{8,0},{12,4},{16,24},{20,28},{24,16},{28,20},{1,9},{5... | collective-permute-start | bytes 344072 | tf_op jit(solution)/shard_map/ppermute | solution.py:1028
  128.8 5.3 %collective-permute-start.31 = (f32[304,128]{1,0:T(8,128)S(1)}, f32[304,128]{1,0:T(8,128)S(1)}, u32[]{:S(2)}, u32[]{:S(2)}) collective-permute-start(f32[304,128]{1,0:T(8,128)S(1)} %pad_maximum_fusion.6), channel_id=1, source_target_pairs={{0,8},{4,12},{8,0},{12,4},{16,24},{20,28},{24,16},{28,20},{1,9},{5... | collective-permute-start | bytes 466952 | tf_op jit(solution)/shard_map/ppermute | solution.py:1028
  129.1 6.1 %collective-permute-start.21 = (f32[448,128]{1,0:T(8,128)S(1)}, f32[448,128]{1,0:T(8,128)S(1)}, u32[]{:S(2)}, u32[]{:S(2)}) collective-permute-start(f32[448,128]{1,0:T(8,128)S(1)} %pad_maximum_fusion.4), channel_id=1, source_target_pairs={{0,4},{4,0},{8,12},{12,8},{16,20},{20,16},{24,28},{28,24},{1,5},{5... | collective-permute-start | bytes 688136 | tf_op jit(solution)/shard_map/ppermute | solution.py:1028
  134.1 7.0 %collective-permute-start.32 = (f32[608,128]{1,0:T(8,128)S(1)}, f32[608,128]{1,0:T(8,128)S(1)}, u32[]{:S(2)}, u32[]{:S(2)}) collective-permute-start(f32[608,128]{1,0:T(8,128)S(1)} %pad_maximum_fusion.3), channel_id=1, source_target_pairs={{0,4},{4,0},{8,12},{12,8},{16,20},{20,16},{24,28},{28,24},{1,5},{5... | collective-permute-start | bytes 933896 | tf_op jit(solution)/shard_map/ppermute | solution.py:1028
  146.9 1.2 collective-permute-start.38
  148.8 4.0 %collective-permute-start.39 = (f32[16,128]{1,0:T(8,128)}, f32[16,128]{1,0:T(8,128)}, u32[]{:S(2)}, u32[]{:S(2)}) collective-permute-start(f32[16,128]{1,0:T(8,128)} %add.92), channel_id=1, source_target_pairs={{0,2},{1,3},{2,0},{3,1},{4,6},{5,7},{6,4},{7,5},{8,10},{9,11},{10,... | collective-permute-start | bytes 24584 | tf_op jit(solution)/shard_map/ppermute | solution.py:1028
  (21 other events, 70.4 us)

commit v2 on v1

--- a/solution.py
+++ b/solution.py
@@ -24,8 +24,8 @@
 LANE = 128
 LEVELS = 3
 FLOW_ROWS = 32
-LOSS_ROW = 31
-VMEM_BYTES = 50 * 1024 * 1024
+STATS_ROWS = 8
+VMEM_BYTES = 20 * 1024 * 1024
 
 
 def round_up(value, unit):
@@ -66,6 +66,47 @@
 
 def pack_rows(level):
     return first_rows(level) + HID + last_rows(level)
+
+
+def pack_start(level):
+    return sum(pack_rows(other) for other in range(LEVELS - 1, level, -1))
+
+
+def flow_block_rows(narrow):
+    return round_up(FLOW_ROWS // narrow, 8) + STATS_ROWS
+
+
+def grad_rows(level, narrow):
+    rows = pack_rows(level) + (flow_block_rows(narrow) if level == 0 else 0)
+    return round_up(rows, 64)
+
+
+def stage_rows(level):
+    padded = round_up(chan(level), 8)
+    half = round_up(chan(level) // 2, 8)
+    sizes = [
+        ("normed", padded),
+        ("mixed", padded),
+        ("share", 8),
+        ("held", padded),
+        ("block", padded),
+        ("prior", half),
+        ("grad", padded),
+        ("small", padded),
+        ("prior_grad", half),
+    ]
+    starts = {}
+    at = 0
+    for name, size in sizes[:6]:
+        starts[name] = at
+        at = at + size
+    starts["rows"] = at
+    at = 0
+    for name, size in sizes[6:]:
+        starts[name] = at
+        at = at + size
+    starts["result_rows"] = at
+    return starts
 
 
 def flow_lengths():
@@ -372,13 +413,6 @@
 def pack_kernel(conv_in_ref, mixer_ref, conv_out_ref, bias_ref, *out_refs):
     in_start = 0
     out_start = 0
-    turned = jnp.concatenate(
-        [
-            conv_out_ref[...],
-            jnp.zeros((LANE, round_up(conv_out_ref.shape[1], LANE) - conv_out_ref.shape[1]), F32),
-        ],
-        1,
-    ).T
     for level in range(LEVELS):
         out_ref = out_refs[level]
         rows, columns = in_rows(level), 9 * chan(level)
@@ -392,10 +426,11 @@
         pieces = pieces + twos + [jnp.zeros((1, LANE), F32)]
         out_ref[0:top, :] = jnp.concatenate(pieces, 0).astype(BF16)
         out_ref[top : top + HID, :] = mixer_ref[level].astype(BF16)
-        tail = turned[out_start : out_start + columns]
+        tail = conv_out_ref[out_start : out_start + columns, :]
         if last_rows(level) > columns:
             tail = jnp.concatenate([tail, jnp.zeros((last_rows(level) - columns, LANE), F32)], 0)
         out_ref[top + HID :, :] = tail.astype(BF16)
+        out_refs[LEVELS][pack_start(level) : pack_start(level) + pack_rows(level), :] = out_ref[...]
         in_start = in_start + rows
         out_start = out_start + columns
 
@@ -444,7 +479,6 @@
             )
         )
     state = exact_dot(order_chooser(3, 8), jnp.concatenate(quarters, 0))
-    at = 0
     for level in range(LEVELS):
         channels = chan(level)
         grid = side(level)
@@ -475,21 +509,17 @@
         row_share = jnp.clip(high - row * unit, 0, unit).astype(F32) / unit
         column_share = jnp.clip(wide - column * unit, 0, unit).astype(F32) / unit
         share = jnp.where(image < images, row_share * column_share, 0.0)
-        normed_ref, mixed_ref, share_ref, held_ref, block_ref = out_refs[at : at + 5]
-        at = at + 5
-        normed_ref[...] = normed
-        mixed_ref[...] = mixed
-        share_ref[...] = share
-        held_ref[...] = held
-        block_ref[...] = jnp.concatenate(
-            [block, jnp.zeros((channels, LANE - channels), F32)], 1
-        )
+        out_ref = out_refs[level]
+        starts = stage_rows(level)
+        out_ref[starts["normed"] : starts["normed"] + channels, :] = normed
+        out_ref[starts["mixed"] : starts["mixed"] + channels, :] = mixed
+        out_ref[starts["share"] : starts["share"] + 8, :] = share
+        out_ref[starts["held"] : starts["held"] + channels, 0:LANE] = held
+        out_ref[starts["block"] : starts["block"] + channels, 0:channels] = block
         if level < LEVELS - 1:
-            prior = flow_block(flat, offsets["priormatrix"], channels // 2, channels)
-            out_refs[at][...] = jnp.concatenate(
-                [prior, jnp.zeros((channels // 2, LANE - channels), F32)], 1
+            out_ref[starts["prior"] : starts["prior"] + channels // 2, 0:channels] = flow_block(
+                flat, offsets["priormatrix"], channels // 2, channels
             )
-            at = at + 1
             state = squeeze(
                 mixed[: channels // 2], squeeze_chooser(grid, images), positions(level + 1, images)
             )
@@ -506,20 +536,11 @@
     is_last = level == LEVELS - 1
     index_ref = refs[0]
     weight_refs = refs[1 : 1 + narrow]
-    mixed_ref, share_ref, held_ref = refs[1 + narrow : 4 + narrow]
-    at = 4 + narrow
-    prior_ref = None
-    if not is_last:
-        prior_ref = refs[at]
-        at = at + 1
-    keep_ref, send_ref, grad_ref, small_ref = refs[at : at + 4]
-    at = at + 4
-    prior_grad_ref = None
-    if not is_last:
-        prior_grad_ref = refs[at]
-        at = at + 1
-    order_ref, slope_one_ref, slope_two_ref, one_ref, two_ref = refs[at:]
-    me = index_ref[0]
+    bases = [pack_start(level) if ref.shape[0] > pack_rows(level) else 0 for ref in weight_refs]
+    stage_ref, keep_ref, send_ref, result_ref = refs[1 + narrow : 5 + narrow]
+    order_ref, slope_one_ref, slope_two_ref, one_ref, two_ref = refs[5 + narrow :]
+    starts = stage_rows(level)
+    me = index_ref[0, 0]
     channels = chan(level)
     half = channels // 2
     count = positions(level, images)
@@ -529,20 +550,23 @@
     width = HID // narrow
 
     def weights(start, length):
-        return jnp.concatenate([ref[start : start + length, :] for ref in weight_refs], 1)
+        return jnp.concatenate(
+            [ref[base + start : base + start + length, :] for ref, base in zip(weight_refs, bases)], 1
+        )
 
     for r_in in range(narrow):
-        start = pl.multiple_of(top + (me ^ r_in) * width, 16)
         for r_out in range(narrow):
+            start = pl.multiple_of(bases[r_out] + top + (me ^ r_in) * width, 16)
             order_ref[r_in * width : (r_in + 1) * width, r_out * LANE : (r_out + 1) * LANE] = (
                 weight_refs[r_out][pl.ds(start, width), :]
             )
     weight_in = weights(0, top)
     weight_mix = order_ref[...]
     weight_out = weights(top + HID, tail)
-    first = mixed_ref[0:half, :]
-    second = mixed_ref[half:channels, :]
-    share = share_ref[0:1, :]
+    mixed = starts["mixed"]
+    first = stage_ref[mixed : mixed + half, :]
+    second = stage_ref[mixed + half : mixed + channels, :]
+    share = stage_ref[starts["share"] : starts["share"] + 1, :]
     pieces = tap_stack(rounded(first), masks, level, 1)
     pieces.append(jnp.ones((3, count), F32))
     pieces.append(jnp.zeros((top - rows - 3, count), F32))
@@ -560,7 +584,7 @@
     two_ref[...] = active.astype(BF16)
     spread = plain_dot(weight_out, two_ref[...])
     net_raw = tap_sum(spread, masks, level, 1, channels)
-    held = held_ref[...]
+    held = stage_ref[starts["held"] : starts["held"] + channels, 0:LANE]
     out_bias, out_scale = held[:, 2:3], held[:, 3:4]
     growth = jnp.exp(3.0 * out_scale)
     output = (net_raw + out_bias) * growth
@@ -575,7 +599,7 @@
         scale = jnp.broadcast_to(scale, joined.shape)
     else:
         joined = latent
-        prior = prior_ref[...][:, :channels]
+        prior = stage_ref[starts["prior"] : starts["prior"] + half, 0:channels]
         stats = exact_rows(prior, first) + held[:, 4:5]
         mean, scale = stats[:half], stats[half:]
     gap = joined - mean
@@ -585,7 +609,6 @@
     total = jnp.sum(jnp.sum(share * log_sigmoid, 0, keepdims=True), 1, keepdims=True) + jnp.sum(
         jnp.sum(share * log_prior, 0, keepdims=True), 1, keepdims=True
     )
-    logs_total = jnp.sum(held[:, 1:2], 0, keepdims=True)
     share_total = jnp.sum(share, 1, keepdims=True)
     grad_joined = share * (gap * shrink)
     grad_scale = share * (1.0 - square)
@@ -611,12 +634,11 @@
         small = put(small, 4, grad_stats)
         grad_first = exact_dot(prior, grad_stats)
         prior_grad = exact_columns(first, grad_stats)
-        prior_grad_ref[...] = jnp.concatenate(
-            [prior_grad, jnp.zeros((half, LANE - channels), F32)], 1
-        )
+        start = starts["prior_grad"]
+        result_ref[start : start + half, 0:channels] = prior_grad
     small = jnp.where(lane == 6, -total, small)
     small = jnp.where(lane == 7, share_total, small)
-    small_ref[...] = small
+    result_ref[starts["small"] : starts["small"] + channels, 0:LANE] = small
     pieces = tap_stack(rounded(grad_net), masks, level, -1)
     if tail > used:
         pieces.append(jnp.zeros((tail - used, count), F32))
@@ -641,86 +663,179 @@
     grad_in = contract_columns(stacked, grad_one)
     store(0, grad_in[: top - 16])
     store(top - 16, grad_in[top - 16 :] + contract_columns(pick, grad_two))
+    rest = keep_ref.shape[1] - pack_rows(level)
+    if rest and level > 0:
+        for ref in (keep_ref, send_ref):
+            ref[:, pack_rows(level) :, :] = jnp.zeros((narrow // 2, rest, LANE), F32)
     grad_stack = plain_dot(weight_in, grad_one)
     grad_first = grad_first + tap_sum(grad_stack, masks, level, -1, half)
-    grad_ref[...] = jnp.concatenate([grad_first, grad_second], 0)
-
-
-def flow_post_kernel(images, *refs):
-    count_ref = refs[0]
-    out_ref = refs[-1]
-    at = 1
-    per_level = []
-    for level in range(LEVELS):
-        number = 5 if level == LEVELS - 1 else 6
-        per_level.append(refs[at : at + number])
-        at = at + number
+    result_ref[0:half, :] = grad_first
+    result_ref[half:channels, :] = grad_second
+
+
+def flow_level(level, images, stage_ref, result_ref, carried, flat):
+    channels = chan(level)
+    half = channels // 2
+    starts = stage_rows(level)
+
+    def part(ref, name, rows, lanes):
+        return ref[starts[name] : starts[name] + rows, 0:lanes]
+
+    count = positions(level, images)
+    offsets = flow_offsets(level)
+    grad = part(result_ref, "grad", channels, count)
+    if carried is not None:
+        grad = grad + jnp.concatenate([carried, jnp.zeros_like(carried)], 0)
+    normed = part(stage_ref, "normed", channels, count)
+    held = part(stage_ref, "held", channels, LANE)
+    small = part(result_ref, "small", channels, LANE)
+    block = part(stage_ref, "block", channels, channels)
+    lower, upper, reverse, diagonal = triangles(block)
+    mixing_left = exact_dot(reverse, lower)
+    grad_normed = exact_rows(exact_dot(mixing_left, upper), grad)
+    grad_mixing = exact_dot(reverse, exact_columns(grad, normed))
+    grad_lower = exact_columns(grad_mixing, upper)
+    grad_upper = exact_rows(lower, grad_mixing)
+    share_total = small[0:1, 7:8]
+    row = iota((channels, channels), 0)
+    column = iota((channels, channels), 1)
+    grad_block = jnp.where(
+        row > column,
+        grad_lower,
+        jnp.where(row < column, grad_upper, grad_upper * diagonal - share_total),
+    )
+    growth = jnp.exp(held[:, 1:2])
+    grad_state = grad_normed * growth
+    grad_bias = jnp.sum(grad_state, 1, keepdims=True)
+    grad_logs = jnp.sum(grad_normed * normed, 1, keepdims=True) - share_total
+    term = flow_block_back(grad_block, offsets["block"], channels, channels)
     turned = jnp.zeros((LANE, LANE), F32)
-    flat = jnp.zeros((FLOW_ROWS, LANE), F32)
-    loss = jnp.zeros((1, 1), F32)
+    for index, (name, offset) in enumerate(column_names(level)):
+        if name == "bias":
+            values = grad_bias
+        elif name == "logs":
+            values = grad_logs
+        else:
+            values = small[:, index : index + 1]
+        turned = turned + flow_column_back(values, offset)
+    if level < LEVELS - 1:
+        term = term + flow_block_back(
+            part(result_ref, "prior_grad", half, channels), offsets["priormatrix"], half, channels
+        )
+    logs_total = jnp.sum(held[:, 1:2], 0, keepdims=True)
+    trace = jnp.sum(
+        jnp.sum(jnp.where(row == column, block, 0.0), 0, keepdims=True), 1, keepdims=True
+    )
+    loss = small[0:1, 6:7] - share_total * (logs_total + trace)
+    term = term + turned.T[:FLOW_ROWS]
+    row = iota((FLOW_ROWS, LANE), 0)
+    lane = iota((FLOW_ROWS, LANE), 1)
+    term = term + jnp.where((row == FLOW_ROWS - 1) & (lane == 0), loss, 0.0)
+    flat = term if flat is None else flat + term
     carried = None
-    for level in (2, 1, 0):
-        channels = chan(level)
-        half = channels // 2
-        grad_ref, normed_ref, held_ref, block_ref, small_ref = per_level[level][:5]
-        offsets = flow_offsets(level)
-        grad = grad_ref[...]
-        if carried is not None:
-            grad = grad + jnp.concatenate([carried, jnp.zeros_like(carried)], 0)
-        normed = normed_ref[...]
-        held = held_ref[...]
-        small = small_ref[...]
-        block = block_ref[...][:, :channels]
-        lower, upper, reverse, diagonal = triangles(block)
-        mixing_left = exact_dot(reverse, lower)
-        grad_normed = exact_rows(exact_dot(mixing_left, upper), grad)
-        grad_mixing = exact_dot(reverse, exact_columns(grad, normed))
-        grad_lower = exact_columns(grad_mixing, upper)
-        grad_upper = exact_rows(lower, grad_mixing)
-        share_total = small[0:1, 7:8]
-        row = iota((channels, channels), 0)
-        column = iota((channels, channels), 1)
-        grad_block = jnp.where(
-            row > column,
-            grad_lower,
-            jnp.where(row < column, grad_upper, grad_upper * diagonal - share_total),
-        )
-        growth = jnp.exp(held[:, 1:2])
-        grad_state = grad_normed * growth
-        grad_bias = jnp.sum(grad_state, 1, keepdims=True)
-        grad_logs = jnp.sum(grad_normed * normed, 1, keepdims=True) - share_total
-        flat = flat + flow_block_back(grad_block, offsets["block"], channels, channels)
-        for index, (name, offset) in enumerate(column_names(level)):
-            if name == "bias":
-                values = grad_bias
-            elif name == "logs":
-                values = grad_logs
-            else:
-                values = small[:, index : index + 1]
-            turned = turned + flow_column_back(values, offset)
-        if level < LEVELS - 1:
-            flat = flat + flow_block_back(
-                per_level[level][5][...][:, :channels], offsets["priormatrix"], half, channels
-            )
-        logs_total = jnp.sum(held[:, 1:2], 0, keepdims=True)
-        trace = jnp.sum(
-            jnp.sum(jnp.where(row == column, block, 0.0), 0, keepdims=True), 1, keepdims=True
-        )
-        loss = loss + small[0:1, 6:7] - share_total * (logs_total + trace)
-        if level > 0:
-            grid = side(level - 1)
-            carried = unsqueeze(
-                grad_state, squeeze_chooser(grid, images), images * grid * grid
-            )
-    flat = flat + turned.T[:FLOW_ROWS]
+    if level > 0:
+        grid = side(level - 1)
+        carried = unsqueeze(grad_state, squeeze_chooser(grid, images), images * grid * grid)
+    return carried, flat
+
+
+def flow_kernel(level, images, *refs):
+    stage_ref, result_ref = refs[:2]
+    carried, flat = None, None
+    if level < LEVELS - 1:
+        carried, flat = refs[2][...], refs[3][...]
+    carried, flat = flow_level(level, images, stage_ref, result_ref, carried, flat)
+    refs[-2][...] = carried
+    refs[-1][...] = flat
+
+
+def last_kernel(images, narrow, *refs):
+    count_ref, index_ref = refs[:2]
+    mine = refs[2 : 2 + narrow]
+    stage_ref, carried_ref, partial_ref, keep_ref, send_ref = refs[2 + narrow : 7 + narrow]
+    result_ref, flat_ref = refs[7 + narrow : 9 + narrow]
+    scratch = refs[9 + narrow :]
+    net_kernel(
+        0, images, narrow, index_ref, *mine, stage_ref, keep_ref, send_ref, result_ref, *scratch
+    )
+    _, flat = flow_level(0, images, stage_ref, result_ref, carried_ref[...], partial_ref[...])
+    loss = flat[FLOW_ROWS - 1 : FLOW_ROWS, 0:1]
     pixels = jnp.zeros((), F32)
     for index in range(images):
         pixels = pixels + (count_ref[index, 0] * count_ref[index, 1]).astype(F32)
-    row = iota((FLOW_ROWS, LANE), 0)
-    lane = iota((FLOW_ROWS, LANE), 1)
-    flat = jnp.where((row == LOSS_ROW) & (lane == 0), loss, flat)
-    flat = jnp.where((row == LOSS_ROW) & (lane == 1), pixels, flat)
-    out_ref[...] = flat
+    lane = iota((STATS_ROWS, LANE), 1)
+    stats = jnp.where(lane == 0, loss, jnp.where(lane == 1, pixels, 0.0))
+    flat_ref[...] = flat
+    share = FLOW_ROWS // narrow
+    start = pack_rows(0)
+    me = index_ref[0, 0]
+    for r in range(narrow):
+        ref = send_ref if r & 1 else keep_ref
+        ref[r // 2, start : start + share, :] = flat_ref[
+            pl.ds(pl.multiple_of((me ^ r) * share, share), share), :
+        ]
+        ref[r // 2, start + share : start + share + STATS_ROWS, :] = stats
+        rest = ref.shape[1] - start - share - STATS_ROWS
+        if rest:
+            ref[r // 2, start + share + STATS_ROWS :, :] = jnp.zeros((rest, LANE), F32)
+
+
+def copy_kernel(from_ref, to_ref):
+    to_ref[...] = from_ref[...]
+
+
+def merge_kernel(exact_in, stage, exact_out, *refs):
+    index_ref, kept_ref, other_ref = refs[:3]
+    rows = kept_ref.shape[1]
+
+    def total(shards, place, length):
+        return kept_ref[shards, place, :] + other_ref[shards, place, :].astype(F32)
+
+    if stage == "shard":
+        keep_ref, send_ref = refs[3:5]
+        count = keep_ref.shape[0]
+        everything = pl.ds(0, rows)
+        keep_ref[...] = total(pl.ds(0, count), everything, rows)
+        sent = total(pl.ds(count, count), everything, rows)
+        send_ref[:, 0:rows, :] = sent.astype(send_ref.dtype)
+        if exact_out:
+            start = pack_rows(0)
+            for shard in range(count):
+                pieces = split_three(sent[shard, start : start + exact_out])
+                send_ref[shard, rows:, :] = jnp.concatenate(pieces, 0).astype(BF16)
+        return
+    if stage is None:
+        refs[3][...] = total(pl.ds(0, kept_ref.shape[0]), pl.ds(0, rows), rows)
+        return
+    keep_ref, send_ref = refs[3:5]
+    half = rows // 2
+    shards = pl.ds(0, kept_ref.shape[0])
+    upper = jnp.where((index_ref[1, 0] & stage) != 0, 1, 0)
+    for ref, place in ((keep_ref, upper), (send_ref, 1 - upper)):
+        ref[...] = total(shards, pl.ds(pl.multiple_of(place * half, 16), half), half).astype(
+            ref.dtype
+        )
+    if exact_in:
+        start = pack_rows(0)
+        for shard in range(kept_ref.shape[0]):
+            pieces = other_ref[shard, rows:, :].astype(F32)
+            whole = pieces[:exact_in] + pieces[exact_in : 2 * exact_in] + pieces[2 * exact_in :]
+            whole = kept_ref[shard, start : start + exact_in, :] + whole
+
+            @pl.when(upper == 1)
+            def _():
+                keep_ref[shard, start - half : start - half + exact_in, :] = whole
+
+            @pl.when(upper == 0)
+            def _():
+                send_ref[shard, start - half : start - half + exact_in, :] = whole
+
+
+def join_kernel(bit, index_ref, mine_ref, other_ref, out_ref):
+    half = mine_ref.shape[1]
+    upper = jnp.where((index_ref[1, 0] & bit) != 0, 1, 0)
+    out_ref[:, pl.ds(pl.multiple_of(upper * half, 8), half), :] = mine_ref[...]
+    out_ref[:, pl.ds(pl.multiple_of((1 - upper) * half, 8), half), :] = other_ref[...]
 
 
 def moments(weight, gradient, first_old, second_old):
@@ -749,7 +864,7 @@
 
 def group_totals(values_in, values_mix, values_out, values_bias):
     row = iota(values_in.shape, 0)
-    lane = iota(values_out.shape, 1)
+    line = iota(values_out.shape, 0)
     sums = []
     start = 0
     for level in range(LEVELS):
@@ -760,7 +875,7 @@
         sums.append(total_of(values_mix[level]))
     start = 0
     for level in range(LEVELS):
-        inside = (lane >= start) & (lane < start + 9 * chan(level))
+        inside = (line >= start) & (line < start + 9 * chan(level))
         sums.append(total_of(jnp.where(inside, values_out, 0.0)))
         start = start + 9 * chan(level)
     for level in range(LEVELS):
@@ -778,27 +893,22 @@
     return masks
 
 
-def moment_kernel(
-    grad_refs_and_rest_count,
-    *refs,
-):
-    grads = refs[:3]
-    flow_grad_ref = refs[3]
-    weight_in, weight_mix, weight_out, weight_bias = refs[4:8]
-    first_in, first_mix, first_out, first_bias = refs[8:12]
-    second_in, second_mix, second_out, second_bias = refs[12:16]
-    outs = refs[16:]
-    total = flow_grad_ref[LOSS_ROW : LOSS_ROW + 1, :]
+def moment_kernel(share, *refs):
+    grads = [ref.at[0] for ref in refs[:3]]
+    weight_in, weight_mix, weight_out, weight_bias = refs[3:7]
+    first_in, first_mix, first_out, first_bias = refs[7:11]
+    second_in, second_mix, second_out, second_bias = refs[11:15]
+    outs = refs[15:]
+    stats_row = pack_rows(0) + share
+    total = grads[0][stats_row : stats_row + 1, :]
     valid_dims = 3.0 * total[:, 1:2]
     scale = 1.0 / (valid_dims * LOG_TWO)
     grad_in = jnp.concatenate([grads[level][0 : in_rows(level), :] for level in range(LEVELS)], 0)
-    columns = weight_out.shape[1]
     tails = [
         grads[level][first_rows(level) + HID : first_rows(level) + HID + 9 * chan(level), :]
         for level in range(LEVELS)
     ]
-    tails.append(jnp.zeros((round_up(columns, LANE) - columns, LANE), F32))
-    grad_out = jnp.concatenate(tails, 0).T[:, :columns]
+    grad_out = jnp.concatenate(tails, 0)
     bias_rows = []
     for level in range(LEVELS):
         bias_rows.append(grads[level][in_rows(level) : in_rows(level) + 1, :])
@@ -841,14 +951,19 @@
         new_in[2] * new_in[2], mix_updates, new_out[2] * new_out[2], new_bias[2] * new_bias[2]
     )
     lane = iota((16, LANE), 1)
-    outs[12][...] = jnp.where(lane == 0, squares_rows(weight_sums), squares_rows(update_sums))
-
-
-def apply_kernel(*refs):
-    sums_ref, flow_grad_ref = refs[0:2]
-    weight_in, weight_mix, weight_out, weight_bias = refs[2:6]
-    update_in, update_mix, update_out, update_bias = refs[6:10]
-    flow_ref, flow_first_ref, flow_second_ref = refs[10:13]
+    outs[12][0:16, :] = jnp.where(lane == 0, squares_rows(weight_sums), squares_rows(update_sums))
+    outs[12][16 : 16 + share, :] = grads[0][pack_rows(0) : pack_rows(0) + share, :]
+    outs[12][16 + share :, :] = grads[0][stats_row : stats_row + STATS_ROWS, :]
+
+
+def apply_kernel(narrow, *refs):
+    index_ref = refs[0]
+    block_refs = refs[1 : 1 + narrow]
+    at = 1 + narrow
+    weight_in, weight_mix, weight_out, weight_bias = refs[at : at + 4]
+    update_in, update_mix, update_out, update_bias = refs[at + 4 : at + 8]
+    flow_ref, flow_first_ref, flow_second_ref = refs[at + 8 : at + 11]
+    at = at + 11
     (
         new_in,
         new_mix,
@@ -860,19 +975,29 @@
         half_out,
         flow_moment,
         flow_square,
-        norm_ref,
-    ) = refs[13:]
-    total = flow_grad_ref[LOSS_ROW : LOSS_ROW + 1, :]
+        weight_norm_ref,
+        update_norm_ref,
+        loss_ref,
+        valid_ref,
+        order_ref,
+    ) = refs[at:]
+    for part in range(narrow):
+        order_ref[index_ref[0, 0] ^ part] = block_refs[part][...]
+    share = FLOW_ROWS // narrow
+    sums = order_ref[0, 0:16, :]
+    for part in range(1, narrow):
+        sums = sums + order_ref[part, 0:16, :]
+    flow_grad = jnp.concatenate([order_ref[part, 16 : 16 + share, :] for part in range(narrow)], 0)
+    total = block_refs[0][16 + share : 17 + share, :]
     valid_dims = 3.0 * total[:, 1:2]
     scale = 1.0 / (valid_dims * LOG_TWO)
     flow = to_flat_rows(flow_ref[...])
     size = flow_ref.shape[0]
     place = iota((FLOW_ROWS, LANE), 0) * LANE + iota((FLOW_ROWS, LANE), 1)
-    flow_grad = jnp.where(place < size, flow_grad_ref[...] * scale, 0.0)
+    flow_grad = jnp.where(place < size, flow_grad * scale, 0.0)
     first_new, second_new, update = moments(
         flow, flow_grad, to_flat_rows(flow_first_ref[...]), to_flat_rows(flow_second_ref[...])
     )
-    sums = sums_ref[...]
     weight_norms = [jnp.sqrt(sums[index : index + 1, 0:1]) for index in range(12)]
     update_norms = [jnp.sqrt(sums[index : index + 1, 1:2]) for index in range(12)]
     masks = flow_masks()
@@ -899,24 +1024,22 @@
         fresh = weight_mix[level] - rates[3 + level] * update_mix[level]
         new_mix[level] = fresh
         half_mix[level] = fresh.astype(BF16)
-    lane = iota(weight_out.shape, 1)
+    row = iota(weight_out.shape, 0)
     edge_one, edge_two = 9 * chan(0), 9 * chan(0) + 9 * chan(1)
-    rate = jnp.where(lane < edge_one, rates[6], jnp.where(lane < edge_two, rates[7], rates[8]))
+    rate = jnp.where(row < edge_one, rates[6], jnp.where(row < edge_two, rates[7], rates[8]))
     fresh = weight_out[...] - rate * update_out[...]
     new_out[...] = fresh
     half_out[...] = fresh.astype(BF16)
     for level in range(LEVELS):
         new_bias[level] = weight_bias[level] - rates[9 + level] * update_bias[level]
-    lane = iota((8, LANE), 1)
-    row = iota((8, LANE), 0)
-    held = jnp.zeros((8, LANE), F32)
-    for index in range(15):
-        held = jnp.where((row == 0) & (lane == index), weight_norms[index], held)
-        held = jnp.where((row == 1) & (lane == index), update_norms[index], held)
-    loss_sum = total[:, 0:1] / LOG_TWO + 8.0 * valid_dims
-    held = jnp.where((row == 2) & (lane == 0), loss_sum, held)
-    held = jnp.where((row == 2) & (lane == 1), valid_dims, held)
-    norm_ref[...] = held
+    lane = iota((1, LANE), 1)
+    for ref, norms in ((weight_norm_ref, weight_norms), (update_norm_ref, update_norms)):
+        held = jnp.zeros((1, LANE), F32)
+        for index in range(15):
+            held = jnp.where(lane == index, norms[index], held)
+        ref[...] = held[:, :15].reshape(15)
+    loss_ref[...] = total[:, 0:1] / LOG_TWO + 8.0 * valid_dims
+    valid_ref[...] = valid_dims
 
 
 def spec_vmem():
@@ -927,100 +1050,106 @@
     return pl.BlockSpec(memory_space=pltpu.SMEM)
 
 
-def call(kernel, outs, scalars, arrays, scratch=(), name=None):
+def call(kernel, outs, scalars, arrays, scratch=(), name=None, after=(), vmem=20):
+    number = len(scalars) + len(arrays)
+
+    def run(*refs):
+        kernel(*refs[:number], *refs[number + len(after) :])
+
     return pl.pallas_call(
-        kernel,
+        run,
         out_shape=tuple(jax.ShapeDtypeStruct(shape, dtype) for shape, dtype in outs),
-        in_specs=[spec_smem()] * len(scalars) + [spec_vmem()] * len(arrays),
+        in_specs=[spec_smem()] * len(scalars)
+        + [spec_vmem()] * len(arrays)
+        + [pl.BlockSpec(memory_space=pl.ANY)] * len(after),
         out_specs=tuple(spec_vmem() for _ in outs),
         scratch_shapes=list(scratch),
-        compiler_params=pltpu.CompilerParams(vmem_limit_bytes=VMEM_BYTES),
+        compiler_params=pltpu.CompilerParams(vmem_limit_bytes=vmem * 1024 * 1024),
+        cost_estimate=pl.CostEstimate(
+            flops=1000, bytes_accessed=1000, transcendentals=0
+        ),
         name=name,
-    )(*scalars, *arrays)
+    )(*scalars, *arrays, *after)
 
 
 def run_pack(conv_in, mixer, conv_out, hidden_bias):
     outs = [((pack_rows(level), LANE), BF16) for level in range(LEVELS)]
-    return call(pack_kernel, outs, (), (conv_in, mixer, conv_out, hidden_bias), name="pack")
-
-
-def run_flow_pre(noise_seeds, valid_shape, images, flow_params):
+    outs.append(((sum(pack_rows(level) for level in range(LEVELS)), LANE), BF16))
+    return call(pack_kernel, outs, (), (conv_in, mixer, conv_out, hidden_bias), name="pack", vmem=56)
+
+
+def run_flow_pre(noise_seeds, valid_shape, images, flow_params, after):
     count = images.shape[1]
-    outs = []
-    for level in range(LEVELS):
-        channels = chan(level)
-        places = positions(level, count)
-        outs = outs + [
-            ((channels, places), F32),
-            ((channels, places), F32),
-            ((8, places), F32),
-            ((channels, LANE), F32),
-            ((channels, LANE), F32),
-        ]
-        if level < LEVELS - 1:
-            outs.append(((channels // 2, LANE), F32))
-    flat = call(
-        flow_pre_kernel, outs, (noise_seeds, valid_shape), (images, flow_params), name="flow_pre"
-    )
-    grouped = []
-    at = 0
-    for level in range(LEVELS):
-        number = 6 if level < LEVELS - 1 else 5
-        grouped.append(flat[at : at + number])
-        at = at + number
-    return grouped
-
-
-def run_net(level, images, index, weights, pre):
+    outs = [((stage_rows(level)["rows"], positions(level, count)), F32) for level in range(LEVELS)]
+    return call(
+        flow_pre_kernel,
+        outs,
+        (noise_seeds, valid_shape),
+        (images, flow_params),
+        name="flow_pre",
+        after=after,
+    )
+
+
+def run_net(level, images, index, weights, stage, after):
     narrow = len(weights)
-    channels = chan(level)
     count = positions(level, images)
     outs = [
-        ((narrow // 2, pack_rows(level), LANE), F32),
-        ((narrow // 2, pack_rows(level), LANE), F32),
-        ((channels, count), F32),
-        ((channels, LANE), F32),
+        ((narrow // 2, grad_rows(level, narrow), LANE), F32),
+        ((narrow // 2, grad_rows(level, narrow), LANE), F32),
+        ((stage_rows(level)["result_rows"], count), F32),
     ]
-    arrays = list(weights) + [pre[1], pre[2], pre[3]]
-    if level < LEVELS - 1:
-        arrays.append(pre[5])
-        outs.append(((channels // 2, LANE), F32))
-    scratch = [
+    return call(
+        functools.partial(net_kernel, level, images, narrow),
+        outs,
+        (),
+        [index] + list(weights) + [stage],
+        net_scratch(count),
+        name="net_%d" % (level + 1),
+        after=after,
+    )
+
+
+def run_flow(level, images, stage, result, carried, after):
+    grid = side(level - 1)
+    outs = [((chan(level - 1) // 2, images * grid * grid), F32), ((FLOW_ROWS, LANE), F32)]
+    return call(
+        functools.partial(flow_kernel, level, images),
+        outs,
+        (),
+        [stage, result] + list(carried),
+        name="flow_%d" % (level + 1),
+        after=after,
+    )
+
+
+def net_scratch(count):
+    return [
         pltpu.VMEM((HID, HID), BF16),
         pltpu.VMEM((HID, count), F32),
         pltpu.VMEM((HID, count), F32),
         pltpu.VMEM((HID, count), BF16),
         pltpu.VMEM((HID, count), BF16),
     ]
+
+
+def run_last(images, index, valid_shape, weights, stage, carried, after):
+    narrow = len(weights)
+    count = positions(0, images)
+    outs = [((narrow // 2, grad_rows(0, narrow), LANE), F32)] * 2
+    scratch = [
+        pltpu.VMEM((stage_rows(0)["result_rows"], count), F32),
+        pltpu.VMEM((FLOW_ROWS, LANE), F32),
+    ]
     return call(
-        functools.partial(net_kernel, level, images, narrow),
+        functools.partial(last_kernel, images, narrow),
         outs,
-        (index,),
-        arrays,
-        scratch,
-        name="net_%d" % (level + 1),
-    )
-
-
-def run_flow_post(images, valid_shape, pre, results):
-    arrays = []
-    for level in range(LEVELS):
-        arrays = arrays + [
-            results[level][2],
-            pre[level][0],
-            pre[level][3],
-            pre[level][4],
-            results[level][3],
-        ]
-        if level < LEVELS - 1:
-            arrays.append(results[level][4])
-    return call(
-        functools.partial(flow_post_kernel, images),
-        [((FLOW_ROWS, LANE), F32)],
         (valid_shape,),
-        arrays,
-        name="flow_post",
-    )[0]
+        [index] + list(weights) + [stage] + list(carried),
+        scratch + net_scratch(count),
+        name="net_1_and_flow",
+        after=after,
+    )
 
 
 def swap(values, axis, step):
@@ -1028,66 +1157,79 @@
     return lax.ppermute(values, axis, [(index, index ^ step) for index in range(size)])
 
 
-def gather_narrow(shard):
-    held = [shard]
-    step = 1
-    while step < lax.axis_size("narrow"):
-        held = held + [swap(value, "narrow", step) for value in held]
-        step = 2 * step
-    return held
-
-
-def sum_everywhere(values):
-    for axis in ("narrow", "wide"):
-        step = 1
-        while step < lax.axis_size(axis):
-            values = values + swap(values, axis, step)
-            step = 2 * step
-    return values
-
-
-def halve(values, axis, step):
-    index = lax.axis_index(axis)
-    rows = values.shape[0] // 2
-    upper = (index & step) != 0
-    low, high = values[:rows], values[rows:]
-    sent = jnp.where(upper, low, high)
-    kept = jnp.where(upper, high, low)
-    return kept + swap(sent, axis, step)
-
-
-def unhalve(values, axis, step):
-    upper = (lax.axis_index(axis) & step) != 0
-    other = swap(values, axis, step)
-    return jnp.concatenate([jnp.where(upper, other, values), jnp.where(upper, values, other)], 0)
-
-
-def sum_wide(values):
-    rows = values.shape[0]
-    size = lax.axis_size("wide")
+def wide_steps():
     steps = []
     step = 1
-    while step < size:
+    while step < lax.axis_size("wide"):
         steps.append(step)
         step = 2 * step
-    split = [step for step in steps if step < 8]
-    unit = 8 * 2 ** len(split)
-    padded = round_up(rows, unit)
-    if padded > rows:
-        values = jnp.pad(values, ((0, padded - rows), (0, 0)))
-    for step in split:
-        values = halve(values, "wide", step)
-    for step in steps[len(split) :]:
-        values = values + swap(values, "wide", step)
-    for step in split[::-1]:
-        values = unhalve(values, "wide", step)
-    return values
-
-
-def reduce_level(keep, send):
-    paired = keep + swap(send, "narrow", 1)
-    shard = paired[0] + swap(paired[1], "narrow", 2)
-    return sum_wide(shard)
+    return steps
+
+
+class Summation:
+    def __init__(self, level, index, stages, exact):
+        self.level, self.index, self.exact = level, index, exact
+        self.stages = stages
+        self.at = -1
+        self.joins = [stage for stage in stages if stage != "shard"][::-1]
+
+    def start(self, keep, send):
+        self.kept = keep
+        self.other = swap(send, "narrow", 1)
+
+    def merge(self, after):
+        exact_in = self.exact if self.at == 0 else 0
+        self.at = self.at + 1
+        shards, rows, _ = self.kept.shape
+        if self.at == len(self.stages):
+            (total,) = call(
+                functools.partial(merge_kernel, 0, None, 0),
+                [((shards, rows, LANE), F32)],
+                (),
+                (self.index, self.kept, self.other),
+                name="total_%d" % (self.level + 1),
+                after=after,
+            )
+            for step in wide_steps():
+                if step not in self.stages:
+                    total = total + swap(total, "wide", step)
+            self.kept = total
+            self.other = swap(total, "wide", self.joins[0])
+            return total
+        stage = self.stages[self.at]
+        exact_out = self.exact if self.at == 0 else 0
+        if stage == "shard":
+            keep, send = (shards // 2, rows, LANE), (shards // 2, rows + 3 * exact_out, LANE)
+        else:
+            keep = send = (shards, rows // 2, LANE)
+        self.kept, sent = call(
+            functools.partial(merge_kernel, exact_in, stage, exact_out),
+            [(keep, F32), (send, BF16 if self.at == 0 else F32)],
+            (),
+            (self.index, self.kept, self.other),
+            name="merge_%d_%d" % (self.level + 1, self.at),
+            after=after,
+        )
+        if stage == "shard":
+            self.other = swap(sent, "narrow", 2)
+        else:
+            self.other = swap(sent, "wide", stage)
+        return self.kept
+
+    def join(self, after):
+        step = self.joins.pop(0)
+        shards, rows, _ = self.kept.shape
+        (self.kept,) = call(
+            functools.partial(join_kernel, step),
+            [((shards, 2 * rows, LANE), F32)],
+            (),
+            (self.index, self.kept, self.other),
+            name="join_%d" % (self.level + 1),
+            after=after,
+        )
+        if self.joins:
+            self.other = swap(self.kept, "wide", self.joins[0])
+        return self.kept
 
 
 def body(
@@ -1111,74 +1253,107 @@
     flow_second,
 ):
     count = images.shape[1]
-    index = lax.axis_index("narrow").astype(jnp.int32).reshape(1)
+    conv_out, conv_out_first, conv_out_second = conv_out.T, conv_out_first.T, conv_out_second.T
+    row = lax.broadcasted_iota(jnp.int32, (8, LANE), 0)
+    index = jnp.where(row == 0, lax.axis_index("narrow"), lax.axis_index("wide")).astype(jnp.int32)
+    narrow = lax.axis_size("narrow")
     packed = run_pack(conv_in, mixer, conv_out, hidden_bias)
-    gathered = [None] * LEVELS
+    paired = swap(packed[LEVELS], "narrow", 1)
+    crossed = [None] * LEVELS
     for level in (2, 1, 0):
-        gathered[level] = gather_narrow(packed[level])
-    pre = run_flow_pre(noise_seeds, valid_shape, images, flow_params)
-    results = [None] * LEVELS
-    grads = [None] * LEVELS
-    for level in (2, 1, 0):
-        results[level] = run_net(level, count, index, gathered[level], pre[level])
-        grads[level] = reduce_level(results[level][0], results[level][1])
-    flow_grad = sum_everywhere(run_flow_post(count, valid_shape, pre, results))
+        crossed[level] = swap(packed[level], "narrow", 2)
+    stage = run_flow_pre(noise_seeds, valid_shape, images, flow_params, (packed[0],))
+
+    def gather(level, after):
+        (copied,) = call(
+            copy_kernel,
+            [(crossed[level].shape, BF16)],
+            (),
+            (crossed[level],),
+            name="copy_%d" % (level + 1),
+            after=after,
+        )
+        return (packed[level], paired, crossed[level], swap(copied, "narrow", 1)), copied
+
+    bits = [step for step in wide_steps() if step < 8]
+    third = Summation(2, index, bits[:1] + ["shard"] + bits[1:], 0)
+    second = Summation(1, index, ["shard"] + bits, 0)
+    first = Summation(0, index, ["shard"] + bits, flow_block_rows(narrow))
+    gathered, token = gather(2, (stage[0],))
+    keep, send, result = run_net(2, count, index, gathered, stage[2], (token,))
+    third.start(keep, send)
+    gathered, token = gather(1, (keep,))
+    carried = run_flow(2, count, stage[2], result, (), (token,))
+    keep, send, result = run_net(1, count, index, gathered, stage[1], (carried[1],))
+    second.start(keep, send)
+    gathered, token = gather(0, (keep,))
+    token = third.merge((token,))
+    carried = run_flow(1, count, stage[1], result, carried, (token,))
+    token = second.merge((carried[1],))
+    keep, send = run_last(count, index, valid_shape, gathered, stage[0], carried, (token,))
+    first.start(keep, send)
+    token = first.merge((keep,))
+    for _ in range(len(bits) + 1):
+        for summation in (second, third, first):
+            token = summation.merge((token,))
+    for _ in range(len(bits)):
+        for summation in (second, third, first):
+            token = summation.join((token,))
+    grads = (first.kept, second.kept, third.kept)
     weights = (conv_in, mixer, conv_out, hidden_bias)
     shapes = [(weight.shape, F32) for weight in weights]
+    share = FLOW_ROWS // narrow
     moved = call(
-        functools.partial(moment_kernel, 0),
-        shapes * 3 + [((16, LANE), F32)],
+        functools.partial(moment_kernel, share),
+        shapes * 3 + [((16 + share + STATS_ROWS, LANE), F32)],
         (),
-        tuple(grads)
-        + (flow_grad,)
+        grads
         + weights
         + (conv_in_first, mixer_first, conv_out_first, bias_first)
         + (conv_in_second, mixer_second, conv_out_second, bias_second),
         name="moments",
     )
-    sums = moved[12]
-    step = 1
-    while step < lax.axis_size("narrow"):
-        sums = sums + swap(sums, "narrow", step)
-        step = 2 * step
+    blocks = [moved[12]] + [swap(moved[12], "narrow", part) for part in range(1, narrow)]
     flow_shape = (flow_params.shape, F32)
     fresh = call(
-        apply_kernel,
+        functools.partial(apply_kernel, narrow),
         shapes
         + [flow_shape]
         + [(weight.shape, BF16) for weight in weights[:3]]
-        + [flow_shape, flow_shape, ((8, LANE), F32)],
+        + [flow_shape, flow_shape, ((15,), F32), ((15,), F32), ((1, 1), F32), ((1, 1), F32)],
+
         (),
-        (sums, flow_grad)
+        (index,)
+        + tuple(blocks)
         + weights
         + tuple(moved[8:12])
         + (flow_params, flow_first, flow_second),
+        scratch=[pltpu.VMEM((narrow,) + moved[12].shape, F32)],
         name="apply",
     )
-    norms = fresh[10]
     return (
         fresh[0],
         fresh[1],
-        fresh[2],
+        fresh[2].T,
         fresh[3],
         fresh[4],
         moved[0],
         moved[1],
-        moved[2],
+        moved[2].T,
         moved[3],
         fresh[8],
         moved[4],
         moved[5],
-        moved[6],
+        moved[6].T,
         moved[7],
         fresh[9],
         fresh[5],
         fresh[6],
-        fresh[7],
-        norms[0, :15],
-        norms[1, :15],
-        norms[2, 0],
-        norms[2, 1],
+        fresh[7].T,
+        fresh[10],
+        fresh[11],
+        fresh[12].reshape(()),
+        fresh[13].reshape(()),
     )
 
 

time: 162 us -> 122 us (0.75)
  waiting for transfers between devices: 73 us -> 54.6 us
  local copies, waits for them, and re-layouts: 16.1 us -> 2.06 us
  other arithmetic: 9.98 us -> 0.01 us
  Pallas kernels: 23.6 us -> 26.1 us
    ppermute x40 -> x34, waiting for transfers between devices: 73 us -> 54.6 us  [swap(): lax.ppermute(values, axis, [(index, index ^ step) for index in range(size)])]
    unnamed x65 -> x44, local copies, waits for them, and re-layouts: 14.1 us -> 1.99 us
    add x22 -> x0, other arithmetic: 7.88 us -> none  [the longest x3 2.79 us: reduce_level(): paired = keep + swap(send, 'narrow', 1)]
    pallas_call x8 -> x36, Pallas kernels: 23.6 us -> 26.1 us  [call(): pl.pallas_call(run, out_shape=tuple((jax.ShapeDtypeStruct(shape, dtype) f...]
    ppermute x40 -> x34, starting transfers between devices: 37.4 us -> 37.4 us  [swap(): lax.ppermute(values, axis, [(index, index ^ step) for index in range(size)])]
  transfers between devices with their start and end apart: 40 -> 34, of which waited for: 26 -> 16; matrix products, arithmetic and copies ran while one was open for 7% -> 0% of each run, Pallas kernels for 9% -> 11%
where the time goes in v2:
time: 122 us; the launch traced here: 121 us
  waiting for transfers between devices  54.6 us (45%)
  starting transfers between devices  37.4 us (31%)
  Pallas kernels  26.1 us (21%)
  local copies, waits for them, and re-layouts  2.06 us (2%)
  between operations  1.35 us (1%)
    ppermute x34, waiting for transfers between devices, swap(): lax.ppermute(values, axis, [(index, index ^ step) for index in range(size)])  54.6 us
    ppermute x34, starting transfers between devices, swap(): lax.ppermute(values, axis, [(index, index ^ step) for index in range(size)])  37.4 us
    pallas_call x36, Pallas kernels, call(): pl.pallas_call(run, out_shape=tuple((jax.ShapeDtypeStruct(shape, dtype) f...  26.1 us
  transfers between devices with their start and end apart: 34, of which 16 were waited for; matrix products, arithmetic and copies ran while one was open for 0% of the time, Pallas kernels for 11%

profile of v2, /device:TPU:0, one launch (start us, length us, event | category | flops | bytes accessed | tf_op | source)
XLA Modules:
  0.0 121.5 jit_solution(7231446851425740730)
XLA Ops:
  0.7 2.4 %pack.1 = (bf16[688,128]{1,0:T(8,128)(2,1)}, bf16[864,128]{1,0:T(8,128)(2,1)}, bf16[1168,128]{1,0:T(8,128)(2,1)}, bf16[2720,128]{1,0:T(8,128)(2,1)}) custom-call(f32[378,128]{1,0:T(8,128)} %refs_5_.1, f32[3,512,128]{2,1,0:T(8,128)} %refs_6_.3, f32[756,128]{1,0:T(8,128)} %bitcast.9, f32[3,2,128]{2,1,0:T(2,128)} %refs_8_.3), custom_call_target="tpu_custom_call" | custom-call | flops 1000 | bytes 1000 | tf_op jit(solution)/shard_map/pack/pallas_call | solution.py:1059
  3.6 2.5 %collective-permute-start.3 = (bf16[1168,128]{1,0:T(8,128)(2,1)}, bf16[1168,128]{1,0:T(8,128)(2,1)S(1)}, u32[]{:S(2)}, u32[]{:S(2)}) collective-permute-start(bf16[1168,128]{1,0:T(8,128)(2,1)} %get-tuple-element.95.refs_1_), channel_id=1, source_target_pairs={{0,2},{1,3},{2,0},{3,1},{4,6},{5,7},{6,4},{7,5},{8,10},{9,11},{10,... | collective-permute-start | bytes 897032 | tf_op jit(solution)/shard_map/ppermute | solution.py:1157
  6.1 0.9 copy-done.5
  7.0 4.7 %flow_pre.1 = (f32[80,512]{1,0:T(8,128)S(1)}, f32[120,128]{1,0:T(8,128)S(1)}, f32[224,128]{1,0:T(8,128)S(1)}) custom-call(s32[2]{0:T(128)S(1)} %copy-done.21, s32[2,2]{1,0:T(2,128)S(1)} %copy-done.18, f32[3,2,1024]{2,1,0:T(2,128)S(1)} %copy-done.15, f32[3852]{0:T(1024)S(1)} %copy-done.13, bf16[688,128]{1,0:T(8,128)(2,1)S(1)} %copy-done.5), custom_call_target="tpu_custom_call" | custom-call | flops 1000 | bytes 1000 | tf_op jit(solution)/shard_map/flow_pre/pallas_call | solution.py:1059
  11.7 2.4 %collective-permute-done.3.refs_0_.refs_3_ = bf16[1168,128]{1,0:T(8,128)(2,1)S(1)} collective-permute-done((bf16[1168,128]{1,0:T(8,128)(2,1)}, bf16[1168,128]{1,0:T(8,128)(2,1)S(1)}, u32[]{:S(2)}, u32[]{:S(2)}) %collective-permute-start.3) | collective-permute-done | bytes 299040 | tf_op jit(solution)/shard_map/ppermute | solution.py:1157
  14.1 1.8 %collective-permute-start.2 = (bf16[864,128]{1,0:T(8,128)(2,1)}, bf16[864,128]{1,0:T(8,128)(2,1)S(1)}, u32[]{:S(2)}, u32[]{:S(2)}) collective-permute-start(bf16[864,128]{1,0:T(8,128)(2,1)} %get-tuple-element.94.refs_1_), channel_id=1, source_target_pairs={{0,2},{1,3},{2,0},{3,1},{4,6},{5,7},{6,4},{7,5},{8,10},{9,11},{10,... | collective-permute-start | bytes 663560 | tf_op jit(solution)/shard_map/ppermute | solution.py:1157
  16.0 1.0 copy-done.9
  17.0 2.4 %net_3.1 = (f32[2,1216,128]{2,1,0:T(8,128)S(1)}, f32[2,1216,128]{2,1,0:T(8,128)S(1)}, f32[120,128]{1,0:T(8,128)S(1)}) custom-call(s32[8,128]{1,0:T(8,128)S(1)} %iota.7.refs_0_.refs_1_, bf16[1168,128]{1,0:T(8,128)(2,1)S(1)} %copy-done.9, bf16[2720,128]{1,0:T(8,128)(2,1)S(1)} %collective-permute-done.refs_2_.refs_3_, ...), custom_call_target="tpu_custom_call" | custom-call | flops 1000 | bytes 1000 | tf_op jit(solution)/shard_map/net_3/pallas_call | solution.py:1059
  19.6 2.6 %collective-permute-done.2.refs_0_.refs_3_ = bf16[864,128]{1,0:T(8,128)(2,1)S(1)} collective-permute-done((bf16[864,128]{1,0:T(8,128)(2,1)}, bf16[864,128]{1,0:T(8,128)(2,1)S(1)}, u32[]{:S(2)}, u32[]{:S(2)}) %collective-permute-start.2) | collective-permute-done | bytes 221216 | tf_op jit(solution)/shard_map/ppermute | solution.py:1157
  22.3 1.4 %flow_3.1 = (f32[12,128]{1,0:T(8,128)S(1)}, f32[32,128]{1,0:T(8,128)S(1)}) custom-call(f32[224,128]{1,0:T(8,128)S(1)} %get-tuple-element.97.refs_5_.refs_0_, f32[120,128]{1,0:T(8,128)S(1)} %get-tuple-element.100.refs_1_, bf16[864,128]{1,0:T(8,128)(2,1)S(1)} %copy_2.1.refs_2_), custom_call_target="tpu_custom_call" | custom-call | flops 1000 | bytes 1000 | tf_op jit(solution)/shard_map/flow_3/pallas_call | solution.py:1059
  23.8 2.1 %net_2.1 = (f32[2,896,128]{2,1,0:T(8,128)S(1)}, f32[2,896,128]{2,1,0:T(8,128)S(1)}, f32[64,128]{1,0:T(8,128)S(1)}) custom-call(s32[8,128]{1,0:T(8,128)S(1)} %iota.7.refs_0_.refs_1_, bf16[864,128]{1,0:T(8,128)(2,1)S(1)} %copy-done.10, bf16[2720,128]{1,0:T(8,128)(2,1)S(1)} %collective-permute-done.refs_2_.refs_3_, ...), custom_call_target="tpu_custom_call" | custom-call | flops 1000 | bytes 1000 | tf_op jit(solution)/shard_map/net_2/pallas_call | solution.py:1059
  25.9 0.5 collective-permute-start.8
  26.5 1.8 %collective-permute-start.1 = (bf16[688,128]{1,0:T(8,128)(2,1)S(1)}, bf16[688,128]{1,0:T(8,128)(2,1)S(1)}, u32[]{:S(2)}, u32[]{:S(2)}) collective-permute-start(bf16[688,128]{1,0:T(8,128)(2,1)S(1)} %copy-done.6), channel_id=1, source_target_pairs={{0,2},{1,3},{2,0},{3,1},{4,6},{5,7},{6,4},{7,5},{8,10},{9,11},{10,... | collective-permute-start | bytes 528392 | tf_op jit(solution)/shard_map/ppermute | solution.py:1157
  28.2 4.7 %collective-permute-done.1.refs_0_.refs_4_ = bf16[688,128]{1,0:T(8,128)(2,1)S(1)} collective-permute-done((bf16[688,128]{1,0:T(8,128)(2,1)S(1)}, bf16[688,128]{1,0:T(8,128)(2,1)S(1)}, u32[]{:S(2)}, u32[]{:S(2)}) %collective-permute-start.1) | collective-permute-done | bytes 176160 | tf_op jit(solution)/shard_map/ppermute | solution.py:1157
  33.2 1.4 %flow_2.1 = (f32[6,512]{1,0:T(8,128)S(1)}, f32[32,128]{1,0:T(8,128)S(1)}) custom-call(f32[120,128]{1,0:T(8,128)S(1)} %get-tuple-element.99.refs_5_.refs_0_, f32[64,128]{1,0:T(8,128)S(1)} %get-tuple-element.103.refs_1_, f32[12,128]{1,0:T(8,128)S(1)} %get-tuple-element.104.refs_2_, f32[32,128]{1,0:T(8,128)S(1)} %get-tuple-element.101.refs_6_.refs_3_, ...), custom_call_target="tpu_custom_call" | custom-call | flops 1000 | bytes 1000 | tf_op jit(solution)/shard_map/flow_2/pallas_call | solution.py:1059
  34.8 4.7 %net_1_and_flow.1 = (f32[2,704,128]{2,1,0:T(8,128)S(1)}, f32[2,704,128]{2,1,0:T(8,128)S(1)}) custom-call(s32[2,2]{1,0:T(2,128)S(1)} %copy-done.18, s32[8,128]{1,0:T(8,128)S(1)} %iota.7.refs_0_.refs_1_, bf16[688,128]{1,0:T(8,128)(2,1)S(1)} %copy-done.6, bf16[2720,128]{1,0:T(8,128)(2,1)S(1)} %collective-permute-done.refs_2_.refs_3_, ...), custom_call_target="tpu_custom_call" | custom-call | flops 1000 | bytes 1000 | tf_op jit(solution)/shard_map/net_1_and_flow/pallas_call | solution.py:1059
  39.5 0.6 collective-permute-start.9
  40.1 1.8 %collective-permute-start.11 = (bf16[2,608,128]{2,1,0:T(8,128)(2,1)S(1)}, bf16[2,608,128]{2,1,0:T(8,128)(2,1)S(1)}, u32[]{:S(2)}, u32[]{:S(2)}) collective-permute-start(bf16[2,608,128]{2,1,0:T(8,128)(2,1)S(1)} %get-tuple-element.115), channel_id=1, source_target_pairs={{0,4},{4,0},{8,12},{12,8},{16,20},{20,16},{24,28},{28,24},{1,5},{5... | collective-permute-start | bytes 933896 | tf_op jit(solution)/shard_map/ppermute | solution.py:1157
  41.9 1.5 %collective-permute-start.12 = (bf16[1,896,128]{2,1,0:T(8,128)(2,1)S(1)}, bf16[1,896,128]{2,1,0:T(8,128)(2,1)S(1)}, u32[]{:S(2)}, u32[]{:S(2)}) collective-permute-start(bf16[1,896,128]{2,1,0:T(8,128)(2,1)S(1)} %get-tuple-element.116), channel_id=1, source_target_pairs={{0,2},{1,3},{2,0},{3,1},{4,6},{5,7},{6,4},{7,5},{8,10},{9,11},{10,... | collective-permute-start | bytes 688136 | tf_op jit(solution)/shard_map/ppermute | solution.py:1157
  43.4 5.7 %collective-permute-done.12.refs_2_ = bf16[1,896,128]{2,1,0:T(8,128)(2,1)S(1)} collective-permute-done((bf16[1,896,128]{2,1,0:T(8,128)(2,1)S(1)}, bf16[1,896,128]{2,1,0:T(8,128)(2,1)S(1)}, u32[]{:S(2)}, u32[]{:S(2)}) %collective-permute-start.12) | collective-permute-done | bytes 229408 | tf_op jit(solution)/shard_map/ppermute | solution.py:1157
  49.5 1.8 %collective-permute-start.14 = (f32[1,608,128]{2,1,0:T(8,128)S(1)}, f32[1,608,128]{2,1,0:T(8,128)S(1)}, u32[]{:S(2)}, u32[]{:S(2)}) collective-permute-start(f32[1,608,128]{2,1,0:T(8,128)S(1)} %get-tuple-element.121), channel_id=1, source_target_pairs={{0,2},{1,3},{2,0},{3,1},{4,6},{5,7},{6,4},{7,5},{8,10},{9,11},{10,... | collective-permute-start | bytes 933896 | tf_op jit(solution)/shard_map/ppermute | solution.py:1157
  51.6 1.7 %collective-permute-start.15 = (f32[1,448,128]{2,1,0:T(8,128)S(1)}, f32[1,448,128]{2,1,0:T(8,128)S(1)}, u32[]{:S(2)}, u32[]{:S(2)}) collective-permute-start(f32[1,448,128]{2,1,0:T(8,128)S(1)} %get-tuple-element.122), channel_id=1, source_target_pairs={{0,4},{4,0},{8,12},{12,8},{16,20},{20,16},{24,28},{28,24},{1,5},{5... | collective-permute-start | bytes 688136 | tf_op jit(solution)/shard_map/ppermute | solution.py:1157
  53.4 8.9 %collective-permute-done.10.refs_2_ = bf16[1,752,128]{2,1,0:T(8,128)(2,1)S(1)} collective-permute-done((bf16[1,752,128]{2,1,0:T(8,128)(2,1)S(1)}, bf16[1,752,128]{2,1,0:T(8,128)(2,1)S(1)}, u32[]{:S(2)}, u32[]{:S(2)}) %collective-permute-start.10) | collective-permute-done | bytes 192544 | tf_op jit(solution)/shard_map/ppermute | solution.py:1157
  62.5 1.8 %collective-permute-start.13 = (f32[1,352,128]{2,1,0:T(8,128)S(1)}, f32[1,352,128]{2,1,0:T(8,128)S(1)}, u32[]{:S(2)}, u32[]{:S(2)}) collective-permute-start(f32[1,352,128]{2,1,0:T(8,128)S(1)} %get-tuple-element.120), channel_id=1, source_target_pairs={{0,4},{4,0},{8,12},{12,8},{16,20},{20,16},{24,28},{28,24},{1,5},{5... | collective-permute-start | bytes 540680 | tf_op jit(solution)/shard_map/ppermute | solution.py:1157
  64.5 1.7 %collective-permute-start.17 = (f32[1,304,128]{2,1,0:T(8,128)S(1)}, f32[1,304,128]{2,1,0:T(8,128)S(1)}, u32[]{:S(2)}, u32[]{:S(2)}) collective-permute-start(f32[1,304,128]{2,1,0:T(8,128)S(1)} %get-tuple-element.127), channel_id=1, source_target_pairs={{0,8},{4,12},{8,0},{12,4},{16,24},{20,28},{24,16},{28,20},{1,9},{5... | collective-permute-start | bytes 466952 | tf_op jit(solution)/shard_map/ppermute | solution.py:1157
  66.6 1.5 %collective-permute-done.13.refs_2_ = f32[1,352,128]{2,1,0:T(8,128)S(1)} collective-permute-done((f32[1,352,128]{2,1,0:T(8,128)S(1)}, f32[1,352,128]{2,1,0:T(8,128)S(1)}, u32[]{:S(2)}, u32[]{:S(2)}) %collective-permute-start.13) | collective-permute-done | bytes 180256 | tf_op jit(solution)/shard_map/ppermute | solution.py:1157
  68.1 1.8 %collective-permute-start.16 = (f32[1,176,128]{2,1,0:T(8,128)S(1)}, f32[1,176,128]{2,1,0:T(8,128)S(1)}, u32[]{:S(2)}, u32[]{:S(2)}) collective-permute-start(f32[1,176,128]{2,1,0:T(8,128)S(1)} %get-tuple-element.126), channel_id=1, source_target_pairs={{0,8},{4,12},{8,0},{12,4},{16,24},{20,28},{24,16},{28,20},{1,9},{5... | collective-permute-start | bytes 270344 | tf_op jit(solution)/shard_map/ppermute | solution.py:1157
  70.0 1.9 %collective-permute-done.18.refs_2_ = f32[1,224,128]{2,1,0:T(8,128)S(1)} collective-permute-done((f32[1,224,128]{2,1,0:T(8,128)S(1)}, f32[1,224,128]{2,1,0:T(8,128)S(1)}, u32[]{:S(2)}, u32[]{:S(2)}) %collective-permute-start.18) | collective-permute-done | bytes 114720 | tf_op jit(solution)/shard_map/ppermute | solution.py:1157
  72.1 3.5 %collective-permute-start.20 = (f32[1,152,128]{2,1,0:T(8,128)S(1)}, f32[1,152,128]{2,1,0:T(8,128)S(1)}, u32[]{:S(2)}, u32[]{:S(2)}) collective-permute-start(f32[1,152,128]{2,1,0:T(8,128)S(1)} %get-tuple-element.133), channel_id=1, source_target_pairs={{0,16},{4,20},{8,24},{12,28},{16,0},{20,4},{24,8},{28,12},{1,17},{... | collective-permute-start | bytes 233480 | tf_op jit(solution)/shard_map/ppermute | solution.py:1157
  75.7 7.9 %collective-permute-done.21.refs_2_ = f32[1,112,128]{2,1,0:T(8,128)S(1)} collective-permute-done((f32[1,112,128]{2,1,0:T(8,128)S(1)}, f32[1,112,128]{2,1,0:T(8,128)S(1)}, u32[]{:S(2)}, u32[]{:S(2)}) %collective-permute-start.21) | collective-permute-done | bytes 57376 | tf_op jit(solution)/shard_map/ppermute | solution.py:1157
  83.7 2.9 %collective-permute-start.24 = (f32[1,112,128]{2,1,0:T(8,128)S(1)}, f32[1,112,128]{2,1,0:T(8,128)S(1)}, u32[]{:S(2)}, u32[]{:S(2)}) collective-permute-start(f32[1,112,128]{2,1,0:T(8,128)S(1)} %total_2.1.refs_3_.refs_1_), channel_id=1, source_target_pairs={{0,16},{4,20},{8,24},{12,28},{16,0},{20,4},{24,8},{28,12},{1,17},{... | collective-permute-start | bytes 172040 | tf_op jit(solution)/shard_map/ppermute | solution.py:1157
  86.7 5.3 %collective-permute-done.19.refs_2_ = f32[1,88,128]{2,1,0:T(8,128)S(1)} collective-permute-done((f32[1,88,128]{2,1,0:T(8,128)S(1)}, f32[1,88,128]{2,1,0:T(8,128)S(1)}, u32[]{:S(2)}, u32[]{:S(2)}) %collective-permute-start.19) | collective-permute-done | bytes 45088 | tf_op jit(solution)/shard_map/ppermute | solution.py:1157
  92.1 1.3 %collective-permute-start.26 = (f32[1,304,128]{2,1,0:T(8,128)S(1)}, f32[1,304,128]{2,1,0:T(8,128)S(1)}, u32[]{:S(2)}, u32[]{:S(2)}) collective-permute-start(f32[1,304,128]{2,1,0:T(8,128)S(1)} %join_3.3.refs_3_.refs_1_), channel_id=1, source_target_pairs={{0,8},{4,12},{8,0},{12,4},{16,24},{20,28},{24,16},{28,20},{1,9},{5... | collective-permute-start | bytes 466952 | tf_op jit(solution)/shard_map/ppermute | solution.py:1157
  93.4 0.8 collective-permute-start.27
  94.2 1.4 %collective-permute-start.22 = (f32[1,88,128]{2,1,0:T(8,128)S(1)}, f32[1,88,128]{2,1,0:T(8,128)S(1)}, u32[]{:S(2)}, u32[]{:S(2)}) collective-permute-start(f32[1,88,128]{2,1,0:T(8,128)S(1)} %total_1.1.refs_3_.refs_1_), channel_id=1, source_target_pairs={{0,16},{4,20},{8,24},{12,28},{16,0},{20,4},{24,8},{28,12},{1,17},{... | collective-permute-start | bytes 135176 | tf_op jit(solution)/shard_map/ppermute | solution.py:1157
  95.7 3.6 %collective-permute-done.22.refs_2_ = f32[1,88,128]{2,1,0:T(8,128)S(1)} collective-permute-done((f32[1,88,128]{2,1,0:T(8,128)S(1)}, f32[1,88,128]{2,1,0:T(8,128)S(1)}, u32[]{:S(2)}, u32[]{:S(2)}) %collective-permute-start.22) | collective-permute-done | bytes 45088 | tf_op jit(solution)/shard_map/ppermute | solution.py:1157
  99.5 1.5 %collective-permute-start.29 = (f32[1,608,128]{2,1,0:T(8,128)S(1)}, f32[1,608,128]{2,1,0:T(8,128)S(1)}, u32[]{:S(2)}, u32[]{:S(2)}) collective-permute-start(f32[1,608,128]{2,1,0:T(8,128)S(1)} %join_3.4.refs_3_.refs_1_), channel_id=1, source_target_pairs={{0,4},{4,0},{8,12},{12,8},{16,20},{20,16},{24,28},{28,24},{1,5},{5... | collective-permute-start | bytes 933896 | tf_op jit(solution)/shard_map/ppermute | solution.py:1157
  101.0 1.3 %collective-permute-start.25 = (f32[1,176,128]{2,1,0:T(8,128)S(1)}, f32[1,176,128]{2,1,0:T(8,128)S(1)}, u32[]{:S(2)}, u32[]{:S(2)}) collective-permute-start(f32[1,176,128]{2,1,0:T(8,128)S(1)} %join_1.3.refs_3_.refs_1_), channel_id=1, source_target_pairs={{0,8},{4,12},{8,0},{12,4},{16,24},{20,28},{24,16},{28,20},{1,9},{5... | collective-permute-start | bytes 270344 | tf_op jit(solution)/shard_map/ppermute | solution.py:1157
  102.3 1.0 collective-permute-start.30
  103.3 2.2 %collective-permute-done.25.refs_2_ = f32[1,176,128]{2,1,0:T(8,128)S(1)} collective-permute-done((f32[1,176,128]{2,1,0:T(8,128)S(1)}, f32[1,176,128]{2,1,0:T(8,128)S(1)}, u32[]{:S(2)}, u32[]{:S(2)}) %collective-permute-start.25) | collective-permute-done | bytes 90144 | tf_op jit(solution)/shard_map/ppermute | solution.py:1157
  105.6 0.7 collective-permute-start.28
  106.2 2.7 %collective-permute-done.30.refs_2_ = f32[1,448,128]{2,1,0:T(8,128)S(1)} collective-permute-done((f32[1,448,128]{2,1,0:T(8,128)S(1)}, f32[1,448,128]{2,1,0:T(8,128)S(1)}, u32[]{:S(2)}, u32[]{:S(2)}) %collective-permute-start.30) | collective-permute-done | bytes 229408 | tf_op jit(solution)/shard_map/ppermute | solution.py:1157
  109.2 1.9 %collective-permute-done.28.refs_2_ = f32[1,352,128]{2,1,0:T(8,128)S(1)} collective-permute-done((f32[1,352,128]{2,1,0:T(8,128)S(1)}, f32[1,352,128]{2,1,0:T(8,128)S(1)}, u32[]{:S(2)}, u32[]{:S(2)}) %collective-permute-start.28) | collective-permute-done | bytes 180256 | tf_op jit(solution)/shard_map/ppermute | solution.py:1157
  111.3 3.4 %moments.1 = (f32[378,128]{1,0:T(8,128)}, f32[3,512,128]{2,1,0:T(8,128)}, f32[756,128]{1,0:T(8,128)}, f32[3,2,128]{2,1,0:T(2,128)}, f32[378,128]{1,0:T(8,128)}, ...) custom-call(f32[1,704,128]{2,1,0:T(8,128)S(1)} %join_1.5.refs_0_, ...), custom_call_target="tpu_custom_call" | custom-call | flops 1000 | bytes 1000 | tf_op jit(solution)/shard_map/moments/pallas_call | solution.py:1059
  114.8 1.7 %collective-permute-start.32 = (f32[32,128]{1,0:T(8,128)S(1)}, f32[32,128]{1,0:T(8,128)S(1)}, u32[]{:S(2)}, u32[]{:S(2)}) collective-permute-start(f32[32,128]{1,0:T(8,128)S(1)} %get-tuple-element.135.refs_1_), channel_id=1, source_target_pairs={{0,2},{1,3},{2,0},{3,1},{4,6},{5,7},{6,4},{7,5},{8,10},{9,11},{10,... | collective-permute-start | bytes 49160 | tf_op jit(solution)/shard_map/ppermute | solution.py:1157
  116.7 1.9 %collective-permute-done.32.refs_3_ = f32[32,128]{1,0:T(8,128)S(1)} collective-permute-done((f32[32,128]{1,0:T(8,128)S(1)}, f32[32,128]{1,0:T(8,128)S(1)}, u32[]{:S(2)}, u32[]{:S(2)}) %collective-permute-start.32) | collective-permute-done | bytes 16416 | tf_op jit(solution)/shard_map/ppermute | solution.py:1157
  118.6 1.1 collective-permute-done.33.refs_4_
  119.7 1.7 %apply.1 = (f32[378,128]{1,0:T(8,128)}, f32[3,512,128]{2,1,0:T(8,128)}, f32[756,128]{1,0:T(8,128)}, f32[3,2,128]{2,1,0:T(2,128)}, f32[3852]{0:T(1024)}, /*index=...) custom-call(s32[8,128]{1,0:T(8,128)S(1)} %iota.7.refs_0_.refs_1_, ...), custom_call_target="tpu_custom_call" | custom-call | flops 1000 | bytes 1000 | tf_op jit(solution)/shard_map/apply/pallas_call | solution.py:1059
  (102 shorter events, 4.3 us)
Async XLA Ops:
  0.7 5.4 %copy-start.15 = (f32[3,2,1024]{2,1,0:T(2,128)S(1)}, f32[3,2,1024]{2,1,0:T(2,128)}, u32[]{:S(2)}) copy-start(f32[3,2,1024]{2,1,0:T(2,128)} %refs_2_.1) | copy-start | bytes 73732
  0.7 5.4 %copy-start.21 = (s32[2]{0:T(128)S(1)}, s32[2]{0:T(128)}, u32[]{:S(2)}) copy-start(s32[2]{0:T(128)} %refs_0_.4) | copy-start | bytes 28
  0.7 5.4 %copy-start.18 = (s32[2,2]{1,0:T(2,128)S(1)}, s32[2,2]{1,0:T(2,128)}, u32[]{:S(2)}) copy-start(s32[2,2]{1,0:T(2,128)} %refs_0_.5) | copy-start | bytes 52
  0.7 5.4 %copy-start.13 = (f32[3852]{0:T(1024)S(1)}, f32[3852]{0:T(1024)}, u32[]{:S(2)}) copy-start(f32[3852]{0:T(1024)} %refs_13_.1) | copy-start | bytes 46228
  3.1 12.8 %collective-permute-start = (bf16[2720,128]{1,0:T(8,128)(2,1)}, bf16[2720,128]{1,0:T(8,128)(2,1)S(1)}, u32[]{:S(2)}, u32[]{:S(2)}) collective-permute-start(bf16[2720,128]{1,0:T(8,128)(2,1)} %get-tuple-element.93), channel_id=1, source_target_pairs={{0,1},{1,0},{2,3},{3,2},{4,5},{5,4},{6,7},{7,6},{8,9},{9,8},{10,11... | collective-permute-start | bytes 2088968 | tf_op jit(solution)/shard_map/ppermute | solution.py:1157
  3.6 10.5 %collective-permute-start.3 = (bf16[1168,128]{1,0:T(8,128)(2,1)}, bf16[1168,128]{1,0:T(8,128)(2,1)S(1)}, u32[]{:S(2)}, u32[]{:S(2)}) collective-permute-start(bf16[1168,128]{1,0:T(8,128)(2,1)} %get-tuple-element.95.refs_1_), channel_id=1, source_target_pairs={{0,2},{1,3},{2,0},{3,1},{4,6},{5,7},{6,4},{7,5},{8,10},{9,11},{10,... | collective-permute-start | bytes 897032 | tf_op jit(solution)/shard_map/ppermute | solution.py:1157
  14.1 1.9 %collective-permute-start.4 = (bf16[1168,128]{1,0:T(8,128)(2,1)S(1)}, bf16[1168,128]{1,0:T(8,128)(2,1)S(1)}, u32[]{:S(2)}, u32[]{:S(2)}) collective-permute-start(bf16[1168,128]{1,0:T(8,128)(2,1)S(1)} %copy_3.1.refs_6_), channel_id=1, source_target_pairs={{0,1},{1,0},{2,3},{3,2},{4,5},{5,4},{6,7},{7,6},{8,9},{9,8},{10,11... | collective-permute-start | bytes 897032 | tf_op jit(solution)/shard_map/ppermute | solution.py:1157
  14.1 8.1 %collective-permute-start.2 = (bf16[864,128]{1,0:T(8,128)(2,1)}, bf16[864,128]{1,0:T(8,128)(2,1)S(1)}, u32[]{:S(2)}, u32[]{:S(2)}) collective-permute-start(bf16[864,128]{1,0:T(8,128)(2,1)} %get-tuple-element.94.refs_1_), channel_id=1, source_target_pairs={{0,2},{1,3},{2,0},{3,1},{4,6},{5,7},{6,4},{7,5},{8,10},{9,11},{10,... | collective-permute-start | bytes 663560 | tf_op jit(solution)/shard_map/ppermute | solution.py:1157
  19.4 4.4 %copy-start.10 = (bf16[864,128]{1,0:T(8,128)(2,1)S(1)}, bf16[864,128]{1,0:T(8,128)(2,1)}, u32[]{:S(2)}) copy-start(bf16[864,128]{1,0:T(8,128)(2,1)} %get-tuple-element.94.refs_1_) | copy-start | bytes 663556
  19.4 13.6 %collective-permute-start.7 = (f32[2,1216,128]{2,1,0:T(8,128)S(1)}, f32[2,1216,128]{2,1,0:T(8,128)S(1)}, u32[]{:S(2)}, u32[]{:S(2)}) collective-permute-start(f32[2,1216,128]{2,1,0:T(8,128)S(1)} %get-tuple-element.105), channel_id=1, source_target_pairs={{0,1},{1,0},{2,3},{3,2},{4,5},{5,4},{6,7},{7,6},{8,9},{9,8},{10,11... | collective-permute-start | bytes 3735560 | tf_op jit(solution)/shard_map/ppermute | solution.py:1157
  22.2 4.2 %copy-start.6 = (bf16[688,128]{1,0:T(8,128)(2,1)S(1)}, bf16[688,128]{1,0:T(8,128)(2,1)}, u32[]{:S(2)}) copy-start(bf16[688,128]{1,0:T(8,128)(2,1)} %get-tuple-element.92.refs_4_.refs_2_) | copy-start | bytes 528388
  22.2 1.5 %collective-permute-start.5 = (bf16[864,128]{1,0:T(8,128)(2,1)S(1)}, bf16[864,128]{1,0:T(8,128)(2,1)S(1)}, u32[]{:S(2)}, u32[]{:S(2)}) collective-permute-start(bf16[864,128]{1,0:T(8,128)(2,1)S(1)} %copy_2.1.refs_2_), channel_id=1, source_target_pairs={{0,1},{1,0},{2,3},{3,2},{4,5},{5,4},{6,7},{7,6},{8,9},{9,8},{10,11... | collective-permute-start | bytes 663560 | tf_op jit(solution)/shard_map/ppermute | solution.py:1157
  25.9 8.7 %collective-permute-start.8 = (f32[2,896,128]{2,1,0:T(8,128)S(1)}, f32[2,896,128]{2,1,0:T(8,128)S(1)}, u32[]{:S(2)}, u32[]{:S(2)}) collective-permute-start(f32[2,896,128]{2,1,0:T(8,128)S(1)} %get-tuple-element.109), channel_id=1, source_target_pairs={{0,1},{1,0},{2,3},{3,2},{4,5},{5,4},{6,7},{7,6},{8,9},{9,8},{10,11... | collective-permute-start | bytes 2752520 | tf_op jit(solution)/shard_map/ppermute | solution.py:1157
  26.5 6.5 %collective-permute-start.1 = (bf16[688,128]{1,0:T(8,128)(2,1)S(1)}, bf16[688,128]{1,0:T(8,128)(2,1)S(1)}, u32[]{:S(2)}, u32[]{:S(2)}) collective-permute-start(bf16[688,128]{1,0:T(8,128)(2,1)S(1)} %copy-done.6), channel_id=1, source_target_pairs={{0,2},{1,3},{2,0},{3,1},{4,6},{5,7},{6,4},{7,5},{8,10},{9,11},{10,... | collective-permute-start | bytes 528392 | tf_op jit(solution)/shard_map/ppermute | solution.py:1157
  32.9 1.9 %collective-permute-start.6 = (bf16[688,128]{1,0:T(8,128)(2,1)S(1)}, bf16[688,128]{1,0:T(8,128)(2,1)S(1)}, u32[]{:S(2)}, u32[]{:S(2)}) collective-permute-start(bf16[688,128]{1,0:T(8,128)(2,1)S(1)} %copy_1.1.refs_3_), channel_id=1, source_target_pairs={{0,1},{1,0},{2,3},{3,2},{4,5},{5,4},{6,7},{7,6},{8,9},{9,8},{10,11... | collective-permute-start | bytes 528392 | tf_op jit(solution)/shard_map/ppermute | solution.py:1157
  39.5 3.8 %collective-permute-start.9 = (f32[2,704,128]{2,1,0:T(8,128)S(1)}, f32[2,704,128]{2,1,0:T(8,128)S(1)}, u32[]{:S(2)}, u32[]{:S(2)}) collective-permute-start(f32[2,704,128]{2,1,0:T(8,128)S(1)} %get-tuple-element.112), channel_id=1, source_target_pairs={{0,1},{1,0},{2,3},{3,2},{4,5},{5,4},{6,7},{7,6},{8,9},{9,8},{10,11... | collective-permute-start | bytes 2162696 | tf_op jit(solution)/shard_map/ppermute | solution.py:1157
  40.1 9.4 %collective-permute-start.11 = (bf16[2,608,128]{2,1,0:T(8,128)(2,1)S(1)}, bf16[2,608,128]{2,1,0:T(8,128)(2,1)S(1)}, u32[]{:S(2)}, u32[]{:S(2)}) collective-permute-start(bf16[2,608,128]{2,1,0:T(8,128)(2,1)S(1)} %get-tuple-element.115), channel_id=1, source_target_pairs={{0,4},{4,0},{8,12},{12,8},{16,20},{20,16},{24,28},{28,24},{1,5},{5... | collective-permute-start | bytes 933896 | tf_op jit(solution)/shard_map/ppermute | solution.py:1157
  41.9 7.3 %collective-permute-start.12 = (bf16[1,896,128]{2,1,0:T(8,128)(2,1)S(1)}, bf16[1,896,128]{2,1,0:T(8,128)(2,1)S(1)}, u32[]{:S(2)}, u32[]{:S(2)}) collective-permute-start(bf16[1,896,128]{2,1,0:T(8,128)(2,1)S(1)} %get-tuple-element.116), channel_id=1, source_target_pairs={{0,2},{1,3},{2,0},{3,1},{4,6},{5,7},{6,4},{7,5},{8,10},{9,11},{10,... | collective-permute-start | bytes 688136 | tf_op jit(solution)/shard_map/ppermute | solution.py:1157
  49.5 14.8 %collective-permute-start.14 = (f32[1,608,128]{2,1,0:T(8,128)S(1)}, f32[1,608,128]{2,1,0:T(8,128)S(1)}, u32[]{:S(2)}, u32[]{:S(2)}) collective-permute-start(f32[1,608,128]{2,1,0:T(8,128)S(1)} %get-tuple-element.121), channel_id=1, source_target_pairs={{0,2},{1,3},{2,0},{3,1},{4,6},{5,7},{6,4},{7,5},{8,10},{9,11},{10,... | collective-permute-start | bytes 933896 | tf_op jit(solution)/shard_map/ppermute | solution.py:1157
  51.3 10.9 %collective-permute-start.10 = (bf16[1,752,128]{2,1,0:T(8,128)(2,1)S(1)}, bf16[1,752,128]{2,1,0:T(8,128)(2,1)S(1)}, u32[]{:S(2)}, u32[]{:S(2)}) collective-permute-start(bf16[1,752,128]{2,1,0:T(8,128)(2,1)S(1)} %get-tuple-element.114), channel_id=1, source_target_pairs={{0,2},{1,3},{2,0},{3,1},{4,6},{5,7},{6,4},{7,5},{8,10},{9,11},{10,... | collective-permute-start | bytes 577544 | tf_op jit(solution)/shard_map/ppermute | solution.py:1157
  51.6 12.7 %collective-permute-start.15 = (f32[1,448,128]{2,1,0:T(8,128)S(1)}, f32[1,448,128]{2,1,0:T(8,128)S(1)}, u32[]{:S(2)}, u32[]{:S(2)}) collective-permute-start(f32[1,448,128]{2,1,0:T(8,128)S(1)} %get-tuple-element.122), channel_id=1, source_target_pairs={{0,4},{4,0},{8,12},{12,8},{16,20},{20,16},{24,28},{28,24},{1,5},{5... | collective-permute-start | bytes 688136 | tf_op jit(solution)/shard_map/ppermute | solution.py:1157
  62.5 5.6 %collective-permute-start.13 = (f32[1,352,128]{2,1,0:T(8,128)S(1)}, f32[1,352,128]{2,1,0:T(8,128)S(1)}, u32[]{:S(2)}, u32[]{:S(2)}) collective-permute-start(f32[1,352,128]{2,1,0:T(8,128)S(1)} %get-tuple-element.120), channel_id=1, source_target_pairs={{0,4},{4,0},{8,12},{12,8},{16,20},{20,16},{24,28},{28,24},{1,5},{5... | collective-permute-start | bytes 540680 | tf_op jit(solution)/shard_map/ppermute | solution.py:1157
  64.5 7.5 %collective-permute-start.17 = (f32[1,304,128]{2,1,0:T(8,128)S(1)}, f32[1,304,128]{2,1,0:T(8,128)S(1)}, u32[]{:S(2)}, u32[]{:S(2)}) collective-permute-start(f32[1,304,128]{2,1,0:T(8,128)S(1)} %get-tuple-element.127), channel_id=1, source_target_pairs={{0,8},{4,12},{8,0},{12,4},{16,24},{20,28},{24,16},{28,20},{1,9},{5... | collective-permute-start | bytes 466952 | tf_op jit(solution)/shard_map/ppermute | solution.py:1157
  66.1 5.8 %collective-permute-start.18 = (f32[1,224,128]{2,1,0:T(8,128)S(1)}, f32[1,224,128]{2,1,0:T(8,128)S(1)}, u32[]{:S(2)}, u32[]{:S(2)}) collective-permute-start(f32[1,224,128]{2,1,0:T(8,128)S(1)} %get-tuple-element.128), channel_id=1, source_target_pairs={{0,8},{4,12},{8,0},{12,4},{16,24},{20,28},{24,16},{28,20},{1,9},{5... | collective-permute-start | bytes 344072 | tf_op jit(solution)/shard_map/ppermute | solution.py:1157
  68.1 7.5 %collective-permute-start.16 = (f32[1,176,128]{2,1,0:T(8,128)S(1)}, f32[1,176,128]{2,1,0:T(8,128)S(1)}, u32[]{:S(2)}, u32[]{:S(2)}) collective-permute-start(f32[1,176,128]{2,1,0:T(8,128)S(1)} %get-tuple-element.126), channel_id=1, source_target_pairs={{0,8},{4,12},{8,0},{12,4},{16,24},{20,28},{24,16},{28,20},{1,9},{5... | collective-permute-start | bytes 270344 | tf_op jit(solution)/shard_map/ppermute | solution.py:1157
  72.1 11.5 %collective-permute-start.20 = (f32[1,152,128]{2,1,0:T(8,128)S(1)}, f32[1,152,128]{2,1,0:T(8,128)S(1)}, u32[]{:S(2)}, u32[]{:S(2)}) collective-permute-start(f32[1,152,128]{2,1,0:T(8,128)S(1)} %get-tuple-element.133), channel_id=1, source_target_pairs={{0,16},{4,20},{8,24},{12,28},{16,0},{20,4},{24,8},{28,12},{1,17},{... | collective-permute-start | bytes 233480 | tf_op jit(solution)/shard_map/ppermute | solution.py:1157
  75.6 8.0 %collective-permute-start.21 = (f32[1,112,128]{2,1,0:T(8,128)S(1)}, f32[1,112,128]{2,1,0:T(8,128)S(1)}, u32[]{:S(2)}, u32[]{:S(2)}) collective-permute-start(f32[1,112,128]{2,1,0:T(8,128)S(1)} %get-tuple-element.134), channel_id=1, source_target_pairs={{0,16},{4,20},{8,24},{12,28},{16,0},{20,4},{24,8},{28,12},{1,17},{... | collective-permute-start | bytes 172040 | tf_op jit(solution)/shard_map/ppermute | solution.py:1157
  83.6 8.4 %collective-permute-start.23 = (f32[1,152,128]{2,1,0:T(8,128)S(1)}, f32[1,152,128]{2,1,0:T(8,128)S(1)}, u32[]{:S(2)}, u32[]{:S(2)}) collective-permute-start(f32[1,152,128]{2,1,0:T(8,128)S(1)} %total_3.1.refs_3_.refs_1_), channel_id=1, source_target_pairs={{0,16},{4,20},{8,24},{12,28},{16,0},{20,4},{24,8},{28,12},{1,17},{... | collective-permute-start | bytes 233480 | tf_op jit(solution)/shard_map/ppermute | solution.py:1157
  83.7 8.3 %collective-permute-start.24 = (f32[1,112,128]{2,1,0:T(8,128)S(1)}, f32[1,112,128]{2,1,0:T(8,128)S(1)}, u32[]{:S(2)}, u32[]{:S(2)}) collective-permute-start(f32[1,112,128]{2,1,0:T(8,128)S(1)} %total_2.1.refs_3_.refs_1_), channel_id=1, source_target_pairs={{0,16},{4,20},{8,24},{12,28},{16,0},{20,4},{24,8},{28,12},{1,17},{... | collective-permute-start | bytes 172040 | tf_op jit(solution)/shard_map/ppermute | solution.py:1157
  86.6 5.4 %collective-permute-start.19 = (f32[1,88,128]{2,1,0:T(8,128)S(1)}, f32[1,88,128]{2,1,0:T(8,128)S(1)}, u32[]{:S(2)}, u32[]{:S(2)}) collective-permute-start(f32[1,88,128]{2,1,0:T(8,128)S(1)} %get-tuple-element.132), channel_id=1, source_target_pairs={{0,16},{4,20},{8,24},{12,28},{16,0},{20,4},{24,8},{28,12},{1,17},{... | collective-permute-start | bytes 135176 | tf_op jit(solution)/shard_map/ppermute | solution.py:1157
  92.1 7.3 %collective-permute-start.26 = (f32[1,304,128]{2,1,0:T(8,128)S(1)}, f32[1,304,128]{2,1,0:T(8,128)S(1)}, u32[]{:S(2)}, u32[]{:S(2)}) collective-permute-start(f32[1,304,128]{2,1,0:T(8,128)S(1)} %join_3.3.refs_3_.refs_1_), channel_id=1, source_target_pairs={{0,8},{4,12},{8,0},{12,4},{16,24},{20,28},{24,16},{28,20},{1,9},{5... | collective-permute-start | bytes 466952 | tf_op jit(solution)/shard_map/ppermute | solution.py:1157
  93.4 5.9 %collective-permute-start.27 = (f32[1,224,128]{2,1,0:T(8,128)S(1)}, f32[1,224,128]{2,1,0:T(8,128)S(1)}, u32[]{:S(2)}, u32[]{:S(2)}) collective-permute-start(f32[1,224,128]{2,1,0:T(8,128)S(1)} %join_2.3.refs_3_.refs_1_), channel_id=1, source_target_pairs={{0,8},{4,12},{8,0},{12,4},{16,24},{20,28},{24,16},{28,20},{1,9},{5... | collective-permute-start | bytes 344072 | tf_op jit(solution)/shard_map/ppermute | solution.py:1157
  94.2 5.1 %collective-permute-start.22 = (f32[1,88,128]{2,1,0:T(8,128)S(1)}, f32[1,88,128]{2,1,0:T(8,128)S(1)}, u32[]{:S(2)}, u32[]{:S(2)}) collective-permute-start(f32[1,88,128]{2,1,0:T(8,128)S(1)} %total_1.1.refs_3_.refs_1_), channel_id=1, source_target_pairs={{0,16},{4,20},{8,24},{12,28},{16,0},{20,4},{24,8},{28,12},{1,17},{... | collective-permute-start | bytes 135176 | tf_op jit(solution)/shard_map/ppermute | solution.py:1157
  99.5 9.6 %collective-permute-start.29 = (f32[1,608,128]{2,1,0:T(8,128)S(1)}, f32[1,608,128]{2,1,0:T(8,128)S(1)}, u32[]{:S(2)}, u32[]{:S(2)}) collective-permute-start(f32[1,608,128]{2,1,0:T(8,128)S(1)} %join_3.4.refs_3_.refs_1_), channel_id=1, source_target_pairs={{0,4},{4,0},{8,12},{12,8},{16,20},{20,16},{24,28},{28,24},{1,5},{5... | collective-permute-start | bytes 933896 | tf_op jit(solution)/shard_map/ppermute | solution.py:1157
  101.0 4.5 %collective-permute-start.25 = (f32[1,176,128]{2,1,0:T(8,128)S(1)}, f32[1,176,128]{2,1,0:T(8,128)S(1)}, u32[]{:S(2)}, u32[]{:S(2)}) collective-permute-start(f32[1,176,128]{2,1,0:T(8,128)S(1)} %join_1.3.refs_3_.refs_1_), channel_id=1, source_target_pairs={{0,8},{4,12},{8,0},{12,4},{16,24},{20,28},{24,16},{28,20},{1,9},{5... | collective-permute-start | bytes 270344 | tf_op jit(solution)/shard_map/ppermute | solution.py:1157
  102.3 6.6 %collective-permute-start.30 = (f32[1,448,128]{2,1,0:T(8,128)S(1)}, f32[1,448,128]{2,1,0:T(8,128)S(1)}, u32[]{:S(2)}, u32[]{:S(2)}) collective-permute-start(f32[1,448,128]{2,1,0:T(8,128)S(1)} %join_2.4.refs_3_.refs_1_), channel_id=1, source_target_pairs={{0,4},{4,0},{8,12},{12,8},{16,20},{20,16},{24,28},{28,24},{1,5},{5... | collective-permute-start | bytes 688136 | tf_op jit(solution)/shard_map/ppermute | solution.py:1157
  105.6 5.6 %collective-permute-start.28 = (f32[1,352,128]{2,1,0:T(8,128)S(1)}, f32[1,352,128]{2,1,0:T(8,128)S(1)}, u32[]{:S(2)}, u32[]{:S(2)}) collective-permute-start(f32[1,352,128]{2,1,0:T(8,128)S(1)} %join_1.4.refs_3_.refs_1_), channel_id=1, source_target_pairs={{0,4},{4,0},{8,12},{12,8},{16,20},{20,16},{24,28},{28,24},{1,5},{5... | collective-permute-start | bytes 540680 | tf_op jit(solution)/shard_map/ppermute | solution.py:1157
  108.9 2.3 %copy-start.7 = (f32[128,756]{0,1:T(8,128)S(1)}, f32[128,756]{0,1:T(8,128)}, u32[]{:S(2)}) copy-start(f32[128,756]{0,1:T(8,128)} %param.28) | copy-start | bytes 1161220
  108.9 2.3 %copy-start.8 = (f32[128,756]{0,1:T(8,128)S(1)}, f32[128,756]{0,1:T(8,128)}, u32[]{:S(2)}) copy-start(f32[128,756]{0,1:T(8,128)} %param.33) | copy-start | bytes 1161220
  108.9 2.3 %copy-start.11 = (f32[378,128]{1,0:T(8,128)S(1)}, f32[378,128]{1,0:T(8,128)}, u32[]{:S(2)}) copy-start(f32[378,128]{1,0:T(8,128)} %refs_7_.1) | copy-start | bytes 580612
  108.9 2.3 %copy-start.12 = (f32[378,128]{1,0:T(8,128)S(1)}, f32[378,128]{1,0:T(8,128)}, u32[]{:S(2)}) copy-start(f32[378,128]{1,0:T(8,128)} %refs_11_.1) | copy-start | bytes 580612
  109.0 2.2 %copy-start = (f32[3,512,128]{2,1,0:T(8,128)S(1)}, f32[3,512,128]{2,1,0:T(8,128)}, u32[]{:S(2)}) copy-start(f32[3,512,128]{2,1,0:T(8,128)} %refs_6_.3) | copy-start | bytes 2359300
  109.0 2.2 %copy-start.1 = (f32[128,756]{0,1:T(8,128)S(1)}, f32[128,756]{0,1:T(8,128)}, u32[]{:S(2)}) copy-start(f32[128,756]{0,1:T(8,128)} %param.23) | copy-start | bytes 1161220
  111.3 8.4 %copy-start.16 = (f32[3852]{0:T(1024)S(1)}, f32[3852]{0:T(1024)}, u32[]{:S(2)}) copy-start(f32[3852]{0:T(1024)} %refs_14_.3) | copy-start | bytes 46228
  111.3 8.3 %copy-start.17 = (f32[3852]{0:T(1024)S(1)}, f32[3852]{0:T(1024)}, u32[]{:S(2)}) copy-start(f32[3852]{0:T(1024)} %refs_15_.1) | copy-start | bytes 46228
  114.8 1.9 %collective-permute-start.31 = (f32[32,128]{1,0:T(8,128)S(1)}, f32[32,128]{1,0:T(8,128)S(1)}, u32[]{:S(2)}, u32[]{:S(2)}) collective-permute-start(f32[32,128]{1,0:T(8,128)S(1)} %get-tuple-element.135.refs_1_), channel_id=1, source_target_pairs={{0,1},{1,0},{2,3},{3,2},{4,5},{5,4},{6,7},{7,6},{8,9},{9,8},{10,11... | collective-permute-start | bytes 49160 | tf_op jit(solution)/shard_map/ppermute | solution.py:1157
  114.8 3.8 %collective-permute-start.32 = (f32[32,128]{1,0:T(8,128)S(1)}, f32[32,128]{1,0:T(8,128)S(1)}, u32[]{:S(2)}, u32[]{:S(2)}) collective-permute-start(f32[32,128]{1,0:T(8,128)S(1)} %get-tuple-element.135.refs_1_), channel_id=1, source_target_pairs={{0,2},{1,3},{2,0},{3,1},{4,6},{5,7},{6,4},{7,5},{8,10},{9,11},{10,... | collective-permute-start | bytes 49160 | tf_op jit(solution)/shard_map/ppermute | solution.py:1157
  116.5 3.2 %collective-permute-start.33 = (f32[32,128]{1,0:T(8,128)S(1)}, f32[32,128]{1,0:T(8,128)S(1)}, u32[]{:S(2)}, u32[]{:S(2)}) collective-permute-start(f32[32,128]{1,0:T(8,128)S(1)} %get-tuple-element.135.refs_1_), channel_id=1, source_target_pairs={{0,3},{1,2},{2,1},{3,0},{4,7},{5,6},{6,5},{7,4},{8,11},{9,10},{10,... | collective-permute-start | bytes 49160 | tf_op jit(solution)/shard_map/ppermute | solution.py:1157
  (8 other events, 15.3 us)

commit v3 on v2

--- a/solution.py
+++ b/solution.py
@@ -25,6 +25,8 @@
 LEVELS = 3
 FLOW_ROWS = 32
 STATS_ROWS = 8
+CODE_BLOCK = 16
+CODE_RANGE = 84.0
 VMEM_BYTES = 20 * 1024 * 1024
 
 
@@ -52,12 +54,16 @@
     return 9 * chan(level) // 2
 
 
+def bias_in_tail(level):
+    return round_up(9 * chan(level), 16) - 9 * chan(level) >= 4 and in_rows(level) % 16 > 10
+
+
 def first_rows(level):
-    return round_up(in_rows(level) + 6, 16)
+    return round_up(in_rows(level) + (3 if bias_in_tail(level) else 6), 16)
 
 
 def second_bias_row(level):
-    return first_rows(level) - 4
+    return (pack_rows(level) if bias_in_tail(level) else first_rows(level)) - 4
 
 
 def last_rows(level):
@@ -76,9 +82,25 @@
     return round_up(FLOW_ROWS // narrow, 8) + STATS_ROWS
 
 
-def grad_rows(level, narrow):
-    rows = pack_rows(level) + (flow_block_rows(narrow) if level == 0 else 0)
-    return round_up(rows, 64)
+CHUNKS = ((0, 1), (2,))
+
+
+def chunk_start(level):
+    for chunk, levels in enumerate(CHUNKS):
+        if level in levels:
+            return chunk, sum(pack_rows(other) for other in levels if other < level)
+    return None
+
+
+def flow_start():
+    return sum(pack_rows(level) for level in CHUNKS[-1])
+
+
+def chunk_rows(chunk, narrow):
+    rows = sum(pack_rows(level) for level in CHUNKS[chunk])
+    if chunk == len(CHUNKS) - 1:
+        rows = rows + flow_block_rows(narrow)
+    return round_up(rows, 8 * CODE_BLOCK)
 
 
 def stage_rows(level):
@@ -91,18 +113,20 @@
         ("held", padded),
         ("block", padded),
         ("prior", half),
+        ("mixing", padded),
+        ("turn", padded),
         ("grad", padded),
         ("small", padded),
         ("prior_grad", half),
     ]
     starts = {}
     at = 0
-    for name, size in sizes[:6]:
+    for name, size in sizes[:8]:
         starts[name] = at
         at = at + size
     starts["rows"] = at
     at = 0
-    for name, size in sizes[6:]:
+    for name, size in sizes[8:]:
         starts[name] = at
         at = at + size
     starts["result_rows"] = at
@@ -244,10 +268,9 @@
     return ordered
 
 
-def unsqueeze(values, chooser, count):
-    channels = values.shape[0] // 4
+def unsqueeze(stacked, chooser, count):
+    channels = stacked.shape[0] // 4
     quarter = count // 4
-    stacked = exact_rows(order_chooser(channels, channels), values)
     laid = jnp.concatenate(
         [stacked[k * channels : (k + 1) * channels, :quarter] for k in range(4)], 1
     )
@@ -410,27 +433,29 @@
     return total
 
 
-def pack_kernel(conv_in_ref, mixer_ref, conv_out_ref, bias_ref, *out_refs):
+def pack_kernel(conv_in_ref, mixer_ref, conv_out_ref, bias_ref, whole_ref):
     in_start = 0
     out_start = 0
     for level in range(LEVELS):
-        out_ref = out_refs[level]
+        out_ref = whole_ref.at[pack_start(level) : pack_start(level) + pack_rows(level)]
         rows, columns = in_rows(level), 9 * chan(level)
         top = first_rows(level)
         ones = split_three(bias_ref[level, 0:1, :])
-        twos = split_three(bias_ref[level, 1:2, :])
-        gap = second_bias_row(level) - rows - 3
-        pieces = [conv_in_ref[in_start : in_start + rows, :]] + ones
-        if gap:
-            pieces.append(jnp.zeros((gap, LANE), F32))
-        pieces = pieces + twos + [jnp.zeros((1, LANE), F32)]
-        out_ref[0:top, :] = jnp.concatenate(pieces, 0).astype(BF16)
+        twos = split_three(bias_ref[level, 1:2, :]) + [jnp.zeros((1, LANE), F32)]
+        head = [conv_in_ref[in_start : in_start + rows, :]] + ones
+        tail = [conv_out_ref[out_start : out_start + columns, :]]
+        for part, size, chosen in (
+            (head, top, not bias_in_tail(level)),
+            (tail, last_rows(level), bias_in_tail(level)),
+        ):
+            used = sum(piece.shape[0] for piece in part) + (4 if chosen else 0)
+            if size > used:
+                part.append(jnp.zeros((size - used, LANE), F32))
+            if chosen:
+                part.extend(twos)
+        out_ref[0:top, :] = jnp.concatenate(head, 0).astype(BF16)
         out_ref[top : top + HID, :] = mixer_ref[level].astype(BF16)
-        tail = conv_out_ref[out_start : out_start + columns, :]
-        if last_rows(level) > columns:
-            tail = jnp.concatenate([tail, jnp.zeros((last_rows(level) - columns, LANE), F32)], 0)
-        out_ref[top + HID :, :] = tail.astype(BF16)
-        out_refs[LEVELS][pack_start(level) : pack_start(level) + pack_rows(level), :] = out_ref[...]
+        out_ref[top + HID :, :] = jnp.concatenate(tail, 0).astype(BF16)
         in_start = in_start + rows
         out_start = out_start + columns
 
@@ -491,7 +516,8 @@
         held = jnp.zeros((channels, LANE), F32)
         for index, column in enumerate(columns):
             held = jnp.where(lane == index, column, held)
-        normed = (state + columns[0]) * jnp.exp(columns[1])
+        growth = jnp.exp(columns[1])
+        normed = (state + columns[0]) * growth
         lower, upper, reverse, _ = triangles(block)
         mixing = exact_dot(exact_dot(reverse, lower), upper)
         mixed = exact_dot(mixing, normed)
@@ -516,6 +542,12 @@
         out_ref[starts["share"] : starts["share"] + 8, :] = share
         out_ref[starts["held"] : starts["held"] + channels, 0:LANE] = held
         out_ref[starts["block"] : starts["block"] + channels, 0:channels] = block
+        out_ref[starts["mixing"] : starts["mixing"] + channels, 0:channels] = mixing
+        if level > 0:
+            order = order_chooser(channels // 4, channels // 4)
+            out_ref[starts["turn"] : starts["turn"] + channels, 0:channels] = exact_dot(
+                mixing, growth * order
+            )
         if level < LEVELS - 1:
             out_ref[starts["prior"] : starts["prior"] + channels // 2, 0:channels] = flow_block(
                 flat, offsets["priormatrix"], channels // 2, channels
@@ -536,7 +568,8 @@
     is_last = level == LEVELS - 1
     index_ref = refs[0]
     weight_refs = refs[1 : 1 + narrow]
-    bases = [pack_start(level) if ref.shape[0] > pack_rows(level) else 0 for ref in weight_refs]
+    base = pack_start(level)
+    out_base = chunk_start(level)[1]
     stage_ref, keep_ref, send_ref, result_ref = refs[1 + narrow : 5 + narrow]
     order_ref, slope_one_ref, slope_two_ref, one_ref, two_ref = refs[5 + narrow :]
     starts = stage_rows(level)
@@ -546,17 +579,18 @@
     count = positions(level, images)
     top, rows = first_rows(level), in_rows(level)
     tail, used = last_rows(level), 9 * channels
+    bias_block = second_bias_row(level) - 12
     masks = tap_masks(level, images)
     width = HID // narrow
 
     def weights(start, length):
         return jnp.concatenate(
-            [ref[base + start : base + start + length, :] for ref, base in zip(weight_refs, bases)], 1
+            [ref[base + start : base + start + length, :] for ref in weight_refs], 1
         )
 
     for r_in in range(narrow):
         for r_out in range(narrow):
-            start = pl.multiple_of(bases[r_out] + top + (me ^ r_in) * width, 16)
+            start = pl.multiple_of(base + top + (me ^ r_in) * width, 16)
             order_ref[r_in * width : (r_in + 1) * width, r_out * LANE : (r_out + 1) * LANE] = (
                 weight_refs[r_out][pl.ds(start, width), :]
             )
@@ -578,7 +612,9 @@
     active, slope = silu_parts(hidden_one)
     slope_one_ref[...] = slope
     one_ref[...] = active.astype(BF16)
-    hidden_two = contract_rows(weight_mix, one_ref[...]) + contract_rows(weights(top - 16, 16), pick)
+    hidden_two = contract_rows(weight_mix, one_ref[...]) + contract_rows(
+        weights(bias_block, 16), pick
+    )
     active, slope = silu_parts(hidden_two)
     slope_two_ref[...] = slope
     two_ref[...] = active.astype(BF16)
@@ -647,13 +683,14 @@
     def store(start, values):
         for r in range(narrow):
             ref = send_ref if r & 1 else keep_ref
-            ref[r // 2, start : start + values.shape[0], :] = values[:, r * LANE : (r + 1) * LANE]
-
-    store(top + HID, contract_columns(grad_spread, two_ref[...]))
+            rows = slice(out_base + start, out_base + start + values.shape[0])
+            ref[r // 2, rows, :] = values[:, r * LANE : (r + 1) * LANE]
+
+    grad_out = contract_columns(grad_spread, two_ref[...])
     grad_two = (contract_rows(weight_out, grad_spread) * slope_two_ref[...]).astype(BF16)
     grad_mix = contract_columns(one_ref[...], grad_two)
     for r_in in range(narrow):
-        start = pl.multiple_of(top + (me ^ r_in) * width, 16)
+        start = pl.multiple_of(out_base + top + (me ^ r_in) * width, 16)
         for r_out in range(narrow):
             ref = send_ref if r_out & 1 else keep_ref
             ref[r_out // 2, pl.ds(start, width), :] = grad_mix[
@@ -661,38 +698,55 @@
             ]
     grad_one = (plain_dot(weight_mix, grad_two) * slope_one_ref[...]).astype(BF16)
     grad_in = contract_columns(stacked, grad_one)
-    store(0, grad_in[: top - 16])
-    store(top - 16, grad_in[top - 16 :] + contract_columns(pick, grad_two))
-    rest = keep_ref.shape[1] - pack_rows(level)
-    if rest and level > 0:
-        for ref in (keep_ref, send_ref):
-            ref[:, pack_rows(level) :, :] = jnp.zeros((narrow // 2, rest, LANE), F32)
+    grad_bias = contract_columns(pick, grad_two)
+    if bias_in_tail(level):
+        grad_out = jnp.concatenate([grad_out[: tail - 16], grad_out[tail - 16 :] + grad_bias], 0)
+    else:
+        grad_in = jnp.concatenate([grad_in[: top - 16], grad_in[top - 16 :] + grad_bias], 0)
+    store(0, grad_in)
+    store(top + HID, grad_out)
     grad_stack = plain_dot(weight_in, grad_one)
     grad_first = grad_first + tap_sum(grad_stack, masks, level, -1, half)
     result_ref[0:half, :] = grad_first
     result_ref[half:channels, :] = grad_second
 
 
-def flow_level(level, images, stage_ref, result_ref, carried, flat):
+def stage_part(level, ref, name, rows, lanes):
+    start = stage_rows(level)[name]
+    return ref[start : start + rows, 0:lanes]
+
+
+def flow_chain(images, stages, results):
+    grads = [None] * LEVELS
+    carried = None
+    for level in (2, 1, 0):
+        channels = chan(level)
+        count = positions(level, images)
+        grad = stage_part(level, results[level], "grad", channels, count)
+        if carried is not None:
+            grad = grad + jnp.concatenate([carried, jnp.zeros_like(carried)], 0)
+        grads[level] = grad
+        if level > 0:
+            turn = stage_part(level, stages[level], "turn", channels, channels)
+            grid = side(level - 1)
+            carried = unsqueeze(
+                exact_rows(turn, grad), squeeze_chooser(grid, images), images * grid * grid
+            )
+    return grads
+
+
+def flow_level(level, images, stage_ref, result_ref, grad):
     channels = chan(level)
     half = channels // 2
-    starts = stage_rows(level)
-
-    def part(ref, name, rows, lanes):
-        return ref[starts[name] : starts[name] + rows, 0:lanes]
-
     count = positions(level, images)
     offsets = flow_offsets(level)
-    grad = part(result_ref, "grad", channels, count)
-    if carried is not None:
-        grad = grad + jnp.concatenate([carried, jnp.zeros_like(carried)], 0)
-    normed = part(stage_ref, "normed", channels, count)
-    held = part(stage_ref, "held", channels, LANE)
-    small = part(result_ref, "small", channels, LANE)
-    block = part(stage_ref, "block", channels, channels)
+    normed = stage_part(level, stage_ref, "normed", channels, count)
+    held = stage_part(level, stage_ref, "held", channels, LANE)
+    block = stage_part(level, stage_ref, "block", channels, channels)
+    mixing = stage_part(level, stage_ref, "mixing", channels, channels)
+    small = stage_part(level, result_ref, "small", channels, LANE)
     lower, upper, reverse, diagonal = triangles(block)
-    mixing_left = exact_dot(reverse, lower)
-    grad_normed = exact_rows(exact_dot(mixing_left, upper), grad)
+    grad_normed = exact_rows(mixing, grad)
     grad_mixing = exact_dot(reverse, exact_columns(grad, normed))
     grad_lower = exact_columns(grad_mixing, upper)
     grad_upper = exact_rows(lower, grad_mixing)
@@ -705,10 +759,9 @@
         jnp.where(row < column, grad_upper, grad_upper * diagonal - share_total),
     )
     growth = jnp.exp(held[:, 1:2])
-    grad_state = grad_normed * growth
-    grad_bias = jnp.sum(grad_state, 1, keepdims=True)
+    grad_bias = jnp.sum(grad_normed, 1, keepdims=True) * growth
     grad_logs = jnp.sum(grad_normed * normed, 1, keepdims=True) - share_total
-    term = flow_block_back(grad_block, offsets["block"], channels, channels)
+    flat = flow_block_back(grad_block, offsets["block"], channels, channels)
     turned = jnp.zeros((LANE, LANE), F32)
     for index, (name, offset) in enumerate(column_names(level)):
         if name == "bias":
@@ -719,47 +772,27 @@
             values = small[:, index : index + 1]
         turned = turned + flow_column_back(values, offset)
     if level < LEVELS - 1:
-        term = term + flow_block_back(
-            part(result_ref, "prior_grad", half, channels), offsets["priormatrix"], half, channels
+        flat = flat + flow_block_back(
+            stage_part(level, result_ref, "prior_grad", half, channels),
+            offsets["priormatrix"],
+            half,
+            channels,
         )
     logs_total = jnp.sum(held[:, 1:2], 0, keepdims=True)
     trace = jnp.sum(
         jnp.sum(jnp.where(row == column, block, 0.0), 0, keepdims=True), 1, keepdims=True
     )
-    loss = small[0:1, 6:7] - share_total * (logs_total + trace)
-    term = term + turned.T[:FLOW_ROWS]
-    row = iota((FLOW_ROWS, LANE), 0)
-    lane = iota((FLOW_ROWS, LANE), 1)
-    term = term + jnp.where((row == FLOW_ROWS - 1) & (lane == 0), loss, 0.0)
-    flat = term if flat is None else flat + term
-    carried = None
-    if level > 0:
-        grid = side(level - 1)
-        carried = unsqueeze(grad_state, squeeze_chooser(grid, images), images * grid * grid)
-    return carried, flat
-
-
-def flow_kernel(level, images, *refs):
-    stage_ref, result_ref = refs[:2]
-    carried, flat = None, None
-    if level < LEVELS - 1:
-        carried, flat = refs[2][...], refs[3][...]
-    carried, flat = flow_level(level, images, stage_ref, result_ref, carried, flat)
-    refs[-2][...] = carried
-    refs[-1][...] = flat
-
-
-def last_kernel(images, narrow, *refs):
-    count_ref, index_ref = refs[:2]
-    mine = refs[2 : 2 + narrow]
-    stage_ref, carried_ref, partial_ref, keep_ref, send_ref = refs[2 + narrow : 7 + narrow]
-    result_ref, flat_ref = refs[7 + narrow : 9 + narrow]
-    scratch = refs[9 + narrow :]
-    net_kernel(
-        0, images, narrow, index_ref, *mine, stage_ref, keep_ref, send_ref, result_ref, *scratch
-    )
-    _, flat = flow_level(0, images, stage_ref, result_ref, carried_ref[...], partial_ref[...])
-    loss = flat[FLOW_ROWS - 1 : FLOW_ROWS, 0:1]
+    return flat, turned, small[0:1, 6:7] - share_total * (logs_total + trace)
+
+
+def flow_back(images, narrow, me, count_ref, stages, results, flat_ref, keep_ref, send_ref):
+    grads = flow_chain(images, stages, results)
+    parts = [
+        flow_level(level, images, stages[level], results[level], grads[level])
+        for level in range(LEVELS)
+    ]
+    flat = sum(part[0] for part in parts) + sum(part[1] for part in parts).T[:FLOW_ROWS]
+    loss = sum(part[2] for part in parts)
     pixels = jnp.zeros((), F32)
     for index in range(images):
         pixels = pixels + (count_ref[index, 0] * count_ref[index, 1]).astype(F32)
@@ -767,75 +800,202 @@
     stats = jnp.where(lane == 0, loss, jnp.where(lane == 1, pixels, 0.0))
     flat_ref[...] = flat
     share = FLOW_ROWS // narrow
-    start = pack_rows(0)
-    me = index_ref[0, 0]
+    start = flow_start()
     for r in range(narrow):
         ref = send_ref if r & 1 else keep_ref
         ref[r // 2, start : start + share, :] = flat_ref[
             pl.ds(pl.multiple_of((me ^ r) * share, share), share), :
         ]
         ref[r // 2, start + share : start + share + STATS_ROWS, :] = stats
-        rest = ref.shape[1] - start - share - STATS_ROWS
+    zero_rows((keep_ref, send_ref), start + share + STATS_ROWS)
+
+
+def zero_rows(refs, start):
+    for ref in refs:
+        rest = ref.shape[1] - start
         if rest:
-            ref[r // 2, start + share + STATS_ROWS :, :] = jnp.zeros((rest, LANE), F32)
-
-
-def copy_kernel(from_ref, to_ref):
-    to_ref[...] = from_ref[...]
-
-
-def merge_kernel(exact_in, stage, exact_out, *refs):
-    index_ref, kept_ref, other_ref = refs[:3]
-    rows = kept_ref.shape[1]
-
-    def total(shards, place, length):
-        return kept_ref[shards, place, :] + other_ref[shards, place, :].astype(F32)
-
-    if stage == "shard":
-        keep_ref, send_ref = refs[3:5]
-        count = keep_ref.shape[0]
-        everything = pl.ds(0, rows)
-        keep_ref[...] = total(pl.ds(0, count), everything, rows)
-        sent = total(pl.ds(count, count), everything, rows)
-        send_ref[:, 0:rows, :] = sent.astype(send_ref.dtype)
-        if exact_out:
-            start = pack_rows(0)
-            for shard in range(count):
-                pieces = split_three(sent[shard, start : start + exact_out])
-                send_ref[shard, rows:, :] = jnp.concatenate(pieces, 0).astype(BF16)
-        return
-    if stage is None:
-        refs[3][...] = total(pl.ds(0, kept_ref.shape[0]), pl.ds(0, rows), rows)
-        return
-    keep_ref, send_ref = refs[3:5]
+            ref[:, start:, :] = jnp.zeros((ref.shape[0], rest, LANE), F32)
+
+
+def nets_kernel(levels, images, narrow, *refs):
+    index_ref = refs[0]
+    mine = refs[1 : 1 + narrow]
+    at = 1 + narrow
+    stages = refs[at : at + len(levels)]
+    at = at + len(levels)
+    keep_ref, send_ref = refs[at : at + 2]
+    results = refs[at + 2 : at + 2 + len(levels)]
+    at = at + 2 + len(levels)
+    for place, level in enumerate(levels):
+        net_kernel(
+            level,
+            images,
+            narrow,
+            index_ref,
+            *mine,
+            stages[place],
+            keep_ref,
+            send_ref,
+            results[place],
+            *refs[at + 5 * place : at + 5 * place + 5],
+        )
+    zero_rows((keep_ref, send_ref), sum(pack_rows(level) for level in levels))
+
+
+def last_kernel(images, narrow, *refs):
+    level = LEVELS - 1
+    count_ref, index_ref = refs[:2]
+    mine = refs[2 : 2 + narrow]
+    at = 2 + narrow
+    stages = refs[at : at + LEVELS]
+    at = at + LEVELS
+    results = refs[at : at + LEVELS - 1]
+    at = at + LEVELS - 1
+    keep_ref, send_ref, result_ref, flat_ref = refs[at : at + 4]
+    net_kernel(
+        level,
+        images,
+        narrow,
+        index_ref,
+        *mine,
+        stages[level],
+        keep_ref,
+        send_ref,
+        result_ref,
+        *refs[at + 4 :],
+    )
+    flow_back(
+        images,
+        narrow,
+        index_ref[0, 0],
+        count_ref,
+        stages,
+        list(results) + [result_ref],
+        flat_ref,
+        keep_ref,
+        send_ref,
+    )
+
+
+def copy_kernel(*refs):
+    half = len(refs) // 2
+    for from_ref, to_ref in zip(refs[:half], refs[half:]):
+        to_ref[...] = from_ref[...]
+
+
+def piece_rows(rows, exact):
+    return rows + round_up(rows // CODE_BLOCK, 16) + 3 * exact
+
+
+def write_piece(ref, values, exact_values=None):
+    rows = values.shape[0]
+    blocks = values.reshape(rows // CODE_BLOCK, CODE_BLOCK, LANE)
+    scale = rounded(jnp.max(jnp.abs(blocks), axis=1) * 1.01)
+    factor = jnp.where(scale > 0.0, CODE_RANGE / scale, 0.0)
+    code = jnp.exp(blocks * factor[:, None, :])
+    ref[0:rows, :] = code.reshape(rows, LANE).astype(BF16)
+    size = round_up(rows // CODE_BLOCK, 16)
+    if size > rows // CODE_BLOCK:
+        scale = jnp.concatenate([scale, jnp.zeros((size - rows // CODE_BLOCK, LANE), F32)], 0)
+    ref[rows : rows + size, :] = scale.astype(BF16)
+    if exact_values is not None:
+        ref[rows + size :, :] = jnp.concatenate(split_three(exact_values), 0).astype(BF16)
+
+
+def read_piece(ref, rows):
+    blocks = jnp.log(ref[0:rows, :].astype(F32)).reshape(rows // CODE_BLOCK, CODE_BLOCK, LANE)
+    scale = ref[rows : rows + round_up(rows // CODE_BLOCK, 16), :].astype(F32)
+    factor = scale[: rows // CODE_BLOCK] * (1.0 / CODE_RANGE)
+    return (blocks * factor[:, None, :]).reshape(rows, LANE)
+
+
+def read_exact(ref, rows, exact):
+    start = rows + round_up(rows // CODE_BLOCK, 16)
+    pieces = ref[start : start + 3 * exact, :].astype(F32)
+    return pieces[:exact] + pieces[exact : 2 * exact] + pieces[2 * exact :]
+
+
+def wide_bit(index_ref, bit):
+    return jnp.where((index_ref[1, 0] & bit) != 0, 1, 0)
+
+
+def exact_place(rows):
+    return flow_start() // rows, flow_start() % rows
+
+
+def square_kernel(exact, index_ref, keep_ref, other_ref, mine_ref, *sent_refs):
+    half = keep_ref.shape[1] // 2
+    upper = wide_bit(index_ref, 1)
+
+    def total(shard, flipped):
+        place = 1 - upper if flipped else upper
+        picked = pl.ds(pl.multiple_of(place * half, 16), half)
+        return keep_ref[shard, picked, :] + other_ref[shard, picked, :]
+
+    mine_ref[...] = total(0, 0)
+    for ref, (shard, flipped) in zip(sent_refs, ((1, 0), (0, 1), (1, 1))):
+        exact_values = None
+        if exact:
+            picked = slice(flow_start(), flow_start() + exact)
+            exact_values = keep_ref[shard, picked, :] + other_ref[shard, picked, :]
+        write_piece(ref, total(shard, flipped), exact_values)
+
+
+def column_kernel(exact, index_ref, mine_ref, *refs):
+    others, (keep_ref, sent_ref, total_ref) = refs[:3], refs[3:]
+    rows = mine_ref.shape[0]
     half = rows // 2
-    shards = pl.ds(0, kept_ref.shape[0])
-    upper = jnp.where((index_ref[1, 0] & stage) != 0, 1, 0)
-    for ref, place in ((keep_ref, upper), (send_ref, 1 - upper)):
-        ref[...] = total(shards, pl.ds(pl.multiple_of(place * half, 16), half), half).astype(
-            ref.dtype
-        )
-    if exact_in:
-        start = pack_rows(0)
-        for shard in range(kept_ref.shape[0]):
-            pieces = other_ref[shard, rows:, :].astype(F32)
-            whole = pieces[:exact_in] + pieces[exact_in : 2 * exact_in] + pieces[2 * exact_in :]
-            whole = kept_ref[shard, start : start + exact_in, :] + whole
-
-            @pl.when(upper == 1)
+    total = mine_ref[...]
+    for other in others:
+        total = total + read_piece(other, rows)
+    total_ref[...] = total
+    exact_values = None
+    if exact:
+        part, start = exact_place(rows)
+        exact_values = mine_ref[start : start + exact, :]
+        for other in others:
+            exact_values = exact_values + read_exact(other, rows, exact)
+
+        @pl.when(wide_bit(index_ref, 1) == part)
+        def _():
+            total_ref[start : start + exact, :] = exact_values
+
+    place = wide_bit(index_ref, 2)
+    keep_ref[...] = total_ref[pl.ds(pl.multiple_of(place * half, 16), half), :]
+    values = total_ref[pl.ds(pl.multiple_of((1 - place) * half, 16), half), :]
+    write_piece(sent_ref, values, exact_values)
+
+
+def code_kernel(exact, index_ref, mine_ref, other_ref, out_ref):
+    rows = mine_ref.shape[0]
+    exact_values = None
+    if exact:
+        _, start = exact_place(rows)
+        exact_values = mine_ref[start : start + exact, :] + read_exact(other_ref, rows, exact)
+    write_piece(out_ref, mine_ref[...] + read_piece(other_ref, rows), exact_values)
+
+
+def recode_kernel(exact, rows, index_ref, mine_ref, other_ref, out_ref):
+    exact_values = None
+    if exact:
+        exact_values = read_exact(mine_ref, rows, exact) + read_exact(other_ref, rows, exact)
+    write_piece(out_ref, read_piece(mine_ref, rows) + read_piece(other_ref, rows), exact_values)
+
+
+def decode_kernel(exact, index_ref, *refs):
+    parts, out_ref = refs[:4], refs[4]
+    rows = out_ref.shape[0] // 4
+    place = 2 * wide_bit(index_ref, 1) + wide_bit(index_ref, 2)
+    for flip, ref in enumerate(parts):
+        start = pl.multiple_of((place ^ flip) * rows, 16)
+        out_ref[pl.ds(start, rows), :] = read_piece(ref, rows)
+    if exact:
+        part, start = exact_place(rows)
+        for flip, ref in enumerate(parts):
+
+            @pl.when((place ^ flip) == part)
             def _():
-                keep_ref[shard, start - half : start - half + exact_in, :] = whole
-
-            @pl.when(upper == 0)
-            def _():
-                send_ref[shard, start - half : start - half + exact_in, :] = whole
-
-
-def join_kernel(bit, index_ref, mine_ref, other_ref, out_ref):
-    half = mine_ref.shape[1]
-    upper = jnp.where((index_ref[1, 0] & bit) != 0, 1, 0)
-    out_ref[:, pl.ds(pl.multiple_of(upper * half, 8), half), :] = mine_ref[...]
-    out_ref[:, pl.ds(pl.multiple_of((1 - upper) * half, 8), half), :] = other_ref[...]
+                out_ref[flow_start() : flow_start() + exact, :] = read_exact(ref, rows, exact)
 
 
 def moments(weight, gradient, first_old, second_old):
@@ -894,13 +1054,17 @@
 
 
 def moment_kernel(share, *refs):
-    grads = [ref.at[0] for ref in refs[:3]]
-    weight_in, weight_mix, weight_out, weight_bias = refs[3:7]
-    first_in, first_mix, first_out, first_bias = refs[7:11]
-    second_in, second_mix, second_out, second_bias = refs[11:15]
-    outs = refs[15:]
-    stats_row = pack_rows(0) + share
-    total = grads[0][stats_row : stats_row + 1, :]
+    chunks = refs[:2]
+    grads = []
+    for level in range(LEVELS):
+        chunk, start = chunk_start(level)
+        grads.append(chunks[chunk].at[start : start + pack_rows(level)])
+    weight_in, weight_mix, weight_out, weight_bias = refs[2:6]
+    first_in, first_mix, first_out, first_bias = refs[6:10]
+    second_in, second_mix, second_out, second_bias = refs[10:14]
+    outs = refs[14:]
+    flow_ref = chunks[-1].at[flow_start() : flow_start() + share + STATS_ROWS]
+    total = flow_ref[share : share + 1, :]
     valid_dims = 3.0 * total[:, 1:2]
     scale = 1.0 / (valid_dims * LOG_TWO)
     grad_in = jnp.concatenate([grads[level][0 : in_rows(level), :] for level in range(LEVELS)], 0)
@@ -952,8 +1116,7 @@
     )
     lane = iota((16, LANE), 1)
     outs[12][0:16, :] = jnp.where(lane == 0, squares_rows(weight_sums), squares_rows(update_sums))
-    outs[12][16 : 16 + share, :] = grads[0][pack_rows(0) : pack_rows(0) + share, :]
-    outs[12][16 + share :, :] = grads[0][stats_row : stats_row + STATS_ROWS, :]
+    outs[12][16:, :] = flow_ref[...]
 
 
 def apply_kernel(narrow, *refs):
@@ -1073,8 +1236,7 @@
 
 
 def run_pack(conv_in, mixer, conv_out, hidden_bias):
-    outs = [((pack_rows(level), LANE), BF16) for level in range(LEVELS)]
-    outs.append(((sum(pack_rows(level) for level in range(LEVELS)), LANE), BF16))
+    outs = [((sum(pack_rows(level) for level in range(LEVELS)), LANE), BF16)]
     return call(pack_kernel, outs, (), (conv_in, mixer, conv_out, hidden_bias), name="pack", vmem=56)
 
 
@@ -1091,34 +1253,22 @@
     )
 
 
-def run_net(level, images, index, weights, stage, after):
+def run_nets(levels, images, index, weights, stages, after):
     narrow = len(weights)
-    count = positions(level, images)
-    outs = [
-        ((narrow // 2, grad_rows(level, narrow), LANE), F32),
-        ((narrow // 2, grad_rows(level, narrow), LANE), F32),
-        ((stage_rows(level)["result_rows"], count), F32),
-    ]
+    rows = chunk_rows(chunk_start(levels[0])[0], narrow)
+    outs = [((narrow // 2, rows, LANE), F32)] * 2
+    scratch = []
+    for level in levels:
+        count = positions(level, images)
+        outs = outs + [((stage_rows(level)["result_rows"], count), F32)]
+        scratch = scratch + net_scratch(count)
     return call(
-        functools.partial(net_kernel, level, images, narrow),
+        functools.partial(nets_kernel, levels, images, narrow),
         outs,
         (),
-        [index] + list(weights) + [stage],
-        net_scratch(count),
-        name="net_%d" % (level + 1),
-        after=after,
-    )
-
-
-def run_flow(level, images, stage, result, carried, after):
-    grid = side(level - 1)
-    outs = [((chan(level - 1) // 2, images * grid * grid), F32), ((FLOW_ROWS, LANE), F32)]
-    return call(
-        functools.partial(flow_kernel, level, images),
-        outs,
-        (),
-        [stage, result] + list(carried),
-        name="flow_%d" % (level + 1),
+        [index] + list(weights) + [stages[level] for level in levels],
+        scratch,
+        name="nets_" + "_".join(str(level + 1) for level in levels),
         after=after,
     )
 
@@ -1133,102 +1283,112 @@
     ]
 
 
-def run_last(images, index, valid_shape, weights, stage, carried, after):
+def run_last(images, index, valid_shape, weights, stages, results, after):
     narrow = len(weights)
-    count = positions(0, images)
-    outs = [((narrow // 2, grad_rows(0, narrow), LANE), F32)] * 2
-    scratch = [
-        pltpu.VMEM((stage_rows(0)["result_rows"], count), F32),
-        pltpu.VMEM((FLOW_ROWS, LANE), F32),
-    ]
+    level = LEVELS - 1
+    count = positions(level, images)
     return call(
         functools.partial(last_kernel, images, narrow),
-        outs,
+        [((narrow // 2, chunk_rows(len(CHUNKS) - 1, narrow), LANE), F32)] * 2,
         (valid_shape,),
-        [index] + list(weights) + [stage] + list(carried),
-        scratch + net_scratch(count),
-        name="net_1_and_flow",
+        [index] + list(weights) + list(stages) + list(results),
+        [
+            pltpu.VMEM((stage_rows(level)["result_rows"], count), F32),
+            pltpu.VMEM((FLOW_ROWS, LANE), F32),
+        ]
+        + net_scratch(count),
+        name="net_3_and_flow",
         after=after,
     )
 
 
-def swap(values, axis, step):
-    size = lax.axis_size(axis)
-    return lax.ppermute(values, axis, [(index, index ^ step) for index in range(size)])
-
-
-def wide_steps():
-    steps = []
-    step = 1
-    while step < lax.axis_size("wide"):
-        steps.append(step)
-        step = 2 * step
-    return steps
+def swap(values, wide, narrow):
+    width = lax.axis_size("narrow")
+    mask = wide * width + narrow
+    count = lax.axis_size("wide") * width
+    return lax.ppermute(values, ("wide", "narrow"), [(place, place ^ mask) for place in range(count)])
 
 
 class Summation:
-    def __init__(self, level, index, stages, exact):
-        self.level, self.index, self.exact = level, index, exact
-        self.stages = stages
-        self.at = -1
-        self.joins = [stage for stage in stages if stage != "shard"][::-1]
+    def __init__(self, chunk, index, exact):
+        self.name, self.index, self.exact = "abc"[chunk], index, exact
 
     def start(self, keep, send):
-        self.kept = keep
-        self.other = swap(send, "narrow", 1)
-
-    def merge(self, after):
-        exact_in = self.exact if self.at == 0 else 0
-        self.at = self.at + 1
-        shards, rows, _ = self.kept.shape
-        if self.at == len(self.stages):
-            (total,) = call(
-                functools.partial(merge_kernel, 0, None, 0),
-                [((shards, rows, LANE), F32)],
-                (),
-                (self.index, self.kept, self.other),
-                name="total_%d" % (self.level + 1),
-                after=after,
-            )
-            for step in wide_steps():
-                if step not in self.stages:
-                    total = total + swap(total, "wide", step)
-            self.kept = total
-            self.other = swap(total, "wide", self.joins[0])
-            return total
-        stage = self.stages[self.at]
-        exact_out = self.exact if self.at == 0 else 0
-        if stage == "shard":
-            keep, send = (shards // 2, rows, LANE), (shards // 2, rows + 3 * exact_out, LANE)
-        else:
-            keep = send = (shards, rows // 2, LANE)
-        self.kept, sent = call(
-            functools.partial(merge_kernel, exact_in, stage, exact_out),
-            [(keep, F32), (send, BF16 if self.at == 0 else F32)],
+        self.kept, self.others = keep, [swap(send, 0, 1)]
+
+    def run(self, kernel, outs, arrays, after, name, scratch=()):
+        return call(
+            kernel,
+            outs,
             (),
-            (self.index, self.kept, self.other),
-            name="merge_%d_%d" % (self.level + 1, self.at),
+            (self.index, *arrays),
+            scratch,
+            name=name + "_" + self.name,
             after=after,
         )
-        if stage == "shard":
-            self.other = swap(sent, "narrow", 2)
-        else:
-            self.other = swap(sent, "wide", stage)
+
+    def square(self, after):
+        rows = self.kept.shape[1] // 2
+        self.kept, *sent = self.run(
+            functools.partial(square_kernel, self.exact),
+            [((rows, LANE), F32)] + [((piece_rows(rows, self.exact), LANE), BF16)] * 3,
+            (self.kept, *self.others),
+            after,
+            "square",
+        )
+        self.others = [swap(sent[0], 0, 2), swap(sent[1], 1, 0), swap(sent[2], 1, 2)]
         return self.kept
 
-    def join(self, after):
-        step = self.joins.pop(0)
-        shards, rows, _ = self.kept.shape
-        (self.kept,) = call(
-            functools.partial(join_kernel, step),
-            [((shards, 2 * rows, LANE), F32)],
-            (),
-            (self.index, self.kept, self.other),
-            name="join_%d" % (self.level + 1),
-            after=after,
+    def column(self, after):
+        rows = self.kept.shape[0]
+        self.rows = rows // 2
+        self.piece = ((piece_rows(self.rows, self.exact), LANE), BF16)
+        self.kept, sent = self.run(
+            functools.partial(column_kernel, self.exact),
+            [((self.rows, LANE), F32), self.piece],
+            (self.kept, *self.others),
+            after,
+            "column",
+            [pltpu.VMEM((rows, LANE), F32)],
         )
-        if self.joins:
-            self.other = swap(self.kept, "wide", self.joins[0])
+        self.others = [swap(sent, 2, 0)]
+        return self.kept
+
+    def code(self, after):
+        (self.kept,) = self.run(
+            functools.partial(code_kernel, self.exact),
+            [self.piece],
+            (self.kept, *self.others),
+            after,
+            "code",
+        )
+        self.others = [swap(self.kept, 4, 0)]
+        return self.kept
+
+    def spread(self, after):
+        step = 4
+        while step < lax.axis_size("wide"):
+            (self.kept,) = self.run(
+                functools.partial(recode_kernel, self.exact, self.rows),
+                [self.piece],
+                (self.kept, *self.others),
+                after,
+                "recode_%d" % step,
+            )
+            step = 2 * step
+            if step < lax.axis_size("wide"):
+                self.others = [swap(self.kept, step, 0)]
+        self.others = [swap(self.kept, 2, 0), swap(self.kept, 1, 0), swap(self.kept, 3, 0)]
+        return self.kept
+
+    def decode(self, rows, after):
+        (self.kept,) = self.run(
+            functools.partial(decode_kernel, self.exact),
+            [((rows, LANE), F32)],
+            (self.kept, *self.others),
+            after,
+            "decode",
+        )
         return self.kept
 
 
@@ -1257,49 +1417,33 @@
     row = lax.broadcasted_iota(jnp.int32, (8, LANE), 0)
     index = jnp.where(row == 0, lax.axis_index("narrow"), lax.axis_index("wide")).astype(jnp.int32)
     narrow = lax.axis_size("narrow")
-    packed = run_pack(conv_in, mixer, conv_out, hidden_bias)
-    paired = swap(packed[LEVELS], "narrow", 1)
-    crossed = [None] * LEVELS
-    for level in (2, 1, 0):
-        crossed[level] = swap(packed[level], "narrow", 2)
-    stage = run_flow_pre(noise_seeds, valid_shape, images, flow_params, (packed[0],))
-
-    def gather(level, after):
-        (copied,) = call(
-            copy_kernel,
-            [(crossed[level].shape, BF16)],
-            (),
-            (crossed[level],),
-            name="copy_%d" % (level + 1),
-            after=after,
-        )
-        return (packed[level], paired, crossed[level], swap(copied, "narrow", 1)), copied
-
-    bits = [step for step in wide_steps() if step < 8]
-    third = Summation(2, index, bits[:1] + ["shard"] + bits[1:], 0)
-    second = Summation(1, index, ["shard"] + bits, 0)
-    first = Summation(0, index, ["shard"] + bits, flow_block_rows(narrow))
-    gathered, token = gather(2, (stage[0],))
-    keep, send, result = run_net(2, count, index, gathered, stage[2], (token,))
-    third.start(keep, send)
-    gathered, token = gather(1, (keep,))
-    carried = run_flow(2, count, stage[2], result, (), (token,))
-    keep, send, result = run_net(1, count, index, gathered, stage[1], (carried[1],))
-    second.start(keep, send)
-    gathered, token = gather(0, (keep,))
-    token = third.merge((token,))
-    carried = run_flow(1, count, stage[1], result, carried, (token,))
-    token = second.merge((carried[1],))
-    keep, send = run_last(count, index, valid_shape, gathered, stage[0], carried, (token,))
-    first.start(keep, send)
-    token = first.merge((keep,))
-    for _ in range(len(bits) + 1):
-        for summation in (second, third, first):
-            token = summation.merge((token,))
-    for _ in range(len(bits)):
-        for summation in (second, third, first):
-            token = summation.join((token,))
-    grads = (first.kept, second.kept, third.kept)
+    (packed,) = run_pack(conv_in, mixer, conv_out, hidden_bias)
+    paired = swap(packed, 0, 1)
+    crossed = swap(packed, 0, 2)
+    stages = run_flow_pre(noise_seeds, valid_shape, images, flow_params, ())
+    arrays = (crossed, *stages)
+    copied, *stages = call(
+        copy_kernel, [(array.shape, array.dtype) for array in arrays], (), arrays, name="copy"
+    )
+    gathered = (packed, paired, crossed, swap(copied, 0, 1))
+    one = Summation(0, index, 0)
+    two = Summation(1, index, flow_block_rows(narrow))
+    keep, send, *results = run_nets(CHUNKS[0], count, index, gathered, stages, (copied,))
+    one.start(keep, send)
+    keep, send = run_last(count, index, valid_shape, gathered, stages, results, (keep,))
+    two.start(keep, send)
+    sizes = one.kept.shape[1], two.kept.shape[1]
+    token = one.square((keep,))
+    token = two.square((token,))
+    token = one.column((token,))
+    token = two.column((token,))
+    token = one.code((token,))
+    token = two.code((token,))
+    token = one.spread((token,))
+    token = two.spread((token,))
+    token = one.decode(sizes[0], (token,))
+    token = two.decode(sizes[1], (token,))
+    grads = (one.kept, two.kept)
     weights = (conv_in, mixer, conv_out, hidden_bias)
     shapes = [(weight.shape, F32) for weight in weights]
     share = FLOW_ROWS // narrow
@@ -1313,7 +1457,7 @@
         + (conv_in_second, mixer_second, conv_out_second, bias_second),
         name="moments",
     )
-    blocks = [moved[12]] + [swap(moved[12], "narrow", part) for part in range(1, narrow)]
+    blocks = [moved[12]] + [swap(moved[12], 0, part) for part in range(1, narrow)]
     flow_shape = (flow_params.shape, F32)
     fresh = call(
         functools.partial(apply_kernel, narrow),

time: 122 us -> 93.5 us (0.77)
  waiting for transfers between devices: 54.6 us -> 35 us
  starting transfers between devices: 37.4 us -> 30 us
  local copies, waits for them, and re-layouts: 2.06 us -> 0.17 us
    ppermute x34 -> x24, waiting for transfers between devices: 54.6 us -> 35 us  [swap(): lax.ppermute(values, ('wide', 'narrow'), [(place, place ^ mask) for place...]
    ppermute x34 -> x24, starting transfers between devices: 37.4 us -> 30 us  [swap(): lax.ppermute(values, ('wide', 'narrow'), [(place, place ^ mask) for place...]
    unnamed x44 -> x38, local copies, waits for them, and re-layouts: 1.99 us -> 0.1 us
    pallas_call x36 -> x17, Pallas kernels: 26.1 us -> 27 us  [call(): pl.pallas_call(run, out_shape=tuple((jax.ShapeDtypeStruct(shape, dtype) f...]
  transfers between devices with their start and end apart: 34 -> 24, of which waited for: 16 -> 12; matrix products, arithmetic and copies ran while one was open for 0% -> 0% of each run, Pallas kernels for 11% -> 16%
where the time goes in v3:
time: 93.5 us; the launch traced here: 93.3 us
  waiting for transfers between devices  35 us (37%)
  starting transfers between devices  30 us (32%)
  Pallas kernels  27 us (29%)
  between operations  1.12 us (1%)
    ppermute x24, waiting for transfers between devices, swap(): lax.ppermute(values, ('wide', 'narrow'), [(place, place ^ mask) for place...  35 us
    ppermute x24, starting transfers between devices, swap(): lax.ppermute(values, ('wide', 'narrow'), [(place, place ^ mask) for place...  30 us
    pallas_call x17, Pallas kernels, call(): pl.pallas_call(run, out_shape=tuple((jax.ShapeDtypeStruct(shape, dtype) f...  27 us
  transfers between devices with their start and end apart: 24, of which 12 were waited for; matrix products, arithmetic and copies ran while one was open for 0% of the time, Pallas kernels for 16%

profile of v3, /device:TPU:0, one launch (start us, length us, event | category | flops | bytes accessed | tf_op | source)
XLA Modules:
  0.0 93.3 jit_solution(17642808958203372982)
XLA Ops:
  0.7 2.2 %pack.1.refs_1_.refs_2_ = bf16[2704,128]{1,0:T(8,128)(2,1)} custom-call(f32[378,128]{1,0:T(8,128)} %refs_5_.3, f32[3,512,128]{2,1,0:T(8,128)} %refs_6_.3, f32[756,128]{1,0:T(8,128)} %bitcast.9, f32[3,2,128]{2,1,0:T(2,128)} %refs_8_.1), custom_call_target="tpu_custom_call" | custom-call | flops 1000 | bytes 1000 | tf_op jit(solution)/shard_map/pack/pallas_call | solution.py:1222
  2.9 2.9 %collective-permute-start.1 = (bf16[2704,128]{1,0:T(8,128)(2,1)}, bf16[2704,128]{1,0:T(8,128)(2,1)S(1)}, u32[]{:S(2)}, u32[]{:S(2)}) collective-permute-start(bf16[2704,128]{1,0:T(8,128)(2,1)} %pack.1.refs_1_.refs_2_), channel_id=1, source_target_pairs={{0,2},{1,3},{2,0},{3,1},{4,6},{5,7},{6,4},{7,5},{8,10},{9,11},{10,... | collective-permute-start | bytes 2076680 | tf_op jit(solution)/shard_map/ppermute | solution.py:1309
  5.9 4.6 %flow_pre.1 = (f32[112,512]{1,0:T(8,128)S(1)}, f32[168,128]{1,0:T(8,128)S(1)}, f32[320,128]{1,0:T(8,128)S(1)}) custom-call(s32[2]{0:T(128)S(1)} %copy-done.18, s32[2,2]{1,0:T(2,128)S(1)} %copy-done.15, f32[3,2,1024]{2,1,0:T(2,128)S(1)} %copy-done.12, f32[3852]{0:T(1024)S(1)} %copy-done.10), custom_call_target="tpu_custom_call" | custom-call | flops 1000 | bytes 1000 | tf_op jit(solution)/shard_map/flow_pre/pallas_call | solution.py:1222
  10.5 11.1 %collective-permute-done.1.refs_0_.refs_3_.refs_4_ = bf16[2704,128]{1,0:T(8,128)(2,1)S(1)} collective-permute-done((bf16[2704,128]{1,0:T(8,128)(2,1)}, bf16[2704,128]{1,0:T(8,128)(2,1)S(1)}, u32[]{:S(2)}, u32[]{:S(2)}) %collective-permute-start.1) | collective-permute-done | bytes 692256 | tf_op jit(solution)/shard_map/ppermute | solution.py:1309
  21.7 0.9 copy.41
  22.6 2.3 %collective-permute-done.2.refs_4_.refs_5_ = bf16[2704,128]{1,0:T(8,128)(2,1)S(1)} collective-permute-done((bf16[2704,128]{1,0:T(8,128)(2,1)}, bf16[2704,128]{1,0:T(8,128)(2,1)S(1)}, u32[]{:S(2)}, u32[]{:S(2)}) %collective-permute-start.2) | collective-permute-done | bytes 692256 | tf_op jit(solution)/shard_map/ppermute | solution.py:1309
  25.0 4.7 %nets_1_2.1 = (f32[2,1536,128]{2,1,0:T(8,128)S(1)}, f32[2,1536,128]{2,1,0:T(8,128)S(1)}, f32[40,512]{1,0:T(8,128)S(1)}, f32[64,128]{1,0:T(8,128)S(1)}) custom-call(s32[8,128]{1,0:T(8,128)S(1)} %iota.7.refs_0_.refs_1_, bf16[2704,128]{1,0:T(8,128)(2,1)S(1)} %copy-done.1, bf16[2704,128]{1,0:T(8,128)(2,1)S(1)} %collective-permute-done.refs_2_.refs_3_, ...), custom_call_target="tpu_custom_call" | custom-call | flops 1000 | bytes 1000 | tf_op jit(solution)/shard_map/nets_1_2/pallas_call | solution.py:1222
  29.7 0.2 collective-permute-start.3
  29.9 6.3 %net_3_and_flow.1 = (f32[2,1280,128]{2,1,0:T(8,128)S(1)}, f32[2,1280,128]{2,1,0:T(8,128)S(1)}) custom-call(s32[2,2]{1,0:T(2,128)S(1)} %copy-done.15, s32[8,128]{1,0:T(8,128)S(1)} %iota.7.refs_0_.refs_1_, bf16[2704,128]{1,0:T(8,128)(2,1)S(1)} %copy-done.1, bf16[2704,128]{1,0:T(8,128)(2,1)S(1)} %collective-permute-done.refs_2_.refs_3_, ...), custom_call_target="tpu_custom_call" | custom-call | flops 1000 | bytes 1000 | tf_op jit(solution)/shard_map/net_3_and_flow/pallas_call | solution.py:1222
  36.2 0.4 collective-permute-start.7
  36.7 0.6 square_a.1
  37.3 1.7 %collective-permute-start.4 = (bf16[816,128]{1,0:T(8,128)(2,1)S(1)}, bf16[816,128]{1,0:T(8,128)(2,1)S(1)}, u32[]{:S(2)}, u32[]{:S(2)}) collective-permute-start(bf16[816,128]{1,0:T(8,128)(2,1)S(1)} %get-tuple-element.87), channel_id=1, source_target_pairs={{0,2},{1,3},{2,0},{3,1},{4,6},{5,7},{6,4},{7,5},{8,10},{9,11},{10,... | collective-permute-start | bytes 626696 | tf_op jit(solution)/shard_map/ppermute | solution.py:1309
  39.0 1.5 %collective-permute-start.5 = (bf16[816,128]{1,0:T(8,128)(2,1)S(1)}, bf16[816,128]{1,0:T(8,128)(2,1)S(1)}, u32[]{:S(2)}, u32[]{:S(2)}) collective-permute-start(bf16[816,128]{1,0:T(8,128)(2,1)S(1)} %get-tuple-element.88), channel_id=1, source_target_pairs={{0,4},{1,5},{2,6},{3,7},{4,0},{5,1},{6,2},{7,3},{8,12},{9,13},{10,... | collective-permute-start | bytes 626696 | tf_op jit(solution)/shard_map/ppermute | solution.py:1309
  40.5 0.3 collective-permute-start.6
  40.8 0.5 square_b.1
  41.3 1.7 %collective-permute-start.9 = (bf16[736,128]{1,0:T(8,128)(2,1)S(1)}, bf16[736,128]{1,0:T(8,128)(2,1)S(1)}, u32[]{:S(2)}, u32[]{:S(2)}) collective-permute-start(bf16[736,128]{1,0:T(8,128)(2,1)S(1)} %get-tuple-element.94), channel_id=1, source_target_pairs={{0,2},{1,3},{2,0},{3,1},{4,6},{5,7},{6,4},{7,5},{8,10},{9,11},{10,... | collective-permute-start | bytes 565256 | tf_op jit(solution)/shard_map/ppermute | solution.py:1309
  43.1 1.5 %collective-permute-start.10 = (bf16[736,128]{1,0:T(8,128)(2,1)S(1)}, bf16[736,128]{1,0:T(8,128)(2,1)S(1)}, u32[]{:S(2)}, u32[]{:S(2)}) collective-permute-start(bf16[736,128]{1,0:T(8,128)(2,1)S(1)} %get-tuple-element.95), channel_id=1, source_target_pairs={{0,4},{1,5},{2,6},{3,7},{4,0},{5,1},{6,2},{7,3},{8,12},{9,13},{10,... | collective-permute-start | bytes 565256 | tf_op jit(solution)/shard_map/ppermute | solution.py:1309
  44.6 0.8 collective-permute-done.4.refs_2_
  45.4 2.6 %collective-permute-start.11 = (bf16[736,128]{1,0:T(8,128)(2,1)S(1)}, bf16[736,128]{1,0:T(8,128)(2,1)S(1)}, u32[]{:S(2)}, u32[]{:S(2)}) collective-permute-start(bf16[736,128]{1,0:T(8,128)(2,1)S(1)} %get-tuple-element.96), channel_id=1, source_target_pairs={{0,6},{1,7},{2,4},{3,5},{4,2},{5,3},{6,0},{7,1},{8,14},{9,15},{10,... | collective-permute-start | bytes 565256 | tf_op jit(solution)/shard_map/ppermute | solution.py:1309
  48.0 3.6 %collective-permute-done.5.refs_3_ = bf16[816,128]{1,0:T(8,128)(2,1)S(1)} collective-permute-done((bf16[816,128]{1,0:T(8,128)(2,1)S(1)}, bf16[816,128]{1,0:T(8,128)(2,1)S(1)}, u32[]{:S(2)}, u32[]{:S(2)}) %collective-permute-start.5) | collective-permute-done | bytes 208928 | tf_op jit(solution)/shard_map/ppermute | solution.py:1309
  51.5 0.5 column_a.1
  52.0 1.6 %collective-permute-start.8 = (bf16[416,128]{1,0:T(8,128)(2,1)S(1)}, bf16[416,128]{1,0:T(8,128)(2,1)S(1)}, u32[]{:S(2)}, u32[]{:S(2)}) collective-permute-start(bf16[416,128]{1,0:T(8,128)(2,1)S(1)} %get-tuple-element.93), channel_id=1, source_target_pairs={{0,8},{1,9},{2,10},{3,11},{4,12},{5,13},{6,14},{7,15},{8,0},{9,1},... | collective-permute-start | bytes 319496 | tf_op jit(solution)/shard_map/ppermute | solution.py:1309
  53.6 0.3 collective-permute-done.9.refs_2_
  53.9 4.6 %collective-permute-done.10.refs_3_ = bf16[736,128]{1,0:T(8,128)(2,1)S(1)} collective-permute-done((bf16[736,128]{1,0:T(8,128)(2,1)S(1)}, bf16[736,128]{1,0:T(8,128)(2,1)S(1)}, u32[]{:S(2)}, u32[]{:S(2)}) %collective-permute-start.10) | collective-permute-done | bytes 188448 | tf_op jit(solution)/shard_map/ppermute | solution.py:1309
  58.5 0.6 column_b.1
  59.3 2.7 %collective-permute-start.12 = (bf16[416,128]{1,0:T(8,128)(2,1)S(1)}, bf16[416,128]{1,0:T(8,128)(2,1)S(1)}, u32[]{:S(2)}, u32[]{:S(2)}) collective-permute-start(bf16[416,128]{1,0:T(8,128)(2,1)S(1)} %code_a.1.refs_3_.refs_1_), channel_id=1, source_target_pairs={{0,16},{1,17},{2,18},{3,19},{4,20},{5,21},{6,22},{7,23},{8,24},{9,... | collective-permute-start | bytes 319496 | tf_op jit(solution)/shard_map/ppermute | solution.py:1309
  61.9 1.6 %collective-permute-start.13 = (bf16[400,128]{1,0:T(8,128)(2,1)S(1)}, bf16[400,128]{1,0:T(8,128)(2,1)S(1)}, u32[]{:S(2)}, u32[]{:S(2)}) collective-permute-start(bf16[400,128]{1,0:T(8,128)(2,1)S(1)} %get-tuple-element.98), channel_id=1, source_target_pairs={{0,8},{1,9},{2,10},{3,11},{4,12},{5,13},{6,14},{7,15},{8,0},{9,1},... | collective-permute-start | bytes 307208 | tf_op jit(solution)/shard_map/ppermute | solution.py:1309
  63.5 3.3 %collective-permute-done.13.refs_2_ = bf16[400,128]{1,0:T(8,128)(2,1)S(1)} collective-permute-done((bf16[400,128]{1,0:T(8,128)(2,1)S(1)}, bf16[400,128]{1,0:T(8,128)(2,1)S(1)}, u32[]{:S(2)}, u32[]{:S(2)}) %collective-permute-start.13) | collective-permute-done | bytes 102432 | tf_op jit(solution)/shard_map/ppermute | solution.py:1309
  66.9 0.2 recode_4_a.1.refs_3_.refs_1_
  67.1 1.5 %collective-permute-start.14 = (bf16[416,128]{1,0:T(8,128)(2,1)S(1)}, bf16[416,128]{1,0:T(8,128)(2,1)S(1)}, u32[]{:S(2)}, u32[]{:S(2)}) collective-permute-start(bf16[416,128]{1,0:T(8,128)(2,1)S(1)} %recode_4_a.1.refs_3_.refs_1_), channel_id=1, source_target_pairs={{0,8},{1,9},{2,10},{3,11},{4,12},{5,13},{6,14},{7,15},{8,0},{9,1},... | collective-permute-start | bytes 319496 | tf_op jit(solution)/shard_map/ppermute | solution.py:1309
  68.6 2.1 %collective-permute-start.17 = (bf16[400,128]{1,0:T(8,128)(2,1)S(1)}, bf16[400,128]{1,0:T(8,128)(2,1)S(1)}, u32[]{:S(2)}, u32[]{:S(2)}) collective-permute-start(bf16[400,128]{1,0:T(8,128)(2,1)S(1)} %code_b.1.refs_3_.refs_1_), channel_id=1, source_target_pairs={{0,16},{1,17},{2,18},{3,19},{4,20},{5,21},{6,22},{7,23},{8,24},{9,... | collective-permute-start | bytes 307208 | tf_op jit(solution)/shard_map/ppermute | solution.py:1309
  70.8 1.2 %collective-permute-start.15 = (bf16[416,128]{1,0:T(8,128)(2,1)S(1)}, bf16[416,128]{1,0:T(8,128)(2,1)S(1)}, u32[]{:S(2)}, u32[]{:S(2)}) collective-permute-start(bf16[416,128]{1,0:T(8,128)(2,1)S(1)} %recode_4_a.1.refs_3_.refs_1_), channel_id=1, source_target_pairs={{0,4},{1,5},{2,6},{3,7},{4,0},{5,1},{6,2},{7,3},{8,12},{9,13},{10,... | collective-permute-start | bytes 319496 | tf_op jit(solution)/shard_map/ppermute | solution.py:1309
  72.0 0.3 collective-permute-start.16
  72.3 2.1 %collective-permute-done.17.refs_2_ = bf16[400,128]{1,0:T(8,128)(2,1)S(1)} collective-permute-done((bf16[400,128]{1,0:T(8,128)(2,1)S(1)}, bf16[400,128]{1,0:T(8,128)(2,1)S(1)}, u32[]{:S(2)}, u32[]{:S(2)}) %collective-permute-start.17) | collective-permute-done | bytes 102432 | tf_op jit(solution)/shard_map/ppermute | solution.py:1309
  74.4 0.1 recode_4_b.1.refs_5_.refs_1_
  74.7 2.1 %collective-permute-start.18 = (bf16[400,128]{1,0:T(8,128)(2,1)S(1)}, bf16[400,128]{1,0:T(8,128)(2,1)S(1)}, u32[]{:S(2)}, u32[]{:S(2)}) collective-permute-start(bf16[400,128]{1,0:T(8,128)(2,1)S(1)} %recode_4_b.1.refs_5_.refs_1_), channel_id=1, source_target_pairs={{0,8},{1,9},{2,10},{3,11},{4,12},{5,13},{6,14},{7,15},{8,0},{9,1},... | collective-permute-start | bytes 307208 | tf_op jit(solution)/shard_map/ppermute | solution.py:1309
  76.8 1.6 %collective-permute-start.19 = (bf16[400,128]{1,0:T(8,128)(2,1)S(1)}, bf16[400,128]{1,0:T(8,128)(2,1)S(1)}, u32[]{:S(2)}, u32[]{:S(2)}) collective-permute-start(bf16[400,128]{1,0:T(8,128)(2,1)S(1)} %recode_4_b.1.refs_5_.refs_1_), channel_id=1, source_target_pairs={{0,4},{1,5},{2,6},{3,7},{4,0},{5,1},{6,2},{7,3},{8,12},{9,13},{10,... | collective-permute-start | bytes 307208 | tf_op jit(solution)/shard_map/ppermute | solution.py:1309
  78.4 0.4 collective-permute-start.20
  78.8 0.2 decode_a.1.refs_5_.refs_0_
  79.0 0.9 collective-permute-done.18.refs_2_
  79.9 1.6 %collective-permute-done.19.refs_3_ = bf16[400,128]{1,0:T(8,128)(2,1)S(1)} collective-permute-done((bf16[400,128]{1,0:T(8,128)(2,1)S(1)}, bf16[400,128]{1,0:T(8,128)(2,1)S(1)}, u32[]{:S(2)}, u32[]{:S(2)}) %collective-permute-start.19) | collective-permute-done | bytes 102432 | tf_op jit(solution)/shard_map/ppermute | solution.py:1309
  81.5 2.5 %collective-permute-done.20.refs_4_ = bf16[400,128]{1,0:T(8,128)(2,1)S(1)} collective-permute-done((bf16[400,128]{1,0:T(8,128)(2,1)S(1)}, bf16[400,128]{1,0:T(8,128)(2,1)S(1)}, u32[]{:S(2)}, u32[]{:S(2)}) %collective-permute-start.20) | collective-permute-done | bytes 102432 | tf_op jit(solution)/shard_map/ppermute | solution.py:1309
  84.0 0.2 decode_b.1.refs_1_
  84.3 3.4 %moments.1 = (f32[378,128]{1,0:T(8,128)}, f32[3,512,128]{2,1,0:T(8,128)}, f32[756,128]{1,0:T(8,128)}, f32[3,2,128]{2,1,0:T(2,128)}, f32[378,128]{1,0:T(8,128)}, ...) custom-call(f32[1536,128]{1,0:T(8,128)S(1)} %decode_a.1.refs_5_.refs, ...), custom_call_target="tpu_custom_call" | custom-call | flops 1000 | bytes 1000 | tf_op jit(solution)/shard_map/moments/pallas_call | solution.py:1222
  87.7 0.4 collective-permute-start.22
  88.1 1.4 %collective-permute-start.23 = (f32[32,128]{1,0:T(8,128)S(1)}, f32[32,128]{1,0:T(8,128)S(1)}, u32[]{:S(2)}, u32[]{:S(2)}) collective-permute-start(f32[32,128]{1,0:T(8,128)S(1)} %get-tuple-element.99.refs_1_), channel_id=1, source_target_pairs={{0,3},{1,2},{2,1},{3,0},{4,7},{5,6},{6,5},{7,4},{8,11},{9,10},{10,... | collective-permute-start | bytes 49160 | tf_op jit(solution)/shard_map/ppermute | solution.py:1309
  89.5 1.9 %collective-permute-done.22.refs_3_ = f32[32,128]{1,0:T(8,128)S(1)} collective-permute-done((f32[32,128]{1,0:T(8,128)S(1)}, f32[32,128]{1,0:T(8,128)S(1)}, u32[]{:S(2)}, u32[]{:S(2)}) %collective-permute-start.22) | collective-permute-done | bytes 16416 | tf_op jit(solution)/shard_map/ppermute | solution.py:1309
  91.5 1.7 %apply.1 = (f32[378,128]{1,0:T(8,128)}, f32[3,512,128]{2,1,0:T(8,128)}, f32[756,128]{1,0:T(8,128)}, f32[3,2,128]{2,1,0:T(2,128)}, f32[3852]{0:T(1024)}, /*index=...) custom-call(s32[8,128]{1,0:T(8,128)S(1)} %iota.7.refs_0_.refs_1_, ...), custom_call_target="tpu_custom_call" | custom-call | flops 1000 | bytes 1000 | tf_op jit(solution)/shard_map/apply/pallas_call | solution.py:1222
  (57 shorter events, 0.5 us)
Async XLA Ops:
  0.7 5.2 %copy-start.18 = (s32[2]{0:T(128)S(1)}, s32[2]{0:T(128)}, u32[]{:S(2)}) copy-start(s32[2]{0:T(128)} %refs_0_.4) | copy-start | bytes 28
  0.7 5.2 %copy-start.15 = (s32[2,2]{1,0:T(2,128)S(1)}, s32[2,2]{1,0:T(2,128)}, u32[]{:S(2)}) copy-start(s32[2,2]{1,0:T(2,128)} %refs_0_.5) | copy-start | bytes 52
  0.7 5.2 %copy-start.12 = (f32[3,2,1024]{2,1,0:T(2,128)S(1)}, f32[3,2,1024]{2,1,0:T(2,128)}, u32[]{:S(2)}) copy-start(f32[3,2,1024]{2,1,0:T(2,128)} %refs_2_.2) | copy-start | bytes 73732
  0.7 5.2 %copy-start.10 = (f32[3852]{0:T(1024)S(1)}, f32[3852]{0:T(1024)}, u32[]{:S(2)}) copy-start(f32[3852]{0:T(1024)} %refs_13_.3) | copy-start | bytes 46228
  2.9 22.1 %copy-start.1 = (bf16[2704,128]{1,0:T(8,128)(2,1)S(1)}, bf16[2704,128]{1,0:T(8,128)(2,1)}, u32[]{:S(2)}) copy-start(bf16[2704,128]{1,0:T(8,128)(2,1)} %pack.1.refs_1_.refs_2_) | copy-start | bytes 2076676
  2.9 18.7 %collective-permute-start.1 = (bf16[2704,128]{1,0:T(8,128)(2,1)}, bf16[2704,128]{1,0:T(8,128)(2,1)S(1)}, u32[]{:S(2)}, u32[]{:S(2)}) collective-permute-start(bf16[2704,128]{1,0:T(8,128)(2,1)} %pack.1.refs_1_.refs_2_), channel_id=1, source_target_pairs={{0,2},{1,3},{2,0},{3,1},{4,6},{5,7},{6,4},{7,5},{8,10},{9,11},{10,... | collective-permute-start | bytes 2076680 | tf_op jit(solution)/shard_map/ppermute | solution.py:1309
  5.9 16.7 %collective-permute-start = (bf16[2704,128]{1,0:T(8,128)(2,1)}, bf16[2704,128]{1,0:T(8,128)(2,1)S(1)}, u32[]{:S(2)}, u32[]{:S(2)}) collective-permute-start(bf16[2704,128]{1,0:T(8,128)(2,1)} %pack.1.refs_1_.refs_2_), channel_id=1, source_target_pairs={{0,1},{1,0},{2,3},{3,2},{4,5},{5,4},{6,7},{7,6},{8,9},{9,8},{10,11... | collective-permute-start | bytes 2076680 | tf_op jit(solution)/shard_map/ppermute | solution.py:1309
  22.6 2.4 %collective-permute-start.2 = (bf16[2704,128]{1,0:T(8,128)(2,1)}, bf16[2704,128]{1,0:T(8,128)(2,1)S(1)}, u32[]{:S(2)}, u32[]{:S(2)}) collective-permute-start(bf16[2704,128]{1,0:T(8,128)(2,1)} %get-tuple-element.77.refs_7_), channel_id=1, source_target_pairs={{0,1},{1,0},{2,3},{3,2},{4,5},{5,4},{6,7},{7,6},{8,9},{9,8},{10,11... | collective-permute-start | bytes 2076680 | tf_op jit(solution)/shard_map/ppermute | solution.py:1309
  29.7 7.0 %collective-permute-start.3 = (f32[2,1536,128]{2,1,0:T(8,128)S(1)}, f32[2,1536,128]{2,1,0:T(8,128)S(1)}, u32[]{:S(2)}, u32[]{:S(2)}) collective-permute-start(f32[2,1536,128]{2,1,0:T(8,128)S(1)} %get-tuple-element.81), channel_id=1, source_target_pairs={{0,1},{1,0},{2,3},{3,2},{4,5},{5,4},{6,7},{7,6},{8,9},{9,8},{10,11... | collective-permute-start | bytes 4718600 | tf_op jit(solution)/shard_map/ppermute | solution.py:1309
  36.2 4.6 %collective-permute-start.7 = (f32[2,1280,128]{2,1,0:T(8,128)S(1)}, f32[2,1280,128]{2,1,0:T(8,128)S(1)}, u32[]{:S(2)}, u32[]{:S(2)}) collective-permute-start(f32[2,1280,128]{2,1,0:T(8,128)S(1)} %get-tuple-element.90), channel_id=1, source_target_pairs={{0,1},{1,0},{2,3},{3,2},{4,5},{5,4},{6,7},{7,6},{8,9},{9,8},{10,11... | collective-permute-start | bytes 3932168 | tf_op jit(solution)/shard_map/ppermute | solution.py:1309
  37.3 8.1 %collective-permute-start.4 = (bf16[816,128]{1,0:T(8,128)(2,1)S(1)}, bf16[816,128]{1,0:T(8,128)(2,1)S(1)}, u32[]{:S(2)}, u32[]{:S(2)}) collective-permute-start(bf16[816,128]{1,0:T(8,128)(2,1)S(1)} %get-tuple-element.87), channel_id=1, source_target_pairs={{0,2},{1,3},{2,0},{3,1},{4,6},{5,7},{6,4},{7,5},{8,10},{9,11},{10,... | collective-permute-start | bytes 626696 | tf_op jit(solution)/shard_map/ppermute | solution.py:1309
  39.0 12.5 %collective-permute-start.5 = (bf16[816,128]{1,0:T(8,128)(2,1)S(1)}, bf16[816,128]{1,0:T(8,128)(2,1)S(1)}, u32[]{:S(2)}, u32[]{:S(2)}) collective-permute-start(bf16[816,128]{1,0:T(8,128)(2,1)S(1)} %get-tuple-element.88), channel_id=1, source_target_pairs={{0,4},{1,5},{2,6},{3,7},{4,0},{5,1},{6,2},{7,3},{8,12},{9,13},{10,... | collective-permute-start | bytes 626696 | tf_op jit(solution)/shard_map/ppermute | solution.py:1309
  40.5 11.0 %collective-permute-start.6 = (bf16[816,128]{1,0:T(8,128)(2,1)S(1)}, bf16[816,128]{1,0:T(8,128)(2,1)S(1)}, u32[]{:S(2)}, u32[]{:S(2)}) collective-permute-start(bf16[816,128]{1,0:T(8,128)(2,1)S(1)} %get-tuple-element.89), channel_id=1, source_target_pairs={{0,6},{1,7},{2,4},{3,5},{4,2},{5,3},{6,0},{7,1},{8,14},{9,15},{10,... | collective-permute-start | bytes 626696 | tf_op jit(solution)/shard_map/ppermute | solution.py:1309
  41.3 12.6 %collective-permute-start.9 = (bf16[736,128]{1,0:T(8,128)(2,1)S(1)}, bf16[736,128]{1,0:T(8,128)(2,1)S(1)}, u32[]{:S(2)}, u32[]{:S(2)}) collective-permute-start(bf16[736,128]{1,0:T(8,128)(2,1)S(1)} %get-tuple-element.94), channel_id=1, source_target_pairs={{0,2},{1,3},{2,0},{3,1},{4,6},{5,7},{6,4},{7,5},{8,10},{9,11},{10,... | collective-permute-start | bytes 565256 | tf_op jit(solution)/shard_map/ppermute | solution.py:1309
  43.1 15.4 %collective-permute-start.10 = (bf16[736,128]{1,0:T(8,128)(2,1)S(1)}, bf16[736,128]{1,0:T(8,128)(2,1)S(1)}, u32[]{:S(2)}, u32[]{:S(2)}) collective-permute-start(bf16[736,128]{1,0:T(8,128)(2,1)S(1)} %get-tuple-element.95), channel_id=1, source_target_pairs={{0,4},{1,5},{2,6},{3,7},{4,0},{5,1},{6,2},{7,3},{8,12},{9,13},{10,... | collective-permute-start | bytes 565256 | tf_op jit(solution)/shard_map/ppermute | solution.py:1309
  45.4 13.1 %collective-permute-start.11 = (bf16[736,128]{1,0:T(8,128)(2,1)S(1)}, bf16[736,128]{1,0:T(8,128)(2,1)S(1)}, u32[]{:S(2)}, u32[]{:S(2)}) collective-permute-start(bf16[736,128]{1,0:T(8,128)(2,1)S(1)} %get-tuple-element.96), channel_id=1, source_target_pairs={{0,6},{1,7},{2,4},{3,5},{4,2},{5,3},{6,0},{7,1},{8,14},{9,15},{10,... | collective-permute-start | bytes 565256 | tf_op jit(solution)/shard_map/ppermute | solution.py:1309
  52.0 7.1 %collective-permute-start.8 = (bf16[416,128]{1,0:T(8,128)(2,1)S(1)}, bf16[416,128]{1,0:T(8,128)(2,1)S(1)}, u32[]{:S(2)}, u32[]{:S(2)}) collective-permute-start(bf16[416,128]{1,0:T(8,128)(2,1)S(1)} %get-tuple-element.93), channel_id=1, source_target_pairs={{0,8},{1,9},{2,10},{3,11},{4,12},{5,13},{6,14},{7,15},{8,0},{9,1},... | collective-permute-start | bytes 319496 | tf_op jit(solution)/shard_map/ppermute | solution.py:1309
  59.3 7.7 %collective-permute-start.12 = (bf16[416,128]{1,0:T(8,128)(2,1)S(1)}, bf16[416,128]{1,0:T(8,128)(2,1)S(1)}, u32[]{:S(2)}, u32[]{:S(2)}) collective-permute-start(bf16[416,128]{1,0:T(8,128)(2,1)S(1)} %code_a.1.refs_3_.refs_1_), channel_id=1, source_target_pairs={{0,16},{1,17},{2,18},{3,19},{4,20},{5,21},{6,22},{7,23},{8,24},{9,... | collective-permute-start | bytes 319496 | tf_op jit(solution)/shard_map/ppermute | solution.py:1309
  61.9 4.9 %collective-permute-start.13 = (bf16[400,128]{1,0:T(8,128)(2,1)S(1)}, bf16[400,128]{1,0:T(8,128)(2,1)S(1)}, u32[]{:S(2)}, u32[]{:S(2)}) collective-permute-start(bf16[400,128]{1,0:T(8,128)(2,1)S(1)} %get-tuple-element.98), channel_id=1, source_target_pairs={{0,8},{1,9},{2,10},{3,11},{4,12},{5,13},{6,14},{7,15},{8,0},{9,1},... | collective-permute-start | bytes 307208 | tf_op jit(solution)/shard_map/ppermute | solution.py:1309
  66.8 17.3 %copy-start.9 = (f32[378,128]{1,0:T(8,128)S(1)}, f32[378,128]{1,0:T(8,128)}, u32[]{:S(2)}) copy-start(f32[378,128]{1,0:T(8,128)} %refs_10_.1) | copy-start | bytes 580612
  66.9 17.2 %copy-start.7 = (f32[128,756]{0,1:T(8,128)S(1)}, f32[128,756]{0,1:T(8,128)}, u32[]{:S(2)}) copy-start(f32[128,756]{0,1:T(8,128)} %param.33) | copy-start | bytes 1161220
  67.1 11.3 %collective-permute-start.14 = (bf16[416,128]{1,0:T(8,128)(2,1)S(1)}, bf16[416,128]{1,0:T(8,128)(2,1)S(1)}, u32[]{:S(2)}, u32[]{:S(2)}) collective-permute-start(bf16[416,128]{1,0:T(8,128)(2,1)S(1)} %recode_4_a.1.refs_3_.refs_1_), channel_id=1, source_target_pairs={{0,8},{1,9},{2,10},{3,11},{4,12},{5,13},{6,14},{7,15},{8,0},{9,1},... | collective-permute-start | bytes 319496 | tf_op jit(solution)/shard_map/ppermute | solution.py:1309
  68.6 5.8 %collective-permute-start.17 = (bf16[400,128]{1,0:T(8,128)(2,1)S(1)}, bf16[400,128]{1,0:T(8,128)(2,1)S(1)}, u32[]{:S(2)}, u32[]{:S(2)}) collective-permute-start(bf16[400,128]{1,0:T(8,128)(2,1)S(1)} %code_b.1.refs_3_.refs_1_), channel_id=1, source_target_pairs={{0,16},{1,17},{2,18},{3,19},{4,20},{5,21},{6,22},{7,23},{8,24},{9,... | collective-permute-start | bytes 307208 | tf_op jit(solution)/shard_map/ppermute | solution.py:1309
  70.8 8.0 %collective-permute-start.15 = (bf16[416,128]{1,0:T(8,128)(2,1)S(1)}, bf16[416,128]{1,0:T(8,128)(2,1)S(1)}, u32[]{:S(2)}, u32[]{:S(2)}) collective-permute-start(bf16[416,128]{1,0:T(8,128)(2,1)S(1)} %recode_4_a.1.refs_3_.refs_1_), channel_id=1, source_target_pairs={{0,4},{1,5},{2,6},{3,7},{4,0},{5,1},{6,2},{7,3},{8,12},{9,13},{10,... | collective-permute-start | bytes 319496 | tf_op jit(solution)/shard_map/ppermute | solution.py:1309
  72.0 6.8 %collective-permute-start.16 = (bf16[416,128]{1,0:T(8,128)(2,1)S(1)}, bf16[416,128]{1,0:T(8,128)(2,1)S(1)}, u32[]{:S(2)}, u32[]{:S(2)}) collective-permute-start(bf16[416,128]{1,0:T(8,128)(2,1)S(1)} %recode_4_a.1.refs_3_.refs_1_), channel_id=1, source_target_pairs={{0,12},{1,13},{2,14},{3,15},{4,8},{5,9},{6,10},{7,11},{8,4},{9,5},... | collective-permute-start | bytes 319496 | tf_op jit(solution)/shard_map/ppermute | solution.py:1309
  74.4 9.7 %copy-start.6 = (f32[128,756]{0,1:T(8,128)S(1)}, f32[128,756]{0,1:T(8,128)}, u32[]{:S(2)}) copy-start(f32[128,756]{0,1:T(8,128)} %param.28) | copy-start | bytes 1161220
  74.6 9.6 %copy-start = (f32[3,512,128]{2,1,0:T(8,128)S(1)}, f32[3,512,128]{2,1,0:T(8,128)}, u32[]{:S(2)}) copy-start(f32[3,512,128]{2,1,0:T(8,128)} %refs_6_.3) | copy-start | bytes 2359300
  74.6 9.6 %copy-start.2 = (f32[128,756]{0,1:T(8,128)S(1)}, f32[128,756]{0,1:T(8,128)}, u32[]{:S(2)}) copy-start(f32[128,756]{0,1:T(8,128)} %param.23) | copy-start | bytes 1161220
  74.6 9.6 %copy-start.3 = (f32[378,128]{1,0:T(8,128)S(1)}, f32[378,128]{1,0:T(8,128)}, u32[]{:S(2)}) copy-start(f32[378,128]{1,0:T(8,128)} %refs_5_.3) | copy-start | bytes 580612
  74.6 9.6 %copy-start.4 = (f32[3,512,128]{2,1,0:T(8,128)S(1)}, f32[3,512,128]{2,1,0:T(8,128)}, u32[]{:S(2)}) copy-start(f32[3,512,128]{2,1,0:T(8,128)} %refs_7_.1) | copy-start | bytes 2359300
  74.6 9.6 %copy-start.5 = (f32[3,512,128]{2,1,0:T(8,128)S(1)}, f32[3,512,128]{2,1,0:T(8,128)}, u32[]{:S(2)}) copy-start(f32[3,512,128]{2,1,0:T(8,128)} %refs_11_.1) | copy-start | bytes 2359300
  74.7 9.6 %copy-start.8 = (f32[378,128]{1,0:T(8,128)S(1)}, f32[378,128]{1,0:T(8,128)}, u32[]{:S(2)}) copy-start(f32[378,128]{1,0:T(8,128)} %refs_6_.2) | copy-start | bytes 580612
  74.7 9.6 %copy-start.11 = (f32[3,2,128]{2,1,0:T(2,128)S(1)}, f32[3,2,128]{2,1,0:T(2,128)}, u32[]{:S(2)}) copy-start(f32[3,2,128]{2,1,0:T(2,128)} %refs_8_.1) | copy-start | bytes 9220
  74.7 9.6 %copy-start.16 = (f32[3,2,128]{2,1,0:T(2,128)S(1)}, f32[3,2,128]{2,1,0:T(2,128)}, u32[]{:S(2)}) copy-start(f32[3,2,128]{2,1,0:T(2,128)} %refs_9_.1) | copy-start | bytes 9220
  74.7 9.6 %copy-start.17 = (f32[3,2,128]{2,1,0:T(2,128)S(1)}, f32[3,2,128]{2,1,0:T(2,128)}, u32[]{:S(2)}) copy-start(f32[3,2,128]{2,1,0:T(2,128)} %refs_13_.2) | copy-start | bytes 9220
  74.7 5.2 %collective-permute-start.18 = (bf16[400,128]{1,0:T(8,128)(2,1)S(1)}, bf16[400,128]{1,0:T(8,128)(2,1)S(1)}, u32[]{:S(2)}, u32[]{:S(2)}) collective-permute-start(bf16[400,128]{1,0:T(8,128)(2,1)S(1)} %recode_4_b.1.refs_5_.refs_1_), channel_id=1, source_target_pairs={{0,8},{1,9},{2,10},{3,11},{4,12},{5,13},{6,14},{7,15},{8,0},{9,1},... | collective-permute-start | bytes 307208 | tf_op jit(solution)/shard_map/ppermute | solution.py:1309
  76.8 4.7 %collective-permute-start.19 = (bf16[400,128]{1,0:T(8,128)(2,1)S(1)}, bf16[400,128]{1,0:T(8,128)(2,1)S(1)}, u32[]{:S(2)}, u32[]{:S(2)}) collective-permute-start(bf16[400,128]{1,0:T(8,128)(2,1)S(1)} %recode_4_b.1.refs_5_.refs_1_), channel_id=1, source_target_pairs={{0,4},{1,5},{2,6},{3,7},{4,0},{5,1},{6,2},{7,3},{8,12},{9,13},{10,... | collective-permute-start | bytes 307208 | tf_op jit(solution)/shard_map/ppermute | solution.py:1309
  78.4 5.6 %collective-permute-start.20 = (bf16[400,128]{1,0:T(8,128)(2,1)S(1)}, bf16[400,128]{1,0:T(8,128)(2,1)S(1)}, u32[]{:S(2)}, u32[]{:S(2)}) collective-permute-start(bf16[400,128]{1,0:T(8,128)(2,1)S(1)} %recode_4_b.1.refs_5_.refs_1_), channel_id=1, source_target_pairs={{0,12},{1,13},{2,14},{3,15},{4,8},{5,9},{6,10},{7,11},{8,4},{9,5},... | collective-permute-start | bytes 307208 | tf_op jit(solution)/shard_map/ppermute | solution.py:1309
  84.3 7.2 %copy-start.13 = (f32[3852]{0:T(1024)S(1)}, f32[3852]{0:T(1024)}, u32[]{:S(2)}) copy-start(f32[3852]{0:T(1024)} %refs_14_.1) | copy-start | bytes 46228
  84.3 7.2 %copy-start.14 = (f32[3852]{0:T(1024)S(1)}, f32[3852]{0:T(1024)}, u32[]{:S(2)}) copy-start(f32[3852]{0:T(1024)} %refs_15_.1) | copy-start | bytes 46228
  87.7 1.9 %collective-permute-start.21 = (f32[32,128]{1,0:T(8,128)S(1)}, f32[32,128]{1,0:T(8,128)S(1)}, u32[]{:S(2)}, u32[]{:S(2)}) collective-permute-start(f32[32,128]{1,0:T(8,128)S(1)} %get-tuple-element.99.refs_1_), channel_id=1, source_target_pairs={{0,1},{1,0},{2,3},{3,2},{4,5},{5,4},{6,7},{7,6},{8,9},{9,8},{10,11... | collective-permute-start | bytes 49160 | tf_op jit(solution)/shard_map/ppermute | solution.py:1309
  87.7 3.8 %collective-permute-start.22 = (f32[32,128]{1,0:T(8,128)S(1)}, f32[32,128]{1,0:T(8,128)S(1)}, u32[]{:S(2)}, u32[]{:S(2)}) collective-permute-start(f32[32,128]{1,0:T(8,128)S(1)} %get-tuple-element.99.refs_1_), channel_id=1, source_target_pairs={{0,2},{1,3},{2,0},{3,1},{4,6},{5,7},{6,4},{7,5},{8,10},{9,11},{10,... | collective-permute-start | bytes 49160 | tf_op jit(solution)/shard_map/ppermute | solution.py:1309
  88.1 3.4 %collective-permute-start.23 = (f32[32,128]{1,0:T(8,128)S(1)}, f32[32,128]{1,0:T(8,128)S(1)}, u32[]{:S(2)}, u32[]{:S(2)}) collective-permute-start(f32[32,128]{1,0:T(8,128)S(1)} %get-tuple-element.99.refs_1_), channel_id=1, source_target_pairs={{0,3},{1,2},{2,1},{3,0},{4,7},{5,6},{6,5},{7,4},{8,11},{9,10},{10,... | collective-permute-start | bytes 49160 | tf_op jit(solution)/shard_map/ppermute | solution.py:1309

commit v4 on v3

--- a/solution.py
+++ b/solution.py
@@ -78,29 +78,22 @@
     return sum(pack_rows(other) for other in range(LEVELS - 1, level, -1))
 
 
-def flow_block_rows(narrow):
-    return round_up(FLOW_ROWS // narrow, 8) + STATS_ROWS
-
-
 CHUNKS = ((0, 1), (2,))
 
 
-def chunk_start(level):
+def chunk_of(level):
     for chunk, levels in enumerate(CHUNKS):
         if level in levels:
-            return chunk, sum(pack_rows(other) for other in levels if other < level)
+            return chunk, sum(pack_rows(other) for other in levels[: levels.index(level)])
     return None
 
 
-def flow_start():
-    return sum(pack_rows(level) for level in CHUNKS[-1])
-
-
-def chunk_rows(chunk, narrow):
-    rows = sum(pack_rows(level) for level in CHUNKS[chunk])
-    if chunk == len(CHUNKS) - 1:
-        rows = rows + flow_block_rows(narrow)
-    return round_up(rows, 8 * CODE_BLOCK)
+def quarter_rows(chunk):
+    return round_up(sum(pack_rows(level) for level in CHUNKS[chunk]), 4 * CODE_BLOCK) // 4
+
+
+def flow_part(chunk):
+    return FLOW_ROWS if chunk == len(CHUNKS) - 1 else 0
 
 
 def stage_rows(level):
@@ -433,7 +426,7 @@
     return total
 
 
-def pack_kernel(conv_in_ref, mixer_ref, conv_out_ref, bias_ref, whole_ref):
+def pack_kernel(valid_ref, conv_in_ref, mixer_ref, conv_out_ref, bias_ref, whole_ref):
     in_start = 0
     out_start = 0
     for level in range(LEVELS):
@@ -458,6 +451,14 @@
         out_ref[top + HID :, :] = jnp.concatenate(tail, 0).astype(BF16)
         in_start = in_start + rows
         out_start = out_start + columns
+    pixels = jnp.int32(0)
+    for image in range(valid_ref.shape[0]):
+        pixels = pixels + valid_ref[image, 0] * valid_ref[image, 1]
+    lane = iota((16, LANE), 1)
+    digits = jnp.where(lane == 0, pixels & 127, 0)
+    for place in (1, 2):
+        digits = jnp.where(lane == place, lax.shift_right_logical(pixels, 7 * place) & 127, digits)
+    whole_ref[pack_start(-1) :, :] = digits.astype(F32).astype(BF16)
 
 
 def flow_pre_kernel(seed_ref, valid_ref, image_ref, flow_ref, *out_refs):
@@ -569,7 +570,7 @@
     index_ref = refs[0]
     weight_refs = refs[1 : 1 + narrow]
     base = pack_start(level)
-    out_base = chunk_start(level)[1]
+    out_base = chunk_of(level)[1]
     stage_ref, keep_ref, send_ref, result_ref = refs[1 + narrow : 5 + narrow]
     order_ref, slope_one_ref, slope_two_ref, one_ref, two_ref = refs[5 + narrow :]
     starts = stage_rows(level)
@@ -785,7 +786,7 @@
     return flat, turned, small[0:1, 6:7] - share_total * (logs_total + trace)
 
 
-def flow_back(images, narrow, me, count_ref, stages, results, flat_ref, keep_ref, send_ref):
+def flow_back(images, stages, results, weights, out_ref):
     grads = flow_chain(images, stages, results)
     parts = [
         flow_level(level, images, stages[level], results[level], grads[level])
@@ -793,21 +794,15 @@
     ]
     flat = sum(part[0] for part in parts) + sum(part[1] for part in parts).T[:FLOW_ROWS]
     loss = sum(part[2] for part in parts)
-    pixels = jnp.zeros((), F32)
-    for index in range(images):
-        pixels = pixels + (count_ref[index, 0] * count_ref[index, 1]).astype(F32)
+    pixels = jnp.zeros((1, 1), F32)
+    start = pack_start(-1)
+    for ref in weights:
+        digits = ref[start : start + 16, :].astype(F32)
+        for place in range(3):
+            pixels = pixels + 128.0**place * digits[0:1, place : place + 1]
     lane = iota((STATS_ROWS, LANE), 1)
-    stats = jnp.where(lane == 0, loss, jnp.where(lane == 1, pixels, 0.0))
-    flat_ref[...] = flat
-    share = FLOW_ROWS // narrow
-    start = flow_start()
-    for r in range(narrow):
-        ref = send_ref if r & 1 else keep_ref
-        ref[r // 2, start : start + share, :] = flat_ref[
-            pl.ds(pl.multiple_of((me ^ r) * share, share), share), :
-        ]
-        ref[r // 2, start + share : start + share + STATS_ROWS, :] = stats
-    zero_rows((keep_ref, send_ref), start + share + STATS_ROWS)
+    out_ref[0:FLOW_ROWS, :] = flat
+    out_ref[FLOW_ROWS:, :] = jnp.where(lane == 0, loss, jnp.where(lane == 1, pixels, 0.0))
 
 
 def zero_rows(refs, start):
@@ -817,15 +812,17 @@
             ref[:, start:, :] = jnp.zeros((ref.shape[0], rest, LANE), F32)
 
 
-def nets_kernel(levels, images, narrow, *refs):
+def nets_kernel(chunk, images, narrow, *refs):
+    levels = CHUNKS[chunk]
+    number = len(levels)
     index_ref = refs[0]
     mine = refs[1 : 1 + narrow]
     at = 1 + narrow
-    stages = refs[at : at + len(levels)]
-    at = at + len(levels)
+    stages = refs[at : at + number]
+    at = at + number
     keep_ref, send_ref = refs[at : at + 2]
-    results = refs[at + 2 : at + 2 + len(levels)]
-    at = at + 2 + len(levels)
+    results = refs[at + 2 : at + 2 + number]
+    at = at + 2 + number
     for place, level in enumerate(levels):
         net_kernel(
             level,
@@ -842,39 +839,10 @@
     zero_rows((keep_ref, send_ref), sum(pack_rows(level) for level in levels))
 
 
-def last_kernel(images, narrow, *refs):
-    level = LEVELS - 1
-    count_ref, index_ref = refs[:2]
-    mine = refs[2 : 2 + narrow]
-    at = 2 + narrow
-    stages = refs[at : at + LEVELS]
-    at = at + LEVELS
-    results = refs[at : at + LEVELS - 1]
-    at = at + LEVELS - 1
-    keep_ref, send_ref, result_ref, flat_ref = refs[at : at + 4]
-    net_kernel(
-        level,
-        images,
-        narrow,
-        index_ref,
-        *mine,
-        stages[level],
-        keep_ref,
-        send_ref,
-        result_ref,
-        *refs[at + 4 :],
-    )
-    flow_back(
-        images,
-        narrow,
-        index_ref[0, 0],
-        count_ref,
-        stages,
-        list(results) + [result_ref],
-        flat_ref,
-        keep_ref,
-        send_ref,
-    )
+def flow_kernel(images, narrow, *refs):
+    stages, results = refs[:LEVELS], refs[LEVELS : 2 * LEVELS]
+    weights, out_ref = refs[2 * LEVELS : -1], refs[-1]
+    flow_back(images, stages, results, weights, out_ref)
 
 
 def copy_kernel(*refs):
@@ -883,119 +851,133 @@
         to_ref[...] = from_ref[...]
 
 
-def piece_rows(rows, exact):
-    return rows + round_up(rows // CODE_BLOCK, 16) + 3 * exact
-
-
-def write_piece(ref, values, exact_values=None):
+def piece_rows(rows):
+    return rows + round_up(rows // CODE_BLOCK, 16)
+
+
+def write_piece(ref, start, values, extra=None):
     rows = values.shape[0]
     blocks = values.reshape(rows // CODE_BLOCK, CODE_BLOCK, LANE)
     scale = rounded(jnp.max(jnp.abs(blocks), axis=1) * 1.01)
     factor = jnp.where(scale > 0.0, CODE_RANGE / scale, 0.0)
     code = jnp.exp(blocks * factor[:, None, :])
-    ref[0:rows, :] = code.reshape(rows, LANE).astype(BF16)
+    ref[start : start + rows, :] = code.reshape(rows, LANE).astype(BF16)
+    tail = [scale] + ([] if extra is None else split_three(extra))
+    used = sum(part.shape[0] for part in tail)
     size = round_up(rows // CODE_BLOCK, 16)
-    if size > rows // CODE_BLOCK:
-        scale = jnp.concatenate([scale, jnp.zeros((size - rows // CODE_BLOCK, LANE), F32)], 0)
-    ref[rows : rows + size, :] = scale.astype(BF16)
-    if exact_values is not None:
-        ref[rows + size :, :] = jnp.concatenate(split_three(exact_values), 0).astype(BF16)
-
-
-def read_piece(ref, rows):
-    blocks = jnp.log(ref[0:rows, :].astype(F32)).reshape(rows // CODE_BLOCK, CODE_BLOCK, LANE)
-    scale = ref[rows : rows + round_up(rows // CODE_BLOCK, 16), :].astype(F32)
+    if size > used:
+        tail.append(jnp.zeros((size - used, LANE), F32))
+    ref[start + rows : start + rows + size, :] = jnp.concatenate(tail, 0).astype(BF16)
+
+
+def read_piece(ref, start, rows):
+    blocks = jnp.log(ref[start : start + rows, :].astype(F32))
+    blocks = blocks.reshape(rows // CODE_BLOCK, CODE_BLOCK, LANE)
+    scale = ref[start + rows : start + piece_rows(rows), :].astype(F32)
     factor = scale[: rows // CODE_BLOCK] * (1.0 / CODE_RANGE)
     return (blocks * factor[:, None, :]).reshape(rows, LANE)
 
 
-def read_exact(ref, rows, exact):
-    start = rows + round_up(rows // CODE_BLOCK, 16)
-    pieces = ref[start : start + 3 * exact, :].astype(F32)
-    return pieces[:exact] + pieces[exact : 2 * exact] + pieces[2 * exact :]
+def read_stats(ref, start, rows):
+    first = start + rows + rows // CODE_BLOCK
+    tail = ref[first : first + 3, :].astype(F32)
+    return tail[0:1] + tail[1:2] + tail[2:3]
 
 
 def wide_bit(index_ref, bit):
     return jnp.where((index_ref[1, 0] & bit) != 0, 1, 0)
 
 
-def exact_place(rows):
-    return flow_start() // rows, flow_start() % rows
-
-
-def square_kernel(exact, index_ref, keep_ref, other_ref, mine_ref, *sent_refs):
-    half = keep_ref.shape[1] // 2
+def square_kernel(chunk, index_ref, keep_ref, other_ref, *refs):
+    flow = None
+    if flow_part(chunk):
+        flow_ref, mine_ref, own_flow_ref, *sent_refs = refs
+        flow = flow_ref[0:FLOW_ROWS, :]
+        stats = flow_ref[FLOW_ROWS : FLOW_ROWS + 1, :]
+        write_piece(own_flow_ref, 0, flow, stats)
+    else:
+        mine_ref, *sent_refs = refs
+    half = 2 * quarter_rows(chunk)
     upper = wide_bit(index_ref, 1)
 
     def total(shard, flipped):
         place = 1 - upper if flipped else upper
-        picked = pl.ds(pl.multiple_of(place * half, 16), half)
+        picked = pl.ds(pl.multiple_of(place * half, CODE_BLOCK), half)
         return keep_ref[shard, picked, :] + other_ref[shard, picked, :]
 
     mine_ref[...] = total(0, 0)
     for ref, (shard, flipped) in zip(sent_refs, ((1, 0), (0, 1), (1, 1))):
-        exact_values = None
-        if exact:
-            picked = slice(flow_start(), flow_start() + exact)
-            exact_values = keep_ref[shard, picked, :] + other_ref[shard, picked, :]
-        write_piece(ref, total(shard, flipped), exact_values)
-
-
-def column_kernel(exact, index_ref, mine_ref, *refs):
-    others, (keep_ref, sent_ref, total_ref) = refs[:3], refs[3:]
-    rows = mine_ref.shape[0]
+        values = total(shard, flipped)
+        if flow is None:
+            write_piece(ref, 0, values)
+        else:
+            write_piece(ref, 0, jnp.concatenate([values, flow], 0), stats)
+
+
+def column_kernel(chunk, index_ref, mine_ref, *refs):
+    rows = 2 * quarter_rows(chunk)
+    more = flow_part(chunk)
+    if more:
+        own_flow_ref, *others, keep_ref, own_next_ref, sent_ref, total_ref = refs
+    else:
+        *others, keep_ref, sent_ref, total_ref = refs
+    total = mine_ref[...]
+    for flip, other in enumerate(others, 1):
+        values = read_piece(other, 0, rows + more)
+        total = total + values[:rows]
+        if more and flip == 2:
+            flow = read_piece(own_flow_ref, 0, FLOW_ROWS) + values[rows:]
+            stats = read_stats(own_flow_ref, 0, FLOW_ROWS) + read_stats(other, 0, rows + more)
+    total_ref[...] = total
     half = rows // 2
-    total = mine_ref[...]
-    for other in others:
-        total = total + read_piece(other, rows)
-    total_ref[...] = total
-    exact_values = None
-    if exact:
-        part, start = exact_place(rows)
-        exact_values = mine_ref[start : start + exact, :]
-        for other in others:
-            exact_values = exact_values + read_exact(other, rows, exact)
-
-        @pl.when(wide_bit(index_ref, 1) == part)
-        def _():
-            total_ref[start : start + exact, :] = exact_values
-
     place = wide_bit(index_ref, 2)
-    keep_ref[...] = total_ref[pl.ds(pl.multiple_of(place * half, 16), half), :]
-    values = total_ref[pl.ds(pl.multiple_of((1 - place) * half, 16), half), :]
-    write_piece(sent_ref, values, exact_values)
-
-
-def code_kernel(exact, index_ref, mine_ref, other_ref, out_ref):
-    rows = mine_ref.shape[0]
-    exact_values = None
-    if exact:
-        _, start = exact_place(rows)
-        exact_values = mine_ref[start : start + exact, :] + read_exact(other_ref, rows, exact)
-    write_piece(out_ref, mine_ref[...] + read_piece(other_ref, rows), exact_values)
-
-
-def recode_kernel(exact, rows, index_ref, mine_ref, other_ref, out_ref):
-    exact_values = None
-    if exact:
-        exact_values = read_exact(mine_ref, rows, exact) + read_exact(other_ref, rows, exact)
-    write_piece(out_ref, read_piece(mine_ref, rows) + read_piece(other_ref, rows), exact_values)
-
-
-def decode_kernel(exact, index_ref, *refs):
-    parts, out_ref = refs[:4], refs[4]
-    rows = out_ref.shape[0] // 4
+    keep_ref[...] = total_ref[pl.ds(pl.multiple_of(place * half, CODE_BLOCK), half), :]
+    values = total_ref[pl.ds(pl.multiple_of((1 - place) * half, CODE_BLOCK), half), :]
+    if more:
+        write_piece(own_next_ref, 0, flow, stats)
+        write_piece(sent_ref, 0, jnp.concatenate([values, flow], 0), stats)
+    else:
+        write_piece(sent_ref, 0, values)
+
+
+def code_kernel(chunk, index_ref, mine_ref, *refs):
+    rows = quarter_rows(chunk)
+    more = flow_part(chunk)
+    if more:
+        own_flow_ref, other_ref, out_ref = refs
+    else:
+        other_ref, out_ref = refs
+    values = read_piece(other_ref, 0, rows + more)
+    total = mine_ref[...] + values[:rows]
+    if more:
+        flow = read_piece(own_flow_ref, 0, FLOW_ROWS) + values[rows:]
+        stats = read_stats(own_flow_ref, 0, FLOW_ROWS) + read_stats(other_ref, 0, rows + more)
+        write_piece(out_ref, 0, jnp.concatenate([total, flow], 0), stats)
+    else:
+        write_piece(out_ref, 0, total)
+
+
+def recode_kernel(chunk, index_ref, mine_ref, other_ref, out_ref):
+    rows = quarter_rows(chunk) + flow_part(chunk)
+    stats = None
+    if flow_part(chunk):
+        stats = read_stats(mine_ref, 0, rows) + read_stats(other_ref, 0, rows)
+    write_piece(out_ref, 0, read_piece(mine_ref, 0, rows) + read_piece(other_ref, 0, rows), stats)
+
+
+def decode_kernel(chunk, index_ref, *refs):
+    parts, outs = refs[:4], refs[4:]
     place = 2 * wide_bit(index_ref, 1) + wide_bit(index_ref, 2)
+    rows, more = quarter_rows(chunk), flow_part(chunk)
     for flip, ref in enumerate(parts):
-        start = pl.multiple_of((place ^ flip) * rows, 16)
-        out_ref[pl.ds(start, rows), :] = read_piece(ref, rows)
-    if exact:
-        part, start = exact_place(rows)
-        for flip, ref in enumerate(parts):
-
-            @pl.when((place ^ flip) == part)
-            def _():
-                out_ref[flow_start() : flow_start() + exact, :] = read_exact(ref, rows, exact)
+        values = read_piece(ref, 0, rows + more)
+        start = pl.multiple_of((place ^ flip) * rows, CODE_BLOCK)
+        outs[0][pl.ds(start, rows), :] = values[:rows]
+        if more and flip == 0:
+            outs[1][0:FLOW_ROWS, :] = values[rows:]
+            outs[1][FLOW_ROWS:, :] = jnp.broadcast_to(
+                read_stats(ref, 0, rows + more), (STATS_ROWS, LANE)
+            )
 
 
 def moments(weight, gradient, first_old, second_old):
@@ -1053,70 +1035,75 @@
     return masks
 
 
-def moment_kernel(share, *refs):
-    chunks = refs[:2]
-    grads = []
+def split_grads(refs, scale):
+    ins, mixes, outs, biases = [], [], [], []
     for level in range(LEVELS):
-        chunk, start = chunk_start(level)
-        grads.append(chunks[chunk].at[start : start + pack_rows(level)])
-    weight_in, weight_mix, weight_out, weight_bias = refs[2:6]
-    first_in, first_mix, first_out, first_bias = refs[6:10]
-    second_in, second_mix, second_out, second_bias = refs[10:14]
-    outs = refs[14:]
-    flow_ref = chunks[-1].at[flow_start() : flow_start() + share + STATS_ROWS]
-    total = flow_ref[share : share + 1, :]
-    valid_dims = 3.0 * total[:, 1:2]
-    scale = 1.0 / (valid_dims * LOG_TWO)
-    grad_in = jnp.concatenate([grads[level][0 : in_rows(level), :] for level in range(LEVELS)], 0)
-    tails = [
-        grads[level][first_rows(level) + HID : first_rows(level) + HID + 9 * chan(level), :]
-        for level in range(LEVELS)
-    ]
-    grad_out = jnp.concatenate(tails, 0)
-    bias_rows = []
-    for level in range(LEVELS):
-        bias_rows.append(grads[level][in_rows(level) : in_rows(level) + 1, :])
-        bias_rows.append(grads[level][second_bias_row(level) : second_bias_row(level) + 1, :])
-    grad_bias = jnp.concatenate(bias_rows, 0)
+        chunk, start = chunk_of(level)
+        ref = refs[chunk]
+
+        def rows(first, count):
+            return ref[start + first : start + first + count, :] * scale
+
+        top = first_rows(level)
+        ins.append(rows(0, in_rows(level)))
+        mixes.append(rows(top, HID))
+        outs.append(rows(top + HID, 9 * chan(level)))
+        biases.append(rows(in_rows(level), 1))
+        biases.append(rows(second_bias_row(level), 1))
+    return jnp.concatenate(ins, 0), mixes, jnp.concatenate(outs, 0), jnp.concatenate(biases, 0)
+
+
+def norm_kernel(*refs):
+    parts, flow_ref = refs[:2], refs[2]
+    weight_in, weight_mix, weight_out, weight_bias = refs[3:7]
+    first_in, first_mix, first_out, first_bias = refs[7:11]
+    second_in, second_mix, second_out, second_bias = refs[11:15]
+    grad_in_ref, grad_mix_ref, grad_out_ref, grad_bias_ref = refs[15:19]
+    update_in, update_mix, update_out, update_bias, block_ref = refs[19:]
+    stats = flow_ref[FLOW_ROWS : FLOW_ROWS + 1, :]
+    scale = 1.0 / (3.0 * stats[:, 1:2] * LOG_TWO)
+    grad_in, grad_mix, grad_out, grad_bias = split_grads(parts, scale)
+    grad_in_ref[...] = grad_in
+    grad_out_ref[...] = grad_out
+    grad_bias_ref[...] = grad_bias
     bias = weight_bias[...].reshape(2 * LEVELS, LANE)
-    new_in = moments(weight_in[...], grad_in * scale, first_in[...], second_in[...])
-    new_out = moments(weight_out[...], grad_out * scale, first_out[...], second_out[...])
+    new_in = moments(weight_in[...], grad_in, first_in[...], second_in[...])[2]
+    new_out = moments(weight_out[...], grad_out, first_out[...], second_out[...])[2]
     new_bias = moments(
         bias,
-        grad_bias * scale,
+        grad_bias,
         first_bias[...].reshape(2 * LEVELS, LANE),
         second_bias[...].reshape(2 * LEVELS, LANE),
-    )
+    )[2]
+    update_in[...] = new_in
+    update_out[...] = new_out
+    update_bias[...] = new_bias.reshape(LEVELS, 2, LANE)
     mix_squares = []
     mix_updates = []
     for level in range(LEVELS):
-        top = first_rows(level)
-        new_mix = moments(
-            weight_mix[level],
-            grads[level][top : top + HID, :] * scale,
-            first_mix[level],
-            second_mix[level],
-        )
-        outs[1][level] = new_mix[0]
-        outs[5][level] = new_mix[1]
-        outs[9][level] = new_mix[2]
+        grad_mix_ref[level] = grad_mix[level]
+        new_mix = moments(weight_mix[level], grad_mix[level], first_mix[level], second_mix[level])[2]
+        update_mix[level] = new_mix
         mix_squares.append(weight_mix[level] * weight_mix[level])
-        mix_updates.append(new_mix[2] * new_mix[2])
-    for index, values in ((0, new_in), (2, new_out), (3, new_bias)):
-        for kind in range(3):
-            value = values[kind]
-            if index == 3:
-                value = value.reshape(LEVELS, 2, LANE)
-            outs[4 * kind + index][...] = value
+        mix_updates.append(new_mix * new_mix)
     weight_sums = group_totals(
         weight_in[...] * weight_in[...], mix_squares, weight_out[...] * weight_out[...], bias * bias
     )
-    update_sums = group_totals(
-        new_in[2] * new_in[2], mix_updates, new_out[2] * new_out[2], new_bias[2] * new_bias[2]
-    )
+    update_sums = group_totals(new_in * new_in, mix_updates, new_out * new_out, new_bias * new_bias)
     lane = iota((16, LANE), 1)
-    outs[12][0:16, :] = jnp.where(lane == 0, squares_rows(weight_sums), squares_rows(update_sums))
-    outs[12][16:, :] = flow_ref[...]
+    block_ref[0:16, :] = jnp.where(lane == 0, squares_rows(weight_sums), squares_rows(update_sums))
+    block_ref[16:, :] = flow_ref[...]
+
+
+def moment_kernel(*refs):
+    grads, firsts, seconds = refs[0:4], refs[4:8], refs[8:12]
+    new_firsts, new_seconds = refs[12:16], refs[16:20]
+    for grad, first, second, new_first, new_second in zip(
+        grads, firsts, seconds, new_firsts, new_seconds
+    ):
+        gradient = grad[...].reshape(first.shape)
+        new_first[...] = FIRST_BETA * first[...] + (1.0 - FIRST_BETA) * gradient
+        new_second[...] = SECOND_BETA * second[...] + (1.0 - SECOND_BETA) * gradient * gradient
 
 
 def apply_kernel(narrow, *refs):
@@ -1146,13 +1133,13 @@
     ) = refs[at:]
     for part in range(narrow):
         order_ref[index_ref[0, 0] ^ part] = block_refs[part][...]
-    share = FLOW_ROWS // narrow
-    sums = order_ref[0, 0:16, :]
+    whole = order_ref[0]
     for part in range(1, narrow):
-        sums = sums + order_ref[part, 0:16, :]
-    flow_grad = jnp.concatenate([order_ref[part, 16 : 16 + share, :] for part in range(narrow)], 0)
-    total = block_refs[0][16 + share : 17 + share, :]
-    valid_dims = 3.0 * total[:, 1:2]
+        whole = whole + order_ref[part]
+    sums = whole[0:16]
+    flow_grad = whole[16 : 16 + FLOW_ROWS]
+    loss = whole[16 + FLOW_ROWS : 17 + FLOW_ROWS, 0:1]
+    valid_dims = 3.0 * block_refs[0][16 + FLOW_ROWS : 17 + FLOW_ROWS, 1:2]
     scale = 1.0 / (valid_dims * LOG_TWO)
     flow = to_flat_rows(flow_ref[...])
     size = flow_ref.shape[0]
@@ -1201,7 +1188,7 @@
         for index in range(15):
             held = jnp.where(lane == index, norms[index], held)
         ref[...] = held[:, :15].reshape(15)
-    loss_ref[...] = total[:, 0:1] / LOG_TWO + 8.0 * valid_dims
+    loss_ref[...] = loss / LOG_TWO + 8.0 * valid_dims
     valid_ref[...] = valid_dims
 
 
@@ -1235,9 +1222,9 @@
     )(*scalars, *arrays, *after)
 
 
-def run_pack(conv_in, mixer, conv_out, hidden_bias):
-    outs = [((sum(pack_rows(level) for level in range(LEVELS)), LANE), BF16)]
-    return call(pack_kernel, outs, (), (conv_in, mixer, conv_out, hidden_bias), name="pack", vmem=56)
+def run_pack(valid_shape, conv_in, mixer, conv_out, hidden_bias):
+    outs = [((pack_start(-1) + 16, LANE), BF16)]
+    return call(pack_kernel, outs, (valid_shape,), (conv_in, mixer, conv_out, hidden_bias), name="pack", vmem=56)
 
 
 def run_flow_pre(noise_seeds, valid_shape, images, flow_params, after):
@@ -1253,22 +1240,21 @@
     )
 
 
-def run_nets(levels, images, index, weights, stages, after):
+def run_nets(chunk, images, index, weights, stages, after):
     narrow = len(weights)
-    rows = chunk_rows(chunk_start(levels[0])[0], narrow)
-    outs = [((narrow // 2, rows, LANE), F32)] * 2
+    outs = [((narrow // 2, 4 * quarter_rows(chunk), LANE), F32)] * 2
     scratch = []
-    for level in levels:
+    for level in CHUNKS[chunk]:
         count = positions(level, images)
         outs = outs + [((stage_rows(level)["result_rows"], count), F32)]
         scratch = scratch + net_scratch(count)
     return call(
-        functools.partial(nets_kernel, levels, images, narrow),
+        functools.partial(nets_kernel, chunk, images, narrow),
         outs,
         (),
-        [index] + list(weights) + [stages[level] for level in levels],
+        [index] + list(weights) + [stages[level] for level in CHUNKS[chunk]],
         scratch,
-        name="nets_" + "_".join(str(level + 1) for level in levels),
+        name="nets_" + "ab"[chunk],
         after=after,
     )
 
@@ -1283,23 +1269,16 @@
     ]
 
 
-def run_last(images, index, valid_shape, weights, stages, results, after):
-    narrow = len(weights)
-    level = LEVELS - 1
-    count = positions(level, images)
-    return call(
-        functools.partial(last_kernel, images, narrow),
-        [((narrow // 2, chunk_rows(len(CHUNKS) - 1, narrow), LANE), F32)] * 2,
-        (valid_shape,),
-        [index] + list(weights) + list(stages) + list(results),
-        [
-            pltpu.VMEM((stage_rows(level)["result_rows"], count), F32),
-            pltpu.VMEM((FLOW_ROWS, LANE), F32),
-        ]
-        + net_scratch(count),
-        name="net_3_and_flow",
+def run_flow(images, weights, stages, results, after):
+    (out,) = call(
+        functools.partial(flow_kernel, images, len(weights)),
+        [((FLOW_ROWS + STATS_ROWS, LANE), F32)],
+        (),
+        list(stages) + list(results) + list(weights),
+        name="flow_back",
         after=after,
     )
+    return out
 
 
 def swap(values, wide, narrow):
@@ -1310,86 +1289,74 @@
 
 
 class Summation:
-    def __init__(self, chunk, index, exact):
-        self.name, self.index, self.exact = "abc"[chunk], index, exact
-
-    def start(self, keep, send):
-        self.kept, self.others = keep, [swap(send, 0, 1)]
-
-    def run(self, kernel, outs, arrays, after, name, scratch=()):
+    def __init__(self, chunk, index, send):
+        self.chunk, self.index = chunk, index
+        self.others = [swap(send, 0, 1)]
+        rows, more = quarter_rows(chunk), flow_part(chunk)
+        self.own_piece = [((piece_rows(FLOW_ROWS), LANE), BF16)] if more else []
+        self.own = ()
+        self.square_piece = ((piece_rows(2 * rows + more), LANE), BF16)
+        self.piece = ((piece_rows(rows + more), LANE), BF16)
+
+    def run(self, kernel, outs, name, after, scratch=(), extra=()):
         return call(
-            kernel,
+            functools.partial(kernel, self.chunk),
             outs,
             (),
-            (self.index, *arrays),
+            (self.index, self.kept, *extra, *self.others),
             scratch,
-            name=name + "_" + self.name,
+            name=name + "_" + "ab"[self.chunk],
             after=after,
         )
 
-    def square(self, after):
-        rows = self.kept.shape[1] // 2
-        self.kept, *sent = self.run(
-            functools.partial(square_kernel, self.exact),
-            [((rows, LANE), F32)] + [((piece_rows(rows, self.exact), LANE), BF16)] * 3,
-            (self.kept, *self.others),
-            after,
-            "square",
+    def square(self, keep, flow, after):
+        rows = 2 * quarter_rows(self.chunk)
+        self.kept, *rest = call(
+            functools.partial(square_kernel, self.chunk),
+            [((rows, LANE), F32)] + self.own_piece + [self.square_piece] * 3,
+            (),
+            (self.index, keep, *self.others, *flow),
+            name="square_" + "ab"[self.chunk],
+            after=after,
         )
+        self.own, sent = tuple(rest[:-3]), rest[-3:]
         self.others = [swap(sent[0], 0, 2), swap(sent[1], 1, 0), swap(sent[2], 1, 2)]
         return self.kept
 
     def column(self, after):
-        rows = self.kept.shape[0]
-        self.rows = rows // 2
-        self.piece = ((piece_rows(self.rows, self.exact), LANE), BF16)
-        self.kept, sent = self.run(
-            functools.partial(column_kernel, self.exact),
-            [((self.rows, LANE), F32), self.piece],
-            (self.kept, *self.others),
+        rows = quarter_rows(self.chunk)
+        self.kept, *rest = self.run(
+            column_kernel,
+            [((rows, LANE), F32)] + self.own_piece + [self.piece],
+            "column",
             after,
-            "column",
-            [pltpu.VMEM((rows, LANE), F32)],
+            [pltpu.VMEM((2 * rows, LANE), F32)],
+            self.own,
         )
-        self.others = [swap(sent, 2, 0)]
+        self.own = tuple(rest[:-1])
+        self.others = [swap(rest[-1], 2, 0)]
         return self.kept
 
     def code(self, after):
-        (self.kept,) = self.run(
-            functools.partial(code_kernel, self.exact),
-            [self.piece],
-            (self.kept, *self.others),
-            after,
-            "code",
-        )
+        (self.kept,) = self.run(code_kernel, [self.piece], "code", after, (), self.own)
         self.others = [swap(self.kept, 4, 0)]
         return self.kept
 
     def spread(self, after):
         step = 4
         while step < lax.axis_size("wide"):
-            (self.kept,) = self.run(
-                functools.partial(recode_kernel, self.exact, self.rows),
-                [self.piece],
-                (self.kept, *self.others),
-                after,
-                "recode_%d" % step,
-            )
+            (self.kept,) = self.run(recode_kernel, [self.piece], "recode_%d" % step, after)
             step = 2 * step
             if step < lax.axis_size("wide"):
                 self.others = [swap(self.kept, step, 0)]
         self.others = [swap(self.kept, 2, 0), swap(self.kept, 1, 0), swap(self.kept, 3, 0)]
         return self.kept
 
-    def decode(self, rows, after):
-        (self.kept,) = self.run(
-            functools.partial(decode_kernel, self.exact),
-            [((rows, LANE), F32)],
-            (self.kept, *self.others),
-            after,
-            "decode",
-        )
-        return self.kept
+    def decode(self, after):
+        shape = [((4 * quarter_rows(self.chunk), LANE), F32)]
+        if flow_part(self.chunk):
+            shape.append(((FLOW_ROWS + STATS_ROWS, LANE), F32))
+        return self.run(decode_kernel, shape, "decode", after)
 
 
 def body(
@@ -1417,7 +1384,7 @@
     row = lax.broadcasted_iota(jnp.int32, (8, LANE), 0)
     index = jnp.where(row == 0, lax.axis_index("narrow"), lax.axis_index("wide")).astype(jnp.int32)
     narrow = lax.axis_size("narrow")
-    (packed,) = run_pack(conv_in, mixer, conv_out, hidden_bias)
+    (packed,) = run_pack(valid_shape, conv_in, mixer, conv_out, hidden_bias)
     paired = swap(packed, 0, 1)
     crossed = swap(packed, 0, 2)
     stages = run_flow_pre(noise_seeds, valid_shape, images, flow_params, ())
@@ -1426,38 +1393,42 @@
         copy_kernel, [(array.shape, array.dtype) for array in arrays], (), arrays, name="copy"
     )
     gathered = (packed, paired, crossed, swap(copied, 0, 1))
-    one = Summation(0, index, 0)
-    two = Summation(1, index, flow_block_rows(narrow))
-    keep, send, *results = run_nets(CHUNKS[0], count, index, gathered, stages, (copied,))
-    one.start(keep, send)
-    keep, send = run_last(count, index, valid_shape, gathered, stages, results, (keep,))
-    two.start(keep, send)
-    sizes = one.kept.shape[1], two.kept.shape[1]
-    token = one.square((keep,))
-    token = two.square((token,))
+    keep_one, send, *results = run_nets(0, count, index, gathered, stages, ())
+    one = Summation(0, index, send)
+    keep_two, send, *more = run_nets(1, count, index, gathered, stages, (keep_one,))
+    results = results + more
+    two = Summation(1, index, send)
+    token = one.square(keep_one, (), (keep_two,))
+    flow = run_flow(count, gathered, stages, results, (token,))
+    token = two.square(keep_two, (flow,), ())
     token = one.column((token,))
     token = two.column((token,))
     token = one.code((token,))
     token = two.code((token,))
     token = one.spread((token,))
     token = two.spread((token,))
-    token = one.decode(sizes[0], (token,))
-    token = two.decode(sizes[1], (token,))
-    grads = (one.kept, two.kept)
+    parts = one.decode((token,))
+    parts = list(parts) + list(two.decode((parts[0],)))
     weights = (conv_in, mixer, conv_out, hidden_bias)
+    firsts = (conv_in_first, mixer_first, conv_out_first, bias_first)
+    seconds = (conv_in_second, mixer_second, conv_out_second, bias_second)
     shapes = [(weight.shape, F32) for weight in weights]
-    share = FLOW_ROWS // narrow
+    grad_shapes = shapes[:3] + [((2 * LEVELS, LANE), F32)]
+    *grads, update_in, update_mix, update_out, update_bias, block = call(
+        norm_kernel,
+        grad_shapes + shapes + [((16 + FLOW_ROWS + STATS_ROWS, LANE), F32)],
+        (),
+        tuple(parts) + weights + firsts + seconds,
+        name="norms",
+    )
+    blocks = [block] + [swap(block, 0, part) for part in range(1, narrow)]
     moved = call(
-        functools.partial(moment_kernel, share),
-        shapes * 3 + [((16 + share + STATS_ROWS, LANE), F32)],
+        moment_kernel,
+        shapes * 2,
         (),
-        grads
-        + weights
-        + (conv_in_first, mixer_first, conv_out_first, bias_first)
-        + (conv_in_second, mixer_second, conv_out_second, bias_second),
+        tuple(grads) + firsts + seconds,
         name="moments",
     )
-    blocks = [moved[12]] + [swap(moved[12], 0, part) for part in range(1, narrow)]
     flow_shape = (flow_params.shape, F32)
     fresh = call(
         functools.partial(apply_kernel, narrow),
@@ -1470,9 +1441,10 @@
         (index,)
         + tuple(blocks)
         + weights
-        + tuple(moved[8:12])
+        + (update_in, update_mix, update_out, update_bias)
         + (flow_params, flow_first, flow_second),
-        scratch=[pltpu.VMEM((narrow,) + moved[12].shape, F32)],
+        scratch=[pltpu.VMEM((narrow,) + block.shape, F32)],
+        after=(moved[3],),
         name="apply",
     )
     return (

time: 93.5 us -> 88.7 us (0.949)
  starting transfers between devices: 30 us -> 26.9 us
  waiting for transfers between devices: 35 us -> 32.7 us
    ppermute x24, starting transfers between devices: 30 us -> 26.9 us  [swap(): lax.ppermute(values, ('wide', 'narrow'), [(place, place ^ mask) for place...]
    ppermute x24, waiting for transfers between devices: 35 us -> 32.7 us  [swap(): lax.ppermute(values, ('wide', 'narrow'), [(place, place ^ mask) for place...]
    pallas_call x17 -> x19, Pallas kernels: 27 us -> 26.8 us  [call(): pl.pallas_call(run, out_shape=tuple((jax.ShapeDtypeStruct(shape, dtype) f...]
  transfers between devices with their start and end apart: 24 -> 24, of which waited for: 12 -> 13; matrix products, arithmetic and copies ran while one was open for 0% -> 0% of each run, Pallas kernels for 16% -> 18%
where the time goes in v4:
time: 88.7 us; the launch traced here: 88.5 us
  waiting for transfers between devices  32.7 us (37%)
  starting transfers between devices  26.9 us (30%)
  Pallas kernels  26.8 us (30%)
  between operations  1.14 us (1%)
    ppermute x24, waiting for transfers between devices, swap(): lax.ppermute(values, ('wide', 'narrow'), [(place, place ^ mask) for place...  32.7 us
    ppermute x24, starting transfers between devices, swap(): lax.ppermute(values, ('wide', 'narrow'), [(place, place ^ mask) for place...  26.9 us
    pallas_call x19, Pallas kernels, call(): pl.pallas_call(run, out_shape=tuple((jax.ShapeDtypeStruct(shape, dtype) f...  26.8 us
  transfers between devices with their start and end apart: 24, of which 13 were waited for; matrix products, arithmetic and copies ran while one was open for 0% of the time, Pallas kernels for 18%

profile of v4, /device:TPU:0, one launch (start us, length us, event | category | flops | bytes accessed | tf_op | source)
XLA Modules:
  0.0 88.5 jit_solution(7475539321260160769)
XLA Ops:
  0.7 2.2 %pack.1.refs_1_.refs_6_ = bf16[2720,128]{1,0:T(8,128)(2,1)} custom-call(s32[2,2]{1,0:T(2,128)} %refs_1_.3, f32[378,128]{1,0:T(8,128)} %refs_5_.3, f32[3,512,128]{2,1,0:T(8,128)} %refs_6_.3, f32[756,128]{1,0:T(8,128)} %bitcast.9, f32[3,2,128]{2,1,0:T(2,128)} %refs_8_.5), custom_call_target="tpu_custom_call" | custom-call | flops 1000 | bytes 1000 | tf_op jit(solution)/shard_map/pack/pallas_call | solution.py:1209
  2.9 2.9 %collective-permute-start.1 = (bf16[2720,128]{1,0:T(8,128)(2,1)}, bf16[2720,128]{1,0:T(8,128)(2,1)S(1)}, u32[]{:S(2)}, u32[]{:S(2)}) collective-permute-start(bf16[2720,128]{1,0:T(8,128)(2,1)} %pack.1.refs_1_.refs_6_), channel_id=1, source_target_pairs={{0,2},{1,3},{2,0},{3,1},{4,6},{5,7},{6,4},{7,5},{8,10},{9,11},{10,... | collective-permute-start | bytes 2088968 | tf_op jit(solution)/shard_map/ppermute | solution.py:1288
  5.9 4.6 %flow_pre.1 = (f32[112,512]{1,0:T(8,128)S(1)}, f32[168,128]{1,0:T(8,128)S(1)}, f32[320,128]{1,0:T(8,128)S(1)}) custom-call(s32[2]{0:T(128)S(1)} %copy-done.19, s32[2,2]{1,0:T(2,128)S(1)} %copy-done.17, f32[3,2,1024]{2,1,0:T(2,128)S(1)} %copy-done.12, f32[3852]{0:T(1024)S(1)} %copy-done.10), custom_call_target="tpu_custom_call" | custom-call | flops 1000 | bytes 1000 | tf_op jit(solution)/shard_map/flow_pre/pallas_call | solution.py:1209
  10.6 11.2 %collective-permute-done.1.refs_0_.refs_3_.refs_8_ = bf16[2720,128]{1,0:T(8,128)(2,1)S(1)} collective-permute-done((bf16[2720,128]{1,0:T(8,128)(2,1)}, bf16[2720,128]{1,0:T(8,128)(2,1)S(1)}, u32[]{:S(2)}, u32[]{:S(2)}) %collective-permute-start.1) | collective-permute-done | bytes 696352 | tf_op jit(solution)/shard_map/ppermute | solution.py:1288
  21.8 0.9 %copy.41 = (bf16[2720,128]{1,0:T(8,128)(2,1)}, f32[112,512]{1,0:T(8,128)S(1)}, f32[168,128]{1,0:T(8,128)S(1)}, f32[320,128]{1,0:T(8,128)S(1)}) custom-call(bf16[2720,128]{1,0:T(8,128)(2,1)S(1)} %collective-permute-done.1.refs_0_.refs_3_.refs_8_, f32[112,512]{1,0:T(8,128)S(1)} %get-tuple-element.83.refs_1_, f32[168,128]{1,0:T(8,128)S(1)} %get-tuple-element.84.refs_2_, ...), custom_call_target="tpu_custom_call" | custom-call | flops 1000 | bytes 1000 | tf_op jit(solution)/shard_map/copy/pallas_call | solution.py:1209
  22.7 2.4 %collective-permute-done.2.refs_4_.refs_9_ = bf16[2720,128]{1,0:T(8,128)(2,1)S(1)} collective-permute-done((bf16[2720,128]{1,0:T(8,128)(2,1)}, bf16[2720,128]{1,0:T(8,128)(2,1)S(1)}, u32[]{:S(2)}, u32[]{:S(2)}) %collective-permute-start.2) | collective-permute-done | bytes 696352 | tf_op jit(solution)/shard_map/ppermute | solution.py:1288
  25.1 4.7 %nets_a.1 = (f32[2,1536,128]{2,1,0:T(8,128)S(1)}, f32[2,1536,128]{2,1,0:T(8,128)S(1)}, f32[40,512]{1,0:T(8,128)S(1)}, f32[64,128]{1,0:T(8,128)S(1)}) custom-call(s32[8,128]{1,0:T(8,128)S(1)} %iota.7.refs_0_, bf16[2720,128]{1,0:T(8,128)(2,1)S(1)} %copy-done, bf16[2720,128]{1,0:T(8,128)(2,1)S(1)} %collective-permute-done.refs_2_.refs_7_, ...), custom_call_target="tpu_custom_call" | custom-call | flops 1000 | bytes 1000 | tf_op jit(solution)/shard_map/nets_a/pallas_call | solution.py:1209
  29.8 0.2 collective-permute-start.3
  30.0 2.4 %nets_b.1 = (f32[2,1216,128]{2,1,0:T(8,128)S(1)}, f32[2,1216,128]{2,1,0:T(8,128)S(1)}, f32[120,128]{1,0:T(8,128)S(1)}) custom-call(s32[8,128]{1,0:T(8,128)S(1)} %iota.7.refs_0_, bf16[2720,128]{1,0:T(8,128)(2,1)S(1)} %copy-done, bf16[2720,128]{1,0:T(8,128)(2,1)S(1)} %collective-permute-done.refs_2_.refs_7_, ...), custom_call_target="tpu_custom_call" | custom-call | flops 1000 | bytes 1000 | tf_op jit(solution)/shard_map/nets_b/pallas_call | solution.py:1209
  32.4 0.4 collective-permute-start.7
  32.9 0.4 collective-permute-done.3.refs_2_
  33.3 0.6 square_a.1
  33.9 1.7 %collective-permute-start.4 = (bf16[816,128]{1,0:T(8,128)(2,1)S(1)}, bf16[816,128]{1,0:T(8,128)(2,1)S(1)}, u32[]{:S(2)}, u32[]{:S(2)}) collective-permute-start(bf16[816,128]{1,0:T(8,128)(2,1)S(1)} %get-tuple-element.94), channel_id=1, source_target_pairs={{0,2},{1,3},{2,0},{3,1},{4,6},{5,7},{6,4},{7,5},{8,10},{9,11},{10,... | collective-permute-start | bytes 626696 | tf_op jit(solution)/shard_map/ppermute | solution.py:1288
  35.6 1.5 %collective-permute-start.5 = (bf16[816,128]{1,0:T(8,128)(2,1)S(1)}, bf16[816,128]{1,0:T(8,128)(2,1)S(1)}, u32[]{:S(2)}, u32[]{:S(2)}) collective-permute-start(bf16[816,128]{1,0:T(8,128)(2,1)S(1)} %get-tuple-element.95), channel_id=1, source_target_pairs={{0,4},{1,5},{2,6},{3,7},{4,0},{5,1},{6,2},{7,3},{8,12},{9,13},{10,... | collective-permute-start | bytes 626696 | tf_op jit(solution)/shard_map/ppermute | solution.py:1288
  37.2 0.3 collective-permute-start.6
  37.5 3.4 %flow_back.1.refs_3_ = f32[40,128]{1,0:T(8,128)S(1)} custom-call(f32[112,512]{1,0:T(8,128)S(1)} %get-tuple-element.87.refs_5_.refs_0_, f32[168,128]{1,0:T(8,128)S(1)} %get-tuple-element.88.refs_6_.refs_1_, f32[320,128]{1,0:T(8,128)S(1)} %get-tuple-element.91.refs_5_.refs_2_, f32[40,512]{1,0:T(8,128)S(1)} %get-tuple-element.98.refs_3_, ...), custom_call_target="tpu_custom_call" | custom-call | flops 1000 | bytes 1000 | tf_op jit(solution)/shard_map/flow_back/pallas_call | solution.py:1209
  40.8 0.5 square_b.1
  41.3 1.7 %collective-permute-start.9 = (bf16[688,128]{1,0:T(8,128)(2,1)S(1)}, bf16[688,128]{1,0:T(8,128)(2,1)S(1)}, u32[]{:S(2)}, u32[]{:S(2)}) collective-permute-start(bf16[688,128]{1,0:T(8,128)(2,1)S(1)} %get-tuple-element.105), channel_id=1, source_target_pairs={{0,2},{1,3},{2,0},{3,1},{4,6},{5,7},{6,4},{7,5},{8,10},{9,11},{10,... | collective-permute-start | bytes 528392 | tf_op jit(solution)/shard_map/ppermute | solution.py:1288
  43.1 1.5 %collective-permute-start.10 = (bf16[688,128]{1,0:T(8,128)(2,1)S(1)}, bf16[688,128]{1,0:T(8,128)(2,1)S(1)}, u32[]{:S(2)}, u32[]{:S(2)}) collective-permute-start(bf16[688,128]{1,0:T(8,128)(2,1)S(1)} %get-tuple-element.106), channel_id=1, source_target_pairs={{0,4},{1,5},{2,6},{3,7},{4,0},{5,1},{6,2},{7,3},{8,12},{9,13},{10,... | collective-permute-start | bytes 528392 | tf_op jit(solution)/shard_map/ppermute | solution.py:1288
  44.6 0.3 collective-permute-start.11
  44.9 2.3 %collective-permute-done.5.refs_3_ = bf16[816,128]{1,0:T(8,128)(2,1)S(1)} collective-permute-done((bf16[816,128]{1,0:T(8,128)(2,1)S(1)}, bf16[816,128]{1,0:T(8,128)(2,1)S(1)}, u32[]{:S(2)}, u32[]{:S(2)}) %collective-permute-start.5) | collective-permute-done | bytes 208928 | tf_op jit(solution)/shard_map/ppermute | solution.py:1288
  47.2 0.4 collective-permute-done.6.refs_4_
  47.6 0.5 column_a.1
  48.1 1.6 %collective-permute-start.8 = (bf16[416,128]{1,0:T(8,128)(2,1)S(1)}, bf16[416,128]{1,0:T(8,128)(2,1)S(1)}, u32[]{:S(2)}, u32[]{:S(2)}) collective-permute-start(bf16[416,128]{1,0:T(8,128)(2,1)S(1)} %get-tuple-element.103), channel_id=1, source_target_pairs={{0,8},{1,9},{2,10},{3,11},{4,12},{5,13},{6,14},{7,15},{8,0},{9,1},... | collective-permute-start | bytes 319496 | tf_op jit(solution)/shard_map/ppermute | solution.py:1288
  49.8 0.5 collective-permute-done.9.refs_3_
  50.3 4.3 %collective-permute-done.10.refs_4_ = bf16[688,128]{1,0:T(8,128)(2,1)S(1)} collective-permute-done((bf16[688,128]{1,0:T(8,128)(2,1)S(1)}, bf16[688,128]{1,0:T(8,128)(2,1)S(1)}, u32[]{:S(2)}, u32[]{:S(2)}) %collective-permute-start.10) | collective-permute-done | bytes 176160 | tf_op jit(solution)/shard_map/ppermute | solution.py:1288
  54.6 0.4 column_b.1
  55.2 2.7 %collective-permute-start.12 = (bf16[416,128]{1,0:T(8,128)(2,1)S(1)}, bf16[416,128]{1,0:T(8,128)(2,1)S(1)}, u32[]{:S(2)}, u32[]{:S(2)}) collective-permute-start(bf16[416,128]{1,0:T(8,128)(2,1)S(1)} %code_a.1.refs_4_.refs_1_), channel_id=1, source_target_pairs={{0,16},{1,17},{2,18},{3,19},{4,20},{5,21},{6,22},{7,23},{8,24},{9,... | collective-permute-start | bytes 319496 | tf_op jit(solution)/shard_map/ppermute | solution.py:1288
  57.8 1.6 %collective-permute-start.13 = (bf16[368,128]{1,0:T(8,128)(2,1)S(1)}, bf16[368,128]{1,0:T(8,128)(2,1)S(1)}, u32[]{:S(2)}, u32[]{:S(2)}) collective-permute-start(bf16[368,128]{1,0:T(8,128)(2,1)S(1)} %get-tuple-element.110), channel_id=1, source_target_pairs={{0,8},{1,9},{2,10},{3,11},{4,12},{5,13},{6,14},{7,15},{8,0},{9,1},... | collective-permute-start | bytes 282632 | tf_op jit(solution)/shard_map/ppermute | solution.py:1288
  59.4 4.1 %collective-permute-done.13.refs_3_ = bf16[368,128]{1,0:T(8,128)(2,1)S(1)} collective-permute-done((bf16[368,128]{1,0:T(8,128)(2,1)S(1)}, bf16[368,128]{1,0:T(8,128)(2,1)S(1)}, u32[]{:S(2)}, u32[]{:S(2)}) %collective-permute-start.13) | collective-permute-done | bytes 94240 | tf_op jit(solution)/shard_map/ppermute | solution.py:1288
  63.5 0.3 code_b.1.refs_3_.refs_1_
  63.9 0.2 recode_4_a.1.refs_3_.refs_1_
  64.1 1.5 %collective-permute-start.16 = (bf16[416,128]{1,0:T(8,128)(2,1)S(1)}, bf16[416,128]{1,0:T(8,128)(2,1)S(1)}, u32[]{:S(2)}, u32[]{:S(2)}) collective-permute-start(bf16[416,128]{1,0:T(8,128)(2,1)S(1)} %recode_4_a.1.refs_3_.refs_1_), channel_id=1, source_target_pairs={{0,12},{1,13},{2,14},{3,15},{4,8},{5,9},{6,10},{7,11},{8,4},{9,5},... | collective-permute-start | bytes 319496 | tf_op jit(solution)/shard_map/ppermute | solution.py:1288
  65.6 1.6 %collective-permute-start.17 = (bf16[368,128]{1,0:T(8,128)(2,1)S(1)}, bf16[368,128]{1,0:T(8,128)(2,1)S(1)}, u32[]{:S(2)}, u32[]{:S(2)}) collective-permute-start(bf16[368,128]{1,0:T(8,128)(2,1)S(1)} %code_b.1.refs_3_.refs_1_), channel_id=1, source_target_pairs={{0,16},{1,17},{2,18},{3,19},{4,20},{5,21},{6,22},{7,23},{8,24},{9,... | collective-permute-start | bytes 282632 | tf_op jit(solution)/shard_map/ppermute | solution.py:1288
  67.2 1.8 %collective-permute-start.15 = (bf16[416,128]{1,0:T(8,128)(2,1)S(1)}, bf16[416,128]{1,0:T(8,128)(2,1)S(1)}, u32[]{:S(2)}, u32[]{:S(2)}) collective-permute-start(bf16[416,128]{1,0:T(8,128)(2,1)S(1)} %recode_4_a.1.refs_3_.refs_1_), channel_id=1, source_target_pairs={{0,4},{1,5},{2,6},{3,7},{4,0},{5,1},{6,2},{7,3},{8,12},{9,13},{10,... | collective-permute-start | bytes 319496 | tf_op jit(solution)/shard_map/ppermute | solution.py:1288
  69.1 3.9 %collective-permute-done.17.refs_2_ = bf16[368,128]{1,0:T(8,128)(2,1)S(1)} collective-permute-done((bf16[368,128]{1,0:T(8,128)(2,1)S(1)}, bf16[368,128]{1,0:T(8,128)(2,1)S(1)}, u32[]{:S(2)}, u32[]{:S(2)}) %collective-permute-start.17) | collective-permute-done | bytes 94240 | tf_op jit(solution)/shard_map/ppermute | solution.py:1288
  73.1 0.9 collective-permute-start.20
  73.9 1.1 %collective-permute-start.19 = (bf16[368,128]{1,0:T(8,128)(2,1)S(1)}, bf16[368,128]{1,0:T(8,128)(2,1)S(1)}, u32[]{:S(2)}, u32[]{:S(2)}) collective-permute-start(bf16[368,128]{1,0:T(8,128)(2,1)S(1)} %recode_4_b.1.refs_5_.refs_1_), channel_id=1, source_target_pairs={{0,4},{1,5},{2,6},{3,7},{4,0},{5,1},{6,2},{7,3},{8,12},{9,13},{10,... | collective-permute-start | bytes 282632 | tf_op jit(solution)/shard_map/ppermute | solution.py:1288
  75.1 1.6 %collective-permute-start.18 = (bf16[368,128]{1,0:T(8,128)(2,1)S(1)}, bf16[368,128]{1,0:T(8,128)(2,1)S(1)}, u32[]{:S(2)}, u32[]{:S(2)}) collective-permute-start(bf16[368,128]{1,0:T(8,128)(2,1)S(1)} %recode_4_b.1.refs_5_.refs_1_), channel_id=1, source_target_pairs={{0,8},{1,9},{2,10},{3,11},{4,12},{5,13},{6,14},{7,15},{8,0},{9,1},... | collective-permute-start | bytes 282632 | tf_op jit(solution)/shard_map/ppermute | solution.py:1288
  76.8 1.9 %collective-permute-done.20.refs_4_ = bf16[368,128]{1,0:T(8,128)(2,1)S(1)} collective-permute-done((bf16[368,128]{1,0:T(8,128)(2,1)S(1)}, bf16[368,128]{1,0:T(8,128)(2,1)S(1)}, u32[]{:S(2)}, u32[]{:S(2)}) %collective-permute-start.20) | collective-permute-done | bytes 94240 | tf_op jit(solution)/shard_map/ppermute | solution.py:1288
  78.7 0.8 collective-permute-done.19.refs_3_
  79.9 2.1 %norms.1 = (f32[378,128]{1,0:T(8,128)S(1)}, f32[3,512,128]{2,1,0:T(8,128)S(1)}, f32[756,128]{1,0:T(8,128)S(1)}, f32[6,128]{1,0:T(8,128)S(1)}, f32[378,128]{1,0:T...) custom-call(f32[1536,128]{1,0:T(8,128)S(1)} %decode_a.1.refs_5_.refs, ...), custom_call_target="tpu_custom_call" | custom-call | flops 1000 | bytes 1000 | tf_op jit(solution)/shard_map/norms/pallas_call | solution.py:1209
  82.0 0.7 collective-permute-start.22
  82.7 1.2 %collective-permute-start.21 = (f32[56,128]{1,0:T(8,128)S(1)}, f32[56,128]{1,0:T(8,128)S(1)}, u32[]{:S(2)}, u32[]{:S(2)}) collective-permute-start(f32[56,128]{1,0:T(8,128)S(1)} %get-tuple-element.113.refs_1_), channel_id=1, source_target_pairs={{0,1},{1,0},{2,3},{3,2},{4,5},{5,4},{6,7},{7,6},{8,9},{9,8},{10,11... | collective-permute-start | bytes 86024 | tf_op jit(solution)/shard_map/ppermute | solution.py:1288
  83.9 1.8 %moments.1 = (f32[378,128]{1,0:T(8,128)}, f32[3,512,128]{2,1,0:T(8,128)}, f32[756,128]{1,0:T(8,128)}, f32[3,2,128]{2,1,0:T(2,128)}, f32[378,128]{1,0:T(8,128)}, ...) custom-call(f32[378,128]{1,0:T(8,128)S(1)} %get-tuple-element.118.refs_0_, ...), custom_call_target="tpu_custom_call" | custom-call | flops 1000 | bytes 1000 | tf_op jit(solution)/shard_map/moments/pallas_call | solution.py:1209
  85.6 0.3 collective-permute-done.22.refs_3_
  86.0 0.7 copy-done.18
  86.7 1.7 %apply.1 = (f32[378,128]{1,0:T(8,128)}, f32[3,512,128]{2,1,0:T(8,128)}, f32[756,128]{1,0:T(8,128)}, f32[3,2,128]{2,1,0:T(2,128)}, f32[3852]{0:T(1024)}, /*index=...) custom-call(s32[8,128]{1,0:T(8,128)S(1)} %iota.7.refs_0_, ...), custom_call_target="tpu_custom_call" | custom-call | flops 1000 | bytes 1000 | tf_op jit(solution)/shard_map/apply/pallas_call | solution.py:1209
  (61 shorter events, 0.9 us)
Async XLA Ops:
  0.7 5.2 %copy-start.17 = (s32[2,2]{1,0:T(2,128)S(1)}, s32[2,2]{1,0:T(2,128)}, u32[]{:S(2)}) copy-start(s32[2,2]{1,0:T(2,128)} %refs_1_.3) | copy-start | bytes 52
  0.7 5.2 %copy-start.10 = (f32[3852]{0:T(1024)S(1)}, f32[3852]{0:T(1024)}, u32[]{:S(2)}) copy-start(f32[3852]{0:T(1024)} %refs_13_.1) | copy-start | bytes 46228
  0.7 5.2 %copy-start.19 = (s32[2]{0:T(128)S(1)}, s32[2]{0:T(128)}, u32[]{:S(2)}) copy-start(s32[2]{0:T(128)} %refs_0_.3) | copy-start | bytes 28
  0.7 5.2 %copy-start.12 = (f32[3,2,1024]{2,1,0:T(2,128)S(1)}, f32[3,2,1024]{2,1,0:T(2,128)}, u32[]{:S(2)}) copy-start(f32[3,2,1024]{2,1,0:T(2,128)} %refs_2_.3) | copy-start | bytes 73732
  2.9 22.2 %copy-start = (bf16[2720,128]{1,0:T(8,128)(2,1)S(1)}, bf16[2720,128]{1,0:T(8,128)(2,1)}, u32[]{:S(2)}) copy-start(bf16[2720,128]{1,0:T(8,128)(2,1)} %pack.1.refs_1_.refs_6_) | copy-start | bytes 2088964
  2.9 18.8 %collective-permute-start.1 = (bf16[2720,128]{1,0:T(8,128)(2,1)}, bf16[2720,128]{1,0:T(8,128)(2,1)S(1)}, u32[]{:S(2)}, u32[]{:S(2)}) collective-permute-start(bf16[2720,128]{1,0:T(8,128)(2,1)} %pack.1.refs_1_.refs_6_), channel_id=1, source_target_pairs={{0,2},{1,3},{2,0},{3,1},{4,6},{5,7},{6,4},{7,5},{8,10},{9,11},{10,... | collective-permute-start | bytes 2088968 | tf_op jit(solution)/shard_map/ppermute | solution.py:1288
  5.9 16.8 %collective-permute-start = (bf16[2720,128]{1,0:T(8,128)(2,1)}, bf16[2720,128]{1,0:T(8,128)(2,1)S(1)}, u32[]{:S(2)}, u32[]{:S(2)}) collective-permute-start(bf16[2720,128]{1,0:T(8,128)(2,1)} %pack.1.refs_1_.refs_6_), channel_id=1, source_target_pairs={{0,1},{1,0},{2,3},{3,2},{4,5},{5,4},{6,7},{7,6},{8,9},{9,8},{10,11... | collective-permute-start | bytes 2088968 | tf_op jit(solution)/shard_map/ppermute | solution.py:1288
  22.7 2.4 %collective-permute-start.2 = (bf16[2720,128]{1,0:T(8,128)(2,1)}, bf16[2720,128]{1,0:T(8,128)(2,1)S(1)}, u32[]{:S(2)}, u32[]{:S(2)}) collective-permute-start(bf16[2720,128]{1,0:T(8,128)(2,1)} %get-tuple-element.86), channel_id=1, source_target_pairs={{0,1},{1,0},{2,3},{3,2},{4,5},{5,4},{6,7},{7,6},{8,9},{9,8},{10,11... | collective-permute-start | bytes 2088968 | tf_op jit(solution)/shard_map/ppermute | solution.py:1288
  29.8 3.5 %collective-permute-start.3 = (f32[2,1536,128]{2,1,0:T(8,128)S(1)}, f32[2,1536,128]{2,1,0:T(8,128)S(1)}, u32[]{:S(2)}, u32[]{:S(2)}) collective-permute-start(f32[2,1536,128]{2,1,0:T(8,128)S(1)} %get-tuple-element.90), channel_id=1, source_target_pairs={{0,1},{1,0},{2,3},{3,2},{4,5},{5,4},{6,7},{7,6},{8,9},{9,8},{10,11... | collective-permute-start | bytes 4718600 | tf_op jit(solution)/shard_map/ppermute | solution.py:1288
  32.4 8.4 %collective-permute-start.7 = (f32[2,1216,128]{2,1,0:T(8,128)S(1)}, f32[2,1216,128]{2,1,0:T(8,128)S(1)}, u32[]{:S(2)}, u32[]{:S(2)}) collective-permute-start(f32[2,1216,128]{2,1,0:T(8,128)S(1)} %get-tuple-element.97), channel_id=1, source_target_pairs={{0,1},{1,0},{2,3},{3,2},{4,5},{5,4},{6,7},{7,6},{8,9},{9,8},{10,11... | collective-permute-start | bytes 3735560 | tf_op jit(solution)/shard_map/ppermute | solution.py:1288
  33.9 10.7 %collective-permute-start.4 = (bf16[816,128]{1,0:T(8,128)(2,1)S(1)}, bf16[816,128]{1,0:T(8,128)(2,1)S(1)}, u32[]{:S(2)}, u32[]{:S(2)}) collective-permute-start(bf16[816,128]{1,0:T(8,128)(2,1)S(1)} %get-tuple-element.94), channel_id=1, source_target_pairs={{0,2},{1,3},{2,0},{3,1},{4,6},{5,7},{6,4},{7,5},{8,10},{9,11},{10,... | collective-permute-start | bytes 626696 | tf_op jit(solution)/shard_map/ppermute | solution.py:1288
  35.6 11.6 %collective-permute-start.5 = (bf16[816,128]{1,0:T(8,128)(2,1)S(1)}, bf16[816,128]{1,0:T(8,128)(2,1)S(1)}, u32[]{:S(2)}, u32[]{:S(2)}) collective-permute-start(bf16[816,128]{1,0:T(8,128)(2,1)S(1)} %get-tuple-element.95), channel_id=1, source_target_pairs={{0,4},{1,5},{2,6},{3,7},{4,0},{5,1},{6,2},{7,3},{8,12},{9,13},{10,... | collective-permute-start | bytes 626696 | tf_op jit(solution)/shard_map/ppermute | solution.py:1288
  37.2 10.5 %collective-permute-start.6 = (bf16[816,128]{1,0:T(8,128)(2,1)S(1)}, bf16[816,128]{1,0:T(8,128)(2,1)S(1)}, u32[]{:S(2)}, u32[]{:S(2)}) collective-permute-start(bf16[816,128]{1,0:T(8,128)(2,1)S(1)} %get-tuple-element.96), channel_id=1, source_target_pairs={{0,6},{1,7},{2,4},{3,5},{4,2},{5,3},{6,0},{7,1},{8,14},{9,15},{10,... | collective-permute-start | bytes 626696 | tf_op jit(solution)/shard_map/ppermute | solution.py:1288
  41.3 9.0 %collective-permute-start.9 = (bf16[688,128]{1,0:T(8,128)(2,1)S(1)}, bf16[688,128]{1,0:T(8,128)(2,1)S(1)}, u32[]{:S(2)}, u32[]{:S(2)}) collective-permute-start(bf16[688,128]{1,0:T(8,128)(2,1)S(1)} %get-tuple-element.105), channel_id=1, source_target_pairs={{0,2},{1,3},{2,0},{3,1},{4,6},{5,7},{6,4},{7,5},{8,10},{9,11},{10,... | collective-permute-start | bytes 528392 | tf_op jit(solution)/shard_map/ppermute | solution.py:1288
  43.1 11.5 %collective-permute-start.10 = (bf16[688,128]{1,0:T(8,128)(2,1)S(1)}, bf16[688,128]{1,0:T(8,128)(2,1)S(1)}, u32[]{:S(2)}, u32[]{:S(2)}) collective-permute-start(bf16[688,128]{1,0:T(8,128)(2,1)S(1)} %get-tuple-element.106), channel_id=1, source_target_pairs={{0,4},{1,5},{2,6},{3,7},{4,0},{5,1},{6,2},{7,3},{8,12},{9,13},{10,... | collective-permute-start | bytes 528392 | tf_op jit(solution)/shard_map/ppermute | solution.py:1288
  44.6 10.0 %collective-permute-start.11 = (bf16[688,128]{1,0:T(8,128)(2,1)S(1)}, bf16[688,128]{1,0:T(8,128)(2,1)S(1)}, u32[]{:S(2)}, u32[]{:S(2)}) collective-permute-start(bf16[688,128]{1,0:T(8,128)(2,1)S(1)} %get-tuple-element.107), channel_id=1, source_target_pairs={{0,6},{1,7},{2,4},{3,5},{4,2},{5,3},{6,0},{7,1},{8,14},{9,15},{10,... | collective-permute-start | bytes 528392 | tf_op jit(solution)/shard_map/ppermute | solution.py:1288
  48.1 6.9 %collective-permute-start.8 = (bf16[416,128]{1,0:T(8,128)(2,1)S(1)}, bf16[416,128]{1,0:T(8,128)(2,1)S(1)}, u32[]{:S(2)}, u32[]{:S(2)}) collective-permute-start(bf16[416,128]{1,0:T(8,128)(2,1)S(1)} %get-tuple-element.103), channel_id=1, source_target_pairs={{0,8},{1,9},{2,10},{3,11},{4,12},{5,13},{6,14},{7,15},{8,0},{9,1},... | collective-permute-start | bytes 319496 | tf_op jit(solution)/shard_map/ppermute | solution.py:1288
  55.0 24.8 %copy-start.8 = (f32[378,128]{1,0:T(8,128)S(1)}, f32[378,128]{1,0:T(8,128)}, u32[]{:S(2)}) copy-start(f32[378,128]{1,0:T(8,128)} %refs_4_.5) | copy-start | bytes 580612
  55.0 24.8 %copy-start.9 = (f32[378,128]{1,0:T(8,128)S(1)}, f32[378,128]{1,0:T(8,128)}, u32[]{:S(2)}) copy-start(f32[378,128]{1,0:T(8,128)} %refs_8_.4) | copy-start | bytes 580612
  55.2 8.7 %collective-permute-start.12 = (bf16[416,128]{1,0:T(8,128)(2,1)S(1)}, bf16[416,128]{1,0:T(8,128)(2,1)S(1)}, u32[]{:S(2)}, u32[]{:S(2)}) collective-permute-start(bf16[416,128]{1,0:T(8,128)(2,1)S(1)} %code_a.1.refs_4_.refs_1_), channel_id=1, source_target_pairs={{0,16},{1,17},{2,18},{3,19},{4,20},{5,21},{6,22},{7,23},{8,24},{9,... | collective-permute-start | bytes 319496 | tf_op jit(solution)/shard_map/ppermute | solution.py:1288
  57.8 5.7 %collective-permute-start.13 = (bf16[368,128]{1,0:T(8,128)(2,1)S(1)}, bf16[368,128]{1,0:T(8,128)(2,1)S(1)}, u32[]{:S(2)}, u32[]{:S(2)}) collective-permute-start(bf16[368,128]{1,0:T(8,128)(2,1)S(1)} %get-tuple-element.110), channel_id=1, source_target_pairs={{0,8},{1,9},{2,10},{3,11},{4,12},{5,13},{6,14},{7,15},{8,0},{9,1},... | collective-permute-start | bytes 282632 | tf_op jit(solution)/shard_map/ppermute | solution.py:1288
  63.5 16.3 %copy-start.6 = (f32[128,756]{0,1:T(8,128)S(1)}, f32[128,756]{0,1:T(8,128)}, u32[]{:S(2)}) copy-start(f32[128,756]{0,1:T(8,128)} %param.28) | copy-start | bytes 1161220
  63.5 16.3 %copy-start.7 = (f32[128,756]{0,1:T(8,128)S(1)}, f32[128,756]{0,1:T(8,128)}, u32[]{:S(2)}) copy-start(f32[128,756]{0,1:T(8,128)} %param.33) | copy-start | bytes 1161220
  63.8 16.0 %copy-start.1 = (f32[3,512,128]{2,1,0:T(8,128)S(1)}, f32[3,512,128]{2,1,0:T(8,128)}, u32[]{:S(2)}) copy-start(f32[3,512,128]{2,1,0:T(8,128)} %refs_6_.3) | copy-start | bytes 2359300
  63.8 16.0 %copy-start.2 = (f32[128,756]{0,1:T(8,128)S(1)}, f32[128,756]{0,1:T(8,128)}, u32[]{:S(2)}) copy-start(f32[128,756]{0,1:T(8,128)} %param.23) | copy-start | bytes 1161220
  63.8 16.0 %copy-start.3 = (f32[3,512,128]{2,1,0:T(8,128)S(1)}, f32[3,512,128]{2,1,0:T(8,128)}, u32[]{:S(2)}) copy-start(f32[3,512,128]{2,1,0:T(8,128)} %refs_5_.2) | copy-start | bytes 2359300
  63.8 16.0 %copy-start.4 = (f32[3,512,128]{2,1,0:T(8,128)S(1)}, f32[3,512,128]{2,1,0:T(8,128)}, u32[]{:S(2)}) copy-start(f32[3,512,128]{2,1,0:T(8,128)} %refs_9_.1) | copy-start | bytes 2359300
  63.8 16.0 %copy-start.5 = (f32[378,128]{1,0:T(8,128)S(1)}, f32[378,128]{1,0:T(8,128)}, u32[]{:S(2)}) copy-start(f32[378,128]{1,0:T(8,128)} %refs_5_.3) | copy-start | bytes 580612
  63.9 16.0 %copy-start.11 = (f32[3,2,128]{2,1,0:T(2,128)S(1)}, f32[3,2,128]{2,1,0:T(2,128)}, u32[]{:S(2)}) copy-start(f32[3,2,128]{2,1,0:T(2,128)} %refs_8_.5) | copy-start | bytes 9220
  63.9 16.0 %copy-start.15 = (f32[3,2,128]{2,1,0:T(2,128)S(1)}, f32[3,2,128]{2,1,0:T(2,128)}, u32[]{:S(2)}) copy-start(f32[3,2,128]{2,1,0:T(2,128)} %refs_7_.3) | copy-start | bytes 9220
  63.9 16.0 %copy-start.16 = (f32[3,2,128]{2,1,0:T(2,128)S(1)}, f32[3,2,128]{2,1,0:T(2,128)}, u32[]{:S(2)}) copy-start(f32[3,2,128]{2,1,0:T(2,128)} %refs_11_.3) | copy-start | bytes 9220
  64.1 11.0 %collective-permute-start.16 = (bf16[416,128]{1,0:T(8,128)(2,1)S(1)}, bf16[416,128]{1,0:T(8,128)(2,1)S(1)}, u32[]{:S(2)}, u32[]{:S(2)}) collective-permute-start(bf16[416,128]{1,0:T(8,128)(2,1)S(1)} %recode_4_a.1.refs_3_.refs_1_), channel_id=1, source_target_pairs={{0,12},{1,13},{2,14},{3,15},{4,8},{5,9},{6,10},{7,11},{8,4},{9,5},... | collective-permute-start | bytes 319496 | tf_op jit(solution)/shard_map/ppermute | solution.py:1288
  65.6 7.4 %collective-permute-start.17 = (bf16[368,128]{1,0:T(8,128)(2,1)S(1)}, bf16[368,128]{1,0:T(8,128)(2,1)S(1)}, u32[]{:S(2)}, u32[]{:S(2)}) collective-permute-start(bf16[368,128]{1,0:T(8,128)(2,1)S(1)} %code_b.1.refs_3_.refs_1_), channel_id=1, source_target_pairs={{0,16},{1,17},{2,18},{3,19},{4,20},{5,21},{6,22},{7,23},{8,24},{9,... | collective-permute-start | bytes 282632 | tf_op jit(solution)/shard_map/ppermute | solution.py:1288
  67.2 9.4 %collective-permute-start.15 = (bf16[416,128]{1,0:T(8,128)(2,1)S(1)}, bf16[416,128]{1,0:T(8,128)(2,1)S(1)}, u32[]{:S(2)}, u32[]{:S(2)}) collective-permute-start(bf16[416,128]{1,0:T(8,128)(2,1)S(1)} %recode_4_a.1.refs_3_.refs_1_), channel_id=1, source_target_pairs={{0,4},{1,5},{2,6},{3,7},{4,0},{5,1},{6,2},{7,3},{8,12},{9,13},{10,... | collective-permute-start | bytes 319496 | tf_op jit(solution)/shard_map/ppermute | solution.py:1288
  69.0 7.6 %collective-permute-start.14 = (bf16[416,128]{1,0:T(8,128)(2,1)S(1)}, bf16[416,128]{1,0:T(8,128)(2,1)S(1)}, u32[]{:S(2)}, u32[]{:S(2)}) collective-permute-start(bf16[416,128]{1,0:T(8,128)(2,1)S(1)} %recode_4_a.1.refs_3_.refs_1_), channel_id=1, source_target_pairs={{0,8},{1,9},{2,10},{3,11},{4,12},{5,13},{6,14},{7,15},{8,0},{9,1},... | collective-permute-start | bytes 319496 | tf_op jit(solution)/shard_map/ppermute | solution.py:1288
  73.1 5.6 %collective-permute-start.20 = (bf16[368,128]{1,0:T(8,128)(2,1)S(1)}, bf16[368,128]{1,0:T(8,128)(2,1)S(1)}, u32[]{:S(2)}, u32[]{:S(2)}) collective-permute-start(bf16[368,128]{1,0:T(8,128)(2,1)S(1)} %recode_4_b.1.refs_5_.refs_1_), channel_id=1, source_target_pairs={{0,12},{1,13},{2,14},{3,15},{4,8},{5,9},{6,10},{7,11},{8,4},{9,5},... | collective-permute-start | bytes 282632 | tf_op jit(solution)/shard_map/ppermute | solution.py:1288
  73.9 5.6 %collective-permute-start.19 = (bf16[368,128]{1,0:T(8,128)(2,1)S(1)}, bf16[368,128]{1,0:T(8,128)(2,1)S(1)}, u32[]{:S(2)}, u32[]{:S(2)}) collective-permute-start(bf16[368,128]{1,0:T(8,128)(2,1)S(1)} %recode_4_b.1.refs_5_.refs_1_), channel_id=1, source_target_pairs={{0,4},{1,5},{2,6},{3,7},{4,0},{5,1},{6,2},{7,3},{8,12},{9,13},{10,... | collective-permute-start | bytes 282632 | tf_op jit(solution)/shard_map/ppermute | solution.py:1288
  75.1 4.6 %collective-permute-start.18 = (bf16[368,128]{1,0:T(8,128)(2,1)S(1)}, bf16[368,128]{1,0:T(8,128)(2,1)S(1)}, u32[]{:S(2)}, u32[]{:S(2)}) collective-permute-start(bf16[368,128]{1,0:T(8,128)(2,1)S(1)} %recode_4_b.1.refs_5_.refs_1_), channel_id=1, source_target_pairs={{0,8},{1,9},{2,10},{3,11},{4,12},{5,13},{6,14},{7,15},{8,0},{9,1},... | collective-permute-start | bytes 282632 | tf_op jit(solution)/shard_map/ppermute | solution.py:1288
  82.0 3.6 %collective-permute-start.23 = (f32[56,128]{1,0:T(8,128)S(1)}, f32[56,128]{1,0:T(8,128)S(1)}, u32[]{:S(2)}, u32[]{:S(2)}) collective-permute-start(f32[56,128]{1,0:T(8,128)S(1)} %get-tuple-element.113.refs_1_), channel_id=1, source_target_pairs={{0,3},{1,2},{2,1},{3,0},{4,7},{5,6},{6,5},{7,4},{8,11},{9,10},{10,... | collective-permute-start | bytes 86024 | tf_op jit(solution)/shard_map/ppermute | solution.py:1288
  82.0 3.9 %collective-permute-start.22 = (f32[56,128]{1,0:T(8,128)S(1)}, f32[56,128]{1,0:T(8,128)S(1)}, u32[]{:S(2)}, u32[]{:S(2)}) collective-permute-start(f32[56,128]{1,0:T(8,128)S(1)} %get-tuple-element.113.refs_1_), channel_id=1, source_target_pairs={{0,2},{1,3},{2,0},{3,1},{4,6},{5,7},{6,4},{7,5},{8,10},{9,11},{10,... | collective-permute-start | bytes 86024 | tf_op jit(solution)/shard_map/ppermute | solution.py:1288
  82.7 3.3 %collective-permute-start.21 = (f32[56,128]{1,0:T(8,128)S(1)}, f32[56,128]{1,0:T(8,128)S(1)}, u32[]{:S(2)}, u32[]{:S(2)}) collective-permute-start(f32[56,128]{1,0:T(8,128)S(1)} %get-tuple-element.113.refs_1_), channel_id=1, source_target_pairs={{0,1},{1,0},{2,3},{3,2},{4,5},{5,4},{6,7},{7,6},{8,9},{9,8},{10,11... | collective-permute-start | bytes 86024 | tf_op jit(solution)/shard_map/ppermute | solution.py:1288
  83.9 2.1 %copy-start.13 = (f32[3852]{0:T(1024)S(1)}, f32[3852]{0:T(1024)}, u32[]{:S(2)}) copy-start(f32[3852]{0:T(1024)} %refs_14_.3) | copy-start | bytes 46228
  83.9 2.1 %copy-start.14 = (f32[3852]{0:T(1024)S(1)}, f32[3852]{0:T(1024)}, u32[]{:S(2)}) copy-start(f32[3852]{0:T(1024)} %refs_15_.1) | copy-start | bytes 46228
  86.0 0.7 copy-start.18

commit v5 on v4

--- a/solution.py
+++ b/solution.py
@@ -78,7 +78,11 @@
     return sum(pack_rows(other) for other in range(LEVELS - 1, level, -1))
 
 
-CHUNKS = ((0, 1), (2,))
+CHUNKS = ((2,), (0, 1))
+
+
+def gather_start(level):
+    return pack_start(level) - (0 if level in CHUNKS[0] else pack_start(CHUNKS[0][0] - 1))
 
 
 def chunk_of(level):
@@ -426,7 +430,7 @@
     return total
 
 
-def pack_kernel(valid_ref, conv_in_ref, mixer_ref, conv_out_ref, bias_ref, whole_ref):
+def pack_kernel(valid_ref, conv_in_ref, mixer_ref, conv_out_ref, bias_ref, whole_ref, *part_refs):
     in_start = 0
     out_start = 0
     for level in range(LEVELS):
@@ -459,9 +463,13 @@
     for place in (1, 2):
         digits = jnp.where(lane == place, lax.shift_right_logical(pixels, 7 * place) & 127, digits)
     whole_ref[pack_start(-1) :, :] = digits.astype(F32).astype(BF16)
-
-
-def flow_pre_kernel(seed_ref, valid_ref, image_ref, flow_ref, *out_refs):
+    cut = part_refs[0].shape[0]
+    part_refs[0][...] = whole_ref[0:cut, :]
+    part_refs[1][...] = whole_ref[cut:, :]
+
+
+def flow_pre_kernel(seed_ref, valid_ref, image_ref, flow_ref, packed_ref, *out_refs):
+    out_refs[LEVELS][...] = packed_ref[...]
     images = image_ref.shape[1]
     flat = to_flat_rows(flow_ref[...])
     turned = jnp.concatenate([flat, jnp.zeros((LANE - FLOW_ROWS, LANE), F32)], 0).T
@@ -568,8 +576,13 @@
 def net_kernel(level, images, narrow, *refs):
     is_last = level == LEVELS - 1
     index_ref = refs[0]
-    weight_refs = refs[1 : 1 + narrow]
-    base = pack_start(level)
+    weight_refs, tails = refs[1 : 1 + narrow], [None] * narrow
+    if isinstance(weight_refs[-1], tuple):
+        weight_refs, tails[-1] = (*weight_refs[:-1], weight_refs[-1][0]), weight_refs[-1][1]
+    bases = [
+        pack_start(level) if ref.shape[0] > pack_start(-1) else gather_start(level)
+        for ref in weight_refs
+    ]
     out_base = chunk_of(level)[1]
     stage_ref, keep_ref, send_ref, result_ref = refs[1 + narrow : 5 + narrow]
     order_ref, slope_one_ref, slope_two_ref, one_ref, two_ref = refs[5 + narrow :]
@@ -585,13 +598,17 @@
     width = HID // narrow
 
     def weights(start, length):
-        return jnp.concatenate(
-            [ref[base + start : base + start + length, :] for ref in weight_refs], 1
-        )
+        parts = []
+        for ref, base, tail in zip(weight_refs, bases, tails):
+            first = base + start
+            if tail is not None and first >= ref.shape[0]:
+                ref, first = tail, first - ref.shape[0]
+            parts.append(ref[first : first + length, :])
+        return jnp.concatenate(parts, 1)
 
     for r_in in range(narrow):
         for r_out in range(narrow):
-            start = pl.multiple_of(base + top + (me ^ r_in) * width, 16)
+            start = pl.multiple_of(bases[r_out] + top + (me ^ r_in) * width, 16)
             order_ref[r_in * width : (r_in + 1) * width, r_out * LANE : (r_out + 1) * LANE] = (
                 weight_refs[r_out][pl.ds(start, width), :]
             )
@@ -795,8 +812,8 @@
     flat = sum(part[0] for part in parts) + sum(part[1] for part in parts).T[:FLOW_ROWS]
     loss = sum(part[2] for part in parts)
     pixels = jnp.zeros((1, 1), F32)
-    start = pack_start(-1)
     for ref in weights:
+        start = ref.shape[0] - 16
         digits = ref[start : start + 16, :].astype(F32)
         for place in range(3):
             pixels = pixels + 128.0**place * digits[0:1, place : place + 1]
@@ -812,12 +829,15 @@
             ref[:, start:, :] = jnp.zeros((ref.shape[0], rest, LANE), F32)
 
 
-def nets_kernel(chunk, images, narrow, *refs):
+def nets_kernel(chunk, images, narrow, split, *refs):
     levels = CHUNKS[chunk]
     number = len(levels)
     index_ref = refs[0]
     mine = refs[1 : 1 + narrow]
     at = 1 + narrow
+    if split:
+        mine = (*mine[:-1], (mine[-1], refs[at]))
+        at = at + 1
     stages = refs[at : at + number]
     at = at + number
     keep_ref, send_ref = refs[at : at + 2]
@@ -851,6 +871,15 @@
         to_ref[...] = from_ref[...]
 
 
+def split_copy_kernel(from_ref, *refs):
+    half = len(refs) // 2 - 1
+    cut = refs[half].shape[0]
+    refs[half][...] = from_ref[0:cut, :]
+    refs[half + 1][...] = from_ref[cut:, :]
+    for source, target in zip(refs[:half], refs[half + 2 :]):
+        target[...] = source[...]
+
+
 def piece_rows(rows):
     return rows + round_up(rows // CODE_BLOCK, 16)
 
@@ -888,7 +917,16 @@
     return jnp.where((index_ref[1, 0] & bit) != 0, 1, 0)
 
 
-def square_kernel(chunk, index_ref, keep_ref, other_ref, *refs):
+def send_kernel(chunk, index_ref, send_ref, *piece_refs):
+    half = 2 * quarter_rows(chunk)
+    for shard in range(2):
+        for place in range(2):
+            values = send_ref[shard, place * half : (place + 1) * half, :]
+            write_piece(piece_refs[2 * shard + place], 0, values)
+
+
+def square_kernel(chunk, index_ref, keep_ref, *refs):
+    other_refs, total_ref, refs = refs[:4], refs[-1], refs[4:-1]
     flow = None
     if flow_part(chunk):
         flow_ref, mine_ref, own_flow_ref, *sent_refs = refs
@@ -899,11 +937,16 @@
         mine_ref, *sent_refs = refs
     half = 2 * quarter_rows(chunk)
     upper = wide_bit(index_ref, 1)
+    for shard in range(2):
+        for place in range(2):
+            picked = slice(place * half, (place + 1) * half)
+            total_ref[shard, picked, :] = keep_ref[shard, picked, :] + read_piece(
+                other_refs[2 * shard + place], 0, half
+            )
 
     def total(shard, flipped):
         place = 1 - upper if flipped else upper
-        picked = pl.ds(pl.multiple_of(place * half, CODE_BLOCK), half)
-        return keep_ref[shard, picked, :] + other_ref[shard, picked, :]
+        return total_ref[shard, pl.ds(pl.multiple_of(place * half, CODE_BLOCK), half), :]
 
     mine_ref[...] = total(0, 0)
     for ref, (shard, flipped) in zip(sent_refs, ((1, 0), (0, 1), (1, 1))):
@@ -965,6 +1008,21 @@
     write_piece(out_ref, 0, read_piece(mine_ref, 0, rows) + read_piece(other_ref, 0, rows), stats)
 
 
+def pair_kernel(chunk, index_ref, mine_ref, other_ref, out_ref):
+    place = wide_bit(index_ref, 2)
+    out_ref[place] = mine_ref[...]
+    out_ref[1 - place] = other_ref[...]
+
+
+def decode_pairs_kernel(chunk, index_ref, mine_ref, other_ref, out_ref):
+    rows = quarter_rows(chunk)
+    upper = wide_bit(index_ref, 1)
+    for place, ref in ((upper, mine_ref), (1 - upper, other_ref)):
+        for near in range(2):
+            start = pl.multiple_of((2 * place + near) * rows, CODE_BLOCK)
+            out_ref[pl.ds(start, rows), :] = read_piece(ref.at[near], 0, rows)
+
+
 def decode_kernel(chunk, index_ref, *refs):
     parts, outs = refs[:4], refs[4:]
     place = 2 * wide_bit(index_ref, 1) + wide_bit(index_ref, 2)
@@ -985,8 +1043,8 @@
     second_new = SECOND_BETA * second_old + (1.0 - SECOND_BETA) * gradient * gradient
     update = (
         first_new
-        / (1.0 - FIRST_BETA**STEP)
-        / (jnp.sqrt(second_new / (1.0 - SECOND_BETA**STEP)) + EPSILON)
+        * (1.0 / (1.0 - FIRST_BETA**STEP))
+        / (jnp.sqrt(second_new * (1.0 / (1.0 - SECOND_BETA**STEP))) + EPSILON)
         + WEIGHT_DECAY * weight
     )
     return first_new, second_new, update
@@ -1098,6 +1156,7 @@
 def moment_kernel(*refs):
     grads, firsts, seconds = refs[0:4], refs[4:8], refs[8:12]
     new_firsts, new_seconds = refs[12:16], refs[16:20]
+    refs[20][...] = jnp.zeros((8, LANE), F32)
     for grad, first, second, new_first, new_second in zip(
         grads, firsts, seconds, new_firsts, new_seconds
     ):
@@ -1223,25 +1282,27 @@
 
 
 def run_pack(valid_shape, conv_in, mixer, conv_out, hidden_bias):
-    outs = [((pack_start(-1) + 16, LANE), BF16)]
+    cut = sum(pack_rows(level) for level in CHUNKS[0])
+    rows = pack_start(-1) + 16
+    outs = [((size, LANE), BF16) for size in (rows, cut, rows - cut)]
     return call(pack_kernel, outs, (valid_shape,), (conv_in, mixer, conv_out, hidden_bias), name="pack", vmem=56)
 
 
-def run_flow_pre(noise_seeds, valid_shape, images, flow_params, after):
+def run_flow_pre(noise_seeds, valid_shape, images, flow_params, packed):
     count = images.shape[1]
     outs = [((stage_rows(level)["rows"], positions(level, count)), F32) for level in range(LEVELS)]
+    outs.append((packed.shape, BF16))
     return call(
         flow_pre_kernel,
         outs,
         (noise_seeds, valid_shape),
-        (images, flow_params),
+        (images, flow_params, packed),
         name="flow_pre",
-        after=after,
     )
 
 
 def run_nets(chunk, images, index, weights, stages, after):
-    narrow = len(weights)
+    narrow = lax.axis_size("narrow")
     outs = [((narrow // 2, 4 * quarter_rows(chunk), LANE), F32)] * 2
     scratch = []
     for level in CHUNKS[chunk]:
@@ -1249,7 +1310,7 @@
         outs = outs + [((stage_rows(level)["result_rows"], count), F32)]
         scratch = scratch + net_scratch(count)
     return call(
-        functools.partial(nets_kernel, chunk, images, narrow),
+        functools.partial(nets_kernel, chunk, images, narrow, len(weights) > narrow),
         outs,
         (),
         [index] + list(weights) + [stages[level] for level in CHUNKS[chunk]],
@@ -1289,10 +1350,13 @@
 
 
 class Summation:
-    def __init__(self, chunk, index, send):
+    def __init__(self, chunk, index, send, after):
         self.chunk, self.index = chunk, index
-        self.others = [swap(send, 0, 1)]
         rows, more = quarter_rows(chunk), flow_part(chunk)
+        self.kept, self.others = send, ()
+        sent = self.run(send_kernel, [((piece_rows(2 * rows), LANE), BF16)] * 4, "send", after)
+        self.token = sent[0]
+        self.others = [swap(piece, 0, 1) for piece in sent]
         self.own_piece = [((piece_rows(FLOW_ROWS), LANE), BF16)] if more else []
         self.own = ()
         self.square_piece = ((piece_rows(2 * rows + more), LANE), BF16)
@@ -1316,6 +1380,7 @@
             [((rows, LANE), F32)] + self.own_piece + [self.square_piece] * 3,
             (),
             (self.index, keep, *self.others, *flow),
+            [pltpu.VMEM((2, 2 * rows, LANE), F32)],
             name="square_" + "ab"[self.chunk],
             after=after,
         )
@@ -1349,14 +1414,21 @@
             step = 2 * step
             if step < lax.axis_size("wide"):
                 self.others = [swap(self.kept, step, 0)]
-        self.others = [swap(self.kept, 2, 0), swap(self.kept, 1, 0), swap(self.kept, 3, 0)]
-        return self.kept
+        token = self.kept
+        if flow_part(self.chunk):
+            self.others = [swap(self.kept, place, 0) for place in (2, 1, 3)]
+        else:
+            self.others = [swap(self.kept, 2, 0)]
+            (self.kept,) = self.run(pair_kernel, [((2,) + self.piece[0], BF16)], "pair", ())
+            self.others = [swap(self.kept, 1, 0)]
+        return token
 
     def decode(self, after):
         shape = [((4 * quarter_rows(self.chunk), LANE), F32)]
         if flow_part(self.chunk):
             shape.append(((FLOW_ROWS + STATS_ROWS, LANE), F32))
-        return self.run(decode_kernel, shape, "decode", after)
+            return self.run(decode_kernel, shape, "decode", after)
+        return self.run(decode_pairs_kernel, shape, "decode", after)
 
 
 def body(
@@ -1384,28 +1456,41 @@
     row = lax.broadcasted_iota(jnp.int32, (8, LANE), 0)
     index = jnp.where(row == 0, lax.axis_index("narrow"), lax.axis_index("wide")).astype(jnp.int32)
     narrow = lax.axis_size("narrow")
-    (packed,) = run_pack(valid_shape, conv_in, mixer, conv_out, hidden_bias)
+    packed, *parts = run_pack(valid_shape, conv_in, mixer, conv_out, hidden_bias)
     paired = swap(packed, 0, 1)
-    crossed = swap(packed, 0, 2)
-    stages = run_flow_pre(noise_seeds, valid_shape, images, flow_params, ())
-    arrays = (crossed, *stages)
-    copied, *stages = call(
-        copy_kernel, [(array.shape, array.dtype) for array in arrays], (), arrays, name="copy"
-    )
-    gathered = (packed, paired, crossed, swap(copied, 0, 1))
-    keep_one, send, *results = run_nets(0, count, index, gathered, stages, ())
-    one = Summation(0, index, send)
-    keep_two, send, *more = run_nets(1, count, index, gathered, stages, (keep_one,))
-    results = results + more
-    two = Summation(1, index, send)
-    token = one.square(keep_one, (), (keep_two,))
-    flow = run_flow(count, gathered, stages, results, (token,))
+    crossed = [swap(part, 0, 2) for part in parts]
+    *stages, own = run_flow_pre(noise_seeds, valid_shape, images, flow_params, packed)
+    cut = first_rows(CHUNKS[0][0]) + HID
+    shapes = [((rows, LANE), BF16) for rows in (cut, crossed[0].shape[0] - cut)]
+    head, tail, *stages = call(
+        split_copy_kernel,
+        shapes + [(stage.shape, F32) for stage in stages],
+        (),
+        (crossed[0], *stages),
+        name="copy_a",
+    )
+    gathered = (own, paired, crossed[0], swap(head, 0, 1), swap(tail, 0, 1))
+    keep_one, send, *last = run_nets(0, count, index, gathered, stages, ())
+    one = Summation(0, index, send, ())
+    token = one.square(keep_one, (), ())
+    (copied,) = call(
+        copy_kernel,
+        [(crossed[1].shape, BF16)],
+        (),
+        (crossed[1],),
+        name="copy_b",
+        after=(token,),
+    )
+    gathered = (own, paired, crossed[1], swap(copied, 0, 1))
+    keep_two, send, *results = run_nets(1, count, index, gathered, stages, (copied,))
+    flow = run_flow(count, gathered, stages, results + last, (keep_two,))
+    token = one.column((flow,))
+    two = Summation(1, index, send, (token,))
     token = two.square(keep_two, (flow,), ())
-    token = one.column((token,))
+    token = one.code((token,))
+    token = one.spread((token,))
     token = two.column((token,))
-    token = one.code((token,))
     token = two.code((token,))
-    token = one.spread((token,))
     token = two.spread((token,))
     parts = one.decode((token,))
     parts = list(parts) + list(two.decode((parts[0],)))
@@ -1424,7 +1509,7 @@
     blocks = [block] + [swap(block, 0, part) for part in range(1, narrow)]
     moved = call(
         moment_kernel,
-        shapes * 2,
+        shapes * 2 + [((8, LANE), F32)],
         (),
         tuple(grads) + firsts + seconds,
         name="moments",
@@ -1444,7 +1529,7 @@
         + (update_in, update_mix, update_out, update_bias)
         + (flow_params, flow_first, flow_second),
         scratch=[pltpu.VMEM((narrow,) + block.shape, F32)],
-        after=(moved[3],),
+        after=(moved[8],),
         name="apply",
     )
     return (

time: 88.7 us -> 82.2 us (0.927)
  waiting for transfers between devices: 32.7 us -> 18.3 us
  local copies, waits for them, and re-layouts: 0.85 us -> 4.03 us
  starting transfers between devices: 26.9 us -> 30 us
  Pallas kernels: 26.8 us -> 28.1 us
    ppermute x24 -> x32, waiting for transfers between devices: 32.7 us -> 18.3 us  [swap(): lax.ppermute(values, ('wide', 'narrow'), [(place, place ^ mask) for place...]
    unnamed x40, local copies, waits for them, and re-layouts: 0.78 us -> 3.96 us
    ppermute x24 -> x32, starting transfers between devices: 26.9 us -> 30 us  [swap(): lax.ppermute(values, ('wide', 'narrow'), [(place, place ^ mask) for place...]
    pallas_call x19 -> x23, Pallas kernels: 26.8 us -> 28.1 us  [call(): pl.pallas_call(run, out_shape=tuple((jax.ShapeDtypeStruct(shape, dtype) f...]
  transfers between devices with their start and end apart: 24 -> 32, of which waited for: 13 -> 20; matrix products, arithmetic and copies ran while one was open for 0% -> 0% of each run, Pallas kernels for 18% -> 23%
where the time goes in v5:
time: 82.2 us; the launch traced here: 81.5 us
  starting transfers between devices  30 us (36%)
  Pallas kernels  28.1 us (34%)
  waiting for transfers between devices  18.3 us (22%)
  local copies, waits for them, and re-layouts  4.03 us (5%)
  between operations  1.12 us (1%)
    ppermute x32, starting transfers between devices, swap(): lax.ppermute(values, ('wide', 'narrow'), [(place, place ^ mask) for place...  30 us
    pallas_call x23, Pallas kernels, call(): pl.pallas_call(run, out_shape=tuple((jax.ShapeDtypeStruct(shape, dtype) f...  28.1 us
    ppermute x32, waiting for transfers between devices, swap(): lax.ppermute(values, ('wide', 'narrow'), [(place, place ^ mask) for place...  18.3 us
    unnamed x40, local copies, waits for them, and re-layouts  3.96 us
  transfers between devices with their start and end apart: 32, of which 20 were waited for; matrix products, arithmetic and copies ran while one was open for 0% of the time, Pallas kernels for 23%

profile of v5, /device:TPU:0, one launch (start us, length us, event | category | flops | bytes accessed | tf_op | source)
XLA Modules:
  0.0 81.5 jit_solution(16710066831942271747)
XLA Ops:
  0.7 2.4 %pack.1 = (bf16[2720,128]{1,0:T(8,128)(2,1)}, bf16[1168,128]{1,0:T(8,128)(2,1)}, bf16[1552,128]{1,0:T(8,128)(2,1)}) custom-call(s32[2,2]{1,0:T(2,128)} %refs_1_.3, f32[378,128]{1,0:T(8,128)} %refs_5_.3, f32[3,512,128]{2,1,0:T(8,128)} %refs_6_.3, f32[756,128]{1,0:T(8,128)} %bitcast.9, f32[3,2,128]{2,1,0:T(2,128)} %refs_8_.5), custom_call_target="tpu_custom_call" | custom-call | flops 1000 | bytes 1000 | tf_op jit(solution)/shard_map/pack/pallas_call | solution.py:1268
  3.1 0.5 collective-permute-start
  3.5 2.5 %collective-permute-start.1 = (bf16[1168,128]{1,0:T(8,128)(2,1)}, bf16[1168,128]{1,0:T(8,128)(2,1)S(1)}, u32[]{:S(2)}, u32[]{:S(2)}) collective-permute-start(bf16[1168,128]{1,0:T(8,128)(2,1)} %get-tuple-element.99), channel_id=1, source_target_pairs={{0,2},{1,3},{2,0},{3,1},{4,6},{5,7},{6,4},{7,5},{8,10},{9,11},{10,... | collective-permute-start | bytes 897032 | tf_op jit(solution)/shard_map/ppermute | solution.py:1349
  6.1 1.1 %copy-done.9 = bf16[2720,128]{1,0:T(8,128)(2,1)S(1)} copy-done((bf16[2720,128]{1,0:T(8,128)(2,1)S(1)}, bf16[2720,128]{1,0:T(8,128)(2,1)}, u32[]{:S(2)}) %copy-start.9) | copy-done | bytes 696344
  7.2 0.7 copy-done.10
  7.9 0.7 copy-done.13
  8.7 0.7 copy-done.18
  9.3 0.7 copy-done.19
  10.0 4.6 %flow_pre.1 = (f32[112,512]{1,0:T(8,128)S(1)}, f32[168,128]{1,0:T(8,128)S(1)}, f32[320,128]{1,0:T(8,128)S(1)}, bf16[2720,128]{1,0:T(8,128)(2,1)S(1)}) custom-call(s32[2]{0:T(128)S(1)} %copy-done.19, s32[2,2]{1,0:T(2,128)S(1)} %copy-done.18, f32[3,2,1024]{2,1,0:T(2,128)S(1)} %copy-done.13, f32[3852]{0:T(1024)S(1)} %copy-done.10, bf16[2720,128]{1,0:T(8,128)(2,1)S(1)} %copy-done.9), custom_call_target="tpu_custom_call" | custom-call | flops 1000 | bytes 1000 | tf_op jit(solution)/shard_map/flow_pre/pallas_call | solution.py:1268
  15.0 0.3 collective-permute-start.3
  15.3 1.1 %collective-permute-done.3.refs_5_ = bf16[432,128]{1,0:T(8,128)(2,1)S(1)} collective-permute-done((bf16[432,128]{1,0:T(8,128)(2,1)S(1)}, bf16[432,128]{1,0:T(8,128)(2,1)S(1)}, u32[]{:S(2)}, u32[]{:S(2)}) %collective-permute-start.3) | collective-permute-done | bytes 110624 | tf_op jit(solution)/shard_map/ppermute | solution.py:1349
  16.4 2.4 %nets_a.1 = (f32[2,1216,128]{2,1,0:T(8,128)S(1)}, f32[2,1216,128]{2,1,0:T(8,128)S(1)}, f32[120,128]{1,0:T(8,128)S(1)}) custom-call(s32[8,128]{1,0:T(8,128)S(1)} %iota.7.refs_0_, bf16[2720,128]{1,0:T(8,128)(2,1)S(1)} %get-tuple-element.98.refs_1_.refs_6_, bf16[2720,128]{1,0:T(8,128)(2,1)S(1)} %collective-permute-done.refs_2_.refs_7_, ...), custom_call_target="tpu_custom_call" | custom-call | flops 1000 | bytes 1000 | tf_op jit(solution)/shard_map/nets_a/pallas_call | solution.py:1268
  18.9 0.5 send_a.1
  19.3 0.3 collective-permute-start.4
  20.4 0.4 collective-permute-done.4.refs_2_
  21.6 0.7 square_a.1
  22.7 2.0 %collective-permute-start.8 = (bf16[656,128]{1,0:T(8,128)(2,1)S(1)}, bf16[656,128]{1,0:T(8,128)(2,1)S(1)}, u32[]{:S(2)}, u32[]{:S(2)}) collective-permute-start(bf16[656,128]{1,0:T(8,128)(2,1)S(1)} %get-tuple-element.113), channel_id=1, source_target_pairs={{0,2},{1,3},{2,0},{3,1},{4,6},{5,7},{6,4},{7,5},{8,10},{9,11},{10,... | collective-permute-start | bytes 503816 | tf_op jit(solution)/shard_map/ppermute | solution.py:1349
  24.6 1.6 %collective-permute-start.9 = (bf16[656,128]{1,0:T(8,128)(2,1)S(1)}, bf16[656,128]{1,0:T(8,128)(2,1)S(1)}, u32[]{:S(2)}, u32[]{:S(2)}) collective-permute-start(bf16[656,128]{1,0:T(8,128)(2,1)S(1)} %get-tuple-element.114), channel_id=1, source_target_pairs={{0,4},{1,5},{2,6},{3,7},{4,0},{5,1},{6,2},{7,3},{8,12},{9,13},{10,... | collective-permute-start | bytes 503816 | tf_op jit(solution)/shard_map/ppermute | solution.py:1349
  26.2 4.7 %nets_b.1 = (f32[2,1536,128]{2,1,0:T(8,128)S(1)}, f32[2,1536,128]{2,1,0:T(8,128)S(1)}, f32[40,512]{1,0:T(8,128)S(1)}, f32[64,128]{1,0:T(8,128)S(1)}) custom-call(s32[8,128]{1,0:T(8,128)S(1)} %iota.7.refs_0_, bf16[2720,128]{1,0:T(8,128)(2,1)S(1)} %get-tuple-element.98.refs_1_.refs_6_, bf16[2720,128]{1,0:T(8,128)(2,1)S(1)} %collective-permute-done.refs_2_.refs_7_, ...), custom_call_target="tpu_custom_call" | custom-call | flops 1000 | bytes 1000 | tf_op jit(solution)/shard_map/nets_b/pallas_call | solution.py:1268
  30.9 3.4 %flow_back.1.refs_5_.refs_6_ = f32[40,128]{1,0:T(8,128)S(1)} custom-call(f32[112,512]{1,0:T(8,128)S(1)} %get-tuple-element.116.refs_5_.refs_0_, f32[168,128]{1,0:T(8,128)S(1)} %get-tuple-element.117.refs_6_.refs_1_, f32[320,128]{1,0:T(8,128)S(1)} %get-tuple-element.105.refs_6_.refs_2_, f32[40,512]{1,0:T(8,128)S(1)} %get-tuple-element.119.refs_3_, ...), custom_call_target="tpu_custom_call" | custom-call | flops 1000 | bytes 1000 | tf_op jit(solution)/shard_map/flow_back/pallas_call | solution.py:1268
  34.4 0.4 column_a.1
  34.8 0.8 send_b.1
  35.6 0.5 collective-permute-start.15
  36.2 0.4 collective-permute-start.17
  36.7 0.4 collective-permute-done.14.refs_2_
  37.1 0.3 collective-permute-done.15.refs_3_
  38.0 0.9 %square_b.1 = (f32[768,128]{1,0:T(8,128)S(1)}, bf16[48,128]{1,0:T(8,128)(2,1)S(1)}, bf16[864,128]{1,0:T(8,128)(2,1)S(1)}, bf16[864,128]{1,0:T(8,128)(2,1)S(1)}, bf16[864,128]{1,0:T(8,128)(2,1)S(1)}) custom-call(s32[8,128]{1,0:T(8,128)S(1)} %iota.7.refs_0_, f32[2,1536,128]{2,1,0:T(8,128)S(1)} %get-tuple-element.122.refs_10_.refs_1_, ...), custom_call_target="tpu_custom_call" | custom-call | flops 1000 | bytes 1000 | tf_op jit(solution)/shard_map/square_b/pallas_call | solution.py:1268
  38.9 1.9 %collective-permute-start.21 = (bf16[864,128]{1,0:T(8,128)(2,1)S(1)}, bf16[864,128]{1,0:T(8,128)(2,1)S(1)}, u32[]{:S(2)}, u32[]{:S(2)}) collective-permute-start(bf16[864,128]{1,0:T(8,128)(2,1)S(1)} %get-tuple-element.132), channel_id=1, source_target_pairs={{0,2},{1,3},{2,0},{3,1},{4,6},{5,7},{6,4},{7,5},{8,10},{9,11},{10,... | collective-permute-start | bytes 663560 | tf_op jit(solution)/shard_map/ppermute | solution.py:1349
  40.8 1.6 %collective-permute-start.22 = (bf16[864,128]{1,0:T(8,128)(2,1)S(1)}, bf16[864,128]{1,0:T(8,128)(2,1)S(1)}, u32[]{:S(2)}, u32[]{:S(2)}) collective-permute-start(bf16[864,128]{1,0:T(8,128)(2,1)S(1)} %get-tuple-element.133), channel_id=1, source_target_pairs={{0,4},{1,5},{2,6},{3,7},{4,0},{5,1},{6,2},{7,3},{8,12},{9,13},{10,... | collective-permute-start | bytes 663560 | tf_op jit(solution)/shard_map/ppermute | solution.py:1349
  42.5 1.9 %collective-permute-start.13 = (bf16[336,128]{1,0:T(8,128)(2,1)S(1)}, bf16[336,128]{1,0:T(8,128)(2,1)S(1)}, u32[]{:S(2)}, u32[]{:S(2)}) collective-permute-start(bf16[336,128]{1,0:T(8,128)(2,1)S(1)} %get-tuple-element.124), channel_id=1, source_target_pairs={{0,8},{1,9},{2,10},{3,11},{4,12},{5,13},{6,14},{7,15},{8,0},{9,1},... | collective-permute-start | bytes 258056 | tf_op jit(solution)/shard_map/ppermute | solution.py:1349
  44.4 2.6 %collective-permute-done.13.refs_2_ = bf16[336,128]{1,0:T(8,128)(2,1)S(1)} collective-permute-done((bf16[336,128]{1,0:T(8,128)(2,1)S(1)}, bf16[336,128]{1,0:T(8,128)(2,1)S(1)}, u32[]{:S(2)}, u32[]{:S(2)}) %collective-permute-start.13) | collective-permute-done | bytes 86048 | tf_op jit(solution)/shard_map/ppermute | solution.py:1349
  47.1 3.0 %collective-permute-start.18 = (bf16[336,128]{1,0:T(8,128)(2,1)S(1)}, bf16[336,128]{1,0:T(8,128)(2,1)S(1)}, u32[]{:S(2)}, u32[]{:S(2)}) collective-permute-start(bf16[336,128]{1,0:T(8,128)(2,1)S(1)} %code_a.1.refs_1_.refs_3_), channel_id=1, source_target_pairs={{0,16},{1,17},{2,18},{3,19},{4,20},{5,21},{6,22},{7,23},{8,24},{9,... | collective-permute-start | bytes 258056 | tf_op jit(solution)/shard_map/ppermute | solution.py:1349
  50.1 2.5 %collective-permute-done.18.refs_2_ = bf16[336,128]{1,0:T(8,128)(2,1)S(1)} collective-permute-done((bf16[336,128]{1,0:T(8,128)(2,1)S(1)}, bf16[336,128]{1,0:T(8,128)(2,1)S(1)}, u32[]{:S(2)}, u32[]{:S(2)}) %collective-permute-start.18) | collective-permute-done | bytes 86048 | tf_op jit(solution)/shard_map/ppermute | solution.py:1349
  52.8 0.5 column_b.1
  53.3 1.9 %collective-permute-start.24 = (bf16[448,128]{1,0:T(8,128)(2,1)S(1)}, bf16[448,128]{1,0:T(8,128)(2,1)S(1)}, u32[]{:S(2)}, u32[]{:S(2)}) collective-permute-start(bf16[448,128]{1,0:T(8,128)(2,1)S(1)} %get-tuple-element.137), channel_id=1, source_target_pairs={{0,8},{1,9},{2,10},{3,11},{4,12},{5,13},{6,14},{7,15},{8,0},{9,1},... | collective-permute-start | bytes 344072 | tf_op jit(solution)/shard_map/ppermute | solution.py:1349
  55.4 3.3 %collective-permute-done.24.refs_3_ = bf16[448,128]{1,0:T(8,128)(2,1)S(1)} collective-permute-done((bf16[448,128]{1,0:T(8,128)(2,1)S(1)}, bf16[448,128]{1,0:T(8,128)(2,1)S(1)}, u32[]{:S(2)}, u32[]{:S(2)}) %collective-permute-start.24) | collective-permute-done | bytes 114720 | tf_op jit(solution)/shard_map/ppermute | solution.py:1349
  59.0 2.8 %collective-permute-start.25 = (bf16[448,128]{1,0:T(8,128)(2,1)S(1)}, bf16[448,128]{1,0:T(8,128)(2,1)S(1)}, u32[]{:S(2)}, u32[]{:S(2)}) collective-permute-start(bf16[448,128]{1,0:T(8,128)(2,1)S(1)} %code_b.1.refs_1_.refs_3_), channel_id=1, source_target_pairs={{0,16},{1,17},{2,18},{3,19},{4,20},{5,21},{6,22},{7,23},{8,24},{9,... | collective-permute-start | bytes 344072 | tf_op jit(solution)/shard_map/ppermute | solution.py:1349
  61.8 1.7 %collective-permute-start.20 = (bf16[2,336,128]{2,1,0:T(8,128)(2,1)S(1)}, bf16[2,336,128]{2,1,0:T(8,128)(2,1)S(1)}, u32[]{:S(2)}, u32[]{:S(2)}) collective-permute-start(bf16[2,336,128]{2,1,0:T(8,128)(2,1)S(1)} %pair_a.1.refs_1_), channel_id=1, source_target_pairs={{0,4},{1,5},{2,6},{3,7},{4,0},{5,1},{6,2},{7,3},{8,12},{9,13},{10,... | collective-permute-start | bytes 516104 | tf_op jit(solution)/shard_map/ppermute | solution.py:1349
  63.4 1.3 %collective-permute-done.25.refs_2_ = bf16[448,128]{1,0:T(8,128)(2,1)S(1)} collective-permute-done((bf16[448,128]{1,0:T(8,128)(2,1)S(1)}, bf16[448,128]{1,0:T(8,128)(2,1)S(1)}, u32[]{:S(2)}, u32[]{:S(2)}) %collective-permute-start.25) | collective-permute-done | bytes 114720 | tf_op jit(solution)/shard_map/ppermute | solution.py:1349
  64.9 3.1 %collective-permute-start.28 = (bf16[448,128]{1,0:T(8,128)(2,1)S(1)}, bf16[448,128]{1,0:T(8,128)(2,1)S(1)}, u32[]{:S(2)}, u32[]{:S(2)}) collective-permute-start(bf16[448,128]{1,0:T(8,128)(2,1)S(1)} %recode_4_b.1.refs_3_.refs_1_), channel_id=1, source_target_pairs={{0,12},{1,13},{2,14},{3,15},{4,8},{5,9},{6,10},{7,11},{8,4},{9,5},... | collective-permute-start | bytes 344072 | tf_op jit(solution)/shard_map/ppermute | solution.py:1349
  68.0 0.4 collective-permute-start.27
  68.6 2.3 %collective-permute-done.20.refs_2_ = bf16[2,336,128]{2,1,0:T(8,128)(2,1)S(1)} collective-permute-done((bf16[2,336,128]{2,1,0:T(8,128)(2,1)S(1)}, bf16[2,336,128]{2,1,0:T(8,128)(2,1)S(1)}, u32[]{:S(2)}, u32[]{:S(2)}) %collective-permute-start.20) | collective-permute-done | bytes 172064 | tf_op jit(solution)/shard_map/ppermute | solution.py:1349
  71.1 1.7 %collective-permute-done.27.refs_3_ = bf16[448,128]{1,0:T(8,128)(2,1)S(1)} collective-permute-done((bf16[448,128]{1,0:T(8,128)(2,1)S(1)}, bf16[448,128]{1,0:T(8,128)(2,1)S(1)}, u32[]{:S(2)}, u32[]{:S(2)}) %collective-permute-start.27) | collective-permute-done | bytes 114720 | tf_op jit(solution)/shard_map/ppermute | solution.py:1349
  72.8 0.4 collective-permute-done.26.refs_2_
  73.5 2.1 %norms.1 = (f32[378,128]{1,0:T(8,128)S(1)}, f32[3,512,128]{2,1,0:T(8,128)S(1)}, f32[756,128]{1,0:T(8,128)S(1)}, f32[6,128]{1,0:T(8,128)S(1)}, f32[378,128]{1,0:T...) custom-call(f32[1216,128]{1,0:T(8,128)S(1)} %decode_a.1.refs_5_.refs, ...), custom_call_target="tpu_custom_call" | custom-call | flops 1000 | bytes 1000 | tf_op jit(solution)/shard_map/norms/pallas_call | solution.py:1268
  75.7 1.6 %collective-permute-start.30 = (f32[56,128]{1,0:T(8,128)S(1)}, f32[56,128]{1,0:T(8,128)S(1)}, u32[]{:S(2)}, u32[]{:S(2)}) collective-permute-start(f32[56,128]{1,0:T(8,128)S(1)} %get-tuple-element.140.refs_1_), channel_id=1, source_target_pairs={{0,2},{1,3},{2,0},{3,1},{4,6},{5,7},{6,4},{7,5},{8,10},{9,11},{10,... | collective-permute-start | bytes 86024 | tf_op jit(solution)/shard_map/ppermute | solution.py:1349
  77.6 1.8 %moments.1 = (f32[378,128]{1,0:T(8,128)}, f32[3,512,128]{2,1,0:T(8,128)}, f32[756,128]{1,0:T(8,128)}, f32[3,2,128]{2,1,0:T(2,128)}, f32[378,128]{1,0:T(8,128)}, ...) custom-call(f32[378,128]{1,0:T(8,128)S(1)} %get-tuple-element.145.refs_0_, ...), custom_call_target="tpu_custom_call" | custom-call | flops 1000 | bytes 1000 | tf_op jit(solution)/shard_map/moments/pallas_call | solution.py:1268
  79.6 1.7 %apply.1 = (f32[378,128]{1,0:T(8,128)}, f32[3,512,128]{2,1,0:T(8,128)}, f32[756,128]{1,0:T(8,128)}, f32[3,2,128]{2,1,0:T(2,128)}, f32[3852]{0:T(1024)}, /*index=...) custom-call(s32[8,128]{1,0:T(8,128)S(1)} %iota.7.refs_0_, ...), custom_call_target="tpu_custom_call" | custom-call | flops 1000 | bytes 1000 | tf_op jit(solution)/shard_map/apply/pallas_call | solution.py:1268
  (81 shorter events, 5.4 us)
Async XLA Ops:
  3.1 13.3 %collective-permute-start = (bf16[2720,128]{1,0:T(8,128)(2,1)}, bf16[2720,128]{1,0:T(8,128)(2,1)S(1)}, u32[]{:S(2)}, u32[]{:S(2)}) collective-permute-start(bf16[2720,128]{1,0:T(8,128)(2,1)} %get-tuple-element.97.refs_4_), channel_id=1, source_target_pairs={{0,1},{1,0},{2,3},{3,2},{4,5},{5,4},{6,7},{7,6},{8,9},{9,8},{10,11... | collective-permute-start | bytes 2088968 | tf_op jit(solution)/shard_map/ppermute | solution.py:1349
  3.5 11.1 %collective-permute-start.1 = (bf16[1168,128]{1,0:T(8,128)(2,1)}, bf16[1168,128]{1,0:T(8,128)(2,1)S(1)}, u32[]{:S(2)}, u32[]{:S(2)}) collective-permute-start(bf16[1168,128]{1,0:T(8,128)(2,1)} %get-tuple-element.99), channel_id=1, source_target_pairs={{0,2},{1,3},{2,0},{3,1},{4,6},{5,7},{6,4},{7,5},{8,10},{9,11},{10,... | collective-permute-start | bytes 897032 | tf_op jit(solution)/shard_map/ppermute | solution.py:1349
  6.0 16.5 %collective-permute-start.11 = (bf16[1552,128]{1,0:T(8,128)(2,1)}, bf16[1552,128]{1,0:T(8,128)(2,1)S(1)}, u32[]{:S(2)}, u32[]{:S(2)}) collective-permute-start(bf16[1552,128]{1,0:T(8,128)(2,1)} %get-tuple-element.118), channel_id=1, source_target_pairs={{0,2},{1,3},{2,0},{3,1},{4,6},{5,7},{6,4},{7,5},{8,10},{9,11},{10,... | collective-permute-start | bytes 1191944 | tf_op jit(solution)/shard_map/ppermute | solution.py:1349
  6.1 1.1 %copy-start.9 = (bf16[2720,128]{1,0:T(8,128)(2,1)S(1)}, bf16[2720,128]{1,0:T(8,128)(2,1)}, u32[]{:S(2)}) copy-start(bf16[2720,128]{1,0:T(8,128)(2,1)} %get-tuple-element.97.refs_4_) | copy-start | bytes 2088964
  14.7 1.7 %collective-permute-start.2 = (bf16[736,128]{1,0:T(8,128)(2,1)S(1)}, bf16[736,128]{1,0:T(8,128)(2,1)S(1)}, u32[]{:S(2)}, u32[]{:S(2)}) collective-permute-start(bf16[736,128]{1,0:T(8,128)(2,1)S(1)} %get-tuple-element.103), channel_id=1, source_target_pairs={{0,1},{1,0},{2,3},{3,2},{4,5},{5,4},{6,7},{7,6},{8,9},{9,8},{10,11... | collective-permute-start | bytes 565256 | tf_op jit(solution)/shard_map/ppermute | solution.py:1349
  15.0 1.4 %collective-permute-start.3 = (bf16[432,128]{1,0:T(8,128)(2,1)S(1)}, bf16[432,128]{1,0:T(8,128)(2,1)S(1)}, u32[]{:S(2)}, u32[]{:S(2)}) collective-permute-start(bf16[432,128]{1,0:T(8,128)(2,1)S(1)} %get-tuple-element.104), channel_id=1, source_target_pairs={{0,1},{1,0},{2,3},{3,2},{4,5},{5,4},{6,7},{7,6},{8,9},{9,8},{10,11... | collective-permute-start | bytes 331784 | tf_op jit(solution)/shard_map/ppermute | solution.py:1349
  19.3 1.5 %collective-permute-start.4 = (bf16[656,128]{1,0:T(8,128)(2,1)S(1)}, bf16[656,128]{1,0:T(8,128)(2,1)S(1)}, u32[]{:S(2)}, u32[]{:S(2)}) collective-permute-start(bf16[656,128]{1,0:T(8,128)(2,1)S(1)} %get-tuple-element.108), channel_id=1, source_target_pairs={{0,1},{1,0},{2,3},{3,2},{4,5},{5,4},{6,7},{7,6},{8,9},{9,8},{10,11... | collective-permute-start | bytes 503816 | tf_op jit(solution)/shard_map/ppermute | solution.py:1349
  19.6 1.4 %collective-permute-start.5 = (bf16[656,128]{1,0:T(8,128)(2,1)S(1)}, bf16[656,128]{1,0:T(8,128)(2,1)S(1)}, u32[]{:S(2)}, u32[]{:S(2)}) collective-permute-start(bf16[656,128]{1,0:T(8,128)(2,1)S(1)} %get-tuple-element.109), channel_id=1, source_target_pairs={{0,1},{1,0},{2,3},{3,2},{4,5},{5,4},{6,7},{7,6},{8,9},{9,8},{10,11... | collective-permute-start | bytes 503816 | tf_op jit(solution)/shard_map/ppermute | solution.py:1349
  19.9 1.4 %collective-permute-start.6 = (bf16[656,128]{1,0:T(8,128)(2,1)S(1)}, bf16[656,128]{1,0:T(8,128)(2,1)S(1)}, u32[]{:S(2)}, u32[]{:S(2)}) collective-permute-start(bf16[656,128]{1,0:T(8,128)(2,1)S(1)} %get-tuple-element.110), channel_id=1, source_target_pairs={{0,1},{1,0},{2,3},{3,2},{4,5},{5,4},{6,7},{7,6},{8,9},{9,8},{10,11... | collective-permute-start | bytes 503816 | tf_op jit(solution)/shard_map/ppermute | solution.py:1349
  20.2 1.4 %collective-permute-start.7 = (bf16[656,128]{1,0:T(8,128)(2,1)S(1)}, bf16[656,128]{1,0:T(8,128)(2,1)S(1)}, u32[]{:S(2)}, u32[]{:S(2)}) collective-permute-start(bf16[656,128]{1,0:T(8,128)(2,1)S(1)} %get-tuple-element.111), channel_id=1, source_target_pairs={{0,1},{1,0},{2,3},{3,2},{4,5},{5,4},{6,7},{7,6},{8,9},{9,8},{10,11... | collective-permute-start | bytes 503816 | tf_op jit(solution)/shard_map/ppermute | solution.py:1349
  22.5 3.6 %collective-permute-start.12 = (bf16[1552,128]{1,0:T(8,128)(2,1)S(1)}, bf16[1552,128]{1,0:T(8,128)(2,1)S(1)}, u32[]{:S(2)}, u32[]{:S(2)}) collective-permute-start(bf16[1552,128]{1,0:T(8,128)(2,1)S(1)} %copy_b.1.refs_7_), channel_id=1, source_target_pairs={{0,1},{1,0},{2,3},{3,2},{4,5},{5,4},{6,7},{7,6},{8,9},{9,8},{10,11... | collective-permute-start | bytes 1191944 | tf_op jit(solution)/shard_map/ppermute | solution.py:1349
  22.7 11.6 %collective-permute-start.8 = (bf16[656,128]{1,0:T(8,128)(2,1)S(1)}, bf16[656,128]{1,0:T(8,128)(2,1)S(1)}, u32[]{:S(2)}, u32[]{:S(2)}) collective-permute-start(bf16[656,128]{1,0:T(8,128)(2,1)S(1)} %get-tuple-element.113), channel_id=1, source_target_pairs={{0,2},{1,3},{2,0},{3,1},{4,6},{5,7},{6,4},{7,5},{8,10},{9,11},{10,... | collective-permute-start | bytes 503816 | tf_op jit(solution)/shard_map/ppermute | solution.py:1349
  24.6 9.8 %collective-permute-start.9 = (bf16[656,128]{1,0:T(8,128)(2,1)S(1)}, bf16[656,128]{1,0:T(8,128)(2,1)S(1)}, u32[]{:S(2)}, u32[]{:S(2)}) collective-permute-start(bf16[656,128]{1,0:T(8,128)(2,1)S(1)} %get-tuple-element.114), channel_id=1, source_target_pairs={{0,4},{1,5},{2,6},{3,7},{4,0},{5,1},{6,2},{7,3},{8,12},{9,13},{10,... | collective-permute-start | bytes 503816 | tf_op jit(solution)/shard_map/ppermute | solution.py:1349
  26.2 8.2 %collective-permute-start.10 = (bf16[656,128]{1,0:T(8,128)(2,1)S(1)}, bf16[656,128]{1,0:T(8,128)(2,1)S(1)}, u32[]{:S(2)}, u32[]{:S(2)}) collective-permute-start(bf16[656,128]{1,0:T(8,128)(2,1)S(1)} %get-tuple-element.115), channel_id=1, source_target_pairs={{0,6},{1,7},{2,4},{3,5},{4,2},{5,3},{6,0},{7,1},{8,14},{9,15},{10,... | collective-permute-start | bytes 503816 | tf_op jit(solution)/shard_map/ppermute | solution.py:1349
  35.6 1.5 %collective-permute-start.14 = (bf16[816,128]{1,0:T(8,128)(2,1)S(1)}, bf16[816,128]{1,0:T(8,128)(2,1)S(1)}, u32[]{:S(2)}, u32[]{:S(2)}) collective-permute-start(bf16[816,128]{1,0:T(8,128)(2,1)S(1)} %get-tuple-element.126), channel_id=1, source_target_pairs={{0,1},{1,0},{2,3},{3,2},{4,5},{5,4},{6,7},{7,6},{8,9},{9,8},{10,11... | collective-permute-start | bytes 626696 | tf_op jit(solution)/shard_map/ppermute | solution.py:1349
  35.6 1.7 %collective-permute-start.15 = (bf16[816,128]{1,0:T(8,128)(2,1)S(1)}, bf16[816,128]{1,0:T(8,128)(2,1)S(1)}, u32[]{:S(2)}, u32[]{:S(2)}) collective-permute-start(bf16[816,128]{1,0:T(8,128)(2,1)S(1)} %get-tuple-element.127), channel_id=1, source_target_pairs={{0,1},{1,0},{2,3},{3,2},{4,5},{5,4},{6,7},{7,6},{8,9},{9,8},{10,11... | collective-permute-start | bytes 626696 | tf_op jit(solution)/shard_map/ppermute | solution.py:1349
  36.1 1.5 %collective-permute-start.16 = (bf16[816,128]{1,0:T(8,128)(2,1)S(1)}, bf16[816,128]{1,0:T(8,128)(2,1)S(1)}, u32[]{:S(2)}, u32[]{:S(2)}) collective-permute-start(bf16[816,128]{1,0:T(8,128)(2,1)S(1)} %get-tuple-element.128), channel_id=1, source_target_pairs={{0,1},{1,0},{2,3},{3,2},{4,5},{5,4},{6,7},{7,6},{8,9},{9,8},{10,11... | collective-permute-start | bytes 626696 | tf_op jit(solution)/shard_map/ppermute | solution.py:1349
  36.2 1.8 %collective-permute-start.17 = (bf16[816,128]{1,0:T(8,128)(2,1)S(1)}, bf16[816,128]{1,0:T(8,128)(2,1)S(1)}, u32[]{:S(2)}, u32[]{:S(2)}) collective-permute-start(bf16[816,128]{1,0:T(8,128)(2,1)S(1)} %get-tuple-element.129), channel_id=1, source_target_pairs={{0,1},{1,0},{2,3},{3,2},{4,5},{5,4},{6,7},{7,6},{8,9},{9,8},{10,11... | collective-permute-start | bytes 626696 | tf_op jit(solution)/shard_map/ppermute | solution.py:1349
  38.9 13.8 %collective-permute-start.21 = (bf16[864,128]{1,0:T(8,128)(2,1)S(1)}, bf16[864,128]{1,0:T(8,128)(2,1)S(1)}, u32[]{:S(2)}, u32[]{:S(2)}) collective-permute-start(bf16[864,128]{1,0:T(8,128)(2,1)S(1)} %get-tuple-element.132), channel_id=1, source_target_pairs={{0,2},{1,3},{2,0},{3,1},{4,6},{5,7},{6,4},{7,5},{8,10},{9,11},{10,... | collective-permute-start | bytes 663560 | tf_op jit(solution)/shard_map/ppermute | solution.py:1349
  40.8 12.0 %collective-permute-start.22 = (bf16[864,128]{1,0:T(8,128)(2,1)S(1)}, bf16[864,128]{1,0:T(8,128)(2,1)S(1)}, u32[]{:S(2)}, u32[]{:S(2)}) collective-permute-start(bf16[864,128]{1,0:T(8,128)(2,1)S(1)} %get-tuple-element.133), channel_id=1, source_target_pairs={{0,4},{1,5},{2,6},{3,7},{4,0},{5,1},{6,2},{7,3},{8,12},{9,13},{10,... | collective-permute-start | bytes 663560 | tf_op jit(solution)/shard_map/ppermute | solution.py:1349
  42.4 10.4 %collective-permute-start.23 = (bf16[864,128]{1,0:T(8,128)(2,1)S(1)}, bf16[864,128]{1,0:T(8,128)(2,1)S(1)}, u32[]{:S(2)}, u32[]{:S(2)}) collective-permute-start(bf16[864,128]{1,0:T(8,128)(2,1)S(1)} %get-tuple-element.134), channel_id=1, source_target_pairs={{0,6},{1,7},{2,4},{3,5},{4,2},{5,3},{6,0},{7,1},{8,14},{9,15},{10,... | collective-permute-start | bytes 663560 | tf_op jit(solution)/shard_map/ppermute | solution.py:1349
  42.5 4.5 %collective-permute-start.13 = (bf16[336,128]{1,0:T(8,128)(2,1)S(1)}, bf16[336,128]{1,0:T(8,128)(2,1)S(1)}, u32[]{:S(2)}, u32[]{:S(2)}) collective-permute-start(bf16[336,128]{1,0:T(8,128)(2,1)S(1)} %get-tuple-element.124), channel_id=1, source_target_pairs={{0,8},{1,9},{2,10},{3,11},{4,12},{5,13},{6,14},{7,15},{8,0},{9,1},... | collective-permute-start | bytes 258056 | tf_op jit(solution)/shard_map/ppermute | solution.py:1349
  47.1 5.5 %collective-permute-start.18 = (bf16[336,128]{1,0:T(8,128)(2,1)S(1)}, bf16[336,128]{1,0:T(8,128)(2,1)S(1)}, u32[]{:S(2)}, u32[]{:S(2)}) collective-permute-start(bf16[336,128]{1,0:T(8,128)(2,1)S(1)} %code_a.1.refs_1_.refs_3_), channel_id=1, source_target_pairs={{0,16},{1,17},{2,18},{3,19},{4,20},{5,21},{6,22},{7,23},{8,24},{9,... | collective-permute-start | bytes 258056 | tf_op jit(solution)/shard_map/ppermute | solution.py:1349
  52.8 20.6 %copy-start.6 = (f32[128,756]{0,1:T(8,128)S(1)}, f32[128,756]{0,1:T(8,128)}, u32[]{:S(2)}) copy-start(f32[128,756]{0,1:T(8,128)} %param.33) | copy-start | bytes 1161220
  52.8 20.6 %copy-start.8 = (f32[378,128]{1,0:T(8,128)S(1)}, f32[378,128]{1,0:T(8,128)}, u32[]{:S(2)}) copy-start(f32[378,128]{1,0:T(8,128)} %refs_8_.4) | copy-start | bytes 580612
  53.3 5.4 %collective-permute-start.24 = (bf16[448,128]{1,0:T(8,128)(2,1)S(1)}, bf16[448,128]{1,0:T(8,128)(2,1)S(1)}, u32[]{:S(2)}, u32[]{:S(2)}) collective-permute-start(bf16[448,128]{1,0:T(8,128)(2,1)S(1)} %get-tuple-element.137), channel_id=1, source_target_pairs={{0,8},{1,9},{2,10},{3,11},{4,12},{5,13},{6,14},{7,15},{8,0},{9,1},... | collective-permute-start | bytes 344072 | tf_op jit(solution)/shard_map/ppermute | solution.py:1349
  55.2 6.5 %collective-permute-start.19 = (bf16[336,128]{1,0:T(8,128)(2,1)S(1)}, bf16[336,128]{1,0:T(8,128)(2,1)S(1)}, u32[]{:S(2)}, u32[]{:S(2)}) collective-permute-start(bf16[336,128]{1,0:T(8,128)(2,1)S(1)} %recode_4_a.1.refs_1_.refs_6_), channel_id=1, source_target_pairs={{0,8},{1,9},{2,10},{3,11},{4,12},{5,13},{6,14},{7,15},{8,0},{9,1},... | collective-permute-start | bytes 258056 | tf_op jit(solution)/shard_map/ppermute | solution.py:1349
  58.7 14.7 %copy-start.5 = (f32[128,756]{0,1:T(8,128)S(1)}, f32[128,756]{0,1:T(8,128)}, u32[]{:S(2)}) copy-start(f32[128,756]{0,1:T(8,128)} %param.28) | copy-start | bytes 1161220
  58.7 14.7 %copy-start.7 = (f32[378,128]{1,0:T(8,128)S(1)}, f32[378,128]{1,0:T(8,128)}, u32[]{:S(2)}) copy-start(f32[378,128]{1,0:T(8,128)} %refs_4_.5) | copy-start | bytes 580612
  58.9 14.6 %copy-start = (f32[3,512,128]{2,1,0:T(8,128)S(1)}, f32[3,512,128]{2,1,0:T(8,128)}, u32[]{:S(2)}) copy-start(f32[3,512,128]{2,1,0:T(8,128)} %refs_6_.3) | copy-start | bytes 2359300
  58.9 14.6 %copy-start.1 = (f32[128,756]{0,1:T(8,128)S(1)}, f32[128,756]{0,1:T(8,128)}, u32[]{:S(2)}) copy-start(f32[128,756]{0,1:T(8,128)} %param.23) | copy-start | bytes 1161220
  58.9 14.6 %copy-start.2 = (f32[3,512,128]{2,1,0:T(8,128)S(1)}, f32[3,512,128]{2,1,0:T(8,128)}, u32[]{:S(2)}) copy-start(f32[3,512,128]{2,1,0:T(8,128)} %refs_5_.2) | copy-start | bytes 2359300
  58.9 14.6 %copy-start.3 = (f32[3,512,128]{2,1,0:T(8,128)S(1)}, f32[3,512,128]{2,1,0:T(8,128)}, u32[]{:S(2)}) copy-start(f32[3,512,128]{2,1,0:T(8,128)} %refs_9_.1) | copy-start | bytes 2359300
  58.9 14.6 %copy-start.4 = (f32[378,128]{1,0:T(8,128)S(1)}, f32[378,128]{1,0:T(8,128)}, u32[]{:S(2)}) copy-start(f32[378,128]{1,0:T(8,128)} %refs_5_.3) | copy-start | bytes 580612
  58.9 14.6 %copy-start.12 = (f32[3,2,128]{2,1,0:T(2,128)S(1)}, f32[3,2,128]{2,1,0:T(2,128)}, u32[]{:S(2)}) copy-start(f32[3,2,128]{2,1,0:T(2,128)} %refs_8_.5) | copy-start | bytes 9220
  58.9 14.6 %copy-start.16 = (f32[3,2,128]{2,1,0:T(2,128)S(1)}, f32[3,2,128]{2,1,0:T(2,128)}, u32[]{:S(2)}) copy-start(f32[3,2,128]{2,1,0:T(2,128)} %refs_7_.3) | copy-start | bytes 9220
  58.9 14.6 %copy-start.17 = (f32[3,2,128]{2,1,0:T(2,128)S(1)}, f32[3,2,128]{2,1,0:T(2,128)}, u32[]{:S(2)}) copy-start(f32[3,2,128]{2,1,0:T(2,128)} %refs_11_.3) | copy-start | bytes 9220
  59.0 5.8 %collective-permute-start.25 = (bf16[448,128]{1,0:T(8,128)(2,1)S(1)}, bf16[448,128]{1,0:T(8,128)(2,1)S(1)}, u32[]{:S(2)}, u32[]{:S(2)}) collective-permute-start(bf16[448,128]{1,0:T(8,128)(2,1)S(1)} %code_b.1.refs_1_.refs_3_), channel_id=1, source_target_pairs={{0,16},{1,17},{2,18},{3,19},{4,20},{5,21},{6,22},{7,23},{8,24},{9,... | collective-permute-start | bytes 344072 | tf_op jit(solution)/shard_map/ppermute | solution.py:1349
  61.8 9.2 %collective-permute-start.20 = (bf16[2,336,128]{2,1,0:T(8,128)(2,1)S(1)}, bf16[2,336,128]{2,1,0:T(8,128)(2,1)S(1)}, u32[]{:S(2)}, u32[]{:S(2)}) collective-permute-start(bf16[2,336,128]{2,1,0:T(8,128)(2,1)S(1)} %pair_a.1.refs_1_), channel_id=1, source_target_pairs={{0,4},{1,5},{2,6},{3,7},{4,0},{5,1},{6,2},{7,3},{8,12},{9,13},{10,... | collective-permute-start | bytes 516104 | tf_op jit(solution)/shard_map/ppermute | solution.py:1349
  64.9 6.2 %collective-permute-start.28 = (bf16[448,128]{1,0:T(8,128)(2,1)S(1)}, bf16[448,128]{1,0:T(8,128)(2,1)S(1)}, u32[]{:S(2)}, u32[]{:S(2)}) collective-permute-start(bf16[448,128]{1,0:T(8,128)(2,1)S(1)} %recode_4_b.1.refs_3_.refs_1_), channel_id=1, source_target_pairs={{0,12},{1,13},{2,14},{3,15},{4,8},{5,9},{6,10},{7,11},{8,4},{9,5},... | collective-permute-start | bytes 344072 | tf_op jit(solution)/shard_map/ppermute | solution.py:1349
  68.0 4.8 %collective-permute-start.27 = (bf16[448,128]{1,0:T(8,128)(2,1)S(1)}, bf16[448,128]{1,0:T(8,128)(2,1)S(1)}, u32[]{:S(2)}, u32[]{:S(2)}) collective-permute-start(bf16[448,128]{1,0:T(8,128)(2,1)S(1)} %recode_4_b.1.refs_3_.refs_1_), channel_id=1, source_target_pairs={{0,4},{1,5},{2,6},{3,7},{4,0},{5,1},{6,2},{7,3},{8,12},{9,13},{10,... | collective-permute-start | bytes 344072 | tf_op jit(solution)/shard_map/ppermute | solution.py:1349
  68.4 4.8 %collective-permute-start.26 = (bf16[448,128]{1,0:T(8,128)(2,1)S(1)}, bf16[448,128]{1,0:T(8,128)(2,1)S(1)}, u32[]{:S(2)}, u32[]{:S(2)}) collective-permute-start(bf16[448,128]{1,0:T(8,128)(2,1)S(1)} %recode_4_b.1.refs_3_.refs_1_), channel_id=1, source_target_pairs={{0,8},{1,9},{2,10},{3,11},{4,12},{5,13},{6,14},{7,15},{8,0},{9,1},... | collective-permute-start | bytes 344072 | tf_op jit(solution)/shard_map/ppermute | solution.py:1349
  75.7 3.7 %collective-permute-start.31 = (f32[56,128]{1,0:T(8,128)S(1)}, f32[56,128]{1,0:T(8,128)S(1)}, u32[]{:S(2)}, u32[]{:S(2)}) collective-permute-start(f32[56,128]{1,0:T(8,128)S(1)} %get-tuple-element.140.refs_1_), channel_id=1, source_target_pairs={{0,3},{1,2},{2,1},{3,0},{4,7},{5,6},{6,5},{7,4},{8,11},{9,10},{10,... | collective-permute-start | bytes 86024 | tf_op jit(solution)/shard_map/ppermute | solution.py:1349
  75.7 3.9 %collective-permute-start.30 = (f32[56,128]{1,0:T(8,128)S(1)}, f32[56,128]{1,0:T(8,128)S(1)}, u32[]{:S(2)}, u32[]{:S(2)}) collective-permute-start(f32[56,128]{1,0:T(8,128)S(1)} %get-tuple-element.140.refs_1_), channel_id=1, source_target_pairs={{0,2},{1,3},{2,0},{3,1},{4,6},{5,7},{6,4},{7,5},{8,10},{9,11},{10,... | collective-permute-start | bytes 86024 | tf_op jit(solution)/shard_map/ppermute | solution.py:1349
  77.2 2.4 %collective-permute-start.29 = (f32[56,128]{1,0:T(8,128)S(1)}, f32[56,128]{1,0:T(8,128)S(1)}, u32[]{:S(2)}, u32[]{:S(2)}) collective-permute-start(f32[56,128]{1,0:T(8,128)S(1)} %get-tuple-element.140.refs_1_), channel_id=1, source_target_pairs={{0,1},{1,0},{2,3},{3,2},{4,5},{5,4},{6,7},{7,6},{8,9},{9,8},{10,11... | collective-permute-start | bytes 86024 | tf_op jit(solution)/shard_map/ppermute | solution.py:1349
  77.5 2.1 %copy-start.11 = (f32[3852]{0:T(1024)S(1)}, f32[3852]{0:T(1024)}, u32[]{:S(2)}) copy-start(f32[3852]{0:T(1024)} %refs_13_.1) | copy-start | bytes 46228
  77.5 2.1 %copy-start.14 = (f32[3852]{0:T(1024)S(1)}, f32[3852]{0:T(1024)}, u32[]{:S(2)}) copy-start(f32[3852]{0:T(1024)} %refs_14_.3) | copy-start | bytes 46228
  77.5 2.1 %copy-start.15 = (f32[3852]{0:T(1024)S(1)}, f32[3852]{0:T(1024)}, u32[]{:S(2)}) copy-start(f32[3852]{0:T(1024)} %refs_15_.1) | copy-start | bytes 46228
  (4 other events, 2.8 us)

commit v6 on v5

--- a/solution.py
+++ b/solution.py
@@ -27,6 +27,8 @@
 STATS_ROWS = 8
 CODE_BLOCK = 16
 CODE_RANGE = 84.0
+SQUARE_ORDER = ((1, 3, 2), (2, 1, 3))
+RETURN_ORDER = (2, 1, 3)
 VMEM_BYTES = 20 * 1024 * 1024
 
 
@@ -965,7 +967,7 @@
     else:
         *others, keep_ref, sent_ref, total_ref = refs
     total = mine_ref[...]
-    for flip, other in enumerate(others, 1):
+    for flip, other in zip(SQUARE_ORDER[chunk], others):
         values = read_piece(other, 0, rows + more)
         total = total + values[:rows]
         if more and flip == 2:
@@ -1027,7 +1029,7 @@
     parts, outs = refs[:4], refs[4:]
     place = 2 * wide_bit(index_ref, 1) + wide_bit(index_ref, 2)
     rows, more = quarter_rows(chunk), flow_part(chunk)
-    for flip, ref in enumerate(parts):
+    for flip, ref in zip((0, *RETURN_ORDER), parts):
         values = read_piece(ref, 0, rows + more)
         start = pl.multiple_of((place ^ flip) * rows, CODE_BLOCK)
         outs[0][pl.ds(start, rows), :] = values[:rows]
@@ -1057,30 +1059,44 @@
 def squares_rows(sums):
     row = iota((16, LANE), 0)
     held = jnp.zeros((16, LANE), F32)
-    for index, value in enumerate(sums):
+    for index, value in sums:
         held = jnp.where(row == index, value, held)
     return held
 
 
-def group_totals(values_in, values_mix, values_out, values_bias):
-    row = iota(values_in.shape, 0)
-    line = iota(values_out.shape, 0)
-    sums = []
+def chunk_spans(chunk):
+    levels = CHUNKS[chunk]
+    base = min(levels)
+    spans = []
+    for size in (in_rows, lambda level: 9 * chan(level), lambda level: 1, lambda level: 2):
+        start = sum(size(level) for level in range(base))
+        spans.append((start, start + sum(size(level) for level in levels)))
+    return spans
+
+
+def level_totals(chunk, values, size):
+    row = iota(values.shape, 0)
+    totals = []
     start = 0
-    for level in range(LEVELS):
-        inside = (row >= start) & (row < start + in_rows(level))
-        sums.append(total_of(jnp.where(inside, values_in, 0.0)))
-        start = start + in_rows(level)
-    for level in range(LEVELS):
-        sums.append(total_of(values_mix[level]))
-    start = 0
-    for level in range(LEVELS):
-        inside = (line >= start) & (line < start + 9 * chan(level))
-        sums.append(total_of(jnp.where(inside, values_out, 0.0)))
-        start = start + 9 * chan(level)
-    for level in range(LEVELS):
-        sums.append(total_of(values_bias[2 * level : 2 * level + 2]))
-    return sums
+    for level in sorted(CHUNKS[chunk]):
+        stop = start + size(level)
+        inside = values
+        if stop - start < values.shape[0]:
+            inside = jnp.where((row >= start) & (row < stop), values, 0.0)
+        totals.append(total_of(inside))
+        start = stop
+    return totals
+
+
+def group_totals(chunk, values_in, values_mix, values_out, values_bias):
+    levels = sorted(CHUNKS[chunk])
+    sums = (
+        (0, level_totals(chunk, values_in, in_rows)),
+        (3, [total_of(values) for values in values_mix]),
+        (6, level_totals(chunk, values_out, lambda level: 9 * chan(level))),
+        (9, level_totals(chunk, values_bias, lambda level: 2)),
+    )
+    return [(base + level, total) for base, totals in sums for level, total in zip(levels, totals)]
 
 
 def flow_masks():
@@ -1093,11 +1109,10 @@
     return masks
 
 
-def split_grads(refs, scale):
+def split_grads(chunk, ref, scale):
     ins, mixes, outs, biases = [], [], [], []
-    for level in range(LEVELS):
-        chunk, start = chunk_of(level)
-        ref = refs[chunk]
+    for level in sorted(CHUNKS[chunk]):
+        start = chunk_of(level)[1]
 
         def rows(first, count):
             return ref[start + first : start + first + count, :] * scale
@@ -1108,61 +1123,73 @@
         outs.append(rows(top + HID, 9 * chan(level)))
         biases.append(rows(in_rows(level), 1))
         biases.append(rows(second_bias_row(level), 1))
-    return jnp.concatenate(ins, 0), mixes, jnp.concatenate(outs, 0), jnp.concatenate(biases, 0)
-
-
-def norm_kernel(*refs):
-    parts, flow_ref = refs[:2], refs[2]
-    weight_in, weight_mix, weight_out, weight_bias = refs[3:7]
-    first_in, first_mix, first_out, first_bias = refs[7:11]
-    second_in, second_mix, second_out, second_bias = refs[11:15]
-    grad_in_ref, grad_mix_ref, grad_out_ref, grad_bias_ref = refs[15:19]
-    update_in, update_mix, update_out, update_bias, block_ref = refs[19:]
-    stats = flow_ref[FLOW_ROWS : FLOW_ROWS + 1, :]
+    join = lambda parts: parts[0] if len(parts) == 1 else jnp.concatenate(parts, 0)
+    return join(ins), mixes, join(outs), join(biases)
+
+
+def norm_kernel(chunk, *refs):
+    last = chunk == len(CHUNKS) - 1
+    part_ref, flow_ref, refs = refs[0], refs[1], refs[2:]
+    if last:
+        sums_ref, refs = refs[0], refs[1:]
+        stats = flow_ref[FLOW_ROWS : FLOW_ROWS + 1, :]
+    else:
+        stats = read_stats(flow_ref, 0, quarter_rows(1) + flow_part(1))
+    weights, firsts, seconds = refs[0:4], refs[4:8], refs[8:12]
+    grads, updates, block_ref = refs[12:16], refs[16:20], refs[20]
     scale = 1.0 / (3.0 * stats[:, 1:2] * LOG_TWO)
-    grad_in, grad_mix, grad_out, grad_bias = split_grads(parts, scale)
-    grad_in_ref[...] = grad_in
-    grad_out_ref[...] = grad_out
-    grad_bias_ref[...] = grad_bias
-    bias = weight_bias[...].reshape(2 * LEVELS, LANE)
-    new_in = moments(weight_in[...], grad_in, first_in[...], second_in[...])[2]
-    new_out = moments(weight_out[...], grad_out, first_out[...], second_out[...])[2]
-    new_bias = moments(
-        bias,
-        grad_bias,
-        first_bias[...].reshape(2 * LEVELS, LANE),
-        second_bias[...].reshape(2 * LEVELS, LANE),
-    )[2]
-    update_in[...] = new_in
-    update_out[...] = new_out
-    update_bias[...] = new_bias.reshape(LEVELS, 2, LANE)
-    mix_squares = []
-    mix_updates = []
-    for level in range(LEVELS):
-        grad_mix_ref[level] = grad_mix[level]
-        new_mix = moments(weight_mix[level], grad_mix[level], first_mix[level], second_mix[level])[2]
-        update_mix[level] = new_mix
-        mix_squares.append(weight_mix[level] * weight_mix[level])
-        mix_updates.append(new_mix * new_mix)
-    weight_sums = group_totals(
-        weight_in[...] * weight_in[...], mix_squares, weight_out[...] * weight_out[...], bias * bias
-    )
-    update_sums = group_totals(new_in * new_in, mix_updates, new_out * new_out, new_bias * new_bias)
+    grad_in, grad_mix, grad_out, grad_bias = split_grads(chunk, part_ref, scale)
+    in_span, out_span, mix_span, bias_span = chunk_spans(chunk)
+    weight_squares = [None] * 4
+    update_squares = [None] * 4
+    for place, span, gradient in ((0, in_span, grad_in), (2, out_span, grad_out)):
+        picked = slice(*span)
+        weight = weights[place][picked, :]
+        update = moments(weight, gradient, firsts[place][picked, :], seconds[place][picked, :])[2]
+        grads[place][...] = gradient
+        updates[place][...] = update
+        weight_squares[place] = weight * weight
+        update_squares[place] = update * update
+    old = [ref[...].reshape(2 * LEVELS, LANE)[slice(*bias_span)] for ref in (weights[3], firsts[3], seconds[3])]
+    update = moments(old[0], grad_bias, old[1], old[2])[2]
+    grads[3][...] = grad_bias
+    updates[3][...] = update
+    weight_squares[3], update_squares[3] = old[0] * old[0], update * update
+    weight_squares[1], update_squares[1] = [], []
+    for place, level in enumerate(range(*mix_span)):
+        weight = weights[1][level]
+        grads[1][place] = grad_mix[place]
+        update = moments(weight, grad_mix[place], firsts[1][level], seconds[1][level])[2]
+        updates[1][place] = update
+        weight_squares[1].append(weight * weight)
+        update_squares[1].append(update * update)
     lane = iota((16, LANE), 1)
-    block_ref[0:16, :] = jnp.where(lane == 0, squares_rows(weight_sums), squares_rows(update_sums))
-    block_ref[16:, :] = flow_ref[...]
+    sums = jnp.where(
+        lane == 0,
+        squares_rows(group_totals(chunk, *weight_squares)),
+        squares_rows(group_totals(chunk, *update_squares)),
+    )
+    if last:
+        block_ref[0:16, :] = sums + sums_ref[...]
+        block_ref[16:, :] = flow_ref[...]
+    else:
+        block_ref[...] = sums
+
+
+def join_chunks(first, last):
+    return jnp.concatenate([last[...], first[...]], 0)
 
 
 def moment_kernel(*refs):
-    grads, firsts, seconds = refs[0:4], refs[4:8], refs[8:12]
-    new_firsts, new_seconds = refs[12:16], refs[16:20]
-    refs[20][...] = jnp.zeros((8, LANE), F32)
-    for grad, first, second, new_first, new_second in zip(
-        grads, firsts, seconds, new_firsts, new_seconds
-    ):
-        gradient = grad[...].reshape(first.shape)
-        new_first[...] = FIRST_BETA * first[...] + (1.0 - FIRST_BETA) * gradient
-        new_second[...] = SECOND_BETA * second[...] + (1.0 - SECOND_BETA) * gradient * gradient
+    one, two, firsts, seconds = refs[0:4], refs[4:8], refs[8:12], refs[12:16]
+    new_firsts, new_seconds = refs[16:20], refs[20:24]
+    refs[24][...] = jnp.zeros((8, LANE), F32)
+    for place in range(4):
+        gradient = join_chunks(one[place], two[place]).reshape(firsts[place].shape)
+        new_firsts[place][...] = FIRST_BETA * firsts[place][...] + (1.0 - FIRST_BETA) * gradient
+        new_seconds[place][...] = (
+            SECOND_BETA * seconds[place][...] + (1.0 - SECOND_BETA) * gradient * gradient
+        )
 
 
 def apply_kernel(narrow, *refs):
@@ -1170,9 +1197,12 @@
     block_refs = refs[1 : 1 + narrow]
     at = 1 + narrow
     weight_in, weight_mix, weight_out, weight_bias = refs[at : at + 4]
-    update_in, update_mix, update_out, update_bias = refs[at + 4 : at + 8]
-    flow_ref, flow_first_ref, flow_second_ref = refs[at + 8 : at + 11]
-    at = at + 11
+    one, two = refs[at + 4 : at + 8], refs[at + 8 : at + 12]
+    flow_ref, flow_first_ref, flow_second_ref = refs[at + 12 : at + 15]
+    at = at + 15
+    update_in, update_out = join_chunks(one[0], two[0]), join_chunks(one[2], two[2])
+    update_bias = join_chunks(one[3], two[3]).reshape(LEVELS, 2, LANE)
+    update_mix = [two[1].at[0], two[1].at[1], one[1].at[0]]
     (
         new_in,
         new_mix,
@@ -1226,17 +1256,17 @@
     row = iota(weight_in.shape, 0)
     edge_one, edge_two = in_rows(0), in_rows(0) + in_rows(1)
     rate = jnp.where(row < edge_one, rates[0], jnp.where(row < edge_two, rates[1], rates[2]))
-    fresh = weight_in[...] - rate * update_in[...]
+    fresh = weight_in[...] - rate * update_in
     new_in[...] = fresh
     half_in[...] = fresh.astype(BF16)
     for level in range(LEVELS):
-        fresh = weight_mix[level] - rates[3 + level] * update_mix[level]
+        fresh = weight_mix[level] - rates[3 + level] * update_mix[level][...]
         new_mix[level] = fresh
         half_mix[level] = fresh.astype(BF16)
     row = iota(weight_out.shape, 0)
     edge_one, edge_two = 9 * chan(0), 9 * chan(0) + 9 * chan(1)
     rate = jnp.where(row < edge_one, rates[6], jnp.where(row < edge_two, rates[7], rates[8]))
-    fresh = weight_out[...] - rate * update_out[...]
+    fresh = weight_out[...] - rate * update_out
     new_out[...] = fresh
     half_out[...] = fresh.astype(BF16)
     for level in range(LEVELS):
@@ -1385,7 +1415,9 @@
             after=after,
         )
         self.own, sent = tuple(rest[:-3]), rest[-3:]
-        self.others = [swap(sent[0], 0, 2), swap(sent[1], 1, 0), swap(sent[2], 1, 2)]
+        partners = {1: (0, 2), 2: (1, 0), 3: (1, 2)}
+        order = SQUARE_ORDER[self.chunk]
+        self.others = [swap(sent[flip - 1], *partners[flip]) for flip in order]
         return self.kept
 
     def column(self, after):
@@ -1416,7 +1448,8 @@
                 self.others = [swap(self.kept, step, 0)]
         token = self.kept
         if flow_part(self.chunk):
-            self.others = [swap(self.kept, place, 0) for place in (2, 1, 3)]
+            partners = {1: 2, 2: 1, 3: 3}
+            self.others = [swap(self.kept, partners[flip], 0) for flip in RETURN_ORDER]
         else:
             self.others = [swap(self.kept, 2, 0)]
             (self.kept,) = self.run(pair_kernel, [((2,) + self.piece[0], BF16)], "pair", ())
@@ -1492,26 +1525,36 @@
     token = two.column((token,))
     token = two.code((token,))
     token = two.spread((token,))
-    parts = one.decode((token,))
-    parts = list(parts) + list(two.decode((parts[0],)))
     weights = (conv_in, mixer, conv_out, hidden_bias)
     firsts = (conv_in_first, mixer_first, conv_out_first, bias_first)
     seconds = (conv_in_second, mixer_second, conv_out_second, bias_second)
     shapes = [(weight.shape, F32) for weight in weights]
-    grad_shapes = shapes[:3] + [((2 * LEVELS, LANE), F32)]
-    *grads, update_in, update_mix, update_out, update_bias, block = call(
-        norm_kernel,
-        grad_shapes + shapes + [((16 + FLOW_ROWS + STATS_ROWS, LANE), F32)],
-        (),
-        tuple(parts) + weights + firsts + seconds,
-        name="norms",
-    )
+
+    def norms(chunk, arrays):
+        spans = [stop - start for start, stop in chunk_spans(chunk)]
+        rows = (spans[0], spans[1], spans[3])
+        in_shape, out_shape, bias_shape = [((count, LANE), F32) for count in rows]
+        part = [in_shape, ((spans[2], HID, LANE), F32), out_shape, bias_shape]
+        size = 16 if chunk == 0 else 16 + FLOW_ROWS + STATS_ROWS
+        *outs, block = call(
+            functools.partial(norm_kernel, chunk),
+            part * 2 + [((size, LANE), F32)],
+            (),
+            tuple(arrays) + weights + firsts + seconds,
+            name="norms_" + "ab"[chunk],
+        )
+        return tuple(outs[:4]), tuple(outs[4:]), block
+
+    (part,) = one.decode((token,))
+    grads_one, updates_one, sums = norms(0, (part, token))
+    part, flow = two.decode((sums,))
+    grads_two, updates_two, block = norms(1, (part, flow, sums))
     blocks = [block] + [swap(block, 0, part) for part in range(1, narrow)]
     moved = call(
         moment_kernel,
         shapes * 2 + [((8, LANE), F32)],
         (),
-        tuple(grads) + firsts + seconds,
+        grads_one + grads_two + firsts + seconds,
         name="moments",
     )
     flow_shape = (flow_params.shape, F32)
@@ -1526,7 +1569,8 @@
         (index,)
         + tuple(blocks)
         + weights
-        + (update_in, update_mix, update_out, update_bias)
+        + updates_one
+        + updates_two
         + (flow_params, flow_first, flow_second),
         scratch=[pltpu.VMEM((narrow,) + block.shape, F32)],
         after=(moved[8],),

time: 82.2 us -> 80.8 us (0.983)
  starting transfers between devices: 30 us -> 28.7 us
    ppermute x32, starting transfers between devices: 30 us -> 28.7 us  [swap(): lax.ppermute(values, ('wide', 'narrow'), [(place, place ^ mask) for place...]
    pallas_call x23 -> x24, Pallas kernels: 28.1 us -> 28.3 us  [call(): pl.pallas_call(run, out_shape=tuple((jax.ShapeDtypeStruct(shape, dtype) f...]
  transfers between devices with their start and end apart: 32 -> 32, of which waited for: 20 -> 17; matrix products, arithmetic and copies ran while one was open for 0% -> 0% of each run, Pallas kernels for 23% -> 25%
where the time goes in v6:
time: 80.8 us; the launch traced here: 80.5 us
  starting transfers between devices  28.7 us (36%)
  Pallas kernels  28.3 us (35%)
  waiting for transfers between devices  18.3 us (23%)
  local copies, waits for them, and re-layouts  4.04 us (5%)
  between operations  1.15 us (1%)
    ppermute x32, starting transfers between devices, swap(): lax.ppermute(values, ('wide', 'narrow'), [(place, place ^ mask) for place...  28.7 us
    pallas_call x24, Pallas kernels, call(): pl.pallas_call(run, out_shape=tuple((jax.ShapeDtypeStruct(shape, dtype) f...  28.3 us
    ppermute x32, waiting for transfers between devices, swap(): lax.ppermute(values, ('wide', 'narrow'), [(place, place ^ mask) for place...  18.3 us
    unnamed x40, local copies, waits for them, and re-layouts  3.97 us
  transfers between devices with their start and end apart: 32, of which 17 were waited for; matrix products, arithmetic and copies ran while one was open for 0% of the time, Pallas kernels for 25%

profile of v6, /device:TPU:0, one launch (start us, length us, event | category | flops | bytes accessed | tf_op | source)
XLA Modules:
  0.0 80.5 jit_solution(13666464590820401589)
XLA Ops:
  0.7 2.4 %pack.1 = (bf16[2720,128]{1,0:T(8,128)(2,1)}, bf16[1168,128]{1,0:T(8,128)(2,1)}, bf16[1552,128]{1,0:T(8,128)(2,1)}) custom-call(s32[2,2]{1,0:T(2,128)} %refs_1_.3, f32[378,128]{1,0:T(8,128)} %refs_5_.3, f32[3,512,128]{2,1,0:T(8,128)} %refs_6_.5, f32[756,128]{1,0:T(8,128)} %bitcast.9, f32[3,2,128]{2,1,0:T(2,128)} %refs_8_.5), custom_call_target="tpu_custom_call" | custom-call | flops 1000 | bytes 1000 | tf_op jit(solution)/shard_map/pack/pallas_call | solution.py:1298
  3.1 0.5 collective-permute-start
  3.5 2.5 %collective-permute-start.2 = (bf16[1168,128]{1,0:T(8,128)(2,1)}, bf16[1168,128]{1,0:T(8,128)(2,1)S(1)}, u32[]{:S(2)}, u32[]{:S(2)}) collective-permute-start(bf16[1168,128]{1,0:T(8,128)(2,1)} %get-tuple-element.109), channel_id=1, source_target_pairs={{0,2},{1,3},{2,0},{3,1},{4,6},{5,7},{6,4},{7,5},{8,10},{9,11},{10,... | collective-permute-start | bytes 897032 | tf_op jit(solution)/shard_map/ppermute | solution.py:1379
  6.1 1.1 %copy-done.9 = bf16[2720,128]{1,0:T(8,128)(2,1)S(1)} copy-done((bf16[2720,128]{1,0:T(8,128)(2,1)S(1)}, bf16[2720,128]{1,0:T(8,128)(2,1)}, u32[]{:S(2)}) %copy-start.9) | copy-done | bytes 696344
  7.2 0.7 copy-done.10
  7.9 0.7 copy-done.15
  8.7 0.7 copy-done.18
  9.3 0.7 copy-done.19
  10.0 4.6 %flow_pre.1 = (f32[112,512]{1,0:T(8,128)S(1)}, f32[168,128]{1,0:T(8,128)S(1)}, f32[320,128]{1,0:T(8,128)S(1)}, bf16[2720,128]{1,0:T(8,128)(2,1)S(1)}) custom-call(s32[2]{0:T(128)S(1)} %copy-done.19, s32[2,2]{1,0:T(2,128)S(1)} %copy-done.18, f32[3,2,1024]{2,1,0:T(2,128)S(1)} %copy-done.15, f32[3852]{0:T(1024)S(1)} %copy-done.10, bf16[2720,128]{1,0:T(8,128)(2,1)S(1)} %copy-done.9), custom_call_target="tpu_custom_call" | custom-call | flops 1000 | bytes 1000 | tf_op jit(solution)/shard_map/flow_pre/pallas_call | solution.py:1298
  15.0 0.3 collective-permute-start.4
  15.3 1.1 %collective-permute-done.4.refs_5_ = bf16[432,128]{1,0:T(8,128)(2,1)S(1)} collective-permute-done((bf16[432,128]{1,0:T(8,128)(2,1)S(1)}, bf16[432,128]{1,0:T(8,128)(2,1)S(1)}, u32[]{:S(2)}, u32[]{:S(2)}) %collective-permute-start.4) | collective-permute-done | bytes 110624 | tf_op jit(solution)/shard_map/ppermute | solution.py:1379
  16.4 2.4 %nets_a.1 = (f32[2,1216,128]{2,1,0:T(8,128)S(1)}, f32[2,1216,128]{2,1,0:T(8,128)S(1)}, f32[120,128]{1,0:T(8,128)S(1)}) custom-call(s32[8,128]{1,0:T(8,128)S(1)} %iota.7.refs_0_, bf16[2720,128]{1,0:T(8,128)(2,1)S(1)} %get-tuple-element.107.refs_1_.refs_6_, bf16[2720,128]{1,0:T(8,128)(2,1)S(1)} %collective-permute-done.refs_2_.refs_7_, ...), custom_call_target="tpu_custom_call" | custom-call | flops 1000 | bytes 1000 | tf_op jit(solution)/shard_map/nets_a/pallas_call | solution.py:1298
  18.9 0.5 send_a.1
  20.4 0.4 collective-permute-done.5.refs_2_
  21.6 0.7 square_a.1
  22.7 2.0 %collective-permute-start.10 = (bf16[656,128]{1,0:T(8,128)(2,1)S(1)}, bf16[656,128]{1,0:T(8,128)(2,1)S(1)}, u32[]{:S(2)}, u32[]{:S(2)}) collective-permute-start(bf16[656,128]{1,0:T(8,128)(2,1)S(1)} %get-tuple-element.127), channel_id=1, source_target_pairs={{0,2},{1,3},{2,0},{3,1},{4,6},{5,7},{6,4},{7,5},{8,10},{9,11},{10,... | collective-permute-start | bytes 503816 | tf_op jit(solution)/shard_map/ppermute | solution.py:1379
  24.6 1.5 %collective-permute-start.11 = (bf16[656,128]{1,0:T(8,128)(2,1)S(1)}, bf16[656,128]{1,0:T(8,128)(2,1)S(1)}, u32[]{:S(2)}, u32[]{:S(2)}) collective-permute-start(bf16[656,128]{1,0:T(8,128)(2,1)S(1)} %get-tuple-element.128), channel_id=1, source_target_pairs={{0,6},{1,7},{2,4},{3,5},{4,2},{5,3},{6,0},{7,1},{8,14},{9,15},{10,... | collective-permute-start | bytes 503816 | tf_op jit(solution)/shard_map/ppermute | solution.py:1379
  26.2 4.7 %nets_b.1 = (f32[2,1536,128]{2,1,0:T(8,128)S(1)}, f32[2,1536,128]{2,1,0:T(8,128)S(1)}, f32[40,512]{1,0:T(8,128)S(1)}, f32[64,128]{1,0:T(8,128)S(1)}) custom-call(s32[8,128]{1,0:T(8,128)S(1)} %iota.7.refs_0_, bf16[2720,128]{1,0:T(8,128)(2,1)S(1)} %get-tuple-element.107.refs_1_.refs_6_, bf16[2720,128]{1,0:T(8,128)(2,1)S(1)} %collective-permute-done.refs_2_.refs_7_, ...), custom_call_target="tpu_custom_call" | custom-call | flops 1000 | bytes 1000 | tf_op jit(solution)/shard_map/nets_b/pallas_call | solution.py:1298
  30.9 3.4 %flow_back.1.refs_5_.refs_6_ = f32[40,128]{1,0:T(8,128)S(1)} custom-call(f32[112,512]{1,0:T(8,128)S(1)} %get-tuple-element.123.refs_5_.refs_0_, f32[168,128]{1,0:T(8,128)S(1)} %get-tuple-element.124.refs_6_.refs_1_, f32[320,128]{1,0:T(8,128)S(1)} %get-tuple-element.115.refs_6_.refs_2_, f32[40,512]{1,0:T(8,128)S(1)} %get-tuple-element.130.refs_3_, ...), custom_call_target="tpu_custom_call" | custom-call | flops 1000 | bytes 1000 | tf_op jit(solution)/shard_map/flow_back/pallas_call | solution.py:1298
  34.3 1.4 %collective-permute-done.12.refs_4_ = bf16[656,128]{1,0:T(8,128)(2,1)S(1)} collective-permute-done((bf16[656,128]{1,0:T(8,128)(2,1)S(1)}, bf16[656,128]{1,0:T(8,128)(2,1)S(1)}, u32[]{:S(2)}, u32[]{:S(2)}) %collective-permute-start.12) | collective-permute-done | bytes 167968 | tf_op jit(solution)/shard_map/ppermute | solution.py:1379
  35.6 0.4 column_a.1
  36.0 0.8 %send_b.1 = (bf16[816,128]{1,0:T(8,128)(2,1)S(1)}, bf16[816,128]{1,0:T(8,128)(2,1)S(1)}, bf16[816,128]{1,0:T(8,128)(2,1)S(1)}, bf16[816,128]{1,0:T(8,128)(2,1)S(1)}) custom-call(s32[8,128]{1,0:T(8,128)S(1)} %iota.7.refs_0_, f32[2,1536,128]{2,1,0:T(8,128)S(1)} %get-tuple-element.126.refs_1_, f32[304,128]{1,0:T(8,128)S(1)} %get-tuple-element.133.refs_2_.refs_1_), custom_call_target="tpu_custom_call" | custom-call | flops 1000 | bytes 1000 | tf_op jit(solution)/shard_map/send_b/pallas_call | solution.py:1298
  36.9 0.5 collective-permute-start.14
  37.5 0.4 collective-permute-start.16
  37.9 0.4 collective-permute-done.13.refs_2_
  39.2 0.9 %square_b.1 = (f32[768,128]{1,0:T(8,128)S(1)}, bf16[48,128]{1,0:T(8,128)(2,1)S(1)}, bf16[864,128]{1,0:T(8,128)(2,1)S(1)}, bf16[864,128]{1,0:T(8,128)(2,1)S(1)}, bf16[864,128]{1,0:T(8,128)(2,1)S(1)}) custom-call(s32[8,128]{1,0:T(8,128)S(1)} %iota.7.refs_0_, f32[2,1536,128]{2,1,0:T(8,128)S(1)} %get-tuple-element.125.refs_10_.refs_1_, ...), custom_call_target="tpu_custom_call" | custom-call | flops 1000 | bytes 1000 | tf_op jit(solution)/shard_map/square_b/pallas_call | solution.py:1298
  40.2 0.8 collective-permute-start.17
  40.9 1.5 %collective-permute-start.18 = (bf16[864,128]{1,0:T(8,128)(2,1)S(1)}, bf16[864,128]{1,0:T(8,128)(2,1)S(1)}, u32[]{:S(2)}, u32[]{:S(2)}) collective-permute-start(bf16[864,128]{1,0:T(8,128)(2,1)S(1)} %get-tuple-element.141), channel_id=1, source_target_pairs={{0,2},{1,3},{2,0},{3,1},{4,6},{5,7},{6,4},{7,5},{8,10},{9,11},{10,... | collective-permute-start | bytes 663560 | tf_op jit(solution)/shard_map/ppermute | solution.py:1379
  42.4 1.3 %collective-permute-start.19 = (bf16[864,128]{1,0:T(8,128)(2,1)S(1)}, bf16[864,128]{1,0:T(8,128)(2,1)S(1)}, u32[]{:S(2)}, u32[]{:S(2)}) collective-permute-start(bf16[864,128]{1,0:T(8,128)(2,1)S(1)} %get-tuple-element.142), channel_id=1, source_target_pairs={{0,6},{1,7},{2,4},{3,5},{4,2},{5,3},{6,0},{7,1},{8,14},{9,15},{10,... | collective-permute-start | bytes 663560 | tf_op jit(solution)/shard_map/ppermute | solution.py:1379
  43.7 1.6 %collective-permute-start.20 = (bf16[336,128]{1,0:T(8,128)(2,1)S(1)}, bf16[336,128]{1,0:T(8,128)(2,1)S(1)}, u32[]{:S(2)}, u32[]{:S(2)}) collective-permute-start(bf16[336,128]{1,0:T(8,128)(2,1)S(1)} %get-tuple-element.143), channel_id=1, source_target_pairs={{0,8},{1,9},{2,10},{3,11},{4,12},{5,13},{6,14},{7,15},{8,0},{9,1},... | collective-permute-start | bytes 258056 | tf_op jit(solution)/shard_map/ppermute | solution.py:1379
  45.3 2.9 %collective-permute-done.20.refs_2_ = bf16[336,128]{1,0:T(8,128)(2,1)S(1)} collective-permute-done((bf16[336,128]{1,0:T(8,128)(2,1)S(1)}, bf16[336,128]{1,0:T(8,128)(2,1)S(1)}, u32[]{:S(2)}, u32[]{:S(2)}) %collective-permute-start.20) | collective-permute-done | bytes 86048 | tf_op jit(solution)/shard_map/ppermute | solution.py:1379
  48.3 2.7 %collective-permute-start.21 = (bf16[336,128]{1,0:T(8,128)(2,1)S(1)}, bf16[336,128]{1,0:T(8,128)(2,1)S(1)}, u32[]{:S(2)}, u32[]{:S(2)}) collective-permute-start(bf16[336,128]{1,0:T(8,128)(2,1)S(1)} %code_a.1.refs_1_.refs_3_), channel_id=1, source_target_pairs={{0,16},{1,17},{2,18},{3,19},{4,20},{5,21},{6,22},{7,23},{8,24},{9,... | collective-permute-start | bytes 258056 | tf_op jit(solution)/shard_map/ppermute | solution.py:1379
  51.0 2.8 %collective-permute-done.21.refs_2_ = bf16[336,128]{1,0:T(8,128)(2,1)S(1)} collective-permute-done((bf16[336,128]{1,0:T(8,128)(2,1)S(1)}, bf16[336,128]{1,0:T(8,128)(2,1)S(1)}, u32[]{:S(2)}, u32[]{:S(2)}) %collective-permute-start.21) | collective-permute-done | bytes 86048 | tf_op jit(solution)/shard_map/ppermute | solution.py:1379
  54.1 0.5 column_b.1
  54.6 1.7 %collective-permute-start.22 = (bf16[448,128]{1,0:T(8,128)(2,1)S(1)}, bf16[448,128]{1,0:T(8,128)(2,1)S(1)}, u32[]{:S(2)}, u32[]{:S(2)}) collective-permute-start(bf16[448,128]{1,0:T(8,128)(2,1)S(1)} %get-tuple-element.146), channel_id=1, source_target_pairs={{0,8},{1,9},{2,10},{3,11},{4,12},{5,13},{6,14},{7,15},{8,0},{9,1},... | collective-permute-start | bytes 344072 | tf_op jit(solution)/shard_map/ppermute | solution.py:1379
  56.2 0.4 collective-permute-start.27
  56.7 2.8 %collective-permute-done.22.refs_3_ = bf16[448,128]{1,0:T(8,128)(2,1)S(1)} collective-permute-done((bf16[448,128]{1,0:T(8,128)(2,1)S(1)}, bf16[448,128]{1,0:T(8,128)(2,1)S(1)}, u32[]{:S(2)}, u32[]{:S(2)}) %collective-permute-start.22) | collective-permute-done | bytes 114720 | tf_op jit(solution)/shard_map/ppermute | solution.py:1379
  59.6 3.0 %collective-permute-start.23 = (bf16[448,128]{1,0:T(8,128)(2,1)S(1)}, bf16[448,128]{1,0:T(8,128)(2,1)S(1)}, u32[]{:S(2)}, u32[]{:S(2)}) collective-permute-start(bf16[448,128]{1,0:T(8,128)(2,1)S(1)} %code_b.1.refs_1_.refs_3_), channel_id=1, source_target_pairs={{0,16},{1,17},{2,18},{3,19},{4,20},{5,21},{6,22},{7,23},{8,24},{9,... | collective-permute-start | bytes 344072 | tf_op jit(solution)/shard_map/ppermute | solution.py:1379
  62.7 0.8 collective-permute-start.28
  63.4 1.9 %collective-permute-done.23.refs_2_ = bf16[448,128]{1,0:T(8,128)(2,1)S(1)} collective-permute-done((bf16[448,128]{1,0:T(8,128)(2,1)S(1)}, bf16[448,128]{1,0:T(8,128)(2,1)S(1)}, u32[]{:S(2)}, u32[]{:S(2)}) %collective-permute-start.23) | collective-permute-done | bytes 114720 | tf_op jit(solution)/shard_map/ppermute | solution.py:1379
  65.6 2.4 %collective-permute-start.26 = (bf16[448,128]{1,0:T(8,128)(2,1)S(1)}, bf16[448,128]{1,0:T(8,128)(2,1)S(1)}, u32[]{:S(2)}, u32[]{:S(2)}) collective-permute-start(bf16[448,128]{1,0:T(8,128)(2,1)S(1)} %recode_4_b.1.refs_3_.refs_1_), channel_id=1, source_target_pairs={{0,12},{1,13},{2,14},{3,15},{4,8},{5,9},{6,10},{7,11},{8,4},{9,5},... | collective-permute-start | bytes 344072 | tf_op jit(solution)/shard_map/ppermute | solution.py:1379
  68.0 1.3 %collective-permute-start.24 = (bf16[448,128]{1,0:T(8,128)(2,1)S(1)}, bf16[448,128]{1,0:T(8,128)(2,1)S(1)}, u32[]{:S(2)}, u32[]{:S(2)}) collective-permute-start(bf16[448,128]{1,0:T(8,128)(2,1)S(1)} %recode_4_b.1.refs_3_.refs_1_), channel_id=1, source_target_pairs={{0,4},{1,5},{2,6},{3,7},{4,0},{5,1},{6,2},{7,3},{8,12},{9,13},{10,... | collective-permute-start | bytes 344072 | tf_op jit(solution)/shard_map/ppermute | solution.py:1379
  69.3 2.5 %collective-permute-done.28.refs_2_ = bf16[2,336,128]{2,1,0:T(8,128)(2,1)S(1)} collective-permute-done((bf16[2,336,128]{2,1,0:T(8,128)(2,1)S(1)}, bf16[2,336,128]{2,1,0:T(8,128)(2,1)S(1)}, u32[]{:S(2)}, u32[]{:S(2)}) %collective-permute-start.28) | collective-permute-done | bytes 172064 | tf_op jit(solution)/shard_map/ppermute | solution.py:1379
  72.1 1.1 %norms_a.1 = (f32[216,128]{1,0:T(8,128)S(1)}, f32[1,512,128]{2,1,0:T(8,128)S(1)}, f32[432,128]{1,0:T(8,128)S(1)}, f32[2,128]{1,0:T(2,128)S(1)}, f32[216,128]{1,0...) custom-call(f32[1216,128]{1,0:T(8,128)S(1)} %decode_a.1.refs_0_, ...), custom_call_target="tpu_custom_call" | custom-call | flops 1000 | bytes 1000 | tf_op jit(solution)/shard_map/norms_a/pallas_call | solution.py:1298
  73.4 1.3 %norms_b.1 = (f32[162,128]{1,0:T(8,128)S(1)}, f32[2,512,128]{2,1,0:T(8,128)S(1)}, f32[324,128]{1,0:T(8,128)S(1)}, f32[4,128]{1,0:T(4,128)S(1)}, f32[162,128]{1,0...) custom-call(f32[1536,128]{1,0:T(8,128)S(1)} %get-tuple-element.148.r, ...), custom_call_target="tpu_custom_call" | custom-call | flops 1000 | bytes 1000 | tf_op jit(solution)/shard_map/norms_b/pallas_call | solution.py:1298
  74.6 1.5 %collective-permute-start.30 = (f32[56,128]{1,0:T(8,128)S(1)}, f32[56,128]{1,0:T(8,128)S(1)}, u32[]{:S(2)}, u32[]{:S(2)}) collective-permute-start(f32[56,128]{1,0:T(8,128)S(1)} %get-tuple-element.150.refs_1_), channel_id=1, source_target_pairs={{0,2},{1,3},{2,0},{3,1},{4,6},{5,7},{6,4},{7,5},{8,10},{9,11},{10,... | collective-permute-start | bytes 86024 | tf_op jit(solution)/shard_map/ppermute | solution.py:1379
  76.5 1.8 %moments.1 = (f32[378,128]{1,0:T(8,128)}, f32[3,512,128]{2,1,0:T(8,128)}, f32[756,128]{1,0:T(8,128)}, f32[3,2,128]{2,1,0:T(2,128)}, f32[378,128]{1,0:T(8,128)}, ...) custom-call(f32[216,128]{1,0:T(8,128)S(1)} %get-tuple-element.159.refs_0_, ...), custom_call_target="tpu_custom_call" | custom-call | flops 1000 | bytes 1000 | tf_op jit(solution)/shard_map/moments/pallas_call | solution.py:1298
  78.6 1.8 %apply.1 = (f32[378,128]{1,0:T(8,128)}, f32[3,512,128]{2,1,0:T(8,128)}, f32[756,128]{1,0:T(8,128)}, f32[3,2,128]{2,1,0:T(2,128)}, f32[3852]{0:T(1024)}, /*index=...) custom-call(s32[8,128]{1,0:T(8,128)S(1)} %iota.7.refs_0_, ...), custom_call_target="tpu_custom_call" | custom-call | flops 1000 | bytes 1000 | tf_op jit(solution)/shard_map/apply/pallas_call | solution.py:1298
  (82 shorter events, 5.4 us)
Async XLA Ops:
  3.1 13.3 %collective-permute-start = (bf16[2720,128]{1,0:T(8,128)(2,1)}, bf16[2720,128]{1,0:T(8,128)(2,1)S(1)}, u32[]{:S(2)}, u32[]{:S(2)}) collective-permute-start(bf16[2720,128]{1,0:T(8,128)(2,1)} %get-tuple-element.106.refs_4_), channel_id=1, source_target_pairs={{0,1},{1,0},{2,3},{3,2},{4,5},{5,4},{6,7},{7,6},{8,9},{9,8},{10,11... | collective-permute-start | bytes 2088968 | tf_op jit(solution)/shard_map/ppermute | solution.py:1379
  3.5 11.1 %collective-permute-start.2 = (bf16[1168,128]{1,0:T(8,128)(2,1)}, bf16[1168,128]{1,0:T(8,128)(2,1)S(1)}, u32[]{:S(2)}, u32[]{:S(2)}) collective-permute-start(bf16[1168,128]{1,0:T(8,128)(2,1)} %get-tuple-element.109), channel_id=1, source_target_pairs={{0,2},{1,3},{2,0},{3,1},{4,6},{5,7},{6,4},{7,5},{8,10},{9,11},{10,... | collective-permute-start | bytes 897032 | tf_op jit(solution)/shard_map/ppermute | solution.py:1379
  6.0 16.5 %collective-permute-start.1 = (bf16[1552,128]{1,0:T(8,128)(2,1)}, bf16[1552,128]{1,0:T(8,128)(2,1)S(1)}, u32[]{:S(2)}, u32[]{:S(2)}) collective-permute-start(bf16[1552,128]{1,0:T(8,128)(2,1)} %get-tuple-element.108), channel_id=1, source_target_pairs={{0,2},{1,3},{2,0},{3,1},{4,6},{5,7},{6,4},{7,5},{8,10},{9,11},{10,... | collective-permute-start | bytes 1191944 | tf_op jit(solution)/shard_map/ppermute | solution.py:1379
  6.1 1.1 %copy-start.9 = (bf16[2720,128]{1,0:T(8,128)(2,1)S(1)}, bf16[2720,128]{1,0:T(8,128)(2,1)}, u32[]{:S(2)}) copy-start(bf16[2720,128]{1,0:T(8,128)(2,1)} %get-tuple-element.106.refs_4_) | copy-start | bytes 2088964
  14.7 1.7 %collective-permute-start.3 = (bf16[736,128]{1,0:T(8,128)(2,1)S(1)}, bf16[736,128]{1,0:T(8,128)(2,1)S(1)}, u32[]{:S(2)}, u32[]{:S(2)}) collective-permute-start(bf16[736,128]{1,0:T(8,128)(2,1)S(1)} %get-tuple-element.113), channel_id=1, source_target_pairs={{0,1},{1,0},{2,3},{3,2},{4,5},{5,4},{6,7},{7,6},{8,9},{9,8},{10,11... | collective-permute-start | bytes 565256 | tf_op jit(solution)/shard_map/ppermute | solution.py:1379
  15.0 1.4 %collective-permute-start.4 = (bf16[432,128]{1,0:T(8,128)(2,1)S(1)}, bf16[432,128]{1,0:T(8,128)(2,1)S(1)}, u32[]{:S(2)}, u32[]{:S(2)}) collective-permute-start(bf16[432,128]{1,0:T(8,128)(2,1)S(1)} %get-tuple-element.114), channel_id=1, source_target_pairs={{0,1},{1,0},{2,3},{3,2},{4,5},{5,4},{6,7},{7,6},{8,9},{9,8},{10,11... | collective-permute-start | bytes 331784 | tf_op jit(solution)/shard_map/ppermute | solution.py:1379
  19.3 1.5 %collective-permute-start.5 = (bf16[656,128]{1,0:T(8,128)(2,1)S(1)}, bf16[656,128]{1,0:T(8,128)(2,1)S(1)}, u32[]{:S(2)}, u32[]{:S(2)}) collective-permute-start(bf16[656,128]{1,0:T(8,128)(2,1)S(1)} %get-tuple-element.118), channel_id=1, source_target_pairs={{0,1},{1,0},{2,3},{3,2},{4,5},{5,4},{6,7},{7,6},{8,9},{9,8},{10,11... | collective-permute-start | bytes 503816 | tf_op jit(solution)/shard_map/ppermute | solution.py:1379
  19.6 1.4 %collective-permute-start.6 = (bf16[656,128]{1,0:T(8,128)(2,1)S(1)}, bf16[656,128]{1,0:T(8,128)(2,1)S(1)}, u32[]{:S(2)}, u32[]{:S(2)}) collective-permute-start(bf16[656,128]{1,0:T(8,128)(2,1)S(1)} %get-tuple-element.119), channel_id=1, source_target_pairs={{0,1},{1,0},{2,3},{3,2},{4,5},{5,4},{6,7},{7,6},{8,9},{9,8},{10,11... | collective-permute-start | bytes 503816 | tf_op jit(solution)/shard_map/ppermute | solution.py:1379
  19.9 1.4 %collective-permute-start.7 = (bf16[656,128]{1,0:T(8,128)(2,1)S(1)}, bf16[656,128]{1,0:T(8,128)(2,1)S(1)}, u32[]{:S(2)}, u32[]{:S(2)}) collective-permute-start(bf16[656,128]{1,0:T(8,128)(2,1)S(1)} %get-tuple-element.120), channel_id=1, source_target_pairs={{0,1},{1,0},{2,3},{3,2},{4,5},{5,4},{6,7},{7,6},{8,9},{9,8},{10,11... | collective-permute-start | bytes 503816 | tf_op jit(solution)/shard_map/ppermute | solution.py:1379
  20.2 1.4 %collective-permute-start.8 = (bf16[656,128]{1,0:T(8,128)(2,1)S(1)}, bf16[656,128]{1,0:T(8,128)(2,1)S(1)}, u32[]{:S(2)}, u32[]{:S(2)}) collective-permute-start(bf16[656,128]{1,0:T(8,128)(2,1)S(1)} %get-tuple-element.121), channel_id=1, source_target_pairs={{0,1},{1,0},{2,3},{3,2},{4,5},{5,4},{6,7},{7,6},{8,9},{9,8},{10,11... | collective-permute-start | bytes 503816 | tf_op jit(solution)/shard_map/ppermute | solution.py:1379
  22.5 3.6 %collective-permute-start.9 = (bf16[1552,128]{1,0:T(8,128)(2,1)S(1)}, bf16[1552,128]{1,0:T(8,128)(2,1)S(1)}, u32[]{:S(2)}, u32[]{:S(2)}) collective-permute-start(bf16[1552,128]{1,0:T(8,128)(2,1)S(1)} %copy_b.1.refs_7_), channel_id=1, source_target_pairs={{0,1},{1,0},{2,3},{3,2},{4,5},{5,4},{6,7},{7,6},{8,9},{9,8},{10,11... | collective-permute-start | bytes 1191944 | tf_op jit(solution)/shard_map/ppermute | solution.py:1379
  22.7 11.6 %collective-permute-start.10 = (bf16[656,128]{1,0:T(8,128)(2,1)S(1)}, bf16[656,128]{1,0:T(8,128)(2,1)S(1)}, u32[]{:S(2)}, u32[]{:S(2)}) collective-permute-start(bf16[656,128]{1,0:T(8,128)(2,1)S(1)} %get-tuple-element.127), channel_id=1, source_target_pairs={{0,2},{1,3},{2,0},{3,1},{4,6},{5,7},{6,4},{7,5},{8,10},{9,11},{10,... | collective-permute-start | bytes 503816 | tf_op jit(solution)/shard_map/ppermute | solution.py:1379
  24.6 9.6 %collective-permute-start.11 = (bf16[656,128]{1,0:T(8,128)(2,1)S(1)}, bf16[656,128]{1,0:T(8,128)(2,1)S(1)}, u32[]{:S(2)}, u32[]{:S(2)}) collective-permute-start(bf16[656,128]{1,0:T(8,128)(2,1)S(1)} %get-tuple-element.128), channel_id=1, source_target_pairs={{0,6},{1,7},{2,4},{3,5},{4,2},{5,3},{6,0},{7,1},{8,14},{9,15},{10,... | collective-permute-start | bytes 503816 | tf_op jit(solution)/shard_map/ppermute | solution.py:1379
  26.2 9.5 %collective-permute-start.12 = (bf16[656,128]{1,0:T(8,128)(2,1)S(1)}, bf16[656,128]{1,0:T(8,128)(2,1)S(1)}, u32[]{:S(2)}, u32[]{:S(2)}) collective-permute-start(bf16[656,128]{1,0:T(8,128)(2,1)S(1)} %get-tuple-element.129), channel_id=1, source_target_pairs={{0,4},{1,5},{2,6},{3,7},{4,0},{5,1},{6,2},{7,3},{8,12},{9,13},{10,... | collective-permute-start | bytes 503816 | tf_op jit(solution)/shard_map/ppermute | solution.py:1379
  36.8 1.5 %collective-permute-start.13 = (bf16[816,128]{1,0:T(8,128)(2,1)S(1)}, bf16[816,128]{1,0:T(8,128)(2,1)S(1)}, u32[]{:S(2)}, u32[]{:S(2)}) collective-permute-start(bf16[816,128]{1,0:T(8,128)(2,1)S(1)} %get-tuple-element.134), channel_id=1, source_target_pairs={{0,1},{1,0},{2,3},{3,2},{4,5},{5,4},{6,7},{7,6},{8,9},{9,8},{10,11... | collective-permute-start | bytes 626696 | tf_op jit(solution)/shard_map/ppermute | solution.py:1379
  36.9 1.7 %collective-permute-start.14 = (bf16[816,128]{1,0:T(8,128)(2,1)S(1)}, bf16[816,128]{1,0:T(8,128)(2,1)S(1)}, u32[]{:S(2)}, u32[]{:S(2)}) collective-permute-start(bf16[816,128]{1,0:T(8,128)(2,1)S(1)} %get-tuple-element.135), channel_id=1, source_target_pairs={{0,1},{1,0},{2,3},{3,2},{4,5},{5,4},{6,7},{7,6},{8,9},{9,8},{10,11... | collective-permute-start | bytes 626696 | tf_op jit(solution)/shard_map/ppermute | solution.py:1379
  37.4 1.5 %collective-permute-start.15 = (bf16[816,128]{1,0:T(8,128)(2,1)S(1)}, bf16[816,128]{1,0:T(8,128)(2,1)S(1)}, u32[]{:S(2)}, u32[]{:S(2)}) collective-permute-start(bf16[816,128]{1,0:T(8,128)(2,1)S(1)} %get-tuple-element.136), channel_id=1, source_target_pairs={{0,1},{1,0},{2,3},{3,2},{4,5},{5,4},{6,7},{7,6},{8,9},{9,8},{10,11... | collective-permute-start | bytes 626696 | tf_op jit(solution)/shard_map/ppermute | solution.py:1379
  37.5 1.8 %collective-permute-start.16 = (bf16[816,128]{1,0:T(8,128)(2,1)S(1)}, bf16[816,128]{1,0:T(8,128)(2,1)S(1)}, u32[]{:S(2)}, u32[]{:S(2)}) collective-permute-start(bf16[816,128]{1,0:T(8,128)(2,1)S(1)} %get-tuple-element.137), channel_id=1, source_target_pairs={{0,1},{1,0},{2,3},{3,2},{4,5},{5,4},{6,7},{7,6},{8,9},{9,8},{10,11... | collective-permute-start | bytes 626696 | tf_op jit(solution)/shard_map/ppermute | solution.py:1379
  40.2 13.8 %collective-permute-start.17 = (bf16[864,128]{1,0:T(8,128)(2,1)S(1)}, bf16[864,128]{1,0:T(8,128)(2,1)S(1)}, u32[]{:S(2)}, u32[]{:S(2)}) collective-permute-start(bf16[864,128]{1,0:T(8,128)(2,1)S(1)} %get-tuple-element.140), channel_id=1, source_target_pairs={{0,4},{1,5},{2,6},{3,7},{4,0},{5,1},{6,2},{7,3},{8,12},{9,13},{10,... | collective-permute-start | bytes 663560 | tf_op jit(solution)/shard_map/ppermute | solution.py:1379
  40.9 13.0 %collective-permute-start.18 = (bf16[864,128]{1,0:T(8,128)(2,1)S(1)}, bf16[864,128]{1,0:T(8,128)(2,1)S(1)}, u32[]{:S(2)}, u32[]{:S(2)}) collective-permute-start(bf16[864,128]{1,0:T(8,128)(2,1)S(1)} %get-tuple-element.141), channel_id=1, source_target_pairs={{0,2},{1,3},{2,0},{3,1},{4,6},{5,7},{6,4},{7,5},{8,10},{9,11},{10,... | collective-permute-start | bytes 663560 | tf_op jit(solution)/shard_map/ppermute | solution.py:1379
  42.4 11.5 %collective-permute-start.19 = (bf16[864,128]{1,0:T(8,128)(2,1)S(1)}, bf16[864,128]{1,0:T(8,128)(2,1)S(1)}, u32[]{:S(2)}, u32[]{:S(2)}) collective-permute-start(bf16[864,128]{1,0:T(8,128)(2,1)S(1)} %get-tuple-element.142), channel_id=1, source_target_pairs={{0,6},{1,7},{2,4},{3,5},{4,2},{5,3},{6,0},{7,1},{8,14},{9,15},{10,... | collective-permute-start | bytes 663560 | tf_op jit(solution)/shard_map/ppermute | solution.py:1379
  43.7 4.5 %collective-permute-start.20 = (bf16[336,128]{1,0:T(8,128)(2,1)S(1)}, bf16[336,128]{1,0:T(8,128)(2,1)S(1)}, u32[]{:S(2)}, u32[]{:S(2)}) collective-permute-start(bf16[336,128]{1,0:T(8,128)(2,1)S(1)} %get-tuple-element.143), channel_id=1, source_target_pairs={{0,8},{1,9},{2,10},{3,11},{4,12},{5,13},{6,14},{7,15},{8,0},{9,1},... | collective-permute-start | bytes 258056 | tf_op jit(solution)/shard_map/ppermute | solution.py:1379
  48.2 23.8 %copy-start.8 = (f32[378,128]{1,0:T(8,128)S(1)}, f32[378,128]{1,0:T(8,128)}, u32[]{:S(2)}) copy-start(f32[378,128]{1,0:T(8,128)} %refs_12_.3) | copy-start | bytes 580612
  48.3 5.4 %collective-permute-start.21 = (bf16[336,128]{1,0:T(8,128)(2,1)S(1)}, bf16[336,128]{1,0:T(8,128)(2,1)S(1)}, u32[]{:S(2)}, u32[]{:S(2)}) collective-permute-start(bf16[336,128]{1,0:T(8,128)(2,1)S(1)} %code_a.1.refs_1_.refs_3_), channel_id=1, source_target_pairs={{0,16},{1,17},{2,18},{3,19},{4,20},{5,21},{6,22},{7,23},{8,24},{9,... | collective-permute-start | bytes 258056 | tf_op jit(solution)/shard_map/ppermute | solution.py:1379
  53.8 18.2 %copy-start.6 = (f32[378,128]{1,0:T(8,128)S(1)}, f32[378,128]{1,0:T(8,128)}, u32[]{:S(2)}) copy-start(f32[378,128]{1,0:T(8,128)} %refs_5_.3) | copy-start | bytes 580612
  53.8 18.2 %copy-start.7 = (f32[378,128]{1,0:T(8,128)S(1)}, f32[378,128]{1,0:T(8,128)}, u32[]{:S(2)}) copy-start(f32[378,128]{1,0:T(8,128)} %refs_8_.4) | copy-start | bytes 580612
  54.0 18.0 %copy-start = (f32[3,512,128]{2,1,0:T(8,128)S(1)}, f32[3,512,128]{2,1,0:T(8,128)}, u32[]{:S(2)}) copy-start(f32[3,512,128]{2,1,0:T(8,128)} %refs_6_.5) | copy-start | bytes 2359300
  54.0 18.0 %copy-start.1 = (f32[3,512,128]{2,1,0:T(8,128)S(1)}, f32[3,512,128]{2,1,0:T(8,128)}, u32[]{:S(2)}) copy-start(f32[3,512,128]{2,1,0:T(8,128)} %refs_9_.3) | copy-start | bytes 2359300
  54.0 18.0 %copy-start.2 = (f32[3,512,128]{2,1,0:T(8,128)S(1)}, f32[3,512,128]{2,1,0:T(8,128)}, u32[]{:S(2)}) copy-start(f32[3,512,128]{2,1,0:T(8,128)} %refs_13_.3) | copy-start | bytes 2359300
  54.0 18.0 %copy-start.3 = (f32[128,756]{0,1:T(8,128)S(1)}, f32[128,756]{0,1:T(8,128)}, u32[]{:S(2)}) copy-start(f32[128,756]{0,1:T(8,128)} %param.23) | copy-start | bytes 1161220
  54.0 18.0 %copy-start.4 = (f32[128,756]{0,1:T(8,128)S(1)}, f32[128,756]{0,1:T(8,128)}, u32[]{:S(2)}) copy-start(f32[128,756]{0,1:T(8,128)} %param.28) | copy-start | bytes 1161220
  54.0 18.0 %copy-start.5 = (f32[128,756]{0,1:T(8,128)S(1)}, f32[128,756]{0,1:T(8,128)}, u32[]{:S(2)}) copy-start(f32[128,756]{0,1:T(8,128)} %param.33) | copy-start | bytes 1161220
  54.0 18.0 %copy-start.12 = (f32[3,2,128]{2,1,0:T(2,128)S(1)}, f32[3,2,128]{2,1,0:T(2,128)}, u32[]{:S(2)}) copy-start(f32[3,2,128]{2,1,0:T(2,128)} %refs_8_.5) | copy-start | bytes 9220
  54.0 18.0 %copy-start.13 = (f32[3,2,128]{2,1,0:T(2,128)S(1)}, f32[3,2,128]{2,1,0:T(2,128)}, u32[]{:S(2)}) copy-start(f32[3,2,128]{2,1,0:T(2,128)} %refs_11_.5) | copy-start | bytes 9220
  54.1 18.0 %copy-start.14 = (f32[3,2,128]{2,1,0:T(2,128)S(1)}, f32[3,2,128]{2,1,0:T(2,128)}, u32[]{:S(2)}) copy-start(f32[3,2,128]{2,1,0:T(2,128)} %refs_15_.1) | copy-start | bytes 9220
  54.6 4.9 %collective-permute-start.22 = (bf16[448,128]{1,0:T(8,128)(2,1)S(1)}, bf16[448,128]{1,0:T(8,128)(2,1)S(1)}, u32[]{:S(2)}, u32[]{:S(2)}) collective-permute-start(bf16[448,128]{1,0:T(8,128)(2,1)S(1)} %get-tuple-element.146), channel_id=1, source_target_pairs={{0,8},{1,9},{2,10},{3,11},{4,12},{5,13},{6,14},{7,15},{8,0},{9,1},... | collective-permute-start | bytes 344072 | tf_op jit(solution)/shard_map/ppermute | solution.py:1379
  56.2 6.4 %collective-permute-start.27 = (bf16[336,128]{1,0:T(8,128)(2,1)S(1)}, bf16[336,128]{1,0:T(8,128)(2,1)S(1)}, u32[]{:S(2)}, u32[]{:S(2)}) collective-permute-start(bf16[336,128]{1,0:T(8,128)(2,1)S(1)} %recode_4_a.1.refs_6_.refs_1_), channel_id=1, source_target_pairs={{0,8},{1,9},{2,10},{3,11},{4,12},{5,13},{6,14},{7,15},{8,0},{9,1},... | collective-permute-start | bytes 258056 | tf_op jit(solution)/shard_map/ppermute | solution.py:1379
  59.6 5.8 %collective-permute-start.23 = (bf16[448,128]{1,0:T(8,128)(2,1)S(1)}, bf16[448,128]{1,0:T(8,128)(2,1)S(1)}, u32[]{:S(2)}, u32[]{:S(2)}) collective-permute-start(bf16[448,128]{1,0:T(8,128)(2,1)S(1)} %code_b.1.refs_1_.refs_3_), channel_id=1, source_target_pairs={{0,16},{1,17},{2,18},{3,19},{4,20},{5,21},{6,22},{7,23},{8,24},{9,... | collective-permute-start | bytes 344072 | tf_op jit(solution)/shard_map/ppermute | solution.py:1379
  62.7 9.2 %collective-permute-start.28 = (bf16[2,336,128]{2,1,0:T(8,128)(2,1)S(1)}, bf16[2,336,128]{2,1,0:T(8,128)(2,1)S(1)}, u32[]{:S(2)}, u32[]{:S(2)}) collective-permute-start(bf16[2,336,128]{2,1,0:T(8,128)(2,1)S(1)} %pair_a.1.refs_1_), channel_id=1, source_target_pairs={{0,4},{1,5},{2,6},{3,7},{4,0},{5,1},{6,2},{7,3},{8,12},{9,13},{10,... | collective-permute-start | bytes 516104 | tf_op jit(solution)/shard_map/ppermute | solution.py:1379
  65.6 7.6 %collective-permute-start.26 = (bf16[448,128]{1,0:T(8,128)(2,1)S(1)}, bf16[448,128]{1,0:T(8,128)(2,1)S(1)}, u32[]{:S(2)}, u32[]{:S(2)}) collective-permute-start(bf16[448,128]{1,0:T(8,128)(2,1)S(1)} %recode_4_b.1.refs_3_.refs_1_), channel_id=1, source_target_pairs={{0,12},{1,13},{2,14},{3,15},{4,8},{5,9},{6,10},{7,11},{8,4},{9,5},... | collective-permute-start | bytes 344072 | tf_op jit(solution)/shard_map/ppermute | solution.py:1379
  68.0 5.2 %collective-permute-start.25 = (bf16[448,128]{1,0:T(8,128)(2,1)S(1)}, bf16[448,128]{1,0:T(8,128)(2,1)S(1)}, u32[]{:S(2)}, u32[]{:S(2)}) collective-permute-start(bf16[448,128]{1,0:T(8,128)(2,1)S(1)} %recode_4_b.1.refs_3_.refs_1_), channel_id=1, source_target_pairs={{0,8},{1,9},{2,10},{3,11},{4,12},{5,13},{6,14},{7,15},{8,0},{9,1},... | collective-permute-start | bytes 344072 | tf_op jit(solution)/shard_map/ppermute | solution.py:1379
  68.0 5.2 %collective-permute-start.24 = (bf16[448,128]{1,0:T(8,128)(2,1)S(1)}, bf16[448,128]{1,0:T(8,128)(2,1)S(1)}, u32[]{:S(2)}, u32[]{:S(2)}) collective-permute-start(bf16[448,128]{1,0:T(8,128)(2,1)S(1)} %recode_4_b.1.refs_3_.refs_1_), channel_id=1, source_target_pairs={{0,4},{1,5},{2,6},{3,7},{4,0},{5,1},{6,2},{7,3},{8,12},{9,13},{10,... | collective-permute-start | bytes 344072 | tf_op jit(solution)/shard_map/ppermute | solution.py:1379
  74.6 3.7 %collective-permute-start.31 = (f32[56,128]{1,0:T(8,128)S(1)}, f32[56,128]{1,0:T(8,128)S(1)}, u32[]{:S(2)}, u32[]{:S(2)}) collective-permute-start(f32[56,128]{1,0:T(8,128)S(1)} %get-tuple-element.150.refs_1_), channel_id=1, source_target_pairs={{0,3},{1,2},{2,1},{3,0},{4,7},{5,6},{6,5},{7,4},{8,11},{9,10},{10,... | collective-permute-start | bytes 86024 | tf_op jit(solution)/shard_map/ppermute | solution.py:1379
  74.6 3.9 %collective-permute-start.30 = (f32[56,128]{1,0:T(8,128)S(1)}, f32[56,128]{1,0:T(8,128)S(1)}, u32[]{:S(2)}, u32[]{:S(2)}) collective-permute-start(f32[56,128]{1,0:T(8,128)S(1)} %get-tuple-element.150.refs_1_), channel_id=1, source_target_pairs={{0,2},{1,3},{2,0},{3,1},{4,6},{5,7},{6,4},{7,5},{8,10},{9,11},{10,... | collective-permute-start | bytes 86024 | tf_op jit(solution)/shard_map/ppermute | solution.py:1379
  76.2 2.4 %collective-permute-start.29 = (f32[56,128]{1,0:T(8,128)S(1)}, f32[56,128]{1,0:T(8,128)S(1)}, u32[]{:S(2)}, u32[]{:S(2)}) collective-permute-start(f32[56,128]{1,0:T(8,128)S(1)} %get-tuple-element.150.refs_1_), channel_id=1, source_target_pairs={{0,1},{1,0},{2,3},{3,2},{4,5},{5,4},{6,7},{7,6},{8,9},{9,8},{10,11... | collective-permute-start | bytes 86024 | tf_op jit(solution)/shard_map/ppermute | solution.py:1379
  76.5 2.1 %copy-start.11 = (f32[3852]{0:T(1024)S(1)}, f32[3852]{0:T(1024)}, u32[]{:S(2)}) copy-start(f32[3852]{0:T(1024)} %refs_17_.1) | copy-start | bytes 46228
  76.5 2.1 %copy-start.16 = (f32[3852]{0:T(1024)S(1)}, f32[3852]{0:T(1024)}, u32[]{:S(2)}) copy-start(f32[3852]{0:T(1024)} %refs_18_.1) | copy-start | bytes 46228
  76.5 2.1 %copy-start.17 = (f32[3852]{0:T(1024)S(1)}, f32[3852]{0:T(1024)}, u32[]{:S(2)}) copy-start(f32[3852]{0:T(1024)} %refs_19_.1) | copy-start | bytes 46228
  (4 other events, 2.8 us)

commit v7 on v6

--- a/solution.py
+++ b/solution.py
@@ -27,7 +27,7 @@
 STATS_ROWS = 8
 CODE_BLOCK = 16
 CODE_RANGE = 84.0
-SQUARE_ORDER = ((1, 3, 2), (2, 1, 3))
+SQUARE_ORDER = ((2, 1, 3), (2, 1, 3))
 RETURN_ORDER = (2, 1, 3)
 VMEM_BYTES = 20 * 1024 * 1024
 
@@ -1002,12 +1002,19 @@
         write_piece(out_ref, 0, total)
 
 
-def recode_kernel(chunk, index_ref, mine_ref, other_ref, out_ref):
-    rows = quarter_rows(chunk) + flow_part(chunk)
+def recode_kernel(chunk, final, index_ref, mine_ref, other_ref, out_ref, *flow_refs):
+    count, more = quarter_rows(chunk), flow_part(chunk)
+    rows = count + more
+    total = read_piece(mine_ref, 0, rows) + read_piece(other_ref, 0, rows)
     stats = None
-    if flow_part(chunk):
+    if more:
         stats = read_stats(mine_ref, 0, rows) + read_stats(other_ref, 0, rows)
-    write_piece(out_ref, 0, read_piece(mine_ref, 0, rows) + read_piece(other_ref, 0, rows), stats)
+    if more and final:
+        write_piece(out_ref, 0, total[:count])
+        flow_refs[0][0:FLOW_ROWS, :] = total[count:]
+        flow_refs[0][FLOW_ROWS:, :] = jnp.broadcast_to(stats, (STATS_ROWS, LANE))
+    else:
+        write_piece(out_ref, 0, total, stats)
 
 
 def pair_kernel(chunk, index_ref, mine_ref, other_ref, out_ref):
@@ -1026,18 +1033,12 @@
 
 
 def decode_kernel(chunk, index_ref, *refs):
-    parts, outs = refs[:4], refs[4:]
+    parts, out_ref = refs[:4], refs[4]
     place = 2 * wide_bit(index_ref, 1) + wide_bit(index_ref, 2)
-    rows, more = quarter_rows(chunk), flow_part(chunk)
+    rows = quarter_rows(chunk)
     for flip, ref in zip((0, *RETURN_ORDER), parts):
-        values = read_piece(ref, 0, rows + more)
         start = pl.multiple_of((place ^ flip) * rows, CODE_BLOCK)
-        outs[0][pl.ds(start, rows), :] = values[:rows]
-        if more and flip == 0:
-            outs[1][0:FLOW_ROWS, :] = values[rows:]
-            outs[1][FLOW_ROWS:, :] = jnp.broadcast_to(
-                read_stats(ref, 0, rows + more), (STATS_ROWS, LANE)
-            )
+        out_ref[pl.ds(start, rows), :] = read_piece(ref, 0, rows)
 
 
 def moments(weight, gradient, first_old, second_old):
@@ -1132,9 +1133,7 @@
     part_ref, flow_ref, refs = refs[0], refs[1], refs[2:]
     if last:
         sums_ref, refs = refs[0], refs[1:]
-        stats = flow_ref[FLOW_ROWS : FLOW_ROWS + 1, :]
-    else:
-        stats = read_stats(flow_ref, 0, quarter_rows(1) + flow_part(1))
+    stats = flow_ref[FLOW_ROWS : FLOW_ROWS + 1, :]
     weights, firsts, seconds = refs[0:4], refs[4:8], refs[8:12]
     grads, updates, block_ref = refs[12:16], refs[16:20], refs[20]
     scale = 1.0 / (3.0 * stats[:, 1:2] * LOG_TWO)
@@ -1392,9 +1391,9 @@
         self.square_piece = ((piece_rows(2 * rows + more), LANE), BF16)
         self.piece = ((piece_rows(rows + more), LANE), BF16)
 
-    def run(self, kernel, outs, name, after, scratch=(), extra=()):
+    def run(self, kernel, outs, name, after, scratch=(), extra=(), more=()):
         return call(
-            functools.partial(kernel, self.chunk),
+            functools.partial(kernel, self.chunk, *more),
             outs,
             (),
             (self.index, self.kept, *extra, *self.others),
@@ -1442,7 +1441,14 @@
     def spread(self, after):
         step = 4
         while step < lax.axis_size("wide"):
-            (self.kept,) = self.run(recode_kernel, [self.piece], "recode_%d" % step, after)
+            final = 2 * step >= lax.axis_size("wide")
+            shapes = [self.piece]
+            if final and flow_part(self.chunk):
+                rows = quarter_rows(self.chunk)
+                shapes = [((piece_rows(rows), LANE), BF16), ((FLOW_ROWS + STATS_ROWS, LANE), F32)]
+            self.kept, *self.flow = self.run(
+                recode_kernel, shapes, "recode_%d" % step, after, (), (), (final,)
+            )
             step = 2 * step
             if step < lax.axis_size("wide"):
                 self.others = [swap(self.kept, step, 0)]
@@ -1459,7 +1465,6 @@
     def decode(self, after):
         shape = [((4 * quarter_rows(self.chunk), LANE), F32)]
         if flow_part(self.chunk):
-            shape.append(((FLOW_ROWS + STATS_ROWS, LANE), F32))
             return self.run(decode_kernel, shape, "decode", after)
         return self.run(decode_pairs_kernel, shape, "decode", after)
 
@@ -1546,8 +1551,9 @@
         return tuple(outs[:4]), tuple(outs[4:]), block
 
     (part,) = one.decode((token,))
-    grads_one, updates_one, sums = norms(0, (part, token))
-    part, flow = two.decode((sums,))
+    (flow,) = two.flow
+    grads_one, updates_one, sums = norms(0, (part, flow))
+    (part,) = two.decode((sums,))
     grads_two, updates_two, block = norms(1, (part, flow, sums))
     blocks = [block] + [swap(block, 0, part) for part in range(1, narrow)]
     moved = call(

time: 80.8 us -> 80.8 us (level)
  waiting for transfers between devices: 18.3 us -> 16.3 us
  starting transfers between devices: 28.7 us -> 30.3 us
    ppermute x32, waiting for transfers between devices: 18.3 us -> 16.3 us  [swap(): lax.ppermute(values, ('wide', 'narrow'), [(place, place ^ mask) for place...]
    ppermute x32, starting transfers between devices: 28.7 us -> 30.3 us  [swap(): lax.ppermute(values, ('wide', 'narrow'), [(place, place ^ mask) for place...]
  transfers between devices with their start and end apart: 32 -> 32, of which waited for: 17 -> 18; matrix products, arithmetic and copies ran while one was open for 0% -> 0% of each run, Pallas kernels for 25% -> 25%
where the time goes in v7:
time: 80.8 us; the launch traced here: 80.1 us
  starting transfers between devices  30.3 us (38%)
  Pallas kernels  28.3 us (35%)
  waiting for transfers between devices  16.3 us (20%)
  local copies, waits for them, and re-layouts  4.04 us (5%)
  between operations  1.14 us (1%)
    ppermute x32, starting transfers between devices, swap(): lax.ppermute(values, ('wide', 'narrow'), [(place, place ^ mask) for place...  30.3 us
    pallas_call x24, Pallas kernels, call(): pl.pallas_call(run, out_shape=tuple((jax.ShapeDtypeStruct(shape, dtype) f...  28.3 us
    ppermute x32, waiting for transfers between devices, swap(): lax.ppermute(values, ('wide', 'narrow'), [(place, place ^ mask) for place...  16.3 us
    unnamed x40, local copies, waits for them, and re-layouts  3.97 us
  transfers between devices with their start and end apart: 32, of which 18 were waited for; matrix products, arithmetic and copies ran while one was open for 0% of the time, Pallas kernels for 25%

profile of v7, /device:TPU:0, one launch (start us, length us, event | category | flops | bytes accessed | tf_op | source)
XLA Modules:
  0.0 80.1 jit_solution(1408417097361775210)
XLA Ops:
  0.7 2.4 %pack.1 = (bf16[2720,128]{1,0:T(8,128)(2,1)}, bf16[1168,128]{1,0:T(8,128)(2,1)}, bf16[1552,128]{1,0:T(8,128)(2,1)}) custom-call(s32[2,2]{1,0:T(2,128)} %refs_1_.3, f32[378,128]{1,0:T(8,128)} %refs_5_.3, f32[3,512,128]{2,1,0:T(8,128)} %refs_6_.5, f32[756,128]{1,0:T(8,128)} %bitcast.9, f32[3,2,128]{2,1,0:T(2,128)} %refs_8_.5), custom_call_target="tpu_custom_call" | custom-call | flops 1000 | bytes 1000 | tf_op jit(solution)/shard_map/pack/pallas_call | solution.py:1297
  3.1 0.5 collective-permute-start
  3.5 2.5 %collective-permute-start.2 = (bf16[1168,128]{1,0:T(8,128)(2,1)}, bf16[1168,128]{1,0:T(8,128)(2,1)S(1)}, u32[]{:S(2)}, u32[]{:S(2)}) collective-permute-start(bf16[1168,128]{1,0:T(8,128)(2,1)} %get-tuple-element.109), channel_id=1, source_target_pairs={{0,2},{1,3},{2,0},{3,1},{4,6},{5,7},{6,4},{7,5},{8,10},{9,11},{10,... | collective-permute-start | bytes 897032 | tf_op jit(solution)/shard_map/ppermute | solution.py:1378
  6.1 1.1 %copy-done.9 = bf16[2720,128]{1,0:T(8,128)(2,1)S(1)} copy-done((bf16[2720,128]{1,0:T(8,128)(2,1)S(1)}, bf16[2720,128]{1,0:T(8,128)(2,1)}, u32[]{:S(2)}) %copy-start.9) | copy-done | bytes 696344
  7.2 0.7 copy-done.10
  7.9 0.7 copy-done.15
  8.7 0.7 copy-done.18
  9.3 0.7 copy-done.19
  10.0 4.6 %flow_pre.1 = (f32[112,512]{1,0:T(8,128)S(1)}, f32[168,128]{1,0:T(8,128)S(1)}, f32[320,128]{1,0:T(8,128)S(1)}, bf16[2720,128]{1,0:T(8,128)(2,1)S(1)}) custom-call(s32[2]{0:T(128)S(1)} %copy-done.19, s32[2,2]{1,0:T(2,128)S(1)} %copy-done.18, f32[3,2,1024]{2,1,0:T(2,128)S(1)} %copy-done.15, f32[3852]{0:T(1024)S(1)} %copy-done.10, bf16[2720,128]{1,0:T(8,128)(2,1)S(1)} %copy-done.9), custom_call_target="tpu_custom_call" | custom-call | flops 1000 | bytes 1000 | tf_op jit(solution)/shard_map/flow_pre/pallas_call | solution.py:1297
  15.0 0.3 collective-permute-start.4
  15.3 1.1 %collective-permute-done.4.refs_5_ = bf16[432,128]{1,0:T(8,128)(2,1)S(1)} collective-permute-done((bf16[432,128]{1,0:T(8,128)(2,1)S(1)}, bf16[432,128]{1,0:T(8,128)(2,1)S(1)}, u32[]{:S(2)}, u32[]{:S(2)}) %collective-permute-start.4) | collective-permute-done | bytes 110624 | tf_op jit(solution)/shard_map/ppermute | solution.py:1378
  16.4 2.4 %nets_a.1 = (f32[2,1216,128]{2,1,0:T(8,128)S(1)}, f32[2,1216,128]{2,1,0:T(8,128)S(1)}, f32[120,128]{1,0:T(8,128)S(1)}) custom-call(s32[8,128]{1,0:T(8,128)S(1)} %iota.7.refs_0_, bf16[2720,128]{1,0:T(8,128)(2,1)S(1)} %get-tuple-element.107.refs_1_.refs_6_, bf16[2720,128]{1,0:T(8,128)(2,1)S(1)} %collective-permute-done.refs_2_.refs_7_, ...), custom_call_target="tpu_custom_call" | custom-call | flops 1000 | bytes 1000 | tf_op jit(solution)/shard_map/nets_a/pallas_call | solution.py:1297
  18.9 0.5 send_a.1
  19.3 0.3 collective-permute-start.5
  20.4 0.4 collective-permute-done.5.refs_2_
  21.6 0.7 square_a.1
  22.7 2.0 %collective-permute-start.10 = (bf16[656,128]{1,0:T(8,128)(2,1)S(1)}, bf16[656,128]{1,0:T(8,128)(2,1)S(1)}, u32[]{:S(2)}, u32[]{:S(2)}) collective-permute-start(bf16[656,128]{1,0:T(8,128)(2,1)S(1)} %get-tuple-element.127), channel_id=1, source_target_pairs={{0,4},{1,5},{2,6},{3,7},{4,0},{5,1},{6,2},{7,3},{8,12},{9,13},{10,... | collective-permute-start | bytes 503816 | tf_op jit(solution)/shard_map/ppermute | solution.py:1378
  24.7 1.5 %collective-permute-start.11 = (bf16[656,128]{1,0:T(8,128)(2,1)S(1)}, bf16[656,128]{1,0:T(8,128)(2,1)S(1)}, u32[]{:S(2)}, u32[]{:S(2)}) collective-permute-start(bf16[656,128]{1,0:T(8,128)(2,1)S(1)} %get-tuple-element.128), channel_id=1, source_target_pairs={{0,2},{1,3},{2,0},{3,1},{4,6},{5,7},{6,4},{7,5},{8,10},{9,11},{10,... | collective-permute-start | bytes 503816 | tf_op jit(solution)/shard_map/ppermute | solution.py:1378
  26.2 4.7 %nets_b.1 = (f32[2,1536,128]{2,1,0:T(8,128)S(1)}, f32[2,1536,128]{2,1,0:T(8,128)S(1)}, f32[40,512]{1,0:T(8,128)S(1)}, f32[64,128]{1,0:T(8,128)S(1)}) custom-call(s32[8,128]{1,0:T(8,128)S(1)} %iota.7.refs_0_, bf16[2720,128]{1,0:T(8,128)(2,1)S(1)} %get-tuple-element.107.refs_1_.refs_6_, bf16[2720,128]{1,0:T(8,128)(2,1)S(1)} %collective-permute-done.refs_2_.refs_7_, ...), custom_call_target="tpu_custom_call" | custom-call | flops 1000 | bytes 1000 | tf_op jit(solution)/shard_map/nets_b/pallas_call | solution.py:1297
  30.9 3.4 %flow_back.1.refs_5_.refs_6_ = f32[40,128]{1,0:T(8,128)S(1)} custom-call(f32[112,512]{1,0:T(8,128)S(1)} %get-tuple-element.123.refs_5_.refs_0_, f32[168,128]{1,0:T(8,128)S(1)} %get-tuple-element.124.refs_6_.refs_1_, f32[320,128]{1,0:T(8,128)S(1)} %get-tuple-element.115.refs_6_.refs_2_, f32[40,512]{1,0:T(8,128)S(1)} %get-tuple-element.130.refs_3_, ...), custom_call_target="tpu_custom_call" | custom-call | flops 1000 | bytes 1000 | tf_op jit(solution)/shard_map/flow_back/pallas_call | solution.py:1297
  34.3 0.4 column_a.1
  34.7 0.8 %send_b.1 = (bf16[816,128]{1,0:T(8,128)(2,1)S(1)}, bf16[816,128]{1,0:T(8,128)(2,1)S(1)}, bf16[816,128]{1,0:T(8,128)(2,1)S(1)}, bf16[816,128]{1,0:T(8,128)(2,1)S(1)}) custom-call(s32[8,128]{1,0:T(8,128)S(1)} %iota.7.refs_0_, f32[2,1536,128]{2,1,0:T(8,128)S(1)} %get-tuple-element.126.refs_1_, f32[304,128]{1,0:T(8,128)S(1)} %get-tuple-element.133.refs_2_.refs_1_), custom_call_target="tpu_custom_call" | custom-call | flops 1000 | bytes 1000 | tf_op jit(solution)/shard_map/send_b/pallas_call | solution.py:1297
  35.5 0.5 collective-permute-start.14
  36.1 0.4 collective-permute-start.16
  36.6 0.4 collective-permute-done.13.refs_2_
  37.9 0.9 %square_b.1 = (f32[768,128]{1,0:T(8,128)S(1)}, bf16[48,128]{1,0:T(8,128)(2,1)S(1)}, bf16[864,128]{1,0:T(8,128)(2,1)S(1)}, bf16[864,128]{1,0:T(8,128)(2,1)S(1)}, bf16[864,128]{1,0:T(8,128)(2,1)S(1)}) custom-call(s32[8,128]{1,0:T(8,128)S(1)} %iota.7.refs_0_, f32[2,1536,128]{2,1,0:T(8,128)S(1)} %get-tuple-element.125.refs_10_.refs_1_, ...), custom_call_target="tpu_custom_call" | custom-call | flops 1000 | bytes 1000 | tf_op jit(solution)/shard_map/square_b/pallas_call | solution.py:1297
  38.8 2.1 %collective-permute-start.17 = (bf16[864,128]{1,0:T(8,128)(2,1)S(1)}, bf16[864,128]{1,0:T(8,128)(2,1)S(1)}, u32[]{:S(2)}, u32[]{:S(2)}) collective-permute-start(bf16[864,128]{1,0:T(8,128)(2,1)S(1)} %get-tuple-element.140), channel_id=1, source_target_pairs={{0,4},{1,5},{2,6},{3,7},{4,0},{5,1},{6,2},{7,3},{8,12},{9,13},{10,... | collective-permute-start | bytes 663560 | tf_op jit(solution)/shard_map/ppermute | solution.py:1378
  40.9 1.5 %collective-permute-start.18 = (bf16[864,128]{1,0:T(8,128)(2,1)S(1)}, bf16[864,128]{1,0:T(8,128)(2,1)S(1)}, u32[]{:S(2)}, u32[]{:S(2)}) collective-permute-start(bf16[864,128]{1,0:T(8,128)(2,1)S(1)} %get-tuple-element.141), channel_id=1, source_target_pairs={{0,2},{1,3},{2,0},{3,1},{4,6},{5,7},{6,4},{7,5},{8,10},{9,11},{10,... | collective-permute-start | bytes 663560 | tf_op jit(solution)/shard_map/ppermute | solution.py:1378
  42.5 1.9 %collective-permute-start.20 = (bf16[336,128]{1,0:T(8,128)(2,1)S(1)}, bf16[336,128]{1,0:T(8,128)(2,1)S(1)}, u32[]{:S(2)}, u32[]{:S(2)}) collective-permute-start(bf16[336,128]{1,0:T(8,128)(2,1)S(1)} %get-tuple-element.143), channel_id=1, source_target_pairs={{0,8},{1,9},{2,10},{3,11},{4,12},{5,13},{6,14},{7,15},{8,0},{9,1},... | collective-permute-start | bytes 258056 | tf_op jit(solution)/shard_map/ppermute | solution.py:1378
  44.4 2.6 %collective-permute-done.20.refs_2_ = bf16[336,128]{1,0:T(8,128)(2,1)S(1)} collective-permute-done((bf16[336,128]{1,0:T(8,128)(2,1)S(1)}, bf16[336,128]{1,0:T(8,128)(2,1)S(1)}, u32[]{:S(2)}, u32[]{:S(2)}) %collective-permute-start.20) | collective-permute-done | bytes 86048 | tf_op jit(solution)/shard_map/ppermute | solution.py:1378
  47.1 3.0 %collective-permute-start.21 = (bf16[336,128]{1,0:T(8,128)(2,1)S(1)}, bf16[336,128]{1,0:T(8,128)(2,1)S(1)}, u32[]{:S(2)}, u32[]{:S(2)}) collective-permute-start(bf16[336,128]{1,0:T(8,128)(2,1)S(1)} %code_a.1.refs_1_.refs_3_), channel_id=1, source_target_pairs={{0,16},{1,17},{2,18},{3,19},{4,20},{5,21},{6,22},{7,23},{8,24},{9,... | collective-permute-start | bytes 258056 | tf_op jit(solution)/shard_map/ppermute | solution.py:1378
  50.1 2.5 %collective-permute-done.21.refs_2_ = bf16[336,128]{1,0:T(8,128)(2,1)S(1)} collective-permute-done((bf16[336,128]{1,0:T(8,128)(2,1)S(1)}, bf16[336,128]{1,0:T(8,128)(2,1)S(1)}, u32[]{:S(2)}, u32[]{:S(2)}) %collective-permute-start.21) | collective-permute-done | bytes 86048 | tf_op jit(solution)/shard_map/ppermute | solution.py:1378
  52.8 0.5 column_b.1
  53.3 2.0 %collective-permute-start.22 = (bf16[448,128]{1,0:T(8,128)(2,1)S(1)}, bf16[448,128]{1,0:T(8,128)(2,1)S(1)}, u32[]{:S(2)}, u32[]{:S(2)}) collective-permute-start(bf16[448,128]{1,0:T(8,128)(2,1)S(1)} %get-tuple-element.146), channel_id=1, source_target_pairs={{0,8},{1,9},{2,10},{3,11},{4,12},{5,13},{6,14},{7,15},{8,0},{9,1},... | collective-permute-start | bytes 344072 | tf_op jit(solution)/shard_map/ppermute | solution.py:1378
  55.4 3.3 %collective-permute-done.22.refs_3_ = bf16[448,128]{1,0:T(8,128)(2,1)S(1)} collective-permute-done((bf16[448,128]{1,0:T(8,128)(2,1)S(1)}, bf16[448,128]{1,0:T(8,128)(2,1)S(1)}, u32[]{:S(2)}, u32[]{:S(2)}) %collective-permute-start.22) | collective-permute-done | bytes 114720 | tf_op jit(solution)/shard_map/ppermute | solution.py:1378
  58.9 2.8 %collective-permute-start.23 = (bf16[448,128]{1,0:T(8,128)(2,1)S(1)}, bf16[448,128]{1,0:T(8,128)(2,1)S(1)}, u32[]{:S(2)}, u32[]{:S(2)}) collective-permute-start(bf16[448,128]{1,0:T(8,128)(2,1)S(1)} %code_b.1.refs_1_.refs_3_), channel_id=1, source_target_pairs={{0,16},{1,17},{2,18},{3,19},{4,20},{5,21},{6,22},{7,23},{8,24},{9,... | collective-permute-start | bytes 344072 | tf_op jit(solution)/shard_map/ppermute | solution.py:1378
  61.8 1.7 %collective-permute-start.28 = (bf16[2,336,128]{2,1,0:T(8,128)(2,1)S(1)}, bf16[2,336,128]{2,1,0:T(8,128)(2,1)S(1)}, u32[]{:S(2)}, u32[]{:S(2)}) collective-permute-start(bf16[2,336,128]{2,1,0:T(8,128)(2,1)S(1)} %pair_a.1.refs_1_), channel_id=1, source_target_pairs={{0,4},{1,5},{2,6},{3,7},{4,0},{5,1},{6,2},{7,3},{8,12},{9,13},{10,... | collective-permute-start | bytes 516104 | tf_op jit(solution)/shard_map/ppermute | solution.py:1378
  63.4 1.2 %collective-permute-done.23.refs_2_ = bf16[448,128]{1,0:T(8,128)(2,1)S(1)} collective-permute-done((bf16[448,128]{1,0:T(8,128)(2,1)S(1)}, bf16[448,128]{1,0:T(8,128)(2,1)S(1)}, u32[]{:S(2)}, u32[]{:S(2)}) %collective-permute-start.23) | collective-permute-done | bytes 114720 | tf_op jit(solution)/shard_map/ppermute | solution.py:1378
  64.8 3.2 %collective-permute-start.26 = (bf16[416,128]{1,0:T(8,128)(2,1)S(1)}, bf16[416,128]{1,0:T(8,128)(2,1)S(1)}, u32[]{:S(2)}, u32[]{:S(2)}) collective-permute-start(bf16[416,128]{1,0:T(8,128)(2,1)S(1)} %get-tuple-element.147.refs_3_.refs_1_), channel_id=1, source_target_pairs={{0,12},{1,13},{2,14},{3,15},{4,8},{5,9},{6,10},{7,11},{8,4},{9,5},... | collective-permute-start | bytes 319496 | tf_op jit(solution)/shard_map/ppermute | solution.py:1378
  68.1 0.6 collective-permute-start.24
  68.7 0.7 collective-permute-done.28.refs_2_
  69.6 1.1 %norms_a.1 = (f32[216,128]{1,0:T(8,128)S(1)}, f32[1,512,128]{2,1,0:T(8,128)S(1)}, f32[432,128]{1,0:T(8,128)S(1)}, f32[2,128]{1,0:T(2,128)S(1)}, f32[216,128]{1,0...) custom-call(f32[1216,128]{1,0:T(8,128)S(1)} %decode_a.1.refs_0_, ...), custom_call_target="tpu_custom_call" | custom-call | flops 1000 | bytes 1000 | tf_op jit(solution)/shard_map/norms_a/pallas_call | solution.py:1297
  70.7 2.0 %collective-permute-done.25.refs_3_ = bf16[416,128]{1,0:T(8,128)(2,1)S(1)} collective-permute-done((bf16[416,128]{1,0:T(8,128)(2,1)S(1)}, bf16[416,128]{1,0:T(8,128)(2,1)S(1)}, u32[]{:S(2)}, u32[]{:S(2)}) %collective-permute-start.25) | collective-permute-done | bytes 106528 | tf_op jit(solution)/shard_map/ppermute | solution.py:1378
  73.0 1.3 %norms_b.1 = (f32[162,128]{1,0:T(8,128)S(1)}, f32[2,512,128]{2,1,0:T(8,128)S(1)}, f32[324,128]{1,0:T(8,128)S(1)}, f32[4,128]{1,0:T(4,128)S(1)}, f32[162,128]{1,0...) custom-call(f32[1536,128]{1,0:T(8,128)S(1)} %decode_b.1.refs_0_, ...), custom_call_target="tpu_custom_call" | custom-call | flops 1000 | bytes 1000 | tf_op jit(solution)/shard_map/norms_b/pallas_call | solution.py:1297
  74.3 1.5 %collective-permute-start.30 = (f32[56,128]{1,0:T(8,128)S(1)}, f32[56,128]{1,0:T(8,128)S(1)}, u32[]{:S(2)}, u32[]{:S(2)}) collective-permute-start(f32[56,128]{1,0:T(8,128)S(1)} %get-tuple-element.150.refs_1_), channel_id=1, source_target_pairs={{0,2},{1,3},{2,0},{3,1},{4,6},{5,7},{6,4},{7,5},{8,10},{9,11},{10,... | collective-permute-start | bytes 86024 | tf_op jit(solution)/shard_map/ppermute | solution.py:1378
  75.8 0.3 collective-permute-start.29
  76.1 1.8 %moments.1 = (f32[378,128]{1,0:T(8,128)}, f32[3,512,128]{2,1,0:T(8,128)}, f32[756,128]{1,0:T(8,128)}, f32[3,2,128]{2,1,0:T(2,128)}, f32[378,128]{1,0:T(8,128)}, ...) custom-call(f32[216,128]{1,0:T(8,128)S(1)} %get-tuple-element.159.refs_0_, ...), custom_call_target="tpu_custom_call" | custom-call | flops 1000 | bytes 1000 | tf_op jit(solution)/shard_map/moments/pallas_call | solution.py:1297
  78.2 1.8 %apply.1 = (f32[378,128]{1,0:T(8,128)}, f32[3,512,128]{2,1,0:T(8,128)}, f32[756,128]{1,0:T(8,128)}, f32[3,2,128]{2,1,0:T(2,128)}, f32[3852]{0:T(1024)}, /*index=...) custom-call(s32[8,128]{1,0:T(8,128)S(1)} %iota.7.refs_0_, ...), custom_call_target="tpu_custom_call" | custom-call | flops 1000 | bytes 1000 | tf_op jit(solution)/shard_map/apply/pallas_call | solution.py:1297
  (82 shorter events, 4.9 us)
Async XLA Ops:
  3.1 13.3 %collective-permute-start = (bf16[2720,128]{1,0:T(8,128)(2,1)}, bf16[2720,128]{1,0:T(8,128)(2,1)S(1)}, u32[]{:S(2)}, u32[]{:S(2)}) collective-permute-start(bf16[2720,128]{1,0:T(8,128)(2,1)} %get-tuple-element.106.refs_4_), channel_id=1, source_target_pairs={{0,1},{1,0},{2,3},{3,2},{4,5},{5,4},{6,7},{7,6},{8,9},{9,8},{10,11... | collective-permute-start | bytes 2088968 | tf_op jit(solution)/shard_map/ppermute | solution.py:1378
  3.5 11.1 %collective-permute-start.2 = (bf16[1168,128]{1,0:T(8,128)(2,1)}, bf16[1168,128]{1,0:T(8,128)(2,1)S(1)}, u32[]{:S(2)}, u32[]{:S(2)}) collective-permute-start(bf16[1168,128]{1,0:T(8,128)(2,1)} %get-tuple-element.109), channel_id=1, source_target_pairs={{0,2},{1,3},{2,0},{3,1},{4,6},{5,7},{6,4},{7,5},{8,10},{9,11},{10,... | collective-permute-start | bytes 897032 | tf_op jit(solution)/shard_map/ppermute | solution.py:1378
  6.0 16.5 %collective-permute-start.1 = (bf16[1552,128]{1,0:T(8,128)(2,1)}, bf16[1552,128]{1,0:T(8,128)(2,1)S(1)}, u32[]{:S(2)}, u32[]{:S(2)}) collective-permute-start(bf16[1552,128]{1,0:T(8,128)(2,1)} %get-tuple-element.108), channel_id=1, source_target_pairs={{0,2},{1,3},{2,0},{3,1},{4,6},{5,7},{6,4},{7,5},{8,10},{9,11},{10,... | collective-permute-start | bytes 1191944 | tf_op jit(solution)/shard_map/ppermute | solution.py:1378
  6.1 1.1 %copy-start.9 = (bf16[2720,128]{1,0:T(8,128)(2,1)S(1)}, bf16[2720,128]{1,0:T(8,128)(2,1)}, u32[]{:S(2)}) copy-start(bf16[2720,128]{1,0:T(8,128)(2,1)} %get-tuple-element.106.refs_4_) | copy-start | bytes 2088964
  14.7 1.7 %collective-permute-start.3 = (bf16[736,128]{1,0:T(8,128)(2,1)S(1)}, bf16[736,128]{1,0:T(8,128)(2,1)S(1)}, u32[]{:S(2)}, u32[]{:S(2)}) collective-permute-start(bf16[736,128]{1,0:T(8,128)(2,1)S(1)} %get-tuple-element.113), channel_id=1, source_target_pairs={{0,1},{1,0},{2,3},{3,2},{4,5},{5,4},{6,7},{7,6},{8,9},{9,8},{10,11... | collective-permute-start | bytes 565256 | tf_op jit(solution)/shard_map/ppermute | solution.py:1378
  15.0 1.4 %collective-permute-start.4 = (bf16[432,128]{1,0:T(8,128)(2,1)S(1)}, bf16[432,128]{1,0:T(8,128)(2,1)S(1)}, u32[]{:S(2)}, u32[]{:S(2)}) collective-permute-start(bf16[432,128]{1,0:T(8,128)(2,1)S(1)} %get-tuple-element.114), channel_id=1, source_target_pairs={{0,1},{1,0},{2,3},{3,2},{4,5},{5,4},{6,7},{7,6},{8,9},{9,8},{10,11... | collective-permute-start | bytes 331784 | tf_op jit(solution)/shard_map/ppermute | solution.py:1378
  19.3 1.5 %collective-permute-start.5 = (bf16[656,128]{1,0:T(8,128)(2,1)S(1)}, bf16[656,128]{1,0:T(8,128)(2,1)S(1)}, u32[]{:S(2)}, u32[]{:S(2)}) collective-permute-start(bf16[656,128]{1,0:T(8,128)(2,1)S(1)} %get-tuple-element.118), channel_id=1, source_target_pairs={{0,1},{1,0},{2,3},{3,2},{4,5},{5,4},{6,7},{7,6},{8,9},{9,8},{10,11... | collective-permute-start | bytes 503816 | tf_op jit(solution)/shard_map/ppermute | solution.py:1378
  19.6 1.4 %collective-permute-start.6 = (bf16[656,128]{1,0:T(8,128)(2,1)S(1)}, bf16[656,128]{1,0:T(8,128)(2,1)S(1)}, u32[]{:S(2)}, u32[]{:S(2)}) collective-permute-start(bf16[656,128]{1,0:T(8,128)(2,1)S(1)} %get-tuple-element.119), channel_id=1, source_target_pairs={{0,1},{1,0},{2,3},{3,2},{4,5},{5,4},{6,7},{7,6},{8,9},{9,8},{10,11... | collective-permute-start | bytes 503816 | tf_op jit(solution)/shard_map/ppermute | solution.py:1378
  19.9 1.4 %collective-permute-start.7 = (bf16[656,128]{1,0:T(8,128)(2,1)S(1)}, bf16[656,128]{1,0:T(8,128)(2,1)S(1)}, u32[]{:S(2)}, u32[]{:S(2)}) collective-permute-start(bf16[656,128]{1,0:T(8,128)(2,1)S(1)} %get-tuple-element.120), channel_id=1, source_target_pairs={{0,1},{1,0},{2,3},{3,2},{4,5},{5,4},{6,7},{7,6},{8,9},{9,8},{10,11... | collective-permute-start | bytes 503816 | tf_op jit(solution)/shard_map/ppermute | solution.py:1378
  20.2 1.4 %collective-permute-start.8 = (bf16[656,128]{1,0:T(8,128)(2,1)S(1)}, bf16[656,128]{1,0:T(8,128)(2,1)S(1)}, u32[]{:S(2)}, u32[]{:S(2)}) collective-permute-start(bf16[656,128]{1,0:T(8,128)(2,1)S(1)} %get-tuple-element.121), channel_id=1, source_target_pairs={{0,1},{1,0},{2,3},{3,2},{4,5},{5,4},{6,7},{7,6},{8,9},{9,8},{10,11... | collective-permute-start | bytes 503816 | tf_op jit(solution)/shard_map/ppermute | solution.py:1378
  22.5 3.6 %collective-permute-start.9 = (bf16[1552,128]{1,0:T(8,128)(2,1)S(1)}, bf16[1552,128]{1,0:T(8,128)(2,1)S(1)}, u32[]{:S(2)}, u32[]{:S(2)}) collective-permute-start(bf16[1552,128]{1,0:T(8,128)(2,1)S(1)} %copy_b.1.refs_7_), channel_id=1, source_target_pairs={{0,1},{1,0},{2,3},{3,2},{4,5},{5,4},{6,7},{7,6},{8,9},{9,8},{10,11... | collective-permute-start | bytes 1191944 | tf_op jit(solution)/shard_map/ppermute | solution.py:1378
  22.7 11.6 %collective-permute-start.10 = (bf16[656,128]{1,0:T(8,128)(2,1)S(1)}, bf16[656,128]{1,0:T(8,128)(2,1)S(1)}, u32[]{:S(2)}, u32[]{:S(2)}) collective-permute-start(bf16[656,128]{1,0:T(8,128)(2,1)S(1)} %get-tuple-element.127), channel_id=1, source_target_pairs={{0,4},{1,5},{2,6},{3,7},{4,0},{5,1},{6,2},{7,3},{8,12},{9,13},{10,... | collective-permute-start | bytes 503816 | tf_op jit(solution)/shard_map/ppermute | solution.py:1378
  24.7 9.6 %collective-permute-start.11 = (bf16[656,128]{1,0:T(8,128)(2,1)S(1)}, bf16[656,128]{1,0:T(8,128)(2,1)S(1)}, u32[]{:S(2)}, u32[]{:S(2)}) collective-permute-start(bf16[656,128]{1,0:T(8,128)(2,1)S(1)} %get-tuple-element.128), channel_id=1, source_target_pairs={{0,2},{1,3},{2,0},{3,1},{4,6},{5,7},{6,4},{7,5},{8,10},{9,11},{10,... | collective-permute-start | bytes 503816 | tf_op jit(solution)/shard_map/ppermute | solution.py:1378
  26.2 8.1 %collective-permute-start.12 = (bf16[656,128]{1,0:T(8,128)(2,1)S(1)}, bf16[656,128]{1,0:T(8,128)(2,1)S(1)}, u32[]{:S(2)}, u32[]{:S(2)}) collective-permute-start(bf16[656,128]{1,0:T(8,128)(2,1)S(1)} %get-tuple-element.129), channel_id=1, source_target_pairs={{0,6},{1,7},{2,4},{3,5},{4,2},{5,3},{6,0},{7,1},{8,14},{9,15},{10,... | collective-permute-start | bytes 503816 | tf_op jit(solution)/shard_map/ppermute | solution.py:1378
  35.5 1.5 %collective-permute-start.13 = (bf16[816,128]{1,0:T(8,128)(2,1)S(1)}, bf16[816,128]{1,0:T(8,128)(2,1)S(1)}, u32[]{:S(2)}, u32[]{:S(2)}) collective-permute-start(bf16[816,128]{1,0:T(8,128)(2,1)S(1)} %get-tuple-element.134), channel_id=1, source_target_pairs={{0,1},{1,0},{2,3},{3,2},{4,5},{5,4},{6,7},{7,6},{8,9},{9,8},{10,11... | collective-permute-start | bytes 626696 | tf_op jit(solution)/shard_map/ppermute | solution.py:1378
  35.5 1.7 %collective-permute-start.14 = (bf16[816,128]{1,0:T(8,128)(2,1)S(1)}, bf16[816,128]{1,0:T(8,128)(2,1)S(1)}, u32[]{:S(2)}, u32[]{:S(2)}) collective-permute-start(bf16[816,128]{1,0:T(8,128)(2,1)S(1)} %get-tuple-element.135), channel_id=1, source_target_pairs={{0,1},{1,0},{2,3},{3,2},{4,5},{5,4},{6,7},{7,6},{8,9},{9,8},{10,11... | collective-permute-start | bytes 626696 | tf_op jit(solution)/shard_map/ppermute | solution.py:1378
  36.0 1.5 %collective-permute-start.15 = (bf16[816,128]{1,0:T(8,128)(2,1)S(1)}, bf16[816,128]{1,0:T(8,128)(2,1)S(1)}, u32[]{:S(2)}, u32[]{:S(2)}) collective-permute-start(bf16[816,128]{1,0:T(8,128)(2,1)S(1)} %get-tuple-element.136), channel_id=1, source_target_pairs={{0,1},{1,0},{2,3},{3,2},{4,5},{5,4},{6,7},{7,6},{8,9},{9,8},{10,11... | collective-permute-start | bytes 626696 | tf_op jit(solution)/shard_map/ppermute | solution.py:1378
  36.1 1.8 %collective-permute-start.16 = (bf16[816,128]{1,0:T(8,128)(2,1)S(1)}, bf16[816,128]{1,0:T(8,128)(2,1)S(1)}, u32[]{:S(2)}, u32[]{:S(2)}) collective-permute-start(bf16[816,128]{1,0:T(8,128)(2,1)S(1)} %get-tuple-element.137), channel_id=1, source_target_pairs={{0,1},{1,0},{2,3},{3,2},{4,5},{5,4},{6,7},{7,6},{8,9},{9,8},{10,11... | collective-permute-start | bytes 626696 | tf_op jit(solution)/shard_map/ppermute | solution.py:1378
  38.8 13.9 %collective-permute-start.17 = (bf16[864,128]{1,0:T(8,128)(2,1)S(1)}, bf16[864,128]{1,0:T(8,128)(2,1)S(1)}, u32[]{:S(2)}, u32[]{:S(2)}) collective-permute-start(bf16[864,128]{1,0:T(8,128)(2,1)S(1)} %get-tuple-element.140), channel_id=1, source_target_pairs={{0,4},{1,5},{2,6},{3,7},{4,0},{5,1},{6,2},{7,3},{8,12},{9,13},{10,... | collective-permute-start | bytes 663560 | tf_op jit(solution)/shard_map/ppermute | solution.py:1378
  40.9 11.8 %collective-permute-start.18 = (bf16[864,128]{1,0:T(8,128)(2,1)S(1)}, bf16[864,128]{1,0:T(8,128)(2,1)S(1)}, u32[]{:S(2)}, u32[]{:S(2)}) collective-permute-start(bf16[864,128]{1,0:T(8,128)(2,1)S(1)} %get-tuple-element.141), channel_id=1, source_target_pairs={{0,2},{1,3},{2,0},{3,1},{4,6},{5,7},{6,4},{7,5},{8,10},{9,11},{10,... | collective-permute-start | bytes 663560 | tf_op jit(solution)/shard_map/ppermute | solution.py:1378
  42.4 10.3 %collective-permute-start.19 = (bf16[864,128]{1,0:T(8,128)(2,1)S(1)}, bf16[864,128]{1,0:T(8,128)(2,1)S(1)}, u32[]{:S(2)}, u32[]{:S(2)}) collective-permute-start(bf16[864,128]{1,0:T(8,128)(2,1)S(1)} %get-tuple-element.142), channel_id=1, source_target_pairs={{0,6},{1,7},{2,4},{3,5},{4,2},{5,3},{6,0},{7,1},{8,14},{9,15},{10,... | collective-permute-start | bytes 663560 | tf_op jit(solution)/shard_map/ppermute | solution.py:1378
  42.5 4.5 %collective-permute-start.20 = (bf16[336,128]{1,0:T(8,128)(2,1)S(1)}, bf16[336,128]{1,0:T(8,128)(2,1)S(1)}, u32[]{:S(2)}, u32[]{:S(2)}) collective-permute-start(bf16[336,128]{1,0:T(8,128)(2,1)S(1)} %get-tuple-element.143), channel_id=1, source_target_pairs={{0,8},{1,9},{2,10},{3,11},{4,12},{5,13},{6,14},{7,15},{8,0},{9,1},... | collective-permute-start | bytes 258056 | tf_op jit(solution)/shard_map/ppermute | solution.py:1378
  47.0 22.6 %copy-start.8 = (f32[378,128]{1,0:T(8,128)S(1)}, f32[378,128]{1,0:T(8,128)}, u32[]{:S(2)}) copy-start(f32[378,128]{1,0:T(8,128)} %refs_12_.3) | copy-start | bytes 580612
  47.1 5.5 %collective-permute-start.21 = (bf16[336,128]{1,0:T(8,128)(2,1)S(1)}, bf16[336,128]{1,0:T(8,128)(2,1)S(1)}, u32[]{:S(2)}, u32[]{:S(2)}) collective-permute-start(bf16[336,128]{1,0:T(8,128)(2,1)S(1)} %code_a.1.refs_1_.refs_3_), channel_id=1, source_target_pairs={{0,16},{1,17},{2,18},{3,19},{4,20},{5,21},{6,22},{7,23},{8,24},{9,... | collective-permute-start | bytes 258056 | tf_op jit(solution)/shard_map/ppermute | solution.py:1378
  52.5 17.0 %copy-start.6 = (f32[378,128]{1,0:T(8,128)S(1)}, f32[378,128]{1,0:T(8,128)}, u32[]{:S(2)}) copy-start(f32[378,128]{1,0:T(8,128)} %refs_5_.3) | copy-start | bytes 580612
  52.6 17.0 %copy-start.7 = (f32[378,128]{1,0:T(8,128)S(1)}, f32[378,128]{1,0:T(8,128)}, u32[]{:S(2)}) copy-start(f32[378,128]{1,0:T(8,128)} %refs_8_.4) | copy-start | bytes 580612
  52.7 16.8 %copy-start = (f32[3,512,128]{2,1,0:T(8,128)S(1)}, f32[3,512,128]{2,1,0:T(8,128)}, u32[]{:S(2)}) copy-start(f32[3,512,128]{2,1,0:T(8,128)} %refs_6_.5) | copy-start | bytes 2359300
  52.7 16.8 %copy-start.1 = (f32[3,512,128]{2,1,0:T(8,128)S(1)}, f32[3,512,128]{2,1,0:T(8,128)}, u32[]{:S(2)}) copy-start(f32[3,512,128]{2,1,0:T(8,128)} %refs_9_.3) | copy-start | bytes 2359300
  52.8 16.8 %copy-start.2 = (f32[3,512,128]{2,1,0:T(8,128)S(1)}, f32[3,512,128]{2,1,0:T(8,128)}, u32[]{:S(2)}) copy-start(f32[3,512,128]{2,1,0:T(8,128)} %refs_13_.3) | copy-start | bytes 2359300
  52.8 16.8 %copy-start.3 = (f32[128,756]{0,1:T(8,128)S(1)}, f32[128,756]{0,1:T(8,128)}, u32[]{:S(2)}) copy-start(f32[128,756]{0,1:T(8,128)} %param.23) | copy-start | bytes 1161220
  52.8 16.8 %copy-start.4 = (f32[128,756]{0,1:T(8,128)S(1)}, f32[128,756]{0,1:T(8,128)}, u32[]{:S(2)}) copy-start(f32[128,756]{0,1:T(8,128)} %param.28) | copy-start | bytes 1161220
  52.8 16.8 %copy-start.5 = (f32[128,756]{0,1:T(8,128)S(1)}, f32[128,756]{0,1:T(8,128)}, u32[]{:S(2)}) copy-start(f32[128,756]{0,1:T(8,128)} %param.33) | copy-start | bytes 1161220
  52.8 16.8 %copy-start.12 = (f32[3,2,128]{2,1,0:T(2,128)S(1)}, f32[3,2,128]{2,1,0:T(2,128)}, u32[]{:S(2)}) copy-start(f32[3,2,128]{2,1,0:T(2,128)} %refs_8_.5) | copy-start | bytes 9220
  52.8 16.8 %copy-start.13 = (f32[3,2,128]{2,1,0:T(2,128)S(1)}, f32[3,2,128]{2,1,0:T(2,128)}, u32[]{:S(2)}) copy-start(f32[3,2,128]{2,1,0:T(2,128)} %refs_11_.5) | copy-start | bytes 9220
  52.8 16.8 %copy-start.14 = (f32[3,2,128]{2,1,0:T(2,128)S(1)}, f32[3,2,128]{2,1,0:T(2,128)}, u32[]{:S(2)}) copy-start(f32[3,2,128]{2,1,0:T(2,128)} %refs_15_.1) | copy-start | bytes 9220
  53.3 5.4 %collective-permute-start.22 = (bf16[448,128]{1,0:T(8,128)(2,1)S(1)}, bf16[448,128]{1,0:T(8,128)(2,1)S(1)}, u32[]{:S(2)}, u32[]{:S(2)}) collective-permute-start(bf16[448,128]{1,0:T(8,128)(2,1)S(1)} %get-tuple-element.146), channel_id=1, source_target_pairs={{0,8},{1,9},{2,10},{3,11},{4,12},{5,13},{6,14},{7,15},{8,0},{9,1},... | collective-permute-start | bytes 344072 | tf_op jit(solution)/shard_map/ppermute | solution.py:1378
  55.3 6.4 %collective-permute-start.27 = (bf16[336,128]{1,0:T(8,128)(2,1)S(1)}, bf16[336,128]{1,0:T(8,128)(2,1)S(1)}, u32[]{:S(2)}, u32[]{:S(2)}) collective-permute-start(bf16[336,128]{1,0:T(8,128)(2,1)S(1)} %recode_4_a.1.refs_6_.refs_1_), channel_id=1, source_target_pairs={{0,8},{1,9},{2,10},{3,11},{4,12},{5,13},{6,14},{7,15},{8,0},{9,1},... | collective-permute-start | bytes 258056 | tf_op jit(solution)/shard_map/ppermute | solution.py:1378
  58.9 5.8 %collective-permute-start.23 = (bf16[448,128]{1,0:T(8,128)(2,1)S(1)}, bf16[448,128]{1,0:T(8,128)(2,1)S(1)}, u32[]{:S(2)}, u32[]{:S(2)}) collective-permute-start(bf16[448,128]{1,0:T(8,128)(2,1)S(1)} %code_b.1.refs_1_.refs_3_), channel_id=1, source_target_pairs={{0,16},{1,17},{2,18},{3,19},{4,20},{5,21},{6,22},{7,23},{8,24},{9,... | collective-permute-start | bytes 344072 | tf_op jit(solution)/shard_map/ppermute | solution.py:1378
  61.8 7.6 %collective-permute-start.28 = (bf16[2,336,128]{2,1,0:T(8,128)(2,1)S(1)}, bf16[2,336,128]{2,1,0:T(8,128)(2,1)S(1)}, u32[]{:S(2)}, u32[]{:S(2)}) collective-permute-start(bf16[2,336,128]{2,1,0:T(8,128)(2,1)S(1)} %pair_a.1.refs_1_), channel_id=1, source_target_pairs={{0,4},{1,5},{2,6},{3,7},{4,0},{5,1},{6,2},{7,3},{8,12},{9,13},{10,... | collective-permute-start | bytes 516104 | tf_op jit(solution)/shard_map/ppermute | solution.py:1378
  64.8 5.9 %collective-permute-start.26 = (bf16[416,128]{1,0:T(8,128)(2,1)S(1)}, bf16[416,128]{1,0:T(8,128)(2,1)S(1)}, u32[]{:S(2)}, u32[]{:S(2)}) collective-permute-start(bf16[416,128]{1,0:T(8,128)(2,1)S(1)} %get-tuple-element.147.refs_3_.refs_1_), channel_id=1, source_target_pairs={{0,12},{1,13},{2,14},{3,15},{4,8},{5,9},{6,10},{7,11},{8,4},{9,5},... | collective-permute-start | bytes 319496 | tf_op jit(solution)/shard_map/ppermute | solution.py:1378
  68.0 4.7 %collective-permute-start.25 = (bf16[416,128]{1,0:T(8,128)(2,1)S(1)}, bf16[416,128]{1,0:T(8,128)(2,1)S(1)}, u32[]{:S(2)}, u32[]{:S(2)}) collective-permute-start(bf16[416,128]{1,0:T(8,128)(2,1)S(1)} %get-tuple-element.147.refs_3_.refs_1_), channel_id=1, source_target_pairs={{0,8},{1,9},{2,10},{3,11},{4,12},{5,13},{6,14},{7,15},{8,0},{9,1},... | collective-permute-start | bytes 319496 | tf_op jit(solution)/shard_map/ppermute | solution.py:1378
  68.1 4.7 %collective-permute-start.24 = (bf16[416,128]{1,0:T(8,128)(2,1)S(1)}, bf16[416,128]{1,0:T(8,128)(2,1)S(1)}, u32[]{:S(2)}, u32[]{:S(2)}) collective-permute-start(bf16[416,128]{1,0:T(8,128)(2,1)S(1)} %get-tuple-element.147.refs_3_.refs_1_), channel_id=1, source_target_pairs={{0,4},{1,5},{2,6},{3,7},{4,0},{5,1},{6,2},{7,3},{8,12},{9,13},{10,... | collective-permute-start | bytes 319496 | tf_op jit(solution)/shard_map/ppermute | solution.py:1378
  74.3 3.7 %collective-permute-start.31 = (f32[56,128]{1,0:T(8,128)S(1)}, f32[56,128]{1,0:T(8,128)S(1)}, u32[]{:S(2)}, u32[]{:S(2)}) collective-permute-start(f32[56,128]{1,0:T(8,128)S(1)} %get-tuple-element.150.refs_1_), channel_id=1, source_target_pairs={{0,3},{1,2},{2,1},{3,0},{4,7},{5,6},{6,5},{7,4},{8,11},{9,10},{10,... | collective-permute-start | bytes 86024 | tf_op jit(solution)/shard_map/ppermute | solution.py:1378
  74.3 3.9 %collective-permute-start.30 = (f32[56,128]{1,0:T(8,128)S(1)}, f32[56,128]{1,0:T(8,128)S(1)}, u32[]{:S(2)}, u32[]{:S(2)}) collective-permute-start(f32[56,128]{1,0:T(8,128)S(1)} %get-tuple-element.150.refs_1_), channel_id=1, source_target_pairs={{0,2},{1,3},{2,0},{3,1},{4,6},{5,7},{6,4},{7,5},{8,10},{9,11},{10,... | collective-permute-start | bytes 86024 | tf_op jit(solution)/shard_map/ppermute | solution.py:1378
  75.8 2.4 %collective-permute-start.29 = (f32[56,128]{1,0:T(8,128)S(1)}, f32[56,128]{1,0:T(8,128)S(1)}, u32[]{:S(2)}, u32[]{:S(2)}) collective-permute-start(f32[56,128]{1,0:T(8,128)S(1)} %get-tuple-element.150.refs_1_), channel_id=1, source_target_pairs={{0,1},{1,0},{2,3},{3,2},{4,5},{5,4},{6,7},{7,6},{8,9},{9,8},{10,11... | collective-permute-start | bytes 86024 | tf_op jit(solution)/shard_map/ppermute | solution.py:1378
  76.1 2.1 %copy-start.11 = (f32[3852]{0:T(1024)S(1)}, f32[3852]{0:T(1024)}, u32[]{:S(2)}) copy-start(f32[3852]{0:T(1024)} %refs_17_.1) | copy-start | bytes 46228
  76.1 2.1 %copy-start.16 = (f32[3852]{0:T(1024)S(1)}, f32[3852]{0:T(1024)}, u32[]{:S(2)}) copy-start(f32[3852]{0:T(1024)} %refs_18_.1) | copy-start | bytes 46228
  76.1 2.1 %copy-start.17 = (f32[3852]{0:T(1024)S(1)}, f32[3852]{0:T(1024)}, u32[]{:S(2)}) copy-start(f32[3852]{0:T(1024)} %refs_19_.1) | copy-start | bytes 46228
  (4 other events, 2.8 us)
